TPU v7x, 32 devices: a whole 2x2x4 slice. The times are simulated.
32 devices in a mesh: grp: 2 (over x), slab: 16 (over z, y, core).
Axes of the slice: x: 2, y: 2, z: 4, core: 2. Of those that a mesh axis runs over, the one named last changes fastest.
Arguments:
- queries: bfloat16 [4096, 1024], P(('grp', 'slab')), parts along dimension 0, may hold values from 0.0099487305 to 10
- library: bfloat16 [16384, 1024], P(('grp', 'slab')), parts along dimension 0, may hold values from 0.0099487305 to 10
- bucket: int32 [4096, 1], P(('grp', 'slab')), parts along dimension 0, may hold values from 0 to 15; in each aligned block of 128 rows (0 to 127, 128 to 255, ...) at most 16 rows name the same one
- query_charge: int32 [4096], P(('grp', 'slab')), parts along dimension 0, may hold values from 1 to 8
- library_charge: int32 [16384], P(('grp', 'slab')), parts along dimension 0, may hold values from 1 to 8
Outputs:
- scores: bfloat16 [4096, 1536], P(('grp', 'slab')), parts along dimension 0
There are 2 independent parts, one for each index of `grp`. A program takes and returns all parts, laid end to end along the dimension named above; each array names one. Nothing has to cross between parts.
Inputs may be any that keep to these rules, and one draw needn't show every extreme that they name: `bucket`: within the rows of one device (aligned blocks of 128 rows) no slab is named more than 16 times, a bound that some block reaches.
All inputs are finite; a program needn't handle non-finite values.
Results may differ from a plain program's by a relative error of at most 0.0033.
Values may be sent and summed in bfloat16 or wider, within the bound.
No kernel may reach another device: no remote copies, remote signals or barrier semaphores. Data moves between devices by JAX's collectives and lax.ppermute only.
A program may use at most 64 MiB of HBM per device.

v0:
```python
import jax
import jax.numpy as jnp
from jax import lax
from jax.sharding import PartitionSpec as P

EPS = 1e-06


def passed_along(value, axis, steps):
    count = lax.axis_size(axis)
    pairs = [(source, (source + steps) % count) for source in range(count)]
    return lax.ppermute(value, axis, pairs)


def normalize(rows):
    values = rows.astype(jnp.float32)
    return (values * lax.rsqrt(jnp.sum(values * values, axis=-1, keepdims=True) + EPS)).astype(
        jnp.bfloat16
    )


def score_block(rows, row_charge, lib_rows, lib_charge):
    raw = lax.dot_general(
        rows, lib_rows, (((1,), (1,)), ((), ())), preferred_element_type=jnp.float32
    )
    keep = (
        jnp.abs(row_charge.astype(jnp.float32)[:, None] - lib_charge.astype(jnp.float32)[None, :])
        <= 2.0
    )
    return jnp.where(keep, raw, 0.0).astype(jnp.bfloat16)


def selector(slot_ids, total):
    places = jnp.arange(total, dtype=jnp.int32)
    return (places[:, None] == slot_ids[None, :]).astype(jnp.bfloat16)


def pick_rows(select, flat):
    return lax.dot_general(
        select, flat, (((0,), (0,)), ((), ())), preferred_element_type=jnp.float32
    ).astype(jnp.bfloat16)


def place_rows(select, values):
    return jnp.dot(select, values, preferred_element_type=jnp.float32).astype(jnp.bfloat16)


def per_device(queries, library, bucket, query_charge, library_charge):
    n_slab = lax.axis_size("slab")
    q_rows = queries.shape[0]
    width = queries.shape[1]
    cap = 2 * q_rows // n_slab
    query_unit = normalize(queries)
    library_unit = normalize(library)
    lib_charge = library_charge.astype(jnp.bfloat16)
    qcharge_col = query_charge.astype(jnp.bfloat16)[:, None]
    target = bucket[:, 0]
    positions = jnp.arange(q_rows, dtype=jnp.int32)
    earlier = (target[:, None] == target[None, :]) & (positions[None, :] < positions[:, None])
    rank = jnp.sum(earlier.astype(jnp.int32), axis=1)
    select_home = selector(target * cap + rank, n_slab * cap)
    outgoing = place_rows(select_home, query_unit).reshape(n_slab, cap, width)
    out_charge = place_rows(select_home, qcharge_col).reshape(n_slab, cap)
    below_rows, below_charge = passed_along((library_unit, lib_charge), "slab", 1)
    above_rows, above_charge = passed_along((library_unit, lib_charge), "slab", -1)
    rows = lax.all_to_all(outgoing, "slab", split_axis=0, concat_axis=0, tiled=True)
    charges = lax.all_to_all(out_charge, "slab", split_axis=0, concat_axis=0, tiled=True)
    count = rows.shape[1]
    flat = rows.reshape(n_slab * count, width)
    flat_charge = charges.reshape(n_slab * count)
    middle = score_block(flat, flat_charge, library_unit, lib_charge)
    lower = score_block(flat, flat_charge, below_rows, below_charge)
    upper = score_block(flat, flat_charge, above_rows, above_charge)
    joined = jnp.concatenate([lower, middle, upper], axis=1)
    joined = joined.reshape(n_slab, count, joined.shape[1])
    returned = lax.all_to_all(joined, "slab", split_axis=0, concat_axis=0, tiled=True)
    flat_back = returned.reshape(returned.shape[0] * returned.shape[1], returned.shape[2])
    return pick_rows(select_home, flat_back)


def solution(mesh):
    placed = (
        P(("grp", "slab"), None),
        P(("grp", "slab"), None),
        P(("grp", "slab"), None),
        P(("grp", "slab")),
        P(("grp", "slab")),
    )
    return jax.shard_map(
        per_device, mesh=mesh, in_specs=placed, out_specs=P(("grp", "slab"), None), check_vma=False
    )
```

profile of v0, /device:TPU:0, one launch (start us, length us, event | category | flops | bytes accessed | tf_op | source)
XLA Modules:
  0.0 80.3 jit_solution(9716600885288865735)
XLA Ops:
  0.0 0.0 copy-start
  0.0 0.9 %convert_reduce_fusion = s32[128]{0:T(128)S(1)} fusion(s32[128]{0:T(128)} %bitcast.22), kind=kLoop, calls=%fused_computation.24 | loop fusion | flops 81792 | bytes 1024 | tf_op jit(solution)/shard_map/reduce_sum | solution.py:60
  0.9 0.7 multiply_add_fusion
  1.6 0.8 fusion.7
  2.4 0.7 all_to_all.16
  3.1 7.4 %all-to-all-start = ((bf16[16,1,16]{2,1,0:T(2,128)(2,1)}), bf16[16,1,16]{2,1,0:T(2,128)(2,1)S(1)}, u32[]{:S(2)}, u32[]{:S(2)}) async-start(bf16[16,1,16]{2,1,0:T(2,128)(2,1)} %all_to_all.16), calls=%async_computation | async-start | bytes 16384 | tf_op jit(solution)/shard_map/all_to_all | solution.py:67
  10.5 1.1 %fusion.3 = f32[128]{0:T(128)S(1)} fusion(bf16[128,1024]{1,0:T(8,128)(2,1)} %param.5), kind=kLoop, calls=%fused_computation.11 | loop fusion | flops 393088 | bytes 262656 | tf_op jit(solution)/shard_map/reduce_sum | solution.py:17
  11.6 2.1 %convolution_convert_fusion.1 = bf16[256,1024]{1,0:T(8,128)(2,1)} fusion(bf16[128,1024]{1,0:T(8,128)(2,1)} %param.5, f32[128]{0:T(128)S(1)} %add_rsqrt_fusion.1, s32[128]{0:T(128)S(1)} %multiply_add_fusion), kind=kOutput, calls=%fused_computation.5 | convolution fusion | flops 67796992 | bytes 787456 | tf_op jit(solution)/shard_map/dot_general | solution.py:45
  13.7 0.0 copy-done
  13.7 0.3 fusion
  14.0 2.8 %all-to-all-done = bf16[16,1,16]{2,1,0:T(2,128)(2,1)S(1)} async-done(((bf16[16,1,16]{2,1,0:T(2,128)(2,1)}), bf16[16,1,16]{2,1,0:T(2,128)(2,1)S(1)}, u32[]{:S(2)}, u32[]{:S(2)}) %all-to-all-start) | async-done | bytes 544 | tf_op jit(solution)/shard_map/all_to_all | solution.py:67
  16.8 3.6 %all-to-all-start.1 = ((bf16[16,16,1024]{2,1,0:T(8,128)(2,1)}), bf16[16,16,1024]{2,1,0:T(8,128)(2,1)S(1)}, u32[]{:S(2)}, u32[]{:S(2)}) async-start(bf16[16,16,1024]{2,1,0:T(8,128)(2,1)} %bitcast.3), calls=%async_computation.1 | async-start | bytes 1048576 | tf_op jit(solution)/shard_map/all_to_all | solution.py:66
  20.4 0.0 copy-start.1
  20.4 0.2 fusion.1
  20.7 4.4 %collective-permute-start.3 = (bf16[512,1024]{1,0:T(8,128)(2,1)S(1)}, bf16[512,1024]{1,0:T(8,128)(2,1)S(1)}, u32[]{:S(2)}, u32[]{:S(2)}) collective-permute-start(bf16[512,1024]{1,0:T(8,128)(2,1)S(1)} %fusion.1), channel_id=1, source_target_pairs={{0,15},{1,0},{2,1},{3,2},{4,3},{5,4},{6,5},{7,6},{8,7},{9,8},{10,9... | collective-permute-start | bytes 3145736 | tf_op jit(solution)/shard_map/ppermute | solution.py:12
  25.1 0.0 collective-permute-start.1
  25.1 0.0 copy-done.1
  25.1 0.1 collective-permute-start
  25.1 4.4 %collective-permute-start.2 = (bf16[512]{0:T(512)(128)(2,1)S(1)}, bf16[512]{0:T(512)(128)(2,1)S(1)}, u32[]{:S(2)}, u32[]{:S(2)}) collective-permute-start(bf16[512]{0:T(512)(128)(2,1)S(1)} %get-tuple-element.6), channel_id=1, source_target_pairs={{0,15},{1,0},{2,1},{3,2},{4,3},{5,4},{6,5},{7,6},{8,7},{9,8},{10,9... | collective-permute-start | bytes 3080 | tf_op jit(solution)/shard_map/ppermute | solution.py:12
  29.6 0.1 reshape.58
  29.7 16.5 %collective-permute-done = bf16[512]{0:T(512)(128)(2,1)S(1)} collective-permute-done((bf16[512]{0:T(512)(128)(2,1)S(1)}, bf16[512]{0:T(512)(128)(2,1)S(1)}, u32[]{:S(2)}, u32[]{:S(2)}) %collective-permute-start) | collective-permute-done | bytes 1056 | tf_op jit(solution)/shard_map/ppermute | solution.py:12
  46.2 0.0 collective-permute-done.2
  46.2 0.0 all-to-all-done.1
  46.3 0.5 fusion.2
  46.7 0.0 collective-permute-done.3
  46.8 0.5 fusion.15
  47.2 0.0 collective-permute-done.1
  47.2 1.7 %select_convert_fusion.1 = (bf16[256,512]{1,0:T(8,128)(2,1)S(1)}, bf16[256,512]{1,0:T(8,128)(2,1)S(1)}) fusion(f32[512]{0:T(512)S(1)} %convert_element_type.68, f32[256]{0:T(256)S(1)} %reshape.58, bf16[256,512]{1,0:T(8,128)(2,1)S(1)} %fusion.15, f32[512]{0:T(512)S(1)} %convert_element_type.77, bf16[256,1024]{1,0:T(8,128)(2,1)S(1)} %bitcast.21, ...), kind=kOutput, calls=%fused_computation.16 | convolution fusion | flops 269484032 | bytes 2364416 | tf_op jit(solution)/shard_map/dot_general | solution.py:23
  49.0 0.1 pad_maximum_fusion
  49.1 30.2 %all_to_all.20 = bf16[16,16,1536]{2,1,0:T(8,128)(2,1)S(1)} all-to-all(bf16[16,16,1536]{2,1,0:T(8,128)(2,1)S(1)} %bitcast.17), channel_id=1, replica_groups=mesh['grp'=2,'slab'=16] {'slab'}, dimensions={0} | all-to-all | bytes 1572864 | tf_op jit(solution)/shard_map/all_to_all | solution.py:76
  79.2 1.1 %convolution_convert_fusion = bf16[128,1536]{1,0:T(8,128)(2,1)} fusion(bf16[256,1536]{1,0:T(8,128)(2,1)S(1)} %bitcast.18, s32[128]{0:T(128)S(1)} %multiply_add_fusion), kind=kOutput, calls=%fused_computation.2 | convolution fusion | flops 100892672 | bytes 1180160 | tf_op jit(solution)/shard_map/dot_general | solution.py:39
  (7 shorter events, 0.1 us)
Async XLA Ops:
  0.0 13.7 %copy-start = (bf16[512,1024]{1,0:T(8,128)(2,1)S(1)}, bf16[512,1024]{1,0:T(8,128)(2,1)}, u32[]{:S(2)}) copy-start(bf16[512,1024]{1,0:T(8,128)(2,1)} %param.6) | copy-start | bytes 3145732
  3.1 13.7 %all-to-all-start = ((bf16[16,1,16]{2,1,0:T(2,128)(2,1)}), bf16[16,1,16]{2,1,0:T(2,128)(2,1)S(1)}, u32[]{:S(2)}, u32[]{:S(2)}) async-start(bf16[16,1,16]{2,1,0:T(2,128)(2,1)} %all_to_all.16), calls=%async_computation | async-start | bytes 16384 | tf_op jit(solution)/shard_map/all_to_all | solution.py:67
  16.8 29.4 %all-to-all-start.1 = ((bf16[16,16,1024]{2,1,0:T(8,128)(2,1)}), bf16[16,16,1024]{2,1,0:T(8,128)(2,1)S(1)}, u32[]{:S(2)}, u32[]{:S(2)}) async-start(bf16[16,16,1024]{2,1,0:T(8,128)(2,1)} %bitcast.3), calls=%async_computation.1 | async-start | bytes 1048576 | tf_op jit(solution)/shard_map/all_to_all | solution.py:66
  20.4 4.7 %copy-start.1 = (s32[512]{0:T(512)S(1)}, s32[512]{0:T(512)}, u32[]{:S(2)}) copy-start(s32[512]{0:T(512)} %param.9) | copy-start | bytes 6148
  20.7 26.1 %collective-permute-start.3 = (bf16[512,1024]{1,0:T(8,128)(2,1)S(1)}, bf16[512,1024]{1,0:T(8,128)(2,1)S(1)}, u32[]{:S(2)}, u32[]{:S(2)}) collective-permute-start(bf16[512,1024]{1,0:T(8,128)(2,1)S(1)} %fusion.1), channel_id=1, source_target_pairs={{0,15},{1,0},{2,1},{3,2},{4,3},{5,4},{6,5},{7,6},{8,7},{9,8},{10,9... | collective-permute-start | bytes 3145736 | tf_op jit(solution)/shard_map/ppermute | solution.py:12
  25.1 22.2 %collective-permute-start.1 = (bf16[512,1024]{1,0:T(8,128)(2,1)S(1)}, bf16[512,1024]{1,0:T(8,128)(2,1)}, u32[]{:S(2)}, u32[]{:S(2)}) collective-permute-start(bf16[512,1024]{1,0:T(8,128)(2,1)S(1)} %fusion.1), channel_id=1, source_target_pairs={{0,1},{1,2},{2,3},{3,4},{4,5},{5,6},{6,7},{7,8},{8,9},{9,10},{10,1... | collective-permute-start | bytes 3145736 | tf_op jit(solution)/shard_map/ppermute | solution.py:12
  25.1 21.2 %collective-permute-start = (bf16[512]{0:T(512)(128)(2,1)S(1)}, bf16[512]{0:T(512)(128)(2,1)S(1)}, u32[]{:S(2)}, u32[]{:S(2)}) collective-permute-start(bf16[512]{0:T(512)(128)(2,1)S(1)} %get-tuple-element.6), channel_id=1, source_target_pairs={{0,1},{1,2},{2,3},{3,4},{4,5},{5,6},{6,7},{7,8},{8,9},{9,10},{10,1... | collective-permute-start | bytes 3080 | tf_op jit(solution)/shard_map/ppermute | solution.py:12
  25.1 21.1 %collective-permute-start.2 = (bf16[512]{0:T(512)(128)(2,1)S(1)}, bf16[512]{0:T(512)(128)(2,1)S(1)}, u32[]{:S(2)}, u32[]{:S(2)}) collective-permute-start(bf16[512]{0:T(512)(128)(2,1)S(1)} %get-tuple-element.6), channel_id=1, source_target_pairs={{0,15},{1,0},{2,1},{3,2},{4,3},{5,4},{6,5},{7,6},{8,7},{9,8},{10,9... | collective-permute-start | bytes 3080 | tf_op jit(solution)/shard_map/ppermute | solution.py:12
where the time goes:
time: 81.1 us; the launch traced here: 80.3 us
  blocking collectives  30.2 us (37%)
  starting transfers between devices  19.8 us (24%)
  waiting for transfers between devices  19.4 us (24%)
  matrix products  6.71 us (8%)
  other arithmetic  3.3 us (4%)
    all_to_all x1, blocking collectives, per_device(): lax.all_to_all(joined, 'slab', split_axis=0, concat_axis=0, tiled=True)  30.2 us
    ppermute x4, waiting for transfers between devices, passed_along(): return lax.ppermute(value, axis, pairs)  16.6 us
    ppermute x4, starting transfers between devices, passed_along(): return lax.ppermute(value, axis, pairs)  8.89 us
    all_to_all x1, starting transfers between devices, per_device(): lax.all_to_all(out_charge, 'slab', split_axis=0, concat_axis=0, tiled=True)  7.39 us
    all_to_all x1, starting transfers between devices, per_device(): lax.all_to_all(outgoing, 'slab', split_axis=0, concat_axis=0, tiled=True)  3.57 us
    dot_general x2, matrix products, place_rows(): jnp.dot(select, values, preferred_element_type=jnp.float32)  2.94 us
    all_to_all x1, waiting for transfers between devices, per_device(): lax.all_to_all(out_charge, 'slab', split_axis=0, concat_axis=0, tiled=True)  2.8 us
    dot_general x3, matrix products, score_block(): lax.dot_general(rows, lib_rows, (((1,), (1,)), ((), ())), preferred_eleme...  2.7 us
  transfers between devices with their start and end apart: 6, of which 2 were waited for; matrix products, arithmetic and copies ran while one was open for 6% of the time, Pallas kernels for 0%

commit v1 on v0

--- a/solution.py
+++ b/solution.py
@@ -1,9 +1,18 @@
+import functools
+
 import jax
 import jax.numpy as jnp
 from jax import lax
+from jax.experimental import pallas as pl
+from jax.experimental.pallas import tpu as pltpu
 from jax.sharding import PartitionSpec as P
 
 EPS = 1e-06
+PLANE = 4
+CAP = 16
+META = 16
+F32 = jnp.float32
+BF16 = jnp.bfloat16
 
 
 def passed_along(value, axis, steps):
@@ -13,47 +22,40 @@
 
 
 def normalize(rows):
-    values = rows.astype(jnp.float32)
-    return (values * lax.rsqrt(jnp.sum(values * values, axis=-1, keepdims=True) + EPS)).astype(
-        jnp.bfloat16
-    )
+    values = rows.astype(F32)
+    return (values * lax.rsqrt(jnp.sum(values * values, axis=-1, keepdims=True) + EPS)).astype(BF16)
 
 
 def score_block(rows, row_charge, lib_rows, lib_charge):
-    raw = lax.dot_general(
-        rows, lib_rows, (((1,), (1,)), ((), ())), preferred_element_type=jnp.float32
-    )
-    keep = (
-        jnp.abs(row_charge.astype(jnp.float32)[:, None] - lib_charge.astype(jnp.float32)[None, :])
-        <= 2.0
-    )
-    return jnp.where(keep, raw, 0.0).astype(jnp.bfloat16)
+    raw = lax.dot_general(rows, lib_rows, (((1,), (1,)), ((), ())), preferred_element_type=F32)
+    keep = jnp.abs(row_charge.astype(F32)[:, None] - lib_charge.astype(F32)[None, :]) <= 2.0
+    return jnp.where(keep, raw, 0.0).astype(BF16)
 
 
 def selector(slot_ids, total):
     places = jnp.arange(total, dtype=jnp.int32)
-    return (places[:, None] == slot_ids[None, :]).astype(jnp.bfloat16)
+    return (places[:, None] == slot_ids[None, :]).astype(BF16)
 
 
 def pick_rows(select, flat):
     return lax.dot_general(
-        select, flat, (((0,), (0,)), ((), ())), preferred_element_type=jnp.float32
-    ).astype(jnp.bfloat16)
+        select, flat, (((0,), (0,)), ((), ())), preferred_element_type=F32
+    ).astype(BF16)
 
 
 def place_rows(select, values):
-    return jnp.dot(select, values, preferred_element_type=jnp.float32).astype(jnp.bfloat16)
-
-
-def per_device(queries, library, bucket, query_charge, library_charge):
+    return jnp.dot(select, values, preferred_element_type=F32).astype(BF16)
+
+
+def general_plan(queries, library, bucket, query_charge, library_charge):
     n_slab = lax.axis_size("slab")
     q_rows = queries.shape[0]
     width = queries.shape[1]
     cap = 2 * q_rows // n_slab
     query_unit = normalize(queries)
     library_unit = normalize(library)
-    lib_charge = library_charge.astype(jnp.bfloat16)
-    qcharge_col = query_charge.astype(jnp.bfloat16)[:, None]
+    lib_charge = library_charge.astype(BF16)
+    qcharge_col = query_charge.astype(BF16)[:, None]
     target = bucket[:, 0]
     positions = jnp.arange(q_rows, dtype=jnp.int32)
     earlier = (target[:, None] == target[None, :]) & (positions[None, :] < positions[:, None])
@@ -78,6 +80,205 @@
     return pick_rows(select_home, flat_back)
 
 
+def swapped(value, mask):
+    count = lax.axis_size("slab")
+    return lax.ppermute(value, "slab", [(i, i ^ mask) for i in range(count)])
+
+
+def unit_rows(values):
+    values = values.astype(F32)
+    return (values * lax.rsqrt(jnp.sum(values * values, axis=-1, keepdims=True) + EPS)).astype(BF16)
+
+
+def query_kernel(q_ref, bucket_ref, charge_ref, a_ref, b_ref, slot_ref):
+    q_rows, width = q_ref.shape
+    half = width // 2
+    unit = unit_rows(q_ref[...])
+    for k in range(0, half, 128):
+        a_ref[k // 128 * q_rows : (k // 128 + 1) * q_rows, :] = unit[:, k : k + 128]
+        b_ref[k // 128 * q_rows : (k // 128 + 1) * q_rows, :] = unit[:, half + k : half + k + 128]
+    along = jnp.broadcast_to(bucket_ref[...].astype(F32), (q_rows, q_rows))
+    down = along.T
+    i = lax.broadcasted_iota(jnp.int32, (q_rows, q_rows), 0)
+    j = lax.broadcasted_iota(jnp.int32, (q_rows, q_rows), 1)
+    earlier = jnp.where((along == down) & (i < j), 1.0, 0.0)
+    rank = jnp.sum(earlier, axis=0, keepdims=True)
+    slot = bucket_ref[...].astype(F32) * CAP + rank
+    slot_ref[...] = slot.astype(jnp.int32)
+    line = lax.broadcasted_iota(jnp.int32, (META, q_rows), 0)
+    charge = charge_ref[...].astype(F32)
+    meta = jnp.where(line == 0, slot, jnp.where(line == 1, charge, 0.0))
+    a_ref[half // 128 * q_rows :, :] = meta.astype(BF16)
+
+
+def library_kernel(lib_ref, charge_ref, a_ref, b_ref):
+    rows, width = lib_ref.shape
+    half = rows // 2
+    for start in range(0, half, 64):
+        a_ref[start : start + 64, :] = unit_rows(lib_ref[start : start + 64, :])
+        b_ref[start : start + 64, :] = unit_rows(lib_ref[half + start : half + start + 64, :])
+    charge = jnp.broadcast_to(charge_ref[...].astype(F32), (META, rows)).astype(BF16)
+    a_ref[half:, :] = jnp.zeros((META, width), BF16)
+    a_ref[half:, :rows] = charge
+
+
+def place_kernel(me_ref, *refs):
+    x_ref, charge_ref = refs[8:]
+    n_slots = (PLANE + 2) * CAP
+    q_rows = refs[1].shape[1]
+    total = 4 * PLANE * CAP
+    first = (me_ref[0] // PLANE * PLANE - 1) * CAP
+    for k in range(4):
+        a_ref, b_ref = refs[2 * k], refs[2 * k + 1]
+        n_chunk = b_ref.shape[0] // q_rows
+        meta = a_ref[n_chunk * q_rows :, :].astype(F32)
+        rel = meta[0:1, :].astype(jnp.int32) - first + total
+        rel = jnp.where(rel >= total, rel - total, rel)
+        rel = jnp.where(rel >= total, rel - total, rel)
+        place = lax.broadcasted_iota(jnp.int32, (n_slots, q_rows), 0) == rel
+        charge = jnp.sum(jnp.where(place, meta[1:2, :], 0.0), axis=1, keepdims=True)
+        charge_ref[k * n_slots : (k + 1) * n_slots, :] = jnp.broadcast_to(charge, (n_slots, 128))
+        select = jnp.where(place, 1.0, 0.0).astype(BF16)
+        for n in range(2 * n_chunk):
+            ref = a_ref if n < n_chunk else b_ref
+            at = n % n_chunk * q_rows
+            x_ref[k * n_slots : (k + 1) * n_slots, n * 128 : (n + 1) * 128] = jnp.dot(
+                select, ref[at : at + q_rows, :], preferred_element_type=F32
+            ).astype(BF16)
+
+
+def score_slabs(slabs, x_ref, charge_ref, lib_refs, out_refs, rows_ref, rcharge_ref):
+    n_slots = (PLANE + 2) * CAP
+    seen = 3 * CAP
+    for n, slab in enumerate(slabs):
+        a_ref, b_ref = lib_refs[2 * n], lib_refs[2 * n + 1]
+        half = b_ref.shape[0]
+        for k in range(4):
+            at = pl.multiple_of(slab * CAP + k * n_slots, CAP)
+            rows_ref[k * seen : (k + 1) * seen, :] = x_ref[pl.ds(at, seen), :]
+            rcharge_ref[k * seen : (k + 1) * seen, :] = charge_ref[pl.ds(at, seen), :]
+        row_charge = rcharge_ref[:, 0:1]
+        for part, ref in enumerate((a_ref, b_ref)):
+            lib_charge = a_ref[half:, part * half : (part + 1) * half].astype(F32)[0:1, :]
+            raw = lax.dot_general(
+                rows_ref[...], ref[:half, :], (((1,), (1,)), ((), ())), preferred_element_type=F32
+            )
+            kept = jnp.where(jnp.abs(row_charge - lib_charge) <= 2.0, raw, 0.0).astype(BF16)
+            for k in range(4):
+                out_refs[k][n * seen : (n + 1) * seen, part * half : (part + 1) * half] = kept[
+                    k * seen : (k + 1) * seen, :
+                ]
+
+
+def near_kernel(me_ref, *refs):
+    q_refs, lib_refs = refs[:8], refs[8:12]
+    out_refs, x_ref, charge_ref = refs[12:16], refs[16], refs[17]
+    place_kernel(me_ref, *q_refs, x_ref, charge_ref)
+    own = me_ref[0] % PLANE
+    score_slabs((own, own ^ 1), x_ref, charge_ref, lib_refs, out_refs, *refs[18:])
+
+
+def far_kernel(me_ref, *refs):
+    x_ref, charge_ref, lib_refs, out_refs = refs[0], refs[1], refs[2:6], refs[6:10]
+    own = me_ref[0] % PLANE
+    score_slabs((own ^ 2, own ^ 3), x_ref, charge_ref, lib_refs, out_refs, *refs[10:])
+
+
+def home_kernel(me_ref, slot_ref, *refs):
+    near, far, out_ref, flat_ref = refs[:4], refs[4:8], refs[8], refs[9]
+    q_rows = slot_ref.shape[1]
+    l_rows = near[0].shape[1]
+    n_slab = 4 * PLANE
+    total = n_slab * CAP
+    slot = slot_ref[...]
+    bucket, rank = slot // CAP, slot % CAP
+    places = lax.broadcasted_iota(jnp.int32, (total, q_rows), 0)
+    for unit in range(3):
+        for m in range(n_slab):
+            ref = (far if m & 2 else near)[m // PLANE]
+            at = (m & 1) * 3 * CAP + (2 - unit) * CAP
+            flat_ref[m * CAP : (m + 1) * CAP, :] = ref[at : at + CAP, :]
+        slab = (bucket + (unit - 1 + n_slab)) % n_slab
+        want = (slab ^ me_ref[0]) * CAP + rank
+        select = jnp.where(places == want, 1.0, 0.0).T.astype(BF16)
+        out_ref[:, unit * l_rows : (unit + 1) * l_rows] = jnp.dot(
+            select, flat_ref[...], preferred_element_type=F32
+        ).astype(BF16)
+
+
+VMEM = pl.BlockSpec(memory_space=pltpu.VMEM)
+SMEM = pl.BlockSpec(memory_space=pltpu.SMEM)
+
+
+def kernel_call(body, outs, args, scratch=(), scalars=0, flops=0):
+    size = sum(a.size * a.dtype.itemsize for a in [*args, *outs])
+    return pl.pallas_call(
+        body,
+        out_shape=[jax.ShapeDtypeStruct(o.shape, o.dtype) for o in outs],
+        in_specs=[SMEM] * scalars + [VMEM] * (len(args) - scalars),
+        out_specs=[VMEM] * len(outs),
+        scratch_shapes=scratch,
+        compiler_params=pltpu.CompilerParams(vmem_limit_bytes=16 * 1024 * 1024),
+        cost_estimate=pl.CostEstimate(flops=flops, bytes_accessed=size, transcendentals=0),
+    )(*args)
+
+
+def shape(*dims, dtype=BF16):
+    return jax.ShapeDtypeStruct(dims, dtype)
+
+
+def line_plan(queries, library, bucket, query_charge, library_charge):
+    q_rows, width = queries.shape
+    l_rows = library.shape[0]
+    me = lax.axis_index("slab").astype(jnp.int32).reshape(1)
+    half = width // 2 // 128 * q_rows
+    qa, qb, slot = kernel_call(
+        query_kernel,
+        [shape(half + META, 128), shape(half, 128), shape(1, q_rows, dtype=jnp.int32)],
+        [queries, bucket.reshape(1, q_rows), query_charge.reshape(1, q_rows)],
+    )
+    la, lb = kernel_call(
+        library_kernel,
+        [shape(l_rows // 2 + META, width), shape(l_rows // 2, width)],
+        [library, library_charge.reshape(1, l_rows)],
+    )
+    q12a, q12b = swapped(qa, 12), swapped(qb, 12)
+    q4a, q4b = swapped(qa, 4), swapped(qb, 4)
+    q8a, q8b = swapped(q12a, 4), swapped(q12b, 4)
+    ya, yb = swapped(la, 2), swapped(lb, 2)
+    ca, cb = swapped(la, 1), swapped(lb, 1)
+    da, db = swapped(ya, 1), swapped(yb, 1)
+    n_slots, seen = (PLANE + 2) * CAP, 3 * CAP
+    blocks = [shape(2 * seen, l_rows)] * 4
+    scratch = [pltpu.VMEM((4 * seen, width), BF16), pltpu.VMEM((4 * seen, 128), F32)]
+    *near, x, x_charge = kernel_call(
+        near_kernel,
+        blocks + [shape(4 * n_slots, width), shape(4 * n_slots, 128, dtype=F32)],
+        [me, qa, qb, q4a, q4b, q8a, q8b, q12a, q12b, la, lb, ca, cb],
+        scratch,
+        scalars=1,
+    )
+    near_back = [near[0]] + [swapped(near[k], 4 * k) for k in (1, 2, 3)]
+    far = kernel_call(far_kernel, blocks, [me, x, x_charge, ya, yb, da, db], scratch, scalars=1)
+    far_back = [far[0]] + [swapped(far[k], 4 * k) for k in (1, 2, 3)]
+    (out,) = kernel_call(
+        home_kernel,
+        [shape(q_rows, 3 * l_rows)],
+        [me, slot, *near_back, *far_back],
+        [pltpu.VMEM((4 * PLANE * CAP, l_rows), BF16)],
+        scalars=1,
+    )
+    return out
+
+
+def per_device(queries, library, bucket, query_charge, library_charge):
+    n_slab = lax.axis_size("slab")
+    q_rows, width = queries.shape
+    fits = n_slab == 4 * PLANE and 2 * q_rows == n_slab * CAP and q_rows == 128
+    plan = line_plan if fits and width % 256 == 0 and library.shape[0] <= width else general_plan
+    return plan(queries, library, bucket, query_charge, library_charge)
+
+
 def solution(mesh):
     placed = (
         P(("grp", "slab"), None),

time: 81.1 us -> 75.3 us (0.928)
  blocking collectives: 30.2 us -> 0 us
  waiting for transfers between devices: 19.4 us -> 33.1 us
  local copies, waits for them, and re-layouts: 0.79 us -> 8.82 us
  starting transfers between devices: 19.8 us -> 27.1 us
  matrix products: 6.71 us -> 0 us
  Pallas kernels: 0 us -> 5.91 us
  other arithmetic: 3.3 us -> 0 us
    all_to_all x1 -> x0, blocking collectives: 30.2 us -> none  [per_device(): lax.all_to_all(joined, 'slab', split_axis=0, concat_axis=0, tiled=True)]
    ppermute x4 -> x18, starting transfers between devices: 8.89 us -> 27.1 us  [swapped(): return lax.ppermute(value, 'slab', [(i, i ^ mask) for i in range(count)])]
    ppermute x4 -> x18, waiting for transfers between devices: 16.6 us -> 33.1 us  [swapped(): return lax.ppermute(value, 'slab', [(i, i ^ mask) for i in range(count)])]
    all_to_all x2 -> x0, starting transfers between devices: 11 us -> none  [the longest x1 7.39 us: per_device(): lax.all_to_all(out_charge, 'slab', split_axis=0, concat_axis=0, tiled=True)]
    unnamed x4 -> x26, local copies, waits for them, and re-layouts: 0.01 us -> 8.82 us
    dot_general x6 -> x0, matrix products: 6.71 us -> none  [the longest x2 2.94 us: place_rows(): jnp.dot(select, values, preferred_element_type=jnp.float32)]
    pallas_call x0 -> x5, Pallas kernels: none -> 5.91 us  [kernel_call(): pl.pallas_call(body, out_shape=[jax.ShapeDtypeStruct(o.shape, o.dtype) fo...]
    all_to_all x2 -> x0, waiting for transfers between devices: 2.8 us -> none  [the longest x1 2.8 us: per_device(): lax.all_to_all(out_charge, 'slab', split_axis=0, concat_axis=0, tiled=True)]
  transfers between devices with their start and end apart: 6 -> 18, of which waited for: 2 -> 10; matrix products, arithmetic and copies ran while one was open for 6% -> 0% of each run, Pallas kernels for 0% -> 6%
where the time goes in v1:
time: 75.3 us; the launch traced here: 75 us
  waiting for transfers between devices  33.1 us (44%)
  starting transfers between devices  27.1 us (36%)
  local copies, waits for them, and re-layouts  8.82 us (12%)
  Pallas kernels  5.91 us (8%)
    ppermute x18, waiting for transfers between devices, swapped(): return lax.ppermute(value, 'slab', [(i, i ^ mask) for i in range(count)])  33.1 us
    ppermute x18, starting transfers between devices, swapped(): return lax.ppermute(value, 'slab', [(i, i ^ mask) for i in range(count)])  27.1 us
    unnamed x26, local copies, waits for them, and re-layouts  8.82 us
    pallas_call x5, Pallas kernels, kernel_call(): pl.pallas_call(body, out_shape=[jax.ShapeDtypeStruct(o.shape, o.dtype) fo...  5.91 us
  transfers between devices with their start and end apart: 18, of which 10 were waited for; matrix products, arithmetic and copies ran while one was open for 0% of the time, Pallas kernels for 6%

profile of v1, /device:TPU:0, one launch (start us, length us, event | category | flops | bytes accessed | tf_op | source)
XLA Modules:
  0.0 75.0 jit_solution(18273302276377648182)
XLA Ops:
  0.0 1.2 %copy-done = bf16[512,1024]{1,0:T(8,128)(2,1)S(1)} copy-done((bf16[512,1024]{1,0:T(8,128)(2,1)S(1)}, bf16[512,1024]{1,0:T(8,128)(2,1)}, u32[]{:S(2)}) %copy-start) | copy-done | bytes 1048600
  1.2 0.7 copy-done.10
  1.9 0.3 shard_map.56
  2.2 3.0 %collective-permute-start.11 = (bf16[272,1024]{1,0:T(8,128)(2,1)S(1)}, bf16[272,1024]{1,0:T(8,128)(2,1)S(1)}, u32[]{:S(2)}, u32[]{:S(2)}) collective-permute-start(bf16[272,1024]{1,0:T(8,128)(2,1)S(1)} %get-tuple-element.23.refs_8_), channel_id=1, source_target_pairs={{0,2},{1,3},{2,0},{3,1},{4,6},{5,7},{6,4},{7,5},{8,10},{9,11},{10,... | collective-permute-start | bytes 1671176 | tf_op jit(solution)/shard_map/ppermute | solution.py:85
  5.3 0.1 collective-permute-start.12
  5.4 0.6 copy-done.11
  6.0 0.0 copy-done.12
  6.0 0.2 shard_map.55
  6.2 2.1 %collective-permute-start.1 = (bf16[512,128]{1,0:T(8,128)(2,1)S(1)}, bf16[512,128]{1,0:T(8,128)(2,1)S(1)}, u32[]{:S(2)}, u32[]{:S(2)}) collective-permute-start(bf16[512,128]{1,0:T(8,128)(2,1)S(1)} %get-tuple-element.22.refs_1_), channel_id=1, source_target_pairs={{0,4},{1,5},{2,6},{3,7},{4,0},{5,1},{6,2},{7,3},{8,12},{9,13},{10,... | collective-permute-start | bytes 393224 | tf_op jit(solution)/shard_map/ppermute | solution.py:85
  8.3 2.5 %collective-permute-start.4 = (bf16[512,128]{1,0:T(8,128)(2,1)S(1)}, bf16[512,128]{1,0:T(8,128)(2,1)S(1)}, u32[]{:S(2)}, u32[]{:S(2)}) collective-permute-start(bf16[512,128]{1,0:T(8,128)(2,1)S(1)} %get-tuple-element.22.refs_1_), channel_id=1, source_target_pairs={{0,12},{1,13},{2,14},{3,15},{4,8},{5,9},{6,10},{7,11},{8,4},{9,5},... | collective-permute-start | bytes 393224 | tf_op jit(solution)/shard_map/ppermute | solution.py:85
  10.8 0.7 copy-done.2
  11.4 0.0 collective-permute-start.6
  11.4 0.3 collective-permute-done.1.refs_3_
  11.7 0.7 copy-done.4
  12.4 2.5 %collective-permute-start = (bf16[528,128]{1,0:T(8,128)(2,1)S(1)}, bf16[528,128]{1,0:T(8,128)(2,1)S(1)}, u32[]{:S(2)}, u32[]{:S(2)}) collective-permute-start(bf16[528,128]{1,0:T(8,128)(2,1)S(1)} %get-tuple-element.21.refs_0_), channel_id=1, source_target_pairs={{0,4},{1,5},{2,6},{3,7},{4,0},{5,1},{6,2},{7,3},{8,12},{9,13},{10,... | collective-permute-start | bytes 405512 | tf_op jit(solution)/shard_map/ppermute | solution.py:85
  14.9 2.1 %collective-permute-done.4.refs_7_ = bf16[512,128]{1,0:T(8,128)(2,1)S(1)} collective-permute-done((bf16[512,128]{1,0:T(8,128)(2,1)S(1)}, bf16[512,128]{1,0:T(8,128)(2,1)S(1)}, u32[]{:S(2)}, u32[]{:S(2)}) %collective-permute-start.4) | collective-permute-done | bytes 131104 | tf_op jit(solution)/shard_map/ppermute | solution.py:85
  17.0 0.0 collective-permute-start.7
  17.0 1.7 %collective-permute-done.11.refs_2_ = bf16[272,1024]{1,0:T(8,128)(2,1)S(1)} collective-permute-done((bf16[272,1024]{1,0:T(8,128)(2,1)S(1)}, bf16[272,1024]{1,0:T(8,128)(2,1)S(1)}, u32[]{:S(2)}, u32[]{:S(2)}) %collective-permute-start.11) | collective-permute-done | bytes 557088 | tf_op jit(solution)/shard_map/ppermute | solution.py:85
  18.7 0.0 collective-permute-start.13
  18.7 10.4 %collective-permute-done.12.refs_3_ = bf16[256,1024]{1,0:T(8,128)(2,1)S(1)} collective-permute-done((bf16[256,1024]{1,0:T(8,128)(2,1)S(1)}, bf16[256,1024]{1,0:T(8,128)(2,1)S(1)}, u32[]{:S(2)}, u32[]{:S(2)}) %collective-permute-start.12) | collective-permute-done | bytes 524320 | tf_op jit(solution)/shard_map/ppermute | solution.py:85
  29.1 0.0 collective-permute-start.14
  29.1 0.0 collective-permute-done.refs_2_
  29.1 3.8 %collective-permute-start.2 = (bf16[528,128]{1,0:T(8,128)(2,1)S(1)}, bf16[528,128]{1,0:T(8,128)(2,1)}, u32[]{:S(2)}, u32[]{:S(2)}) collective-permute-start(bf16[528,128]{1,0:T(8,128)(2,1)S(1)} %get-tuple-element.21.refs_0_), channel_id=1, source_target_pairs={{0,12},{1,13},{2,14},{3,15},{4,8},{5,9},{6,10},{7,11},{8,4},{9,5},... | collective-permute-start | bytes 405512 | tf_op jit(solution)/shard_map/ppermute | solution.py:85
  33.0 4.5 %collective-permute-done.2.refs_6_ = bf16[528,128]{1,0:T(8,128)(2,1)} collective-permute-done((bf16[528,128]{1,0:T(8,128)(2,1)S(1)}, bf16[528,128]{1,0:T(8,128)(2,1)}, u32[]{:S(2)}, u32[]{:S(2)}) %collective-permute-start.2) | collective-permute-done | bytes 135200 | tf_op jit(solution)/shard_map/ppermute | solution.py:85
  37.4 2.5 %collective-permute-start.5 = (bf16[512,128]{1,0:T(8,128)(2,1)S(1)}, bf16[512,128]{1,0:T(8,128)(2,1)S(1)}, u32[]{:S(2)}, u32[]{:S(2)}) collective-permute-start(bf16[512,128]{1,0:T(8,128)(2,1)S(1)} %collective-permute-done.4.refs_7_), channel_id=1, source_target_pairs={{0,4},{1,5},{2,6},{3,7},{4,0},{5,1},{6,2},{7,3},{8,12},{9,13},{10,... | collective-permute-start | bytes 393224 | tf_op jit(solution)/shard_map/ppermute | solution.py:85
  39.9 0.7 copy-done.6
  40.6 2.7 %collective-permute-done.5.refs_5_ = bf16[512,128]{1,0:T(8,128)(2,1)S(1)} collective-permute-done((bf16[512,128]{1,0:T(8,128)(2,1)S(1)}, bf16[512,128]{1,0:T(8,128)(2,1)S(1)}, u32[]{:S(2)}, u32[]{:S(2)}) %collective-permute-start.5) | collective-permute-done | bytes 131104 | tf_op jit(solution)/shard_map/ppermute | solution.py:85
  43.3 0.7 copy-done.8
  44.0 1.7 %collective-permute-start.3 = (bf16[528,128]{1,0:T(8,128)(2,1)}, bf16[528,128]{1,0:T(8,128)(2,1)}, u32[]{:S(2)}, u32[]{:S(2)}) collective-permute-start(bf16[528,128]{1,0:T(8,128)(2,1)} %collective-permute-done.2.refs_6_), channel_id=1, source_target_pairs={{0,4},{1,5},{2,6},{3,7},{4,0},{5,1},{6,2},{7,3},{8,12},{9,13},{10,... | collective-permute-start | bytes 405512 | tf_op jit(solution)/shard_map/ppermute | solution.py:85
  45.7 3.6 %collective-permute-done.3.refs_4_ = bf16[528,128]{1,0:T(8,128)(2,1)} collective-permute-done((bf16[528,128]{1,0:T(8,128)(2,1)}, bf16[528,128]{1,0:T(8,128)(2,1)}, u32[]{:S(2)}, u32[]{:S(2)}) %collective-permute-start.3) | collective-permute-done | bytes 135200 | tf_op jit(solution)/shard_map/ppermute | solution.py:85
  49.3 0.0 collective-permute-done.7.refs_11_
  49.3 0.0 collective-permute-done.6.refs_10_
  49.3 0.9 %copy-done.3 = bf16[512,128]{1,0:T(8,128)(2,1)S(1)} copy-done((bf16[512,128]{1,0:T(8,128)(2,1)S(1)}, bf16[512,128]{1,0:T(8,128)(2,1)}, u32[]{:S(2)}) %copy-start.3) | copy-done | bytes 131096
  50.2 0.9 %copy-done.5 = bf16[512,128]{1,0:T(8,128)(2,1)S(1)} copy-done((bf16[512,128]{1,0:T(8,128)(2,1)S(1)}, bf16[512,128]{1,0:T(8,128)(2,1)}, u32[]{:S(2)}) %copy-start.5) | copy-done | bytes 131096
  51.1 0.9 %copy-done.7 = bf16[512,128]{1,0:T(8,128)(2,1)S(1)} copy-done((bf16[512,128]{1,0:T(8,128)(2,1)S(1)}, bf16[512,128]{1,0:T(8,128)(2,1)}, u32[]{:S(2)}) %copy-start.7) | copy-done | bytes 131096
  52.0 0.9 %copy-done.9 = bf16[512,128]{1,0:T(8,128)(2,1)S(1)} copy-done((bf16[512,128]{1,0:T(8,128)(2,1)S(1)}, bf16[512,128]{1,0:T(8,128)(2,1)}, u32[]{:S(2)}) %copy-start.9) | copy-done | bytes 131096
  52.9 2.4 %shard_map.57 = (bf16[96,512]{1,0:T(8,128)(2,1)S(1)}, bf16[96,512]{1,0:T(8,128)(2,1)S(1)}, bf16[96,512]{1,0:T(8,128)(2,1)S(1)}, bf16[96,512]{1,0:T(8,128)(2,1)S(...) custom-call(s32[1]{0:T(128)} %bitcast.me_ref, bf16[528,128]{1,0:T(8,128)(2,1)S(1)} %get-tuple-element.21.refs_0_, ...), custom_call_target="tpu_custom_call" | custom-call | bytes 4603908 | tf_op jit(solution)/shard_map/pallas_call | solution.py:215
  55.4 1.8 %collective-permute-start.8 = (bf16[96,512]{1,0:T(8,128)(2,1)S(1)}, bf16[96,512]{1,0:T(8,128)(2,1)S(1)}, u32[]{:S(2)}, u32[]{:S(2)}) collective-permute-start(bf16[96,512]{1,0:T(8,128)(2,1)S(1)} %get-tuple-element.26), channel_id=1, source_target_pairs={{0,4},{1,5},{2,6},{3,7},{4,0},{5,1},{6,2},{7,3},{8,12},{9,13},{10,... | collective-permute-start | bytes 294920 | tf_op jit(solution)/shard_map/ppermute | solution.py:85
  57.2 1.5 %collective-permute-start.9 = (bf16[96,512]{1,0:T(8,128)(2,1)S(1)}, bf16[96,512]{1,0:T(8,128)(2,1)S(1)}, u32[]{:S(2)}, u32[]{:S(2)}) collective-permute-start(bf16[96,512]{1,0:T(8,128)(2,1)S(1)} %get-tuple-element.27), channel_id=1, source_target_pairs={{0,8},{1,9},{2,10},{3,11},{4,12},{5,13},{6,14},{7,15},{8,0},{9,1},... | collective-permute-start | bytes 294920 | tf_op jit(solution)/shard_map/ppermute | solution.py:85
  58.7 1.1 %collective-permute-start.10 = (bf16[96,512]{1,0:T(8,128)(2,1)S(1)}, bf16[96,512]{1,0:T(8,128)(2,1)S(1)}, u32[]{:S(2)}, u32[]{:S(2)}) collective-permute-start(bf16[96,512]{1,0:T(8,128)(2,1)S(1)} %get-tuple-element.28), channel_id=1, source_target_pairs={{0,12},{1,13},{2,14},{3,15},{4,8},{5,9},{6,10},{7,11},{8,4},{9,5},... | collective-permute-start | bytes 294920 | tf_op jit(solution)/shard_map/ppermute | solution.py:85
  59.8 1.9 %shard_map.58 = (bf16[96,512]{1,0:T(8,128)(2,1)S(1)}, bf16[96,512]{1,0:T(8,128)(2,1)S(1)}, bf16[96,512]{1,0:T(8,128)(2,1)S(1)}, bf16[96,512]{1,0:T(8,128)(2,1)S(1)}) custom-call(s32[1]{0:T(128)} %bitcast.me_ref, bf16[384,1024]{1,0:T(8,128)(2,1)S(1)} %get-tuple-element.29.refs_0_, f32[384,128]{1,0:T(8,128)S(1)} %get-tuple-element.30.refs_1_, ...), custom_call_target="tpu_custom_call" | custom-call | bytes 3538948 | tf_op jit(solution)/shard_map/pallas_call | solution.py:215
  61.7 0.9 %collective-permute-start.15 = (bf16[96,512]{1,0:T(8,128)(2,1)S(1)}, bf16[96,512]{1,0:T(8,128)(2,1)S(1)}, u32[]{:S(2)}, u32[]{:S(2)}) collective-permute-start(bf16[96,512]{1,0:T(8,128)(2,1)S(1)} %get-tuple-element.32), channel_id=1, source_target_pairs={{0,4},{1,5},{2,6},{3,7},{4,0},{5,1},{6,2},{7,3},{8,12},{9,13},{10,... | collective-permute-start | bytes 294920 | tf_op jit(solution)/shard_map/ppermute | solution.py:85
  62.6 2.4 %collective-permute-start.16 = (bf16[96,512]{1,0:T(8,128)(2,1)S(1)}, bf16[96,512]{1,0:T(8,128)(2,1)S(1)}, u32[]{:S(2)}, u32[]{:S(2)}) collective-permute-start(bf16[96,512]{1,0:T(8,128)(2,1)S(1)} %get-tuple-element.33), channel_id=1, source_target_pairs={{0,8},{1,9},{2,10},{3,11},{4,12},{5,13},{6,14},{7,15},{8,0},{9,1},... | collective-permute-start | bytes 294920 | tf_op jit(solution)/shard_map/ppermute | solution.py:85
  65.1 1.1 %collective-permute-start.17 = (bf16[96,512]{1,0:T(8,128)(2,1)S(1)}, bf16[96,512]{1,0:T(8,128)(2,1)S(1)}, u32[]{:S(2)}, u32[]{:S(2)}) collective-permute-start(bf16[96,512]{1,0:T(8,128)(2,1)S(1)} %get-tuple-element.34), channel_id=1, source_target_pairs={{0,12},{1,13},{2,14},{3,15},{4,8},{5,9},{6,10},{7,11},{8,4},{9,5},... | collective-permute-start | bytes 294920 | tf_op jit(solution)/shard_map/ppermute | solution.py:85
  66.2 1.6 %collective-permute-done.9.refs_2_ = bf16[96,512]{1,0:T(8,128)(2,1)S(1)} collective-permute-done((bf16[96,512]{1,0:T(8,128)(2,1)S(1)}, bf16[96,512]{1,0:T(8,128)(2,1)S(1)}, u32[]{:S(2)}, u32[]{:S(2)}) %collective-permute-start.9) | collective-permute-done | bytes 98336 | tf_op jit(solution)/shard_map/ppermute | solution.py:85
  67.8 0.8 %collective-permute-done.15.refs_5_ = bf16[96,512]{1,0:T(8,128)(2,1)S(1)} collective-permute-done((bf16[96,512]{1,0:T(8,128)(2,1)S(1)}, bf16[96,512]{1,0:T(8,128)(2,1)S(1)}, u32[]{:S(2)}, u32[]{:S(2)}) %collective-permute-start.15) | collective-permute-done | bytes 98336 | tf_op jit(solution)/shard_map/ppermute | solution.py:85
  68.6 5.3 %collective-permute-done.16.refs_6_ = bf16[96,512]{1,0:T(8,128)(2,1)S(1)} collective-permute-done((bf16[96,512]{1,0:T(8,128)(2,1)S(1)}, bf16[96,512]{1,0:T(8,128)(2,1)S(1)}, u32[]{:S(2)}, u32[]{:S(2)}) %collective-permute-start.16) | collective-permute-done | bytes 98336 | tf_op jit(solution)/shard_map/ppermute | solution.py:85
  73.9 1.1 %shard_map.59 = bf16[128,1536]{1,0:T(8,128)(2,1)} custom-call(s32[1]{0:T(128)} %bitcast.me_ref, s32[1,128]{1,0:T(1,128)S(1)} %get-tuple-element.20.slot_ref, bf16[96,512]{1,0:T(8,128)(2,1)S(1)} %get-tuple-element.25.refs_0_, bf16[96,512]{1,0:T(8,128)(2,1)S(1)} %collective-permute-done.8.refs_1_, bf16[96,512]{1,0:T(8,128)(2,1)S(1)} %collective-permute-done.9.refs_2_, ...), custom_call_target="tpu_custom_call" | custom-call | bytes 1180164 | tf_op jit(solution)/shard_map/pallas_call | solution.py:215
  (19 shorter events, 0.0 us)
Async XLA Ops:
  0.0 1.2 %copy-start = (bf16[512,1024]{1,0:T(8,128)(2,1)S(1)}, bf16[512,1024]{1,0:T(8,128)(2,1)}, u32[]{:S(2)}) copy-start(bf16[512,1024]{1,0:T(8,128)(2,1)} %lib_ref.1) | copy-start | bytes 3145732
  1.2 0.7 copy-start.10
  1.9 3.4 %copy-start.1 = (bf16[128,1024]{1,0:T(8,128)(2,1)S(1)}, bf16[128,1024]{1,0:T(8,128)(2,1)}, u32[]{:S(2)}) copy-start(bf16[128,1024]{1,0:T(8,128)(2,1)} %q_ref.1) | copy-start | bytes 786436
  2.2 16.5 %collective-permute-start.11 = (bf16[272,1024]{1,0:T(8,128)(2,1)S(1)}, bf16[272,1024]{1,0:T(8,128)(2,1)S(1)}, u32[]{:S(2)}, u32[]{:S(2)}) collective-permute-start(bf16[272,1024]{1,0:T(8,128)(2,1)S(1)} %get-tuple-element.23.refs_8_), channel_id=1, source_target_pairs={{0,2},{1,3},{2,0},{3,1},{4,6},{5,7},{6,4},{7,5},{8,10},{9,11},{10,... | collective-permute-start | bytes 1671176 | tf_op jit(solution)/shard_map/ppermute | solution.py:85
  5.3 23.9 %collective-permute-start.12 = (bf16[256,1024]{1,0:T(8,128)(2,1)S(1)}, bf16[256,1024]{1,0:T(8,128)(2,1)S(1)}, u32[]{:S(2)}, u32[]{:S(2)}) collective-permute-start(bf16[256,1024]{1,0:T(8,128)(2,1)S(1)} %get-tuple-element.24.refs_9_), channel_id=1, source_target_pairs={{0,2},{1,3},{2,0},{3,1},{4,6},{5,7},{6,4},{7,5},{8,10},{9,11},{10,... | collective-permute-start | bytes 1572872 | tf_op jit(solution)/shard_map/ppermute | solution.py:85
  5.3 0.7 copy-start.11
  5.3 0.7 copy-start.12
  6.2 5.5 %collective-permute-start.1 = (bf16[512,128]{1,0:T(8,128)(2,1)S(1)}, bf16[512,128]{1,0:T(8,128)(2,1)S(1)}, u32[]{:S(2)}, u32[]{:S(2)}) collective-permute-start(bf16[512,128]{1,0:T(8,128)(2,1)S(1)} %get-tuple-element.22.refs_1_), channel_id=1, source_target_pairs={{0,4},{1,5},{2,6},{3,7},{4,0},{5,1},{6,2},{7,3},{8,12},{9,13},{10,... | collective-permute-start | bytes 393224 | tf_op jit(solution)/shard_map/ppermute | solution.py:85
  8.3 8.7 %collective-permute-start.4 = (bf16[512,128]{1,0:T(8,128)(2,1)S(1)}, bf16[512,128]{1,0:T(8,128)(2,1)S(1)}, u32[]{:S(2)}, u32[]{:S(2)}) collective-permute-start(bf16[512,128]{1,0:T(8,128)(2,1)S(1)} %get-tuple-element.22.refs_1_), channel_id=1, source_target_pairs={{0,12},{1,13},{2,14},{3,15},{4,8},{5,9},{6,10},{7,11},{8,4},{9,5},... | collective-permute-start | bytes 393224 | tf_op jit(solution)/shard_map/ppermute | solution.py:85
  10.8 0.7 copy-start.2
  11.4 37.9 %collective-permute-start.6 = (bf16[272,1024]{1,0:T(8,128)(2,1)S(1)}, bf16[272,1024]{1,0:T(8,128)(2,1)S(1)}, u32[]{:S(2)}, u32[]{:S(2)}) collective-permute-start(bf16[272,1024]{1,0:T(8,128)(2,1)S(1)} %get-tuple-element.23.refs_8_), channel_id=1, source_target_pairs={{0,1},{1,0},{2,3},{3,2},{4,5},{5,4},{6,7},{7,6},{8,9},{9,8},{10,11... | collective-permute-start | bytes 1671176 | tf_op jit(solution)/shard_map/ppermute | solution.py:85
  11.7 0.7 copy-start.4
  12.4 16.7 %collective-permute-start = (bf16[528,128]{1,0:T(8,128)(2,1)S(1)}, bf16[528,128]{1,0:T(8,128)(2,1)S(1)}, u32[]{:S(2)}, u32[]{:S(2)}) collective-permute-start(bf16[528,128]{1,0:T(8,128)(2,1)S(1)} %get-tuple-element.21.refs_0_), channel_id=1, source_target_pairs={{0,4},{1,5},{2,6},{3,7},{4,0},{5,1},{6,2},{7,3},{8,12},{9,13},{10,... | collective-permute-start | bytes 405512 | tf_op jit(solution)/shard_map/ppermute | solution.py:85
  17.0 32.3 %collective-permute-start.7 = (bf16[256,1024]{1,0:T(8,128)(2,1)S(1)}, bf16[256,1024]{1,0:T(8,128)(2,1)}, u32[]{:S(2)}, u32[]{:S(2)}) collective-permute-start(bf16[256,1024]{1,0:T(8,128)(2,1)S(1)} %get-tuple-element.24.refs_9_), channel_id=1, source_target_pairs={{0,1},{1,0},{2,3},{3,2},{4,5},{5,4},{6,7},{7,6},{8,9},{9,8},{10,11... | collective-permute-start | bytes 1572872 | tf_op jit(solution)/shard_map/ppermute | solution.py:85
  18.7 41.1 %collective-permute-start.13 = (bf16[272,1024]{1,0:T(8,128)(2,1)S(1)}, bf16[272,1024]{1,0:T(8,128)(2,1)S(1)}, u32[]{:S(2)}, u32[]{:S(2)}) collective-permute-start(bf16[272,1024]{1,0:T(8,128)(2,1)S(1)} %collective-permute-done.11.refs_2_), channel_id=1, source_target_pairs={{0,1},{1,0},{2,3},{3,2},{4,5},{5,4},{6,7},{7,6},{8,9},{9,8},{10,11... | collective-permute-start | bytes 1671176 | tf_op jit(solution)/shard_map/ppermute | solution.py:85
  29.1 30.7 %collective-permute-start.14 = (bf16[256,1024]{1,0:T(8,128)(2,1)S(1)}, bf16[256,1024]{1,0:T(8,128)(2,1)}, u32[]{:S(2)}, u32[]{:S(2)}) collective-permute-start(bf16[256,1024]{1,0:T(8,128)(2,1)S(1)} %collective-permute-done.12.refs_3_), channel_id=1, source_target_pairs={{0,1},{1,0},{2,3},{3,2},{4,5},{5,4},{6,7},{7,6},{8,9},{9,8},{10,11... | collective-permute-start | bytes 1572872 | tf_op jit(solution)/shard_map/ppermute | solution.py:85
  29.1 8.3 %collective-permute-start.2 = (bf16[528,128]{1,0:T(8,128)(2,1)S(1)}, bf16[528,128]{1,0:T(8,128)(2,1)}, u32[]{:S(2)}, u32[]{:S(2)}) collective-permute-start(bf16[528,128]{1,0:T(8,128)(2,1)S(1)} %get-tuple-element.21.refs_0_), channel_id=1, source_target_pairs={{0,12},{1,13},{2,14},{3,15},{4,8},{5,9},{6,10},{7,11},{8,4},{9,5},... | collective-permute-start | bytes 405512 | tf_op jit(solution)/shard_map/ppermute | solution.py:85
  37.4 5.9 %collective-permute-start.5 = (bf16[512,128]{1,0:T(8,128)(2,1)S(1)}, bf16[512,128]{1,0:T(8,128)(2,1)S(1)}, u32[]{:S(2)}, u32[]{:S(2)}) collective-permute-start(bf16[512,128]{1,0:T(8,128)(2,1)S(1)} %collective-permute-done.4.refs_7_), channel_id=1, source_target_pairs={{0,4},{1,5},{2,6},{3,7},{4,0},{5,1},{6,2},{7,3},{8,12},{9,13},{10,... | collective-permute-start | bytes 393224 | tf_op jit(solution)/shard_map/ppermute | solution.py:85
  39.9 0.7 copy-start.6
  43.3 0.7 copy-start.8
  44.0 5.3 %collective-permute-start.3 = (bf16[528,128]{1,0:T(8,128)(2,1)}, bf16[528,128]{1,0:T(8,128)(2,1)}, u32[]{:S(2)}, u32[]{:S(2)}) collective-permute-start(bf16[528,128]{1,0:T(8,128)(2,1)} %collective-permute-done.2.refs_6_), channel_id=1, source_target_pairs={{0,4},{1,5},{2,6},{3,7},{4,0},{5,1},{6,2},{7,3},{8,12},{9,13},{10,... | collective-permute-start | bytes 405512 | tf_op jit(solution)/shard_map/ppermute | solution.py:85
  49.3 0.9 %copy-start.3 = (bf16[512,128]{1,0:T(8,128)(2,1)S(1)}, bf16[512,128]{1,0:T(8,128)(2,1)}, u32[]{:S(2)}) copy-start(bf16[512,128]{1,0:T(8,128)(2,1)} %copy-done.2) | copy-start | bytes 393220
  50.2 0.9 %copy-start.5 = (bf16[512,128]{1,0:T(8,128)(2,1)S(1)}, bf16[512,128]{1,0:T(8,128)(2,1)}, u32[]{:S(2)}) copy-start(bf16[512,128]{1,0:T(8,128)(2,1)} %copy-done.4) | copy-start | bytes 393220
  51.1 0.9 %copy-start.7 = (bf16[512,128]{1,0:T(8,128)(2,1)S(1)}, bf16[512,128]{1,0:T(8,128)(2,1)}, u32[]{:S(2)}) copy-start(bf16[512,128]{1,0:T(8,128)(2,1)} %copy-done.6) | copy-start | bytes 393220
  52.0 0.9 %copy-start.9 = (bf16[512,128]{1,0:T(8,128)(2,1)S(1)}, bf16[512,128]{1,0:T(8,128)(2,1)}, u32[]{:S(2)}) copy-start(bf16[512,128]{1,0:T(8,128)(2,1)} %copy-done.8) | copy-start | bytes 393220
  55.4 9.7 %collective-permute-start.8 = (bf16[96,512]{1,0:T(8,128)(2,1)S(1)}, bf16[96,512]{1,0:T(8,128)(2,1)S(1)}, u32[]{:S(2)}, u32[]{:S(2)}) collective-permute-start(bf16[96,512]{1,0:T(8,128)(2,1)S(1)} %get-tuple-element.26), channel_id=1, source_target_pairs={{0,4},{1,5},{2,6},{3,7},{4,0},{5,1},{6,2},{7,3},{8,12},{9,13},{10,... | collective-permute-start | bytes 294920 | tf_op jit(solution)/shard_map/ppermute | solution.py:85
  57.2 10.6 %collective-permute-start.9 = (bf16[96,512]{1,0:T(8,128)(2,1)S(1)}, bf16[96,512]{1,0:T(8,128)(2,1)S(1)}, u32[]{:S(2)}, u32[]{:S(2)}) collective-permute-start(bf16[96,512]{1,0:T(8,128)(2,1)S(1)} %get-tuple-element.27), channel_id=1, source_target_pairs={{0,8},{1,9},{2,10},{3,11},{4,12},{5,13},{6,14},{7,15},{8,0},{9,1},... | collective-permute-start | bytes 294920 | tf_op jit(solution)/shard_map/ppermute | solution.py:85
  58.7 9.1 %collective-permute-start.10 = (bf16[96,512]{1,0:T(8,128)(2,1)S(1)}, bf16[96,512]{1,0:T(8,128)(2,1)S(1)}, u32[]{:S(2)}, u32[]{:S(2)}) collective-permute-start(bf16[96,512]{1,0:T(8,128)(2,1)S(1)} %get-tuple-element.28), channel_id=1, source_target_pairs={{0,12},{1,13},{2,14},{3,15},{4,8},{5,9},{6,10},{7,11},{8,4},{9,5},... | collective-permute-start | bytes 294920 | tf_op jit(solution)/shard_map/ppermute | solution.py:85
  61.7 6.9 %collective-permute-start.15 = (bf16[96,512]{1,0:T(8,128)(2,1)S(1)}, bf16[96,512]{1,0:T(8,128)(2,1)S(1)}, u32[]{:S(2)}, u32[]{:S(2)}) collective-permute-start(bf16[96,512]{1,0:T(8,128)(2,1)S(1)} %get-tuple-element.32), channel_id=1, source_target_pairs={{0,4},{1,5},{2,6},{3,7},{4,0},{5,1},{6,2},{7,3},{8,12},{9,13},{10,... | collective-permute-start | bytes 294920 | tf_op jit(solution)/shard_map/ppermute | solution.py:85
  62.6 11.3 %collective-permute-start.16 = (bf16[96,512]{1,0:T(8,128)(2,1)S(1)}, bf16[96,512]{1,0:T(8,128)(2,1)S(1)}, u32[]{:S(2)}, u32[]{:S(2)}) collective-permute-start(bf16[96,512]{1,0:T(8,128)(2,1)S(1)} %get-tuple-element.33), channel_id=1, source_target_pairs={{0,8},{1,9},{2,10},{3,11},{4,12},{5,13},{6,14},{7,15},{8,0},{9,1},... | collective-permute-start | bytes 294920 | tf_op jit(solution)/shard_map/ppermute | solution.py:85
  65.1 8.8 %collective-permute-start.17 = (bf16[96,512]{1,0:T(8,128)(2,1)S(1)}, bf16[96,512]{1,0:T(8,128)(2,1)S(1)}, u32[]{:S(2)}, u32[]{:S(2)}) collective-permute-start(bf16[96,512]{1,0:T(8,128)(2,1)S(1)} %get-tuple-element.34), channel_id=1, source_target_pairs={{0,12},{1,13},{2,14},{3,15},{4,8},{5,9},{6,10},{7,11},{8,4},{9,5},... | collective-permute-start | bytes 294920 | tf_op jit(solution)/shard_map/ppermute | solution.py:85

commit v2 on v0

--- a/solution.py
+++ b/solution.py
@@ -1,9 +1,18 @@
+import functools
+
 import jax
 import jax.numpy as jnp
 from jax import lax
+from jax.experimental import pallas as pl
+from jax.experimental.pallas import tpu as pltpu
 from jax.sharding import PartitionSpec as P
 
 EPS = 1e-06
+PLANE = 4
+CAP = 16
+META = 16
+F32 = jnp.float32
+BF16 = jnp.bfloat16
 
 
 def passed_along(value, axis, steps):
@@ -13,47 +22,40 @@
 
 
 def normalize(rows):
-    values = rows.astype(jnp.float32)
-    return (values * lax.rsqrt(jnp.sum(values * values, axis=-1, keepdims=True) + EPS)).astype(
-        jnp.bfloat16
-    )
+    values = rows.astype(F32)
+    return (values * lax.rsqrt(jnp.sum(values * values, axis=-1, keepdims=True) + EPS)).astype(BF16)
 
 
 def score_block(rows, row_charge, lib_rows, lib_charge):
-    raw = lax.dot_general(
-        rows, lib_rows, (((1,), (1,)), ((), ())), preferred_element_type=jnp.float32
-    )
-    keep = (
-        jnp.abs(row_charge.astype(jnp.float32)[:, None] - lib_charge.astype(jnp.float32)[None, :])
-        <= 2.0
-    )
-    return jnp.where(keep, raw, 0.0).astype(jnp.bfloat16)
+    raw = lax.dot_general(rows, lib_rows, (((1,), (1,)), ((), ())), preferred_element_type=F32)
+    keep = jnp.abs(row_charge.astype(F32)[:, None] - lib_charge.astype(F32)[None, :]) <= 2.0
+    return jnp.where(keep, raw, 0.0).astype(BF16)
 
 
 def selector(slot_ids, total):
     places = jnp.arange(total, dtype=jnp.int32)
-    return (places[:, None] == slot_ids[None, :]).astype(jnp.bfloat16)
+    return (places[:, None] == slot_ids[None, :]).astype(BF16)
 
 
 def pick_rows(select, flat):
     return lax.dot_general(
-        select, flat, (((0,), (0,)), ((), ())), preferred_element_type=jnp.float32
-    ).astype(jnp.bfloat16)
+        select, flat, (((0,), (0,)), ((), ())), preferred_element_type=F32
+    ).astype(BF16)
 
 
 def place_rows(select, values):
-    return jnp.dot(select, values, preferred_element_type=jnp.float32).astype(jnp.bfloat16)
-
-
-def per_device(queries, library, bucket, query_charge, library_charge):
+    return jnp.dot(select, values, preferred_element_type=F32).astype(BF16)
+
+
+def general_plan(queries, library, bucket, query_charge, library_charge):
     n_slab = lax.axis_size("slab")
     q_rows = queries.shape[0]
     width = queries.shape[1]
     cap = 2 * q_rows // n_slab
     query_unit = normalize(queries)
     library_unit = normalize(library)
-    lib_charge = library_charge.astype(jnp.bfloat16)
-    qcharge_col = query_charge.astype(jnp.bfloat16)[:, None]
+    lib_charge = library_charge.astype(BF16)
+    qcharge_col = query_charge.astype(BF16)[:, None]
     target = bucket[:, 0]
     positions = jnp.arange(q_rows, dtype=jnp.int32)
     earlier = (target[:, None] == target[None, :]) & (positions[None, :] < positions[:, None])
@@ -78,6 +80,207 @@
     return pick_rows(select_home, flat_back)
 
 
+def swapped(value, mask):
+    count = lax.axis_size("slab")
+    return lax.ppermute(value, "slab", [(i, i ^ mask) for i in range(count)])
+
+
+def unit_rows(values):
+    values = values.astype(F32)
+    return (values * lax.rsqrt(jnp.sum(values * values, axis=-1, keepdims=True) + EPS)).astype(BF16)
+
+
+def prep_kernel(me_ref, q_hbm, lib_hbm, bucket_hbm, qcharge_hbm, lcharge_hbm, *refs):
+    out_refs, lib_out, slot_ref = refs[:4], refs[4], refs[5]
+    q_ref, lib_ref, bucket_ref, qcharge_ref, lcharge_ref, sem = refs[6:]
+    copies = [
+        pltpu.make_async_copy(source, target, sem.at[n])
+        for n, (source, target) in enumerate(
+            [
+                (bucket_hbm, bucket_ref),
+                (qcharge_hbm, qcharge_ref),
+                (q_hbm, q_ref),
+                (lcharge_hbm, lcharge_ref),
+                (lib_hbm, lib_ref),
+            ]
+        )
+    ]
+    for copy in copies:
+        copy.start()
+    q_rows, width = q_ref.shape
+    n_slots = (PLANE + 2) * CAP
+    total = 4 * PLANE * CAP
+    copies[0].wait()
+    copies[1].wait()
+    bucket = bucket_ref[...]
+    along = jnp.broadcast_to(bucket.astype(F32), (q_rows, q_rows))
+    i = lax.broadcasted_iota(jnp.int32, (q_rows, q_rows), 0)
+    j = lax.broadcasted_iota(jnp.int32, (q_rows, q_rows), 1)
+    earlier = jnp.where((along == along.T) & (i < j), 1.0, 0.0)
+    rank = jnp.sum(earlier, axis=0, keepdims=True)
+    slot = bucket * CAP + rank.astype(jnp.int32)
+    slot_ref[...] = slot
+    charge = jnp.broadcast_to(qcharge_ref[...].astype(F32), (META, q_rows)).astype(BF16)
+    copies[2].wait()
+    unit = unit_rows(q_ref[...])
+    for k in range(4):
+        plane = (me_ref[0] // PLANE) ^ k
+        rel = (slot + (total - (plane * PLANE - 1) * CAP)) % total
+        place = lax.broadcasted_iota(jnp.int32, (q_rows, q_rows), 0) == rel
+        select = jnp.where(place, 1.0, 0.0).astype(BF16)
+        rows = jnp.dot(select[:n_slots, :], unit, preferred_element_type=F32).astype(BF16)
+        for n in range(width // 128):
+            out_refs[k][n * n_slots : (n + 1) * n_slots, :] = rows[:, n * 128 : (n + 1) * 128]
+        placed = lax.dot_general(
+            charge, select, (((1,), (1,)), ((), ())), preferred_element_type=F32
+        )
+        out_refs[k][width // 128 * n_slots :, :] = placed.astype(BF16)
+    copies[3].wait()
+    copies[4].wait()
+    rows = lib_ref.shape[0]
+    for start in range(0, rows, 64):
+        lib_out[start : start + 64, :] = unit_rows(lib_ref[start : start + 64, :])
+    lib_out[rows:, :] = jnp.zeros((META, width), BF16)
+    lib_out[rows:, :rows] = jnp.broadcast_to(lcharge_ref[...].astype(F32), (META, rows)).astype(BF16)
+
+
+def score_kernel(turn, me_ref, *refs):
+    q_refs, lib_refs, out_refs, rows_ref, charge_ref = refs[:4], refs[4:6], refs[6:10], refs[10], refs[11]
+    n_slots, seen = (PLANE + 2) * CAP, 3 * CAP
+    for n, lib in enumerate(lib_refs):
+        width = lib.shape[1]
+        l_rows = lib.shape[0] - META
+        at = pl.multiple_of(((me_ref[0] % PLANE) ^ (turn ^ n)) * CAP, CAP)
+        for k in range(4):
+            for c in range(width // 128):
+                rows_ref[k * seen : (k + 1) * seen, c * 128 : (c + 1) * 128] = q_refs[k][
+                    pl.ds(pl.multiple_of(at + c * n_slots, CAP), seen), :
+                ]
+            if n == 0:
+                line = q_refs[k][width // 128 * n_slots :, :].astype(F32)[0:1, :]
+                charge_ref[k] = jnp.broadcast_to(line, (128, 128)).T
+        lib_charge = lib[l_rows:, :l_rows].astype(F32)[0:1, :]
+        raw = lax.dot_general(
+            rows_ref[...], lib[:l_rows, :], (((1,), (1,)), ((), ())), preferred_element_type=F32
+        )
+        for k in range(4):
+            row_charge = charge_ref[k, pl.ds(at, seen), :][:, 0:1]
+            kept = jnp.abs(row_charge - lib_charge) <= 2.0
+            out_refs[k][n * seen : (n + 1) * seen, :] = jnp.where(
+                kept, raw[k * seen : (k + 1) * seen, :], 0.0
+            ).astype(BF16)
+
+
+def home_kernel(me_ref, slot_ref, *refs):
+    near, far, out_ref, flat_ref = refs[:4], refs[4:8], refs[8], refs[9]
+    q_rows = slot_ref.shape[1]
+    l_rows = near[0].shape[1]
+    n_slab = 4 * PLANE
+    total = n_slab * CAP
+    slot = slot_ref[...]
+    bucket, rank = slot // CAP, slot % CAP
+    places = lax.broadcasted_iota(jnp.int32, (total, q_rows), 0)
+    for unit in range(3):
+        for m in range(n_slab):
+            ref = (far if m & 2 else near)[m // PLANE]
+            at = (m & 1) * 3 * CAP + (2 - unit) * CAP
+            flat_ref[m * CAP : (m + 1) * CAP, :] = ref[at : at + CAP, :]
+        slab = (bucket + (unit - 1 + n_slab)) % n_slab
+        want = (slab ^ me_ref[0]) * CAP + rank
+        select = jnp.where(places == want, 1.0, 0.0).T.astype(BF16)
+        out_ref[:, unit * l_rows : (unit + 1) * l_rows] = jnp.dot(
+            select, flat_ref[...], preferred_element_type=F32
+        ).astype(BF16)
+
+
+VMEM = pl.BlockSpec(memory_space=pltpu.VMEM)
+SMEM = pl.BlockSpec(memory_space=pltpu.SMEM)
+HBM = pl.BlockSpec(memory_space=pltpu.HBM)
+
+
+def kernel_call(body, outs, args, specs, scratch=(), flops=0):
+    size = sum(a.size * a.dtype.itemsize for a in [*args, *outs])
+    return pl.pallas_call(
+        body,
+        out_shape=[jax.ShapeDtypeStruct(o.shape, o.dtype) for o in outs],
+        in_specs=specs,
+        out_specs=[VMEM] * len(outs),
+        scratch_shapes=scratch,
+        compiler_params=pltpu.CompilerParams(vmem_limit_bytes=12 * 1024 * 1024),
+        cost_estimate=pl.CostEstimate(flops=flops, bytes_accessed=size, transcendentals=0),
+    )(*args)
+
+
+def shape(*dims, dtype=BF16):
+    return jax.ShapeDtypeStruct(dims, dtype)
+
+
+def line_plan(queries, library, bucket, query_charge, library_charge):
+    q_rows, width = queries.shape
+    l_rows = library.shape[0]
+    me = lax.axis_index("slab").astype(jnp.int32).reshape(1)
+    n_slots, seen = (PLANE + 2) * CAP, 3 * CAP
+    int32 = jnp.int32
+    q0, q4, q8, q12, lib, slot = kernel_call(
+        prep_kernel,
+        [shape(width // 128 * n_slots + META, 128)] * 4
+        + [shape(l_rows + META, width), shape(1, q_rows, dtype=int32)],
+        [
+            me,
+            queries,
+            library,
+            bucket.reshape(1, q_rows),
+            query_charge.reshape(1, q_rows),
+            library_charge.reshape(1, l_rows),
+        ],
+        [SMEM] + [HBM] * 5,
+        [
+            pltpu.VMEM((q_rows, width), BF16),
+            pltpu.VMEM((l_rows, width), BF16),
+            pltpu.VMEM((1, q_rows), int32),
+            pltpu.VMEM((1, q_rows), int32),
+            pltpu.VMEM((1, l_rows), int32),
+            pltpu.SemaphoreType.DMA((5,)),
+        ],
+    )
+    q12, q8, q4 = swapped(q12, 12), swapped(q8, 8), swapped(q4, 4)
+    lib_y, lib_c = swapped(lib, 2), swapped(lib, 1)
+    scratch = [pltpu.VMEM((4 * seen, width), BF16), pltpu.VMEM((4, 128, 128), F32)]
+
+    def scores(turn, one, other):
+        blocks = kernel_call(
+            functools.partial(score_kernel, turn),
+            [shape(2 * seen, l_rows)] * 4,
+            [me, q0, q4, q8, q12, one, other],
+            [SMEM] + [VMEM] * 6,
+            scratch,
+            flops=2 * 2 * 4 * seen * l_rows * width,
+        )
+        far, middle, close = swapped(blocks[3], 12), swapped(blocks[2], 8), swapped(blocks[1], 4)
+        return [blocks[0], close, middle, far]
+
+    near = scores(0, lib, lib_c)
+    lib_y, near[0] = lax.optimization_barrier((lib_y, near[0]))
+    lib_d = swapped(lib_y, 1)
+    far = scores(2, lib_y, lib_d)
+    (out,) = kernel_call(
+        home_kernel,
+        [shape(q_rows, 3 * l_rows)],
+        [me, slot, *near, *far],
+        [SMEM] + [VMEM] * 9,
+        [pltpu.VMEM((4 * PLANE * CAP, l_rows), BF16)],
+    )
+    return out
+
+
+def per_device(queries, library, bucket, query_charge, library_charge):
+    n_slab = lax.axis_size("slab")
+    q_rows, width = queries.shape
+    fits = n_slab == 4 * PLANE and 2 * q_rows == n_slab * CAP and q_rows == 128
+    plan = line_plan if fits and width % 256 == 0 and library.shape[0] <= width else general_plan
+    return plan(queries, library, bucket, query_charge, library_charge)
+
+
 def solution(mesh):
     placed = (
         P(("grp", "slab"), None),

time: 81.1 us -> 55.2 us (0.68)
  blocking collectives: 30.2 us -> 0 us
  waiting for transfers between devices: 19.4 us -> 30.1 us
  matrix products: 6.71 us -> 0 us
  Pallas kernels: 0 us -> 4 us
  local copies, waits for them, and re-layouts: 0.79 us -> 4.16 us
  other arithmetic: 3.3 us -> 0 us
  starting transfers between devices: 19.8 us -> 16.7 us
    all_to_all x1 -> x0, blocking collectives: 30.2 us -> none  [per_device(): lax.all_to_all(joined, 'slab', split_axis=0, concat_axis=0, tiled=True)]
    ppermute x4 -> x12, waiting for transfers between devices: 16.6 us -> 30.1 us  [swapped(): return lax.ppermute(value, 'slab', [(i, i ^ mask) for i in range(count)])]
    all_to_all x2 -> x0, starting transfers between devices: 11 us -> none  [the longest x1 7.39 us: per_device(): lax.all_to_all(out_charge, 'slab', split_axis=0, concat_axis=0, tiled=True)]
    ppermute x4 -> x12, starting transfers between devices: 8.89 us -> 16.7 us  [swapped(): return lax.ppermute(value, 'slab', [(i, i ^ mask) for i in range(count)])]
    dot_general x6 -> x0, matrix products: 6.71 us -> none  [the longest x2 2.94 us: place_rows(): jnp.dot(select, values, preferred_element_type=jnp.float32)]
    unnamed x4 -> x10, local copies, waits for them, and re-layouts: 0.01 us -> 4.16 us
    pallas_call x0 -> x4, Pallas kernels: none -> 4 us  [kernel_call(): pl.pallas_call(body, out_shape=[jax.ShapeDtypeStruct(o.shape, o.dtype) fo...]
    all_to_all x2 -> x0, waiting for transfers between devices: 2.8 us -> none  [the longest x1 2.8 us: per_device(): lax.all_to_all(out_charge, 'slab', split_axis=0, concat_axis=0, tiled=True)]
  transfers between devices with their start and end apart: 6 -> 12, of which waited for: 2 -> 5; matrix products, arithmetic and copies ran while one was open for 6% -> 0% of each run, Pallas kernels for 0% -> 3%
where the time goes in v2:
time: 55.2 us; the launch traced here: 55 us
  waiting for transfers between devices  30.1 us (55%)
  starting transfers between devices  16.7 us (30%)
  local copies, waits for them, and re-layouts  4.16 us (8%)
  Pallas kernels  4 us (7%)
    ppermute x12, waiting for transfers between devices, swapped(): return lax.ppermute(value, 'slab', [(i, i ^ mask) for i in range(count)])  30.1 us
    ppermute x12, starting transfers between devices, swapped(): return lax.ppermute(value, 'slab', [(i, i ^ mask) for i in range(count)])  16.7 us
    unnamed x10, local copies, waits for them, and re-layouts  4.16 us
    pallas_call x4, Pallas kernels, kernel_call(): pl.pallas_call(body, out_shape=[jax.ShapeDtypeStruct(o.shape, o.dtype) fo...  4 us
  transfers between devices with their start and end apart: 12, of which 5 were waited for; matrix products, arithmetic and copies ran while one was open for 0% of the time, Pallas kernels for 3%

profile of v2, /device:TPU:0, one launch (start us, length us, event | category | flops | bytes accessed | tf_op | source)
XLA Modules:
  0.0 55.0 jit_solution(7686069548614721419)
XLA Ops:
  0.0 0.0 copy-start
  0.0 1.2 %copy-done = bf16[512,1024]{1,0:T(8,128)(2,1)S(1)} copy-done((bf16[512,1024]{1,0:T(8,128)(2,1)S(1)}, bf16[512,1024]{1,0:T(8,128)(2,1)}, u32[]{:S(2)}) %copy-start) | copy-done | bytes 1048600
  1.2 0.0 copy-start.1
  1.2 0.9 %copy-done.1 = bf16[128,1024]{1,0:T(8,128)(2,1)S(1)} copy-done((bf16[128,1024]{1,0:T(8,128)(2,1)S(1)}, bf16[128,1024]{1,0:T(8,128)(2,1)}, u32[]{:S(2)}) %copy-start.1) | copy-done | bytes 262168
  2.2 0.0 copy-start.2
  2.2 0.7 %copy-done.2 = s32[512]{0:T(512)S(1)} copy-done((s32[512]{0:T(512)S(1)}, s32[512]{0:T(512)}, u32[]{:S(2)}) %copy-start.2) | copy-done | bytes 2072
  2.9 0.0 copy-start.3
  2.9 0.7 %copy-done.3 = s32[128,1]{0,1:T(1,128)S(1)} copy-done((s32[128,1]{0,1:T(1,128)S(1)}, s32[128,1]{0,1:T(1,128)}, u32[]{:S(2)}) %copy-start.3) | copy-done | bytes 536
  3.5 0.0 copy-start.4
  3.5 0.7 %copy-done.4 = s32[128]{0:T(128)S(1)} copy-done((s32[128]{0:T(128)S(1)}, s32[128]{0:T(128)}, u32[]{:S(2)}) %copy-start.4) | copy-done | bytes 536
  4.2 1.1 %shard_map.55 = (bf16[784,128]{1,0:T(8,128)(2,1)S(1)}, bf16[784,128]{1,0:T(8,128)(2,1)S(1)}, bf16[784,128]{1,0:T(8,128)(2,1)S(1)}, bf16[784,128]{1,0:T(8,128)(2,...) custom-call(s32[1]{0:T(128)} %bitcast.me_ref, bf16[128,1024]{1,0:T(8,128)(2,1)S(1)} %copy-done.1, ...), custom_call_target="tpu_custom_call" | custom-call | bytes 3198468 | tf_op jit(solution)/shard_map/pallas_call | solution.py:203
  5.3 0.5 collective-permute-start.4
  5.8 2.6 %collective-permute-start = (bf16[528,1024]{1,0:T(8,128)(2,1)S(1)}, bf16[528,1024]{1,0:T(8,128)(2,1)S(1)}, u32[]{:S(2)}, u32[]{:S(2)}) collective-permute-start(bf16[528,1024]{1,0:T(8,128)(2,1)S(1)} %get-tuple-element.22.refs_4_), channel_id=1, source_target_pairs={{0,2},{1,3},{2,0},{3,1},{4,6},{5,7},{6,4},{7,5},{8,10},{9,11},{10,... | collective-permute-start | bytes 3244040 | tf_op jit(solution)/shard_map/ppermute | solution.py:85
  8.4 1.6 %collective-permute-start.1 = (bf16[784,128]{1,0:T(8,128)(2,1)S(1)}, bf16[784,128]{1,0:T(8,128)(2,1)S(1)}, u32[]{:S(2)}, u32[]{:S(2)}) collective-permute-start(bf16[784,128]{1,0:T(8,128)(2,1)S(1)} %get-tuple-element.24), channel_id=1, source_target_pairs={{0,4},{1,5},{2,6},{3,7},{4,0},{5,1},{6,2},{7,3},{8,12},{9,13},{10,... | collective-permute-start | bytes 602120 | tf_op jit(solution)/shard_map/ppermute | solution.py:85
  10.0 2.6 %collective-permute-start.2 = (bf16[784,128]{1,0:T(8,128)(2,1)S(1)}, bf16[784,128]{1,0:T(8,128)(2,1)S(1)}, u32[]{:S(2)}, u32[]{:S(2)}) collective-permute-start(bf16[784,128]{1,0:T(8,128)(2,1)S(1)} %get-tuple-element.25), channel_id=1, source_target_pairs={{0,8},{1,9},{2,10},{3,11},{4,12},{5,13},{6,14},{7,15},{8,0},{9,1},... | collective-permute-start | bytes 602120 | tf_op jit(solution)/shard_map/ppermute | solution.py:85
  12.6 0.2 collective-permute-start.3
  12.8 6.4 %collective-permute-done.1.refs_1_ = bf16[784,128]{1,0:T(8,128)(2,1)S(1)} collective-permute-done((bf16[784,128]{1,0:T(8,128)(2,1)S(1)}, bf16[784,128]{1,0:T(8,128)(2,1)S(1)}, u32[]{:S(2)}, u32[]{:S(2)}) %collective-permute-start.1) | collective-permute-done | bytes 200736 | tf_op jit(solution)/shard_map/ppermute | solution.py:85
  19.2 8.2 %collective-permute-done.2.refs_2_ = bf16[784,128]{1,0:T(8,128)(2,1)S(1)} collective-permute-done((bf16[784,128]{1,0:T(8,128)(2,1)S(1)}, bf16[784,128]{1,0:T(8,128)(2,1)S(1)}, u32[]{:S(2)}, u32[]{:S(2)}) %collective-permute-start.2) | collective-permute-done | bytes 200736 | tf_op jit(solution)/shard_map/ppermute | solution.py:85
  27.3 0.0 collective-permute-done.3.refs_3_
  27.4 0.0 collective-permute-done.4.refs_5_
  27.4 0.9 %shard_map.56 = (bf16[96,512]{1,0:T(8,128)(2,1)S(1)}, bf16[96,512]{1,0:T(8,128)(2,1)S(1)}, bf16[96,512]{1,0:T(8,128)(2,1)S(1)}, bf16[96,512]{1,0:T(8,128)(2,1)S(1)}) custom-call(s32[1]{0:T(128)} %bitcast.me_ref, bf16[784,128]{1,0:T(8,128)(2,1)S(1)} %get-tuple-element.23.refs_0_, bf16[784,128]{1,0:T(8,128)(2,1)S(1)} %collective-permute-done.1.refs_1_, ...), custom_call_target="tpu_custom_call" | custom-call | flops 402653184 | bytes 3358724 | tf_op jit(solution)/shard_map/pallas_call | solution.py:203
  28.3 4.6 %collective-permute-done.refs_4_ = bf16[528,1024]{1,0:T(8,128)(2,1)S(1)} collective-permute-done((bf16[528,1024]{1,0:T(8,128)(2,1)S(1)}, bf16[528,1024]{1,0:T(8,128)(2,1)S(1)}, u32[]{:S(2)}, u32[]{:S(2)}) %collective-permute-start) | collective-permute-done | bytes 1081376 | tf_op jit(solution)/shard_map/ppermute | solution.py:85
  32.8 0.0 collective-permute-start.8
  32.9 1.8 %collective-permute-start.5 = (bf16[96,512]{1,0:T(8,128)(2,1)S(1)}, bf16[96,512]{1,0:T(8,128)(2,1)S(1)}, u32[]{:S(2)}, u32[]{:S(2)}) collective-permute-start(bf16[96,512]{1,0:T(8,128)(2,1)S(1)} %get-tuple-element.29), channel_id=1, source_target_pairs={{0,4},{1,5},{2,6},{3,7},{4,0},{5,1},{6,2},{7,3},{8,12},{9,13},{10,... | collective-permute-start | bytes 294920 | tf_op jit(solution)/shard_map/ppermute | solution.py:85
  34.7 2.6 %collective-permute-start.6 = (bf16[96,512]{1,0:T(8,128)(2,1)S(1)}, bf16[96,512]{1,0:T(8,128)(2,1)S(1)}, u32[]{:S(2)}, u32[]{:S(2)}) collective-permute-start(bf16[96,512]{1,0:T(8,128)(2,1)S(1)} %get-tuple-element.30), channel_id=1, source_target_pairs={{0,8},{1,9},{2,10},{3,11},{4,12},{5,13},{6,14},{7,15},{8,0},{9,1},... | collective-permute-start | bytes 294920 | tf_op jit(solution)/shard_map/ppermute | solution.py:85
  37.3 0.0 collective-permute-start.7
  37.3 0.0 collective-permute-done.8.refs_5_
  37.3 0.9 %shard_map.57 = (bf16[96,512]{1,0:T(8,128)(2,1)S(1)}, bf16[96,512]{1,0:T(8,128)(2,1)S(1)}, bf16[96,512]{1,0:T(8,128)(2,1)S(1)}, bf16[96,512]{1,0:T(8,128)(2,1)S(1)}) custom-call(s32[1]{0:T(128)} %bitcast.me_ref, bf16[784,128]{1,0:T(8,128)(2,1)S(1)} %get-tuple-element.23.refs_0_, bf16[784,128]{1,0:T(8,128)(2,1)S(1)} %collective-permute-done.1.refs_1_, ...), custom_call_target="tpu_custom_call" | custom-call | flops 402653184 | bytes 3358724 | tf_op jit(solution)/shard_map/pallas_call | solution.py:203
  38.2 1.0 %collective-permute-start.9 = (bf16[96,512]{1,0:T(8,128)(2,1)S(1)}, bf16[96,512]{1,0:T(8,128)(2,1)S(1)}, u32[]{:S(2)}, u32[]{:S(2)}) collective-permute-start(bf16[96,512]{1,0:T(8,128)(2,1)S(1)} %get-tuple-element.34), channel_id=1, source_target_pairs={{0,4},{1,5},{2,6},{3,7},{4,0},{5,1},{6,2},{7,3},{8,12},{9,13},{10,... | collective-permute-start | bytes 294920 | tf_op jit(solution)/shard_map/ppermute | solution.py:85
  39.1 3.5 %collective-permute-start.10 = (bf16[96,512]{1,0:T(8,128)(2,1)S(1)}, bf16[96,512]{1,0:T(8,128)(2,1)S(1)}, u32[]{:S(2)}, u32[]{:S(2)}) collective-permute-start(bf16[96,512]{1,0:T(8,128)(2,1)S(1)} %get-tuple-element.35), channel_id=1, source_target_pairs={{0,8},{1,9},{2,10},{3,11},{4,12},{5,13},{6,14},{7,15},{8,0},{9,1},... | collective-permute-start | bytes 294920 | tf_op jit(solution)/shard_map/ppermute | solution.py:85
  42.6 0.0 collective-permute-done.5.refs_1_
  42.6 0.3 collective-permute-start.11
  43.0 2.5 %collective-permute-done.6.refs_2_ = bf16[96,512]{1,0:T(8,128)(2,1)S(1)} collective-permute-done((bf16[96,512]{1,0:T(8,128)(2,1)S(1)}, bf16[96,512]{1,0:T(8,128)(2,1)S(1)}, u32[]{:S(2)}, u32[]{:S(2)}) %collective-permute-start.6) | collective-permute-done | bytes 98336 | tf_op jit(solution)/shard_map/ppermute | solution.py:85
  45.5 0.0 collective-permute-done.7.refs_3_
  45.5 0.0 collective-permute-done.9.refs_5_
  45.5 8.4 %collective-permute-done.10.refs_6_ = bf16[96,512]{1,0:T(8,128)(2,1)S(1)} collective-permute-done((bf16[96,512]{1,0:T(8,128)(2,1)S(1)}, bf16[96,512]{1,0:T(8,128)(2,1)S(1)}, u32[]{:S(2)}, u32[]{:S(2)}) %collective-permute-start.10) | collective-permute-done | bytes 98336 | tf_op jit(solution)/shard_map/ppermute | solution.py:85
  53.9 0.0 collective-permute-done.11.refs_7_
  53.9 1.1 %shard_map.58 = bf16[128,1536]{1,0:T(8,128)(2,1)} custom-call(s32[1]{0:T(128)} %bitcast.me_ref, s32[1,128]{1,0:T(1,128)S(1)} %get-tuple-element.21.slot_ref, bf16[96,512]{1,0:T(8,128)(2,1)S(1)} %get-tuple-element.28.refs_0_, bf16[96,512]{1,0:T(8,128)(2,1)S(1)} %collective-permute-done.5.refs_1_, bf16[96,512]{1,0:T(8,128)(2,1)S(1)} %collective-permute-done.6.refs_2_, ...), custom_call_target="tpu_custom_call" | custom-call | bytes 1180164 | tf_op jit(solution)/shard_map/pallas_call | solution.py:203
Async XLA Ops:
  0.0 1.2 %copy-start = (bf16[512,1024]{1,0:T(8,128)(2,1)S(1)}, bf16[512,1024]{1,0:T(8,128)(2,1)}, u32[]{:S(2)}) copy-start(bf16[512,1024]{1,0:T(8,128)(2,1)} %lib_hbm.1) | copy-start | bytes 3145732
  1.2 0.9 %copy-start.1 = (bf16[128,1024]{1,0:T(8,128)(2,1)S(1)}, bf16[128,1024]{1,0:T(8,128)(2,1)}, u32[]{:S(2)}) copy-start(bf16[128,1024]{1,0:T(8,128)(2,1)} %q_hbm.1) | copy-start | bytes 786436
  2.2 0.7 %copy-start.2 = (s32[512]{0:T(512)S(1)}, s32[512]{0:T(512)}, u32[]{:S(2)}) copy-start(s32[512]{0:T(512)} %param.9) | copy-start | bytes 6148
  2.9 0.7 %copy-start.3 = (s32[128,1]{0,1:T(1,128)S(1)}, s32[128,1]{0,1:T(1,128)}, u32[]{:S(2)}) copy-start(s32[128,1]{0,1:T(1,128)} %param.7) | copy-start | bytes 1540
  3.5 0.7 %copy-start.4 = (s32[128]{0:T(128)S(1)}, s32[128]{0:T(128)}, u32[]{:S(2)}) copy-start(s32[128]{0:T(128)} %param.8) | copy-start | bytes 1540
  5.3 22.1 %collective-permute-start.4 = (bf16[528,1024]{1,0:T(8,128)(2,1)S(1)}, bf16[528,1024]{1,0:T(8,128)(2,1)S(1)}, u32[]{:S(2)}, u32[]{:S(2)}) collective-permute-start(bf16[528,1024]{1,0:T(8,128)(2,1)S(1)} %get-tuple-element.22.refs_4_), channel_id=1, source_target_pairs={{0,1},{1,0},{2,3},{3,2},{4,5},{5,4},{6,7},{7,6},{8,9},{9,8},{10,11... | collective-permute-start | bytes 3244040 | tf_op jit(solution)/shard_map/ppermute | solution.py:85
  5.8 27.0 %collective-permute-start = (bf16[528,1024]{1,0:T(8,128)(2,1)S(1)}, bf16[528,1024]{1,0:T(8,128)(2,1)S(1)}, u32[]{:S(2)}, u32[]{:S(2)}) collective-permute-start(bf16[528,1024]{1,0:T(8,128)(2,1)S(1)} %get-tuple-element.22.refs_4_), channel_id=1, source_target_pairs={{0,2},{1,3},{2,0},{3,1},{4,6},{5,7},{6,4},{7,5},{8,10},{9,11},{10,... | collective-permute-start | bytes 3244040 | tf_op jit(solution)/shard_map/ppermute | solution.py:85
  8.4 10.8 %collective-permute-start.1 = (bf16[784,128]{1,0:T(8,128)(2,1)S(1)}, bf16[784,128]{1,0:T(8,128)(2,1)S(1)}, u32[]{:S(2)}, u32[]{:S(2)}) collective-permute-start(bf16[784,128]{1,0:T(8,128)(2,1)S(1)} %get-tuple-element.24), channel_id=1, source_target_pairs={{0,4},{1,5},{2,6},{3,7},{4,0},{5,1},{6,2},{7,3},{8,12},{9,13},{10,... | collective-permute-start | bytes 602120 | tf_op jit(solution)/shard_map/ppermute | solution.py:85
  10.0 17.4 %collective-permute-start.2 = (bf16[784,128]{1,0:T(8,128)(2,1)S(1)}, bf16[784,128]{1,0:T(8,128)(2,1)S(1)}, u32[]{:S(2)}, u32[]{:S(2)}) collective-permute-start(bf16[784,128]{1,0:T(8,128)(2,1)S(1)} %get-tuple-element.25), channel_id=1, source_target_pairs={{0,8},{1,9},{2,10},{3,11},{4,12},{5,13},{6,14},{7,15},{8,0},{9,1},... | collective-permute-start | bytes 602120 | tf_op jit(solution)/shard_map/ppermute | solution.py:85
  12.6 14.8 %collective-permute-start.3 = (bf16[784,128]{1,0:T(8,128)(2,1)S(1)}, bf16[784,128]{1,0:T(8,128)(2,1)S(1)}, u32[]{:S(2)}, u32[]{:S(2)}) collective-permute-start(bf16[784,128]{1,0:T(8,128)(2,1)S(1)} %get-tuple-element.26), channel_id=1, source_target_pairs={{0,12},{1,13},{2,14},{3,15},{4,8},{5,9},{6,10},{7,11},{8,4},{9,5},... | collective-permute-start | bytes 602120 | tf_op jit(solution)/shard_map/ppermute | solution.py:85
  32.8 4.4 %collective-permute-start.8 = (bf16[528,1024]{1,0:T(8,128)(2,1)S(1)}, bf16[528,1024]{1,0:T(8,128)(2,1)S(1)}, u32[]{:S(2)}, u32[]{:S(2)}) collective-permute-start(bf16[528,1024]{1,0:T(8,128)(2,1)S(1)} %collective-permute-done.refs_4_), channel_id=1, source_target_pairs={{0,1},{1,0},{2,3},{3,2},{4,5},{5,4},{6,7},{7,6},{8,9},{9,8},{10,11... | collective-permute-start | bytes 3244040 | tf_op jit(solution)/shard_map/ppermute | solution.py:85
  32.9 9.8 %collective-permute-start.5 = (bf16[96,512]{1,0:T(8,128)(2,1)S(1)}, bf16[96,512]{1,0:T(8,128)(2,1)S(1)}, u32[]{:S(2)}, u32[]{:S(2)}) collective-permute-start(bf16[96,512]{1,0:T(8,128)(2,1)S(1)} %get-tuple-element.29), channel_id=1, source_target_pairs={{0,4},{1,5},{2,6},{3,7},{4,0},{5,1},{6,2},{7,3},{8,12},{9,13},{10,... | collective-permute-start | bytes 294920 | tf_op jit(solution)/shard_map/ppermute | solution.py:85
  34.7 10.8 %collective-permute-start.6 = (bf16[96,512]{1,0:T(8,128)(2,1)S(1)}, bf16[96,512]{1,0:T(8,128)(2,1)S(1)}, u32[]{:S(2)}, u32[]{:S(2)}) collective-permute-start(bf16[96,512]{1,0:T(8,128)(2,1)S(1)} %get-tuple-element.30), channel_id=1, source_target_pairs={{0,8},{1,9},{2,10},{3,11},{4,12},{5,13},{6,14},{7,15},{8,0},{9,1},... | collective-permute-start | bytes 294920 | tf_op jit(solution)/shard_map/ppermute | solution.py:85
  37.3 8.2 %collective-permute-start.7 = (bf16[96,512]{1,0:T(8,128)(2,1)S(1)}, bf16[96,512]{1,0:T(8,128)(2,1)S(1)}, u32[]{:S(2)}, u32[]{:S(2)}) collective-permute-start(bf16[96,512]{1,0:T(8,128)(2,1)S(1)} %get-tuple-element.31), channel_id=1, source_target_pairs={{0,12},{1,13},{2,14},{3,15},{4,8},{5,9},{6,10},{7,11},{8,4},{9,5},... | collective-permute-start | bytes 294920 | tf_op jit(solution)/shard_map/ppermute | solution.py:85
  38.2 7.3 %collective-permute-start.9 = (bf16[96,512]{1,0:T(8,128)(2,1)S(1)}, bf16[96,512]{1,0:T(8,128)(2,1)S(1)}, u32[]{:S(2)}, u32[]{:S(2)}) collective-permute-start(bf16[96,512]{1,0:T(8,128)(2,1)S(1)} %get-tuple-element.34), channel_id=1, source_target_pairs={{0,4},{1,5},{2,6},{3,7},{4,0},{5,1},{6,2},{7,3},{8,12},{9,13},{10,... | collective-permute-start | bytes 294920 | tf_op jit(solution)/shard_map/ppermute | solution.py:85
  39.1 14.7 %collective-permute-start.10 = (bf16[96,512]{1,0:T(8,128)(2,1)S(1)}, bf16[96,512]{1,0:T(8,128)(2,1)S(1)}, u32[]{:S(2)}, u32[]{:S(2)}) collective-permute-start(bf16[96,512]{1,0:T(8,128)(2,1)S(1)} %get-tuple-element.35), channel_id=1, source_target_pairs={{0,8},{1,9},{2,10},{3,11},{4,12},{5,13},{6,14},{7,15},{8,0},{9,1},... | collective-permute-start | bytes 294920 | tf_op jit(solution)/shard_map/ppermute | solution.py:85
  42.6 11.3 %collective-permute-start.11 = (bf16[96,512]{1,0:T(8,128)(2,1)S(1)}, bf16[96,512]{1,0:T(8,128)(2,1)S(1)}, u32[]{:S(2)}, u32[]{:S(2)}) collective-permute-start(bf16[96,512]{1,0:T(8,128)(2,1)S(1)} %get-tuple-element.36), channel_id=1, source_target_pairs={{0,12},{1,13},{2,14},{3,15},{4,8},{5,9},{6,10},{7,11},{8,4},{9,5},... | collective-permute-start | bytes 294920 | tf_op jit(solution)/shard_map/ppermute | solution.py:85

commit v3 on v2

--- a/solution.py
+++ b/solution.py
@@ -11,6 +11,8 @@
 PLANE = 4
 CAP = 16
 META = 16
+PREP_LIMIT = 12 * 1024 * 1024
+COST = 1
 F32 = jnp.float32
 BF16 = jnp.bfloat16
 
@@ -90,9 +92,9 @@
     return (values * lax.rsqrt(jnp.sum(values * values, axis=-1, keepdims=True) + EPS)).astype(BF16)
 
 
-def prep_kernel(me_ref, q_hbm, lib_hbm, bucket_hbm, qcharge_hbm, lcharge_hbm, *refs):
-    out_refs, lib_out, slot_ref = refs[:4], refs[4], refs[5]
-    q_ref, lib_ref, bucket_ref, qcharge_ref, lcharge_ref, sem = refs[6:]
+def prep_kernel(me_ref, q_hbm, bucket_hbm, qcharge_hbm, lcharge_hbm, *refs):
+    out_refs, slot_ref, lcharge_out = refs[:4], refs[4], refs[5]
+    q_ref, bucket_ref, qcharge_ref, lcharge_ref, sem = refs[6:]
     copies = [
         pltpu.make_async_copy(source, target, sem.at[n])
         for n, (source, target) in enumerate(
@@ -101,7 +103,6 @@
                 (qcharge_hbm, qcharge_ref),
                 (q_hbm, q_ref),
                 (lcharge_hbm, lcharge_ref),
-                (lib_hbm, lib_ref),
             ]
         )
     ]
@@ -136,20 +137,30 @@
         )
         out_refs[k][width // 128 * n_slots :, :] = placed.astype(BF16)
     copies[3].wait()
-    copies[4].wait()
-    rows = lib_ref.shape[0]
-    for start in range(0, rows, 64):
-        lib_out[start : start + 64, :] = unit_rows(lib_ref[start : start + 64, :])
-    lib_out[rows:, :] = jnp.zeros((META, width), BF16)
-    lib_out[rows:, :rows] = jnp.broadcast_to(lcharge_ref[...].astype(F32), (META, rows)).astype(BF16)
+    lcharge = jnp.broadcast_to(lcharge_ref[...].astype(F32), lcharge_out.shape)
+    lcharge_out[...] = lcharge.astype(BF16)
+
+
+def unit_kernel(*refs):
+    count = len(refs) // 2
+    for source, target in zip(refs[:count], refs[count:]):
+        for start in range(0, source.shape[0], 64):
+            target[start : start + 64, :] = unit_rows(source[start : start + 64, :])
+
+
+def pair_kernel(one_ref, other_ref, out_ref):
+    line = lax.broadcasted_iota(jnp.int32, out_ref.shape, 0)
+    one, other = one_ref[...].astype(F32), other_ref[...].astype(F32)
+    out_ref[...] = jnp.where(line == 0, one, other).astype(BF16)
 
 
 def score_kernel(turn, me_ref, *refs):
-    q_refs, lib_refs, out_refs, rows_ref, charge_ref = refs[:4], refs[4:6], refs[6:10], refs[10], refs[11]
+    lcharge_ref, lib_refs, out_refs = refs[4], refs[5:7], refs[7:11]
+    q_refs = refs[3::-1]
+    rows_ref, charge_ref = refs[11:]
     n_slots, seen = (PLANE + 2) * CAP, 3 * CAP
     for n, lib in enumerate(lib_refs):
         width = lib.shape[1]
-        l_rows = lib.shape[0] - META
         at = pl.multiple_of(((me_ref[0] % PLANE) ^ (turn ^ n)) * CAP, CAP)
         for k in range(4):
             for c in range(width // 128):
@@ -159,20 +170,20 @@
             if n == 0:
                 line = q_refs[k][width // 128 * n_slots :, :].astype(F32)[0:1, :]
                 charge_ref[k] = jnp.broadcast_to(line, (128, 128)).T
-        lib_charge = lib[l_rows:, :l_rows].astype(F32)[0:1, :]
-        raw = lax.dot_general(
-            rows_ref[...], lib[:l_rows, :], (((1,), (1,)), ((), ())), preferred_element_type=F32
+        lib_charge = lcharge_ref[...].astype(F32)[n : n + 1, :]
+        products = lax.dot_general(
+            rows_ref[...], lib[...], (((1,), (1,)), ((), ())), preferred_element_type=F32
         )
         for k in range(4):
             row_charge = charge_ref[k, pl.ds(at, seen), :][:, 0:1]
             kept = jnp.abs(row_charge - lib_charge) <= 2.0
             out_refs[k][n * seen : (n + 1) * seen, :] = jnp.where(
-                kept, raw[k * seen : (k + 1) * seen, :], 0.0
+                kept, products[k * seen : (k + 1) * seen, :], 0.0
             ).astype(BF16)
 
 
 def home_kernel(me_ref, slot_ref, *refs):
-    near, far, out_ref, flat_ref = refs[:4], refs[4:8], refs[8], refs[9]
+    near, far, out_ref, flat_ref = refs[3::-1], refs[7:3:-1], refs[8], refs[9]
     q_rows = slot_ref.shape[1]
     l_rows = near[0].shape[1]
     n_slab = 4 * PLANE
@@ -198,16 +209,18 @@
 HBM = pl.BlockSpec(memory_space=pltpu.HBM)
 
 
-def kernel_call(body, outs, args, specs, scratch=(), flops=0):
-    size = sum(a.size * a.dtype.itemsize for a in [*args, *outs])
+MIB = 1024 * 1024
+
+
+def kernel_call(body, outs, args, specs, scratch=(), limit=12 * MIB):
     return pl.pallas_call(
         body,
         out_shape=[jax.ShapeDtypeStruct(o.shape, o.dtype) for o in outs],
         in_specs=specs,
         out_specs=[VMEM] * len(outs),
         scratch_shapes=scratch,
-        compiler_params=pltpu.CompilerParams(vmem_limit_bytes=12 * 1024 * 1024),
-        cost_estimate=pl.CostEstimate(flops=flops, bytes_accessed=size, transcendentals=0),
+        compiler_params=pltpu.CompilerParams(vmem_limit_bytes=limit),
+        cost_estimate=pl.CostEstimate(flops=0, bytes_accessed=COST, transcendentals=0),
     )(*args)
 
 
@@ -221,48 +234,57 @@
     me = lax.axis_index("slab").astype(jnp.int32).reshape(1)
     n_slots, seen = (PLANE + 2) * CAP, 3 * CAP
     int32 = jnp.int32
-    q0, q4, q8, q12, lib, slot = kernel_call(
+    raw_y, raw_c = swapped(library, 2), swapped(library, 1)
+    q0, q4, q8, q12, slot, charge = kernel_call(
         prep_kernel,
         [shape(width // 128 * n_slots + META, 128)] * 4
-        + [shape(l_rows + META, width), shape(1, q_rows, dtype=int32)],
+        + [shape(1, q_rows, dtype=int32), shape(META, l_rows)],
         [
             me,
             queries,
-            library,
             bucket.reshape(1, q_rows),
             query_charge.reshape(1, q_rows),
             library_charge.reshape(1, l_rows),
         ],
-        [SMEM] + [HBM] * 5,
+        [SMEM] + [HBM] * 4,
         [
             pltpu.VMEM((q_rows, width), BF16),
-            pltpu.VMEM((l_rows, width), BF16),
             pltpu.VMEM((1, q_rows), int32),
             pltpu.VMEM((1, q_rows), int32),
             pltpu.VMEM((1, l_rows), int32),
-            pltpu.SemaphoreType.DMA((5,)),
+            pltpu.SemaphoreType.DMA((4,)),
         ],
+        limit=PREP_LIMIT,
     )
     q12, q8, q4 = swapped(q12, 12), swapped(q8, 8), swapped(q4, 4)
-    lib_y, lib_c = swapped(lib, 2), swapped(lib, 1)
+    lib = shape(l_rows, width)
+    unit, unit_c = kernel_call(unit_kernel, [lib] * 2, [library, raw_c], [VMEM] * 2)
+    charge_c = swapped(charge, 1)
+    (near_charge,) = kernel_call(pair_kernel, [charge], [charge, charge_c], [VMEM] * 2)
+    far_charge = swapped(near_charge, 2)
     scratch = [pltpu.VMEM((4 * seen, width), BF16), pltpu.VMEM((4, 128, 128), F32)]
 
-    def scores(turn, one, other):
+    def scores(turn, charges, *units):
         blocks = kernel_call(
             functools.partial(score_kernel, turn),
             [shape(2 * seen, l_rows)] * 4,
-            [me, q0, q4, q8, q12, one, other],
-            [SMEM] + [VMEM] * 6,
+            [me, q12, q8, q4, q0, charges, *units],
+            [SMEM] + [VMEM] * 7,
             scratch,
-            flops=2 * 2 * 4 * seen * l_rows * width,
         )
+        return blocks
+
+    def returned(blocks):
         far, middle, close = swapped(blocks[3], 12), swapped(blocks[2], 8), swapped(blocks[1], 4)
-        return [blocks[0], close, middle, far]
-
-    near = scores(0, lib, lib_c)
-    lib_y, near[0] = lax.optimization_barrier((lib_y, near[0]))
-    lib_d = swapped(lib_y, 1)
-    far = scores(2, lib_y, lib_d)
+        return [far, middle, close, blocks[0]]
+
+    near = list(scores(0, near_charge, unit, unit_c))
+    raw_y, near[0] = lax.optimization_barrier((raw_y, near[0]))
+    raw_d = swapped(raw_y, 1)
+    near = returned(near)
+    (unit_y,) = kernel_call(unit_kernel, [lib], [raw_y], [VMEM])
+    (unit_d,) = kernel_call(unit_kernel, [lib], [raw_d], [VMEM])
+    far = returned(scores(2, far_charge, unit_y, unit_d))
     (out,) = kernel_call(
         home_kernel,
         [shape(q_rows, 3 * l_rows)],

time: 55.2 us -> 49.5 us (0.90)
  waiting for transfers between devices: 30.1 us -> 23.8 us
  local copies, waits for them, and re-layouts: 4.16 us -> 2.85 us
  starting transfers between devices: 16.7 us -> 17.7 us
  Pallas kernels: 4 us -> 4.9 us
    ppermute x12 -> x14, waiting for transfers between devices: 30.1 us -> 23.8 us  [swapped(): return lax.ppermute(value, 'slab', [(i, i ^ mask) for i in range(count)])]
    unnamed x10, local copies, waits for them, and re-layouts: 4.16 us -> 2.85 us
    ppermute x12 -> x14, starting transfers between devices: 16.7 us -> 17.7 us  [swapped(): return lax.ppermute(value, 'slab', [(i, i ^ mask) for i in range(count)])]
    pallas_call x4 -> x8, Pallas kernels: 4 us -> 4.9 us  [kernel_call(): pl.pallas_call(body, out_shape=[jax.ShapeDtypeStruct(o.shape, o.dtype) fo...]
  transfers between devices with their start and end apart: 12 -> 14, of which waited for: 5 -> 5; matrix products, arithmetic and copies ran while one was open for 0% -> 0% of each run, Pallas kernels for 3% -> 8%
where the time goes in v3:
time: 49.5 us; the launch traced here: 49.3 us
  waiting for transfers between devices  23.8 us (48%)
  starting transfers between devices  17.7 us (36%)
  Pallas kernels  4.9 us (10%)
  local copies, waits for them, and re-layouts  2.85 us (6%)
    ppermute x14, waiting for transfers between devices, swapped(): return lax.ppermute(value, 'slab', [(i, i ^ mask) for i in range(count)])  23.8 us
    ppermute x14, starting transfers between devices, swapped(): return lax.ppermute(value, 'slab', [(i, i ^ mask) for i in range(count)])  17.7 us
    pallas_call x8, Pallas kernels, kernel_call(): pl.pallas_call(body, out_shape=[jax.ShapeDtypeStruct(o.shape, o.dtype) fo...  4.9 us
    unnamed x10, local copies, waits for them, and re-layouts  2.85 us
  transfers between devices with their start and end apart: 14, of which 5 were waited for; matrix products, arithmetic and copies ran while one was open for 0% of the time, Pallas kernels for 8%

profile of v3, /device:TPU:0, one launch (start us, length us, event | category | flops | bytes accessed | tf_op | source)
XLA Modules:
  0.0 49.3 jit_solution(13696537359055826322)
XLA Ops:
  0.0 0.5 collective-permute-start.4
  0.5 2.5 %collective-permute-start.8 = (bf16[512,1024]{1,0:T(8,128)(2,1)}, bf16[512,1024]{1,0:T(8,128)(2,1)S(1)}, u32[]{:S(2)}, u32[]{:S(2)}) collective-permute-start(bf16[512,1024]{1,0:T(8,128)(2,1)} %refs_0_.1), channel_id=1, source_target_pairs={{0,2},{1,3},{2,0},{3,1},{4,6},{5,7},{6,4},{7,5},{8,10},{9,11},{10,... | collective-permute-start | bytes 3145736 | tf_op jit(solution)/shard_map/ppermute | solution.py:87
  3.0 0.0 copy-start.2
  3.0 0.0 copy-start.3
  3.0 0.0 copy-start.4
  3.0 0.7 %copy-done.2 = s32[512]{0:T(512)S(1)} copy-done((s32[512]{0:T(512)S(1)}, s32[512]{0:T(512)}, u32[]{:S(2)}) %copy-start.2) | copy-done | bytes 2072
  3.7 0.0 copy-done.3
  3.7 0.0 copy-done.4
  3.7 0.0 copy-start.1
  3.7 0.9 %copy-done.1 = bf16[128,1024]{1,0:T(8,128)(2,1)S(1)} copy-done((bf16[128,1024]{1,0:T(8,128)(2,1)S(1)}, bf16[128,1024]{1,0:T(8,128)(2,1)}, u32[]{:S(2)}) %copy-start.1) | copy-done | bytes 262168
  4.6 0.7 %shard_map.55 = (bf16[784,128]{1,0:T(8,128)(2,1)S(1)}, bf16[784,128]{1,0:T(8,128)(2,1)S(1)}, bf16[784,128]{1,0:T(8,128)(2,1)S(1)}, bf16[784,128]{1,0:T(8,128)(2,...) custom-call(s32[1]{0:T(128)} %bitcast.me_ref, bf16[128,1024]{1,0:T(8,128)(2,1)S(1)} %copy-done.1, ...), custom_call_target="tpu_custom_call" | custom-call | bytes 1 | tf_op jit(solution)/shard_map/pallas_call | solution.py:216
  5.3 0.3 collective-permute-start.3
  5.6 3.6 %collective-permute-start = (bf16[784,128]{1,0:T(8,128)(2,1)S(1)}, bf16[784,128]{1,0:T(8,128)(2,1)S(1)}, u32[]{:S(2)}, u32[]{:S(2)}) collective-permute-start(bf16[784,128]{1,0:T(8,128)(2,1)S(1)} %get-tuple-element.24), channel_id=1, source_target_pairs={{0,12},{1,13},{2,14},{3,15},{4,8},{5,9},{6,10},{7,11},{8,4},{9,5},... | collective-permute-start | bytes 602120 | tf_op jit(solution)/shard_map/ppermute | solution.py:87
  9.2 0.0 collective-permute-start.1
  9.2 0.0 collective-permute-done.3.other_ref
  9.2 0.8 %collective-permute-start.2 = (bf16[784,128]{1,0:T(8,128)(2,1)S(1)}, bf16[784,128]{1,0:T(8,128)(2,1)S(1)}, u32[]{:S(2)}, u32[]{:S(2)}) collective-permute-start(bf16[784,128]{1,0:T(8,128)(2,1)S(1)} %get-tuple-element.26), channel_id=1, source_target_pairs={{0,4},{1,5},{2,6},{3,7},{4,0},{5,1},{6,2},{7,3},{8,12},{9,13},{10,... | collective-permute-start | bytes 602120 | tf_op jit(solution)/shard_map/ppermute | solution.py:87
  10.0 0.0 collective-permute-done.4.refs_1_
  10.0 0.0 copy-start
  10.0 1.2 %copy-done = bf16[512,1024]{1,0:T(8,128)(2,1)S(1)} copy-done((bf16[512,1024]{1,0:T(8,128)(2,1)S(1)}, bf16[512,1024]{1,0:T(8,128)(2,1)}, u32[]{:S(2)}) %copy-start) | copy-done | bytes 1048600
  11.3 0.6 %shard_map.57 = (bf16[512,1024]{1,0:T(8,128)(2,1)S(1)}, bf16[512,1024]{1,0:T(8,128)(2,1)S(1)}) custom-call(bf16[512,1024]{1,0:T(8,128)(2,1)S(1)} %copy-done, bf16[512,1024]{1,0:T(8,128)(2,1)S(1)} %collective-permute-done.4.refs_1_), custom_call_target="tpu_custom_call" | custom-call | bytes 1 | tf_op jit(solution)/shard_map/pallas_call | solution.py:216
  11.9 3.5 %collective-permute-done.refs_0_ = bf16[784,128]{1,0:T(8,128)(2,1)S(1)} collective-permute-done((bf16[784,128]{1,0:T(8,128)(2,1)S(1)}, bf16[784,128]{1,0:T(8,128)(2,1)S(1)}, u32[]{:S(2)}, u32[]{:S(2)}) %collective-permute-start) | collective-permute-done | bytes 200736 | tf_op jit(solution)/shard_map/ppermute | solution.py:87
  15.4 11.3 %collective-permute-done.1.refs_1_ = bf16[784,128]{1,0:T(8,128)(2,1)S(1)} collective-permute-done((bf16[784,128]{1,0:T(8,128)(2,1)S(1)}, bf16[784,128]{1,0:T(8,128)(2,1)S(1)}, u32[]{:S(2)}, u32[]{:S(2)}) %collective-permute-start.1) | collective-permute-done | bytes 200736 | tf_op jit(solution)/shard_map/ppermute | solution.py:87
  26.7 0.0 collective-permute-done.2.refs_2_
  26.7 0.9 %shard_map.58 = (bf16[96,512]{1,0:T(8,128)(2,1)S(1)}, bf16[96,512]{1,0:T(8,128)(2,1)S(1)}, bf16[96,512]{1,0:T(8,128)(2,1)S(1)}, bf16[96,512]{1,0:T(8,128)(2,1)S(1)}) custom-call(s32[1]{0:T(128)} %bitcast.me_ref, bf16[784,128]{1,0:T(8,128)(2,1)S(1)} %collective-permute-done.refs_0_, bf16[784,128]{1,0:T(8,128)(2,1)S(1)} %collective-permute-done.1.refs_1_, ...), custom_call_target="tpu_custom_call" | custom-call | bytes 1 | tf_op jit(solution)/shard_map/pallas_call | solution.py:216
  27.6 0.0 collective-permute-done.8.refs_0_
  27.6 0.1 collective-permute-start.10
  27.7 3.1 %collective-permute-start.5 = (bf16[96,512]{1,0:T(8,128)(2,1)S(1)}, bf16[96,512]{1,0:T(8,128)(2,1)S(1)}, u32[]{:S(2)}, u32[]{:S(2)}) collective-permute-start(bf16[96,512]{1,0:T(8,128)(2,1)S(1)} %get-tuple-element.31), channel_id=1, source_target_pairs={{0,12},{1,13},{2,14},{3,15},{4,8},{5,9},{6,10},{7,11},{8,4},{9,5},... | collective-permute-start | bytes 294920 | tf_op jit(solution)/shard_map/ppermute | solution.py:87
  30.8 1.5 %collective-permute-start.9 = (bf16[16,512]{1,0:T(8,128)(2,1)S(1)}, bf16[16,512]{1,0:T(8,128)(2,1)S(1)}, u32[]{:S(2)}, u32[]{:S(2)}) collective-permute-start(bf16[16,512]{1,0:T(8,128)(2,1)S(1)} %shard_map.56.refs_4_), channel_id=1, source_target_pairs={{0,2},{1,3},{2,0},{3,1},{4,6},{5,7},{6,4},{7,5},{8,10},{9,11},{10,... | collective-permute-start | bytes 49160 | tf_op jit(solution)/shard_map/ppermute | solution.py:87
  32.4 0.3 shard_map.59.refs_5_
  32.7 0.1 collective-permute-start.6
  32.8 0.8 %collective-permute-start.7 = (bf16[96,512]{1,0:T(8,128)(2,1)S(1)}, bf16[96,512]{1,0:T(8,128)(2,1)S(1)}, u32[]{:S(2)}, u32[]{:S(2)}) collective-permute-start(bf16[96,512]{1,0:T(8,128)(2,1)S(1)} %get-tuple-element.33), channel_id=1, source_target_pairs={{0,4},{1,5},{2,6},{3,7},{4,0},{5,1},{6,2},{7,3},{8,12},{9,13},{10,... | collective-permute-start | bytes 294920 | tf_op jit(solution)/shard_map/ppermute | solution.py:87
  33.5 0.0 collective-permute-done.10.refs_0_
  33.5 0.3 shard_map.60.refs_6_
  33.9 0.7 %collective-permute-done.9.refs_4_ = bf16[16,512]{1,0:T(8,128)(2,1)S(1)} collective-permute-done((bf16[16,512]{1,0:T(8,128)(2,1)S(1)}, bf16[16,512]{1,0:T(8,128)(2,1)S(1)}, u32[]{:S(2)}, u32[]{:S(2)}) %collective-permute-start.9) | collective-permute-done | bytes 16416 | tf_op jit(solution)/shard_map/ppermute | solution.py:87
  34.6 0.9 %shard_map.61 = (bf16[96,512]{1,0:T(8,128)(2,1)S(1)}, bf16[96,512]{1,0:T(8,128)(2,1)S(1)}, bf16[96,512]{1,0:T(8,128)(2,1)S(1)}, bf16[96,512]{1,0:T(8,128)(2,1)S(1)}) custom-call(s32[1]{0:T(128)} %bitcast.me_ref, bf16[784,128]{1,0:T(8,128)(2,1)S(1)} %collective-permute-done.refs_0_, bf16[784,128]{1,0:T(8,128)(2,1)S(1)} %collective-permute-done.1.refs_1_, ...), custom_call_target="tpu_custom_call" | custom-call | bytes 1 | tf_op jit(solution)/shard_map/pallas_call | solution.py:216
  35.5 3.0 %collective-permute-start.11 = (bf16[96,512]{1,0:T(8,128)(2,1)S(1)}, bf16[96,512]{1,0:T(8,128)(2,1)S(1)}, u32[]{:S(2)}, u32[]{:S(2)}) collective-permute-start(bf16[96,512]{1,0:T(8,128)(2,1)S(1)} %get-tuple-element.37), channel_id=1, source_target_pairs={{0,12},{1,13},{2,14},{3,15},{4,8},{5,9},{6,10},{7,11},{8,4},{9,5},... | collective-permute-start | bytes 294920 | tf_op jit(solution)/shard_map/ppermute | solution.py:87
  38.5 0.0 collective-permute-start.12
  38.5 0.0 collective-permute-done.5.refs_0_
  38.5 1.5 %collective-permute-start.13 = (bf16[96,512]{1,0:T(8,128)(2,1)S(1)}, bf16[96,512]{1,0:T(8,128)(2,1)S(1)}, u32[]{:S(2)}, u32[]{:S(2)}) collective-permute-start(bf16[96,512]{1,0:T(8,128)(2,1)S(1)} %get-tuple-element.39), channel_id=1, source_target_pairs={{0,4},{1,5},{2,6},{3,7},{4,0},{5,1},{6,2},{7,3},{8,12},{9,13},{10,... | collective-permute-start | bytes 294920 | tf_op jit(solution)/shard_map/ppermute | solution.py:87
  39.9 3.4 %collective-permute-done.6.refs_1_ = bf16[96,512]{1,0:T(8,128)(2,1)S(1)} collective-permute-done((bf16[96,512]{1,0:T(8,128)(2,1)S(1)}, bf16[96,512]{1,0:T(8,128)(2,1)S(1)}, u32[]{:S(2)}, u32[]{:S(2)}) %collective-permute-start.6) | collective-permute-done | bytes 98336 | tf_op jit(solution)/shard_map/ppermute | solution.py:87
  43.3 0.0 collective-permute-done.7.refs_2_
  43.3 0.0 collective-permute-done.11.refs_4_
  43.3 4.9 %collective-permute-done.12.refs_5_ = bf16[96,512]{1,0:T(8,128)(2,1)S(1)} collective-permute-done((bf16[96,512]{1,0:T(8,128)(2,1)S(1)}, bf16[96,512]{1,0:T(8,128)(2,1)S(1)}, u32[]{:S(2)}, u32[]{:S(2)}) %collective-permute-start.12) | collective-permute-done | bytes 98336 | tf_op jit(solution)/shard_map/ppermute | solution.py:87
  48.2 0.0 collective-permute-done.13.refs_6_
  48.2 1.1 %shard_map.62 = bf16[128,1536]{1,0:T(8,128)(2,1)} custom-call(s32[1]{0:T(128)} %bitcast.me_ref, s32[1,128]{1,0:T(1,128)S(1)} %get-tuple-element.23.slot_ref, bf16[96,512]{1,0:T(8,128)(2,1)S(1)} %collective-permute-done.5.refs_0_, bf16[96,512]{1,0:T(8,128)(2,1)S(1)} %collective-permute-done.6.refs_1_, bf16[96,512]{1,0:T(8,128)(2,1)S(1)} %collective-permute-done.7.refs_2_, ...), custom_call_target="tpu_custom_call" | custom-call | bytes 1 | tf_op jit(solution)/shard_map/pallas_call | solution.py:216
  (1 shorter events, 0.0 us)
Async XLA Ops:
  0.0 10.0 %collective-permute-start.4 = (bf16[512,1024]{1,0:T(8,128)(2,1)}, bf16[512,1024]{1,0:T(8,128)(2,1)S(1)}, u32[]{:S(2)}, u32[]{:S(2)}) collective-permute-start(bf16[512,1024]{1,0:T(8,128)(2,1)} %refs_0_.1), channel_id=1, source_target_pairs={{0,1},{1,0},{2,3},{3,2},{4,5},{5,4},{6,7},{7,6},{8,9},{9,8},{10,11... | collective-permute-start | bytes 3145736 | tf_op jit(solution)/shard_map/ppermute | solution.py:87
  0.5 27.2 %collective-permute-start.8 = (bf16[512,1024]{1,0:T(8,128)(2,1)}, bf16[512,1024]{1,0:T(8,128)(2,1)S(1)}, u32[]{:S(2)}, u32[]{:S(2)}) collective-permute-start(bf16[512,1024]{1,0:T(8,128)(2,1)} %refs_0_.1), channel_id=1, source_target_pairs={{0,2},{1,3},{2,0},{3,1},{4,6},{5,7},{6,4},{7,5},{8,10},{9,11},{10,... | collective-permute-start | bytes 3145736 | tf_op jit(solution)/shard_map/ppermute | solution.py:87
  3.0 0.7 %copy-start.2 = (s32[512]{0:T(512)S(1)}, s32[512]{0:T(512)}, u32[]{:S(2)}) copy-start(s32[512]{0:T(512)} %param.9) | copy-start | bytes 6148
  3.0 0.7 %copy-start.3 = (s32[128,1]{0,1:T(1,128)S(1)}, s32[128,1]{0,1:T(1,128)}, u32[]{:S(2)}) copy-start(s32[128,1]{0,1:T(1,128)} %param.7) | copy-start | bytes 1540
  3.0 0.7 %copy-start.4 = (s32[128]{0:T(128)S(1)}, s32[128]{0:T(128)}, u32[]{:S(2)}) copy-start(s32[128]{0:T(128)} %param.8) | copy-start | bytes 1540
  3.7 1.0 %copy-start.1 = (bf16[128,1024]{1,0:T(8,128)(2,1)S(1)}, bf16[128,1024]{1,0:T(8,128)(2,1)}, u32[]{:S(2)}) copy-start(bf16[128,1024]{1,0:T(8,128)(2,1)} %q_hbm.1) | copy-start | bytes 786436
  5.3 3.9 %collective-permute-start.3 = (bf16[16,512]{1,0:T(8,128)(2,1)S(1)}, bf16[16,512]{1,0:T(8,128)(2,1)S(1)}, u32[]{:S(2)}, u32[]{:S(2)}) collective-permute-start(bf16[16,512]{1,0:T(8,128)(2,1)S(1)} %get-tuple-element.28.one_ref), channel_id=1, source_target_pairs={{0,1},{1,0},{2,3},{3,2},{4,5},{5,4},{6,7},{7,6},{8,9},{9,8},{10,11... | collective-permute-start | bytes 49160 | tf_op jit(solution)/shard_map/ppermute | solution.py:87
  5.6 9.8 %collective-permute-start = (bf16[784,128]{1,0:T(8,128)(2,1)S(1)}, bf16[784,128]{1,0:T(8,128)(2,1)S(1)}, u32[]{:S(2)}, u32[]{:S(2)}) collective-permute-start(bf16[784,128]{1,0:T(8,128)(2,1)S(1)} %get-tuple-element.24), channel_id=1, source_target_pairs={{0,12},{1,13},{2,14},{3,15},{4,8},{5,9},{6,10},{7,11},{8,4},{9,5},... | collective-permute-start | bytes 602120 | tf_op jit(solution)/shard_map/ppermute | solution.py:87
  9.2 17.5 %collective-permute-start.1 = (bf16[784,128]{1,0:T(8,128)(2,1)S(1)}, bf16[784,128]{1,0:T(8,128)(2,1)S(1)}, u32[]{:S(2)}, u32[]{:S(2)}) collective-permute-start(bf16[784,128]{1,0:T(8,128)(2,1)S(1)} %get-tuple-element.25), channel_id=1, source_target_pairs={{0,8},{1,9},{2,10},{3,11},{4,12},{5,13},{6,14},{7,15},{8,0},{9,1},... | collective-permute-start | bytes 602120 | tf_op jit(solution)/shard_map/ppermute | solution.py:87
  9.2 17.5 %collective-permute-start.2 = (bf16[784,128]{1,0:T(8,128)(2,1)S(1)}, bf16[784,128]{1,0:T(8,128)(2,1)S(1)}, u32[]{:S(2)}, u32[]{:S(2)}) collective-permute-start(bf16[784,128]{1,0:T(8,128)(2,1)S(1)} %get-tuple-element.26), channel_id=1, source_target_pairs={{0,4},{1,5},{2,6},{3,7},{4,0},{5,1},{6,2},{7,3},{8,12},{9,13},{10,... | collective-permute-start | bytes 602120 | tf_op jit(solution)/shard_map/ppermute | solution.py:87
  10.0 1.2 %copy-start = (bf16[512,1024]{1,0:T(8,128)(2,1)S(1)}, bf16[512,1024]{1,0:T(8,128)(2,1)}, u32[]{:S(2)}) copy-start(bf16[512,1024]{1,0:T(8,128)(2,1)} %refs_0_.1) | copy-start | bytes 3145732
  27.6 5.9 %collective-permute-start.10 = (bf16[512,1024]{1,0:T(8,128)(2,1)S(1)}, bf16[512,1024]{1,0:T(8,128)(2,1)S(1)}, u32[]{:S(2)}, u32[]{:S(2)}) collective-permute-start(bf16[512,1024]{1,0:T(8,128)(2,1)S(1)} %collective-permute-done.8.refs_0_), channel_id=1, source_target_pairs={{0,1},{1,0},{2,3},{3,2},{4,5},{5,4},{6,7},{7,6},{8,9},{9,8},{10,11... | collective-permute-start | bytes 3145736 | tf_op jit(solution)/shard_map/ppermute | solution.py:87
  27.7 10.8 %collective-permute-start.5 = (bf16[96,512]{1,0:T(8,128)(2,1)S(1)}, bf16[96,512]{1,0:T(8,128)(2,1)S(1)}, u32[]{:S(2)}, u32[]{:S(2)}) collective-permute-start(bf16[96,512]{1,0:T(8,128)(2,1)S(1)} %get-tuple-element.31), channel_id=1, source_target_pairs={{0,12},{1,13},{2,14},{3,15},{4,8},{5,9},{6,10},{7,11},{8,4},{9,5},... | collective-permute-start | bytes 294920 | tf_op jit(solution)/shard_map/ppermute | solution.py:87
  30.8 3.7 %collective-permute-start.9 = (bf16[16,512]{1,0:T(8,128)(2,1)S(1)}, bf16[16,512]{1,0:T(8,128)(2,1)S(1)}, u32[]{:S(2)}, u32[]{:S(2)}) collective-permute-start(bf16[16,512]{1,0:T(8,128)(2,1)S(1)} %shard_map.56.refs_4_), channel_id=1, source_target_pairs={{0,2},{1,3},{2,0},{3,1},{4,6},{5,7},{6,4},{7,5},{8,10},{9,11},{10,... | collective-permute-start | bytes 49160 | tf_op jit(solution)/shard_map/ppermute | solution.py:87
  32.7 10.6 %collective-permute-start.6 = (bf16[96,512]{1,0:T(8,128)(2,1)S(1)}, bf16[96,512]{1,0:T(8,128)(2,1)S(1)}, u32[]{:S(2)}, u32[]{:S(2)}) collective-permute-start(bf16[96,512]{1,0:T(8,128)(2,1)S(1)} %get-tuple-element.32), channel_id=1, source_target_pairs={{0,8},{1,9},{2,10},{3,11},{4,12},{5,13},{6,14},{7,15},{8,0},{9,1},... | collective-permute-start | bytes 294920 | tf_op jit(solution)/shard_map/ppermute | solution.py:87
  32.8 10.6 %collective-permute-start.7 = (bf16[96,512]{1,0:T(8,128)(2,1)S(1)}, bf16[96,512]{1,0:T(8,128)(2,1)S(1)}, u32[]{:S(2)}, u32[]{:S(2)}) collective-permute-start(bf16[96,512]{1,0:T(8,128)(2,1)S(1)} %get-tuple-element.33), channel_id=1, source_target_pairs={{0,4},{1,5},{2,6},{3,7},{4,0},{5,1},{6,2},{7,3},{8,12},{9,13},{10,... | collective-permute-start | bytes 294920 | tf_op jit(solution)/shard_map/ppermute | solution.py:87
  35.5 7.8 %collective-permute-start.11 = (bf16[96,512]{1,0:T(8,128)(2,1)S(1)}, bf16[96,512]{1,0:T(8,128)(2,1)S(1)}, u32[]{:S(2)}, u32[]{:S(2)}) collective-permute-start(bf16[96,512]{1,0:T(8,128)(2,1)S(1)} %get-tuple-element.37), channel_id=1, source_target_pairs={{0,12},{1,13},{2,14},{3,15},{4,8},{5,9},{6,10},{7,11},{8,4},{9,5},... | collective-permute-start | bytes 294920 | tf_op jit(solution)/shard_map/ppermute | solution.py:87
  38.5 9.7 %collective-permute-start.12 = (bf16[96,512]{1,0:T(8,128)(2,1)S(1)}, bf16[96,512]{1,0:T(8,128)(2,1)S(1)}, u32[]{:S(2)}, u32[]{:S(2)}) collective-permute-start(bf16[96,512]{1,0:T(8,128)(2,1)S(1)} %get-tuple-element.38), channel_id=1, source_target_pairs={{0,8},{1,9},{2,10},{3,11},{4,12},{5,13},{6,14},{7,15},{8,0},{9,1},... | collective-permute-start | bytes 294920 | tf_op jit(solution)/shard_map/ppermute | solution.py:87
  38.5 9.7 %collective-permute-start.13 = (bf16[96,512]{1,0:T(8,128)(2,1)S(1)}, bf16[96,512]{1,0:T(8,128)(2,1)S(1)}, u32[]{:S(2)}, u32[]{:S(2)}) collective-permute-start(bf16[96,512]{1,0:T(8,128)(2,1)S(1)} %get-tuple-element.39), channel_id=1, source_target_pairs={{0,4},{1,5},{2,6},{3,7},{4,0},{5,1},{6,2},{7,3},{8,12},{9,13},{10,... | collective-permute-start | bytes 294920 | tf_op jit(solution)/shard_map/ppermute | solution.py:87

commit v4 on v3

--- a/solution.py
+++ b/solution.py
@@ -11,8 +11,6 @@
 PLANE = 4
 CAP = 16
 META = 16
-PREP_LIMIT = 12 * 1024 * 1024
-COST = 1
 F32 = jnp.float32
 BF16 = jnp.bfloat16
 
@@ -92,53 +90,36 @@
     return (values * lax.rsqrt(jnp.sum(values * values, axis=-1, keepdims=True) + EPS)).astype(BF16)
 
 
-def prep_kernel(me_ref, q_hbm, bucket_hbm, qcharge_hbm, lcharge_hbm, *refs):
-    out_refs, slot_ref, lcharge_out = refs[:4], refs[4], refs[5]
-    q_ref, bucket_ref, qcharge_ref, lcharge_ref, sem = refs[6:]
-    copies = [
-        pltpu.make_async_copy(source, target, sem.at[n])
-        for n, (source, target) in enumerate(
-            [
-                (bucket_hbm, bucket_ref),
-                (qcharge_hbm, qcharge_ref),
-                (q_hbm, q_ref),
-                (lcharge_hbm, lcharge_ref),
-            ]
-        )
-    ]
-    for copy in copies:
-        copy.start()
-    q_rows, width = q_ref.shape
-    n_slots = (PLANE + 2) * CAP
-    total = 4 * PLANE * CAP
-    copies[0].wait()
-    copies[1].wait()
+def slot_kernel(bucket_ref, qcharge_ref, lcharge_ref, slot_ref, qcharge_out, lcharge_out):
+    q_rows = bucket_ref.shape[1]
     bucket = bucket_ref[...]
     along = jnp.broadcast_to(bucket.astype(F32), (q_rows, q_rows))
     i = lax.broadcasted_iota(jnp.int32, (q_rows, q_rows), 0)
     j = lax.broadcasted_iota(jnp.int32, (q_rows, q_rows), 1)
     earlier = jnp.where((along == along.T) & (i < j), 1.0, 0.0)
     rank = jnp.sum(earlier, axis=0, keepdims=True)
-    slot = bucket * CAP + rank.astype(jnp.int32)
-    slot_ref[...] = slot
-    charge = jnp.broadcast_to(qcharge_ref[...].astype(F32), (META, q_rows)).astype(BF16)
-    copies[2].wait()
+    slot_ref[...] = bucket * CAP + rank.astype(jnp.int32)
+    for source, target in ((qcharge_ref, qcharge_out), (lcharge_ref, lcharge_out)):
+        target[...] = jnp.broadcast_to(source[...].astype(F32), target.shape).astype(BF16)
+
+
+def query_kernel(me_ref, slot_ref, charge_ref, q_ref, *out_refs):
+    q_rows, width = q_ref.shape
+    n_slots = (PLANE + 2) * CAP
+    total = 4 * PLANE * CAP
     unit = unit_rows(q_ref[...])
     for k in range(4):
         plane = (me_ref[0] // PLANE) ^ k
-        rel = (slot + (total - (plane * PLANE - 1) * CAP)) % total
+        rel = (slot_ref[...] + (total - (plane * PLANE - 1) * CAP)) % total
         place = lax.broadcasted_iota(jnp.int32, (q_rows, q_rows), 0) == rel
         select = jnp.where(place, 1.0, 0.0).astype(BF16)
         rows = jnp.dot(select[:n_slots, :], unit, preferred_element_type=F32).astype(BF16)
         for n in range(width // 128):
             out_refs[k][n * n_slots : (n + 1) * n_slots, :] = rows[:, n * 128 : (n + 1) * 128]
         placed = lax.dot_general(
-            charge, select, (((1,), (1,)), ((), ())), preferred_element_type=F32
+            charge_ref[...], select, (((1,), (1,)), ((), ())), preferred_element_type=F32
         )
         out_refs[k][width // 128 * n_slots :, :] = placed.astype(BF16)
-    copies[3].wait()
-    lcharge = jnp.broadcast_to(lcharge_ref[...].astype(F32), lcharge_out.shape)
-    lcharge_out[...] = lcharge.astype(BF16)
 
 
 def unit_kernel(*refs):
@@ -156,7 +137,7 @@
 
 def score_kernel(turn, me_ref, *refs):
     lcharge_ref, lib_refs, out_refs = refs[4], refs[5:7], refs[7:11]
-    q_refs = refs[3::-1]
+    q_refs = [refs[at] for at in (3, 1, 0, 2)]
     rows_ref, charge_ref = refs[11:]
     n_slots, seen = (PLANE + 2) * CAP, 3 * CAP
     for n, lib in enumerate(lib_refs):
@@ -183,7 +164,8 @@
 
 
 def home_kernel(me_ref, slot_ref, *refs):
-    near, far, out_ref, flat_ref = refs[3::-1], refs[7:3:-1], refs[8], refs[9]
+    near, far = ([refs[first + at] for at in (3, 1, 0, 2)] for first in (0, 4))
+    out_ref, flat_ref = refs[8], refs[9]
     q_rows = slot_ref.shape[1]
     l_rows = near[0].shape[1]
     n_slab = 4 * PLANE
@@ -206,21 +188,20 @@
 
 VMEM = pl.BlockSpec(memory_space=pltpu.VMEM)
 SMEM = pl.BlockSpec(memory_space=pltpu.SMEM)
-HBM = pl.BlockSpec(memory_space=pltpu.HBM)
 
 
 MIB = 1024 * 1024
 
 
-def kernel_call(body, outs, args, specs, scratch=(), limit=12 * MIB):
+def kernel_call(body, outs, args, specs, scratch=(), cost=1):
     return pl.pallas_call(
         body,
         out_shape=[jax.ShapeDtypeStruct(o.shape, o.dtype) for o in outs],
         in_specs=specs,
         out_specs=[VMEM] * len(outs),
         scratch_shapes=scratch,
-        compiler_params=pltpu.CompilerParams(vmem_limit_bytes=limit),
-        cost_estimate=pl.CostEstimate(flops=0, bytes_accessed=COST, transcendentals=0),
+        compiler_params=pltpu.CompilerParams(vmem_limit_bytes=12 * MIB),
+        cost_estimate=pl.CostEstimate(flops=0, bytes_accessed=cost, transcendentals=0),
     )(*args)
 
 
@@ -235,26 +216,18 @@
     n_slots, seen = (PLANE + 2) * CAP, 3 * CAP
     int32 = jnp.int32
     raw_y, raw_c = swapped(library, 2), swapped(library, 1)
-    q0, q4, q8, q12, slot, charge = kernel_call(
-        prep_kernel,
-        [shape(width // 128 * n_slots + META, 128)] * 4
-        + [shape(1, q_rows, dtype=int32), shape(META, l_rows)],
-        [
-            me,
-            queries,
-            bucket.reshape(1, q_rows),
-            query_charge.reshape(1, q_rows),
-            library_charge.reshape(1, l_rows),
-        ],
-        [SMEM] + [HBM] * 4,
-        [
-            pltpu.VMEM((q_rows, width), BF16),
-            pltpu.VMEM((1, q_rows), int32),
-            pltpu.VMEM((1, q_rows), int32),
-            pltpu.VMEM((1, l_rows), int32),
-            pltpu.SemaphoreType.DMA((4,)),
-        ],
-        limit=PREP_LIMIT,
+    slot, qcharge, charge = kernel_call(
+        slot_kernel,
+        [shape(1, q_rows, dtype=int32), shape(META, q_rows), shape(META, l_rows)],
+        [x.reshape(1, -1) for x in (bucket, query_charge, library_charge)],
+        [VMEM] * 3,
+        cost=1,
+    )
+    q0, q4, q8, q12 = kernel_call(
+        query_kernel,
+        [shape(width // 128 * n_slots + META, 128)] * 4,
+        [me, slot, qcharge, queries],
+        [SMEM] + [VMEM] * 3,
     )
     q12, q8, q4 = swapped(q12, 12), swapped(q8, 8), swapped(q4, 4)
     lib = shape(l_rows, width)
@@ -268,7 +241,7 @@
         blocks = kernel_call(
             functools.partial(score_kernel, turn),
             [shape(2 * seen, l_rows)] * 4,
-            [me, q12, q8, q4, q0, charges, *units],
+            [me, q8, q4, q12, q0, charges, *units],
             [SMEM] + [VMEM] * 7,
             scratch,
         )
@@ -276,7 +249,7 @@
 
     def returned(blocks):
         far, middle, close = swapped(blocks[3], 12), swapped(blocks[2], 8), swapped(blocks[1], 4)
-        return [far, middle, close, blocks[0]]
+        return [middle, close, far, blocks[0]]
 
     near = list(scores(0, near_charge, unit, unit_c))
     raw_y, near[0] = lax.optimization_barrier((raw_y, near[0]))

time: 49.5 us -> 48.2 us (0.974)
  waiting for transfers between devices: 23.8 us -> 21 us
  starting transfers between devices: 17.7 us -> 19 us
    ppermute x14, waiting for transfers between devices: 23.8 us -> 21 us  [swapped(): return lax.ppermute(value, 'slab', [(i, i ^ mask) for i in range(count)])]
    ppermute x14, starting transfers between devices: 17.7 us -> 19 us  [swapped(): return lax.ppermute(value, 'slab', [(i, i ^ mask) for i in range(count)])]
    pallas_call x8 -> x9, Pallas kernels: 4.9 us -> 4.83 us  [kernel_call(): pl.pallas_call(body, out_shape=[jax.ShapeDtypeStruct(o.shape, o.dtype) fo...]
  transfers between devices with their start and end apart: 14 -> 14, of which waited for: 5 -> 6; matrix products, arithmetic and copies ran while one was open for 0% -> 0% of each run, Pallas kernels for 8% -> 8%
where the time goes in v4:
time: 48.2 us; the launch traced here: 47.7 us
  waiting for transfers between devices  21 us (44%)
  starting transfers between devices  19 us (39%)
  Pallas kernels  4.83 us (10%)
  local copies, waits for them, and re-layouts  2.85 us (6%)
    ppermute x14, waiting for transfers between devices, swapped(): return lax.ppermute(value, 'slab', [(i, i ^ mask) for i in range(count)])  21 us
    ppermute x14, starting transfers between devices, swapped(): return lax.ppermute(value, 'slab', [(i, i ^ mask) for i in range(count)])  19 us
    pallas_call x9, Pallas kernels, kernel_call(): pl.pallas_call(body, out_shape=[jax.ShapeDtypeStruct(o.shape, o.dtype) fo...  4.83 us
    unnamed x10, local copies, waits for them, and re-layouts  2.85 us
  transfers between devices with their start and end apart: 14, of which 6 were waited for; matrix products, arithmetic and copies ran while one was open for 0% of the time, Pallas kernels for 8%

profile of v4, /device:TPU:0, one launch (start us, length us, event | category | flops | bytes accessed | tf_op | source)
XLA Modules:
  0.0 47.7 jit_solution(18185950442598812456)
XLA Ops:
  0.0 0.5 collective-permute-start.4
  0.5 2.5 %collective-permute-start.8 = (bf16[512,1024]{1,0:T(8,128)(2,1)}, bf16[512,1024]{1,0:T(8,128)(2,1)S(1)}, u32[]{:S(2)}, u32[]{:S(2)}) collective-permute-start(bf16[512,1024]{1,0:T(8,128)(2,1)} %refs_0_.1), channel_id=1, source_target_pairs={{0,2},{1,3},{2,0},{3,1},{4,6},{5,7},{6,4},{7,5},{8,10},{9,11},{10,... | collective-permute-start | bytes 3145736 | tf_op jit(solution)/shard_map/ppermute | solution.py:85
  3.0 0.0 copy-start.2
  3.0 0.0 copy-start.3
  3.0 0.0 copy-start.4
  3.0 0.7 %copy-done.2 = s32[512]{0:T(512)S(1)} copy-done((s32[512]{0:T(512)S(1)}, s32[512]{0:T(512)}, u32[]{:S(2)}) %copy-start.2) | copy-done | bytes 2072
  3.7 0.0 copy-done.3
  3.7 0.0 copy-done.4
  3.7 0.1 shard_map.55
  3.8 0.3 collective-permute-start.3
  4.1 0.0 copy-start.1
  4.1 0.9 %copy-done.1 = bf16[128,1024]{1,0:T(8,128)(2,1)S(1)} copy-done((bf16[128,1024]{1,0:T(8,128)(2,1)S(1)}, bf16[128,1024]{1,0:T(8,128)(2,1)}, u32[]{:S(2)}) %copy-start.1) | copy-done | bytes 262168
  5.0 0.5 %shard_map.56 = (bf16[784,128]{1,0:T(8,128)(2,1)S(1)}, bf16[784,128]{1,0:T(8,128)(2,1)S(1)}, bf16[784,128]{1,0:T(8,128)(2,1)S(1)}, bf16[784,128]{1,0:T(8,128)(2,1)S(1)}) custom-call(s32[1]{0:T(128)} %bitcast.me_ref, s32[1,128]{1,0:T(1,128)S(1)} %get-tuple-element.24.slot_ref, bf16[16,128]{1,0:T(8,128)(2,1)S(1)} %get-tuple-element.25.charge_ref, ...), custom_call_target="tpu_custom_call" | custom-call | bytes 1 | tf_op jit(solution)/shard_map/pallas_call | solution.py:197
  5.5 2.7 %collective-permute-start = (bf16[784,128]{1,0:T(8,128)(2,1)S(1)}, bf16[784,128]{1,0:T(8,128)(2,1)S(1)}, u32[]{:S(2)}, u32[]{:S(2)}) collective-permute-start(bf16[784,128]{1,0:T(8,128)(2,1)S(1)} %get-tuple-element.26), channel_id=1, source_target_pairs={{0,8},{1,9},{2,10},{3,11},{4,12},{5,13},{6,14},{7,15},{8,0},{9,1},... | collective-permute-start | bytes 602120 | tf_op jit(solution)/shard_map/ppermute | solution.py:85
  8.2 1.6 %collective-permute-start.1 = (bf16[784,128]{1,0:T(8,128)(2,1)S(1)}, bf16[784,128]{1,0:T(8,128)(2,1)S(1)}, u32[]{:S(2)}, u32[]{:S(2)}) collective-permute-start(bf16[784,128]{1,0:T(8,128)(2,1)S(1)} %get-tuple-element.27), channel_id=1, source_target_pairs={{0,4},{1,5},{2,6},{3,7},{4,0},{5,1},{6,2},{7,3},{8,12},{9,13},{10,... | collective-permute-start | bytes 602120 | tf_op jit(solution)/shard_map/ppermute | solution.py:85
  9.8 0.0 collective-permute-done.3.other_ref
  9.8 0.2 collective-permute-start.2
  10.0 0.0 collective-permute-done.4.refs_1_
  10.0 0.0 copy-start
  10.0 1.2 %copy-done = bf16[512,1024]{1,0:T(8,128)(2,1)S(1)} copy-done((bf16[512,1024]{1,0:T(8,128)(2,1)S(1)}, bf16[512,1024]{1,0:T(8,128)(2,1)}, u32[]{:S(2)}) %copy-start) | copy-done | bytes 1048600
  11.2 0.6 %shard_map.58 = (bf16[512,1024]{1,0:T(8,128)(2,1)S(1)}, bf16[512,1024]{1,0:T(8,128)(2,1)S(1)}) custom-call(bf16[512,1024]{1,0:T(8,128)(2,1)S(1)} %copy-done, bf16[512,1024]{1,0:T(8,128)(2,1)S(1)} %collective-permute-done.4.refs_1_), custom_call_target="tpu_custom_call" | custom-call | bytes 1 | tf_op jit(solution)/shard_map/pallas_call | solution.py:197
  11.9 7.1 %collective-permute-done.refs_0_ = bf16[784,128]{1,0:T(8,128)(2,1)S(1)} collective-permute-done((bf16[784,128]{1,0:T(8,128)(2,1)S(1)}, bf16[784,128]{1,0:T(8,128)(2,1)S(1)}, u32[]{:S(2)}, u32[]{:S(2)}) %collective-permute-start) | collective-permute-done | bytes 200736 | tf_op jit(solution)/shard_map/ppermute | solution.py:85
  18.9 0.0 collective-permute-done.1.refs_1_
  18.9 4.5 %collective-permute-done.2.refs_2_ = bf16[784,128]{1,0:T(8,128)(2,1)S(1)} collective-permute-done((bf16[784,128]{1,0:T(8,128)(2,1)S(1)}, bf16[784,128]{1,0:T(8,128)(2,1)S(1)}, u32[]{:S(2)}, u32[]{:S(2)}) %collective-permute-start.2) | collective-permute-done | bytes 200736 | tf_op jit(solution)/shard_map/ppermute | solution.py:85
  23.5 0.9 %shard_map.59 = (bf16[96,512]{1,0:T(8,128)(2,1)S(1)}, bf16[96,512]{1,0:T(8,128)(2,1)S(1)}, bf16[96,512]{1,0:T(8,128)(2,1)S(1)}, bf16[96,512]{1,0:T(8,128)(2,1)S(1)}) custom-call(s32[1]{0:T(128)} %bitcast.me_ref, bf16[784,128]{1,0:T(8,128)(2,1)S(1)} %collective-permute-done.refs_0_, bf16[784,128]{1,0:T(8,128)(2,1)S(1)} %collective-permute-done.1.refs_1_, ...), custom_call_target="tpu_custom_call" | custom-call | bytes 1 | tf_op jit(solution)/shard_map/pallas_call | solution.py:197
  24.4 2.6 %collective-permute-done.8.refs_0_ = bf16[512,1024]{1,0:T(8,128)(2,1)S(1)} collective-permute-done((bf16[512,1024]{1,0:T(8,128)(2,1)}, bf16[512,1024]{1,0:T(8,128)(2,1)S(1)}, u32[]{:S(2)}, u32[]{:S(2)}) %collective-permute-start.8) | collective-permute-done | bytes 1048608 | tf_op jit(solution)/shard_map/ppermute | solution.py:85
  27.0 0.0 collective-permute-start.10
  27.0 3.2 %collective-permute-start.5 = (bf16[96,512]{1,0:T(8,128)(2,1)S(1)}, bf16[96,512]{1,0:T(8,128)(2,1)S(1)}, u32[]{:S(2)}, u32[]{:S(2)}) collective-permute-start(bf16[96,512]{1,0:T(8,128)(2,1)S(1)} %get-tuple-element.33), channel_id=1, source_target_pairs={{0,8},{1,9},{2,10},{3,11},{4,12},{5,13},{6,14},{7,15},{8,0},{9,1},... | collective-permute-start | bytes 294920 | tf_op jit(solution)/shard_map/ppermute | solution.py:85
  30.3 1.1 %collective-permute-start.9 = (bf16[16,512]{1,0:T(8,128)(2,1)S(1)}, bf16[16,512]{1,0:T(8,128)(2,1)S(1)}, u32[]{:S(2)}, u32[]{:S(2)}) collective-permute-start(bf16[16,512]{1,0:T(8,128)(2,1)S(1)} %shard_map.57.refs_4_), channel_id=1, source_target_pairs={{0,2},{1,3},{2,0},{3,1},{4,6},{5,7},{6,4},{7,5},{8,10},{9,11},{10,... | collective-permute-start | bytes 49160 | tf_op jit(solution)/shard_map/ppermute | solution.py:85
  31.3 0.3 shard_map.60.refs_5_
  31.7 1.6 %collective-permute-start.6 = (bf16[96,512]{1,0:T(8,128)(2,1)S(1)}, bf16[96,512]{1,0:T(8,128)(2,1)S(1)}, u32[]{:S(2)}, u32[]{:S(2)}) collective-permute-start(bf16[96,512]{1,0:T(8,128)(2,1)S(1)} %get-tuple-element.34), channel_id=1, source_target_pairs={{0,4},{1,5},{2,6},{3,7},{4,0},{5,1},{6,2},{7,3},{8,12},{9,13},{10,... | collective-permute-start | bytes 294920 | tf_op jit(solution)/shard_map/ppermute | solution.py:85
  33.3 0.2 collective-permute-start.7
  33.5 0.0 collective-permute-done.10.refs_0_
  33.5 0.3 shard_map.61.refs_6_
  33.9 0.1 collective-permute-done.9.refs_4_
  34.0 0.9 %shard_map.62 = (bf16[96,512]{1,0:T(8,128)(2,1)S(1)}, bf16[96,512]{1,0:T(8,128)(2,1)S(1)}, bf16[96,512]{1,0:T(8,128)(2,1)S(1)}, bf16[96,512]{1,0:T(8,128)(2,1)S(1)}) custom-call(s32[1]{0:T(128)} %bitcast.me_ref, bf16[784,128]{1,0:T(8,128)(2,1)S(1)} %collective-permute-done.refs_0_, bf16[784,128]{1,0:T(8,128)(2,1)S(1)} %collective-permute-done.1.refs_1_, ...), custom_call_target="tpu_custom_call" | custom-call | bytes 1 | tf_op jit(solution)/shard_map/pallas_call | solution.py:197
  34.9 1.6 %collective-permute-start.11 = (bf16[96,512]{1,0:T(8,128)(2,1)S(1)}, bf16[96,512]{1,0:T(8,128)(2,1)S(1)}, u32[]{:S(2)}, u32[]{:S(2)}) collective-permute-start(bf16[96,512]{1,0:T(8,128)(2,1)S(1)} %get-tuple-element.39), channel_id=1, source_target_pairs={{0,8},{1,9},{2,10},{3,11},{4,12},{5,13},{6,14},{7,15},{8,0},{9,1},... | collective-permute-start | bytes 294920 | tf_op jit(solution)/shard_map/ppermute | solution.py:85
  36.5 2.5 %collective-permute-start.12 = (bf16[96,512]{1,0:T(8,128)(2,1)S(1)}, bf16[96,512]{1,0:T(8,128)(2,1)S(1)}, u32[]{:S(2)}, u32[]{:S(2)}) collective-permute-start(bf16[96,512]{1,0:T(8,128)(2,1)S(1)} %get-tuple-element.40), channel_id=1, source_target_pairs={{0,4},{1,5},{2,6},{3,7},{4,0},{5,1},{6,2},{7,3},{8,12},{9,13},{10,... | collective-permute-start | bytes 294920 | tf_op jit(solution)/shard_map/ppermute | solution.py:85
  39.0 0.0 collective-permute-done.5.refs_0_
  39.0 1.0 %collective-permute-start.13 = (bf16[96,512]{1,0:T(8,128)(2,1)S(1)}, bf16[96,512]{1,0:T(8,128)(2,1)S(1)}, u32[]{:S(2)}, u32[]{:S(2)}) collective-permute-start(bf16[96,512]{1,0:T(8,128)(2,1)S(1)} %get-tuple-element.41), channel_id=1, source_target_pairs={{0,12},{1,13},{2,14},{3,15},{4,8},{5,9},{6,10},{7,11},{8,4},{9,5},... | collective-permute-start | bytes 294920 | tf_op jit(solution)/shard_map/ppermute | solution.py:85
  40.0 0.0 collective-permute-done.6.refs_1_
  40.0 0.8 %collective-permute-done.7.refs_2_ = bf16[96,512]{1,0:T(8,128)(2,1)S(1)} collective-permute-done((bf16[96,512]{1,0:T(8,128)(2,1)S(1)}, bf16[96,512]{1,0:T(8,128)(2,1)S(1)}, u32[]{:S(2)}, u32[]{:S(2)}) %collective-permute-start.7) | collective-permute-done | bytes 98336 | tf_op jit(solution)/shard_map/ppermute | solution.py:85
  40.8 5.9 %collective-permute-done.11.refs_4_ = bf16[96,512]{1,0:T(8,128)(2,1)S(1)} collective-permute-done((bf16[96,512]{1,0:T(8,128)(2,1)S(1)}, bf16[96,512]{1,0:T(8,128)(2,1)S(1)}, u32[]{:S(2)}, u32[]{:S(2)}) %collective-permute-start.11) | collective-permute-done | bytes 98336 | tf_op jit(solution)/shard_map/ppermute | solution.py:85
  46.7 0.0 collective-permute-done.12.refs_5_
  46.7 0.0 collective-permute-done.13.refs_6_
  46.7 1.1 %shard_map.63 = bf16[128,1536]{1,0:T(8,128)(2,1)} custom-call(s32[1]{0:T(128)} %bitcast.me_ref, s32[1,128]{1,0:T(1,128)S(1)} %get-tuple-element.24.slot_ref, bf16[96,512]{1,0:T(8,128)(2,1)S(1)} %collective-permute-done.5.refs_0_, bf16[96,512]{1,0:T(8,128)(2,1)S(1)} %collective-permute-done.6.refs_1_, bf16[96,512]{1,0:T(8,128)(2,1)S(1)} %collective-permute-done.7.refs_2_, ...), custom_call_target="tpu_custom_call" | custom-call | bytes 1 | tf_op jit(solution)/shard_map/pallas_call | solution.py:197
  (1 shorter events, 0.0 us)
Async XLA Ops:
  0.0 10.0 %collective-permute-start.4 = (bf16[512,1024]{1,0:T(8,128)(2,1)}, bf16[512,1024]{1,0:T(8,128)(2,1)S(1)}, u32[]{:S(2)}, u32[]{:S(2)}) collective-permute-start(bf16[512,1024]{1,0:T(8,128)(2,1)} %refs_0_.1), channel_id=1, source_target_pairs={{0,1},{1,0},{2,3},{3,2},{4,5},{5,4},{6,7},{7,6},{8,9},{9,8},{10,11... | collective-permute-start | bytes 3145736 | tf_op jit(solution)/shard_map/ppermute | solution.py:85
  0.5 26.6 %collective-permute-start.8 = (bf16[512,1024]{1,0:T(8,128)(2,1)}, bf16[512,1024]{1,0:T(8,128)(2,1)S(1)}, u32[]{:S(2)}, u32[]{:S(2)}) collective-permute-start(bf16[512,1024]{1,0:T(8,128)(2,1)} %refs_0_.1), channel_id=1, source_target_pairs={{0,2},{1,3},{2,0},{3,1},{4,6},{5,7},{6,4},{7,5},{8,10},{9,11},{10,... | collective-permute-start | bytes 3145736 | tf_op jit(solution)/shard_map/ppermute | solution.py:85
  3.0 0.7 %copy-start.2 = (s32[512]{0:T(512)S(1)}, s32[512]{0:T(512)}, u32[]{:S(2)}) copy-start(s32[512]{0:T(512)} %param.9) | copy-start | bytes 6148
  3.0 0.7 %copy-start.3 = (s32[128,1]{0,1:T(1,128)S(1)}, s32[128,1]{0,1:T(1,128)}, u32[]{:S(2)}) copy-start(s32[128,1]{0,1:T(1,128)} %param.7) | copy-start | bytes 1540
  3.0 0.7 %copy-start.4 = (s32[128]{0:T(128)S(1)}, s32[128]{0:T(128)}, u32[]{:S(2)}) copy-start(s32[128]{0:T(128)} %param.8) | copy-start | bytes 1540
  3.8 6.0 %collective-permute-start.3 = (bf16[16,512]{1,0:T(8,128)(2,1)S(1)}, bf16[16,512]{1,0:T(8,128)(2,1)S(1)}, u32[]{:S(2)}, u32[]{:S(2)}) collective-permute-start(bf16[16,512]{1,0:T(8,128)(2,1)S(1)} %get-tuple-element.30.one_ref), channel_id=1, source_target_pairs={{0,1},{1,0},{2,3},{3,2},{4,5},{5,4},{6,7},{7,6},{8,9},{9,8},{10,11... | collective-permute-start | bytes 49160 | tf_op jit(solution)/shard_map/ppermute | solution.py:85
  4.1 0.9 %copy-start.1 = (bf16[128,1024]{1,0:T(8,128)(2,1)S(1)}, bf16[128,1024]{1,0:T(8,128)(2,1)}, u32[]{:S(2)}) copy-start(bf16[128,1024]{1,0:T(8,128)(2,1)} %q_ref.1) | copy-start | bytes 786436
  5.5 13.4 %collective-permute-start = (bf16[784,128]{1,0:T(8,128)(2,1)S(1)}, bf16[784,128]{1,0:T(8,128)(2,1)S(1)}, u32[]{:S(2)}, u32[]{:S(2)}) collective-permute-start(bf16[784,128]{1,0:T(8,128)(2,1)S(1)} %get-tuple-element.26), channel_id=1, source_target_pairs={{0,8},{1,9},{2,10},{3,11},{4,12},{5,13},{6,14},{7,15},{8,0},{9,1},... | collective-permute-start | bytes 602120 | tf_op jit(solution)/shard_map/ppermute | solution.py:85
  8.2 10.7 %collective-permute-start.1 = (bf16[784,128]{1,0:T(8,128)(2,1)S(1)}, bf16[784,128]{1,0:T(8,128)(2,1)S(1)}, u32[]{:S(2)}, u32[]{:S(2)}) collective-permute-start(bf16[784,128]{1,0:T(8,128)(2,1)S(1)} %get-tuple-element.27), channel_id=1, source_target_pairs={{0,4},{1,5},{2,6},{3,7},{4,0},{5,1},{6,2},{7,3},{8,12},{9,13},{10,... | collective-permute-start | bytes 602120 | tf_op jit(solution)/shard_map/ppermute | solution.py:85
  9.8 13.7 %collective-permute-start.2 = (bf16[784,128]{1,0:T(8,128)(2,1)S(1)}, bf16[784,128]{1,0:T(8,128)(2,1)S(1)}, u32[]{:S(2)}, u32[]{:S(2)}) collective-permute-start(bf16[784,128]{1,0:T(8,128)(2,1)S(1)} %get-tuple-element.28), channel_id=1, source_target_pairs={{0,12},{1,13},{2,14},{3,15},{4,8},{5,9},{6,10},{7,11},{8,4},{9,5},... | collective-permute-start | bytes 602120 | tf_op jit(solution)/shard_map/ppermute | solution.py:85
  10.0 1.2 %copy-start = (bf16[512,1024]{1,0:T(8,128)(2,1)S(1)}, bf16[512,1024]{1,0:T(8,128)(2,1)}, u32[]{:S(2)}) copy-start(bf16[512,1024]{1,0:T(8,128)(2,1)} %refs_0_.1) | copy-start | bytes 3145732
  27.0 6.5 %collective-permute-start.10 = (bf16[512,1024]{1,0:T(8,128)(2,1)S(1)}, bf16[512,1024]{1,0:T(8,128)(2,1)S(1)}, u32[]{:S(2)}, u32[]{:S(2)}) collective-permute-start(bf16[512,1024]{1,0:T(8,128)(2,1)S(1)} %collective-permute-done.8.refs_0_), channel_id=1, source_target_pairs={{0,1},{1,0},{2,3},{3,2},{4,5},{5,4},{6,7},{7,6},{8,9},{9,8},{10,11... | collective-permute-start | bytes 3145736 | tf_op jit(solution)/shard_map/ppermute | solution.py:85
  27.0 12.0 %collective-permute-start.5 = (bf16[96,512]{1,0:T(8,128)(2,1)S(1)}, bf16[96,512]{1,0:T(8,128)(2,1)S(1)}, u32[]{:S(2)}, u32[]{:S(2)}) collective-permute-start(bf16[96,512]{1,0:T(8,128)(2,1)S(1)} %get-tuple-element.33), channel_id=1, source_target_pairs={{0,8},{1,9},{2,10},{3,11},{4,12},{5,13},{6,14},{7,15},{8,0},{9,1},... | collective-permute-start | bytes 294920 | tf_op jit(solution)/shard_map/ppermute | solution.py:85
  30.3 3.7 %collective-permute-start.9 = (bf16[16,512]{1,0:T(8,128)(2,1)S(1)}, bf16[16,512]{1,0:T(8,128)(2,1)S(1)}, u32[]{:S(2)}, u32[]{:S(2)}) collective-permute-start(bf16[16,512]{1,0:T(8,128)(2,1)S(1)} %shard_map.57.refs_4_), channel_id=1, source_target_pairs={{0,2},{1,3},{2,0},{3,1},{4,6},{5,7},{6,4},{7,5},{8,10},{9,11},{10,... | collective-permute-start | bytes 49160 | tf_op jit(solution)/shard_map/ppermute | solution.py:85
  31.7 8.3 %collective-permute-start.6 = (bf16[96,512]{1,0:T(8,128)(2,1)S(1)}, bf16[96,512]{1,0:T(8,128)(2,1)S(1)}, u32[]{:S(2)}, u32[]{:S(2)}) collective-permute-start(bf16[96,512]{1,0:T(8,128)(2,1)S(1)} %get-tuple-element.34), channel_id=1, source_target_pairs={{0,4},{1,5},{2,6},{3,7},{4,0},{5,1},{6,2},{7,3},{8,12},{9,13},{10,... | collective-permute-start | bytes 294920 | tf_op jit(solution)/shard_map/ppermute | solution.py:85
  33.3 7.5 %collective-permute-start.7 = (bf16[96,512]{1,0:T(8,128)(2,1)S(1)}, bf16[96,512]{1,0:T(8,128)(2,1)S(1)}, u32[]{:S(2)}, u32[]{:S(2)}) collective-permute-start(bf16[96,512]{1,0:T(8,128)(2,1)S(1)} %get-tuple-element.35), channel_id=1, source_target_pairs={{0,12},{1,13},{2,14},{3,15},{4,8},{5,9},{6,10},{7,11},{8,4},{9,5},... | collective-permute-start | bytes 294920 | tf_op jit(solution)/shard_map/ppermute | solution.py:85
  34.9 11.8 %collective-permute-start.11 = (bf16[96,512]{1,0:T(8,128)(2,1)S(1)}, bf16[96,512]{1,0:T(8,128)(2,1)S(1)}, u32[]{:S(2)}, u32[]{:S(2)}) collective-permute-start(bf16[96,512]{1,0:T(8,128)(2,1)S(1)} %get-tuple-element.39), channel_id=1, source_target_pairs={{0,8},{1,9},{2,10},{3,11},{4,12},{5,13},{6,14},{7,15},{8,0},{9,1},... | collective-permute-start | bytes 294920 | tf_op jit(solution)/shard_map/ppermute | solution.py:85
  36.5 10.1 %collective-permute-start.12 = (bf16[96,512]{1,0:T(8,128)(2,1)S(1)}, bf16[96,512]{1,0:T(8,128)(2,1)S(1)}, u32[]{:S(2)}, u32[]{:S(2)}) collective-permute-start(bf16[96,512]{1,0:T(8,128)(2,1)S(1)} %get-tuple-element.40), channel_id=1, source_target_pairs={{0,4},{1,5},{2,6},{3,7},{4,0},{5,1},{6,2},{7,3},{8,12},{9,13},{10,... | collective-permute-start | bytes 294920 | tf_op jit(solution)/shard_map/ppermute | solution.py:85
  39.0 7.6 %collective-permute-start.13 = (bf16[96,512]{1,0:T(8,128)(2,1)S(1)}, bf16[96,512]{1,0:T(8,128)(2,1)S(1)}, u32[]{:S(2)}, u32[]{:S(2)}) collective-permute-start(bf16[96,512]{1,0:T(8,128)(2,1)S(1)} %get-tuple-element.41), channel_id=1, source_target_pairs={{0,12},{1,13},{2,14},{3,15},{4,8},{5,9},{6,10},{7,11},{8,4},{9,5},... | collective-permute-start | bytes 294920 | tf_op jit(solution)/shard_map/ppermute | solution.py:85

commit v5 on v4

--- a/solution.py
+++ b/solution.py
@@ -135,15 +135,15 @@
     out_ref[...] = jnp.where(line == 0, one, other).astype(BF16)
 
 
-def score_kernel(turn, me_ref, *refs):
-    lcharge_ref, lib_refs, out_refs = refs[4], refs[5:7], refs[7:11]
-    q_refs = [refs[at] for at in (3, 1, 0, 2)]
-    rows_ref, charge_ref = refs[11:]
+def score_kernel(count, turn, me_ref, *refs):
+    q_refs, refs = refs[:count], refs[count:]
+    lcharge_ref, lib_refs, out_refs = refs[0], refs[1:3], refs[3 : 3 + count]
+    rows_ref, charge_ref = refs[3 + count :]
     n_slots, seen = (PLANE + 2) * CAP, 3 * CAP
     for n, lib in enumerate(lib_refs):
         width = lib.shape[1]
         at = pl.multiple_of(((me_ref[0] % PLANE) ^ (turn ^ n)) * CAP, CAP)
-        for k in range(4):
+        for k in range(count):
             for c in range(width // 128):
                 rows_ref[k * seen : (k + 1) * seen, c * 128 : (c + 1) * 128] = q_refs[k][
                     pl.ds(pl.multiple_of(at + c * n_slots, CAP), seen), :
@@ -155,7 +155,7 @@
         products = lax.dot_general(
             rows_ref[...], lib[...], (((1,), (1,)), ((), ())), preferred_element_type=F32
         )
-        for k in range(4):
+        for k in range(count):
             row_charge = charge_ref[k, pl.ds(at, seen), :][:, 0:1]
             kept = jnp.abs(row_charge - lib_charge) <= 2.0
             out_refs[k][n * seen : (n + 1) * seen, :] = jnp.where(
@@ -164,7 +164,8 @@
 
 
 def home_kernel(me_ref, slot_ref, *refs):
-    near, far = ([refs[first + at] for at in (3, 1, 0, 2)] for first in (0, 4))
+    near = [refs[at] for at in (0, 1, 2, 3)]
+    far = [refs[4 + at] for at in (3, 1, 0, 2)]
     out_ref, flat_ref = refs[8], refs[9]
     q_rows = slot_ref.shape[1]
     l_rows = near[0].shape[1]
@@ -235,29 +236,30 @@
     charge_c = swapped(charge, 1)
     (near_charge,) = kernel_call(pair_kernel, [charge], [charge, charge_c], [VMEM] * 2)
     far_charge = swapped(near_charge, 2)
-    scratch = [pltpu.VMEM((4 * seen, width), BF16), pltpu.VMEM((4, 128, 128), F32)]
-
-    def scores(turn, charges, *units):
-        blocks = kernel_call(
-            functools.partial(score_kernel, turn),
-            [shape(2 * seen, l_rows)] * 4,
-            [me, q8, q4, q12, q0, charges, *units],
-            [SMEM] + [VMEM] * 7,
-            scratch,
+
+    def scores(turn, q_blocks, *parts):
+        count = len(q_blocks)
+        return kernel_call(
+            functools.partial(score_kernel, count, turn),
+            [shape(2 * seen, l_rows)] * count,
+            [me, *q_blocks, *parts],
+            [SMEM] + [VMEM] * (count + len(parts)),
+            [pltpu.VMEM((count * seen, width), BF16), pltpu.VMEM((count, 128, 128), F32)],
         )
-        return blocks
-
-    def returned(blocks):
-        far, middle, close = swapped(blocks[3], 12), swapped(blocks[2], 8), swapped(blocks[1], 4)
-        return [middle, close, far, blocks[0]]
-
-    near = list(scores(0, near_charge, unit, unit_c))
-    raw_y, near[0] = lax.optimization_barrier((raw_y, near[0]))
+
+    near8, near4, near0 = scores(0, [q8, q4, q0], near_charge, unit, unit_c)
+    near8, near4 = swapped(near8, 8), swapped(near4, 4)
+    raw_y, q12, near8, near4, far_charge = lax.optimization_barrier(
+        (raw_y, q12, near8, near4, far_charge)
+    )
     raw_d = swapped(raw_y, 1)
-    near = returned(near)
+    (near12,) = scores(0, [q12], near_charge, unit, unit_c)
+    near12 = swapped(near12, 12)
     (unit_y,) = kernel_call(unit_kernel, [lib], [raw_y], [VMEM])
     (unit_d,) = kernel_call(unit_kernel, [lib], [raw_d], [VMEM])
-    far = returned(scores(2, far_charge, unit_y, unit_d))
+    far8, far4, far12, far0 = scores(2, [q8, q4, q12, q0], far_charge, unit_y, unit_d)
+    far8, far4, far12 = swapped(far8, 8), swapped(far4, 4), swapped(far12, 12)
+    near, far = [near0, near4, near8, near12], [far8, far4, far12, far0]
     (out,) = kernel_call(
         home_kernel,
         [shape(q_rows, 3 * l_rows)],

time: 48.2 us -> 47.1 us (0.977)
  waiting for transfers between devices: 21 us -> 18.6 us
  Pallas kernels: 4.83 us -> 5.57 us
  starting transfers between devices: 19 us -> 19.7 us
    ppermute x14, waiting for transfers between devices: 21 us -> 18.6 us  [swapped(): return lax.ppermute(value, 'slab', [(i, i ^ mask) for i in range(count)])]
    pallas_call x9 -> x10, Pallas kernels: 4.83 us -> 5.57 us  [kernel_call(): pl.pallas_call(body, out_shape=[jax.ShapeDtypeStruct(o.shape, o.dtype) fo...]
    ppermute x14, starting transfers between devices: 19 us -> 19.7 us  [swapped(): return lax.ppermute(value, 'slab', [(i, i ^ mask) for i in range(count)])]
  transfers between devices with their start and end apart: 14 -> 14, of which waited for: 6 -> 7; matrix products, arithmetic and copies ran while one was open for 0% -> 0% of each run, Pallas kernels for 8% -> 10%
where the time goes in v5:
time: 47.1 us; the launch traced here: 46.7 us
  starting transfers between devices  19.7 us (42%)
  waiting for transfers between devices  18.6 us (39%)
  Pallas kernels  5.57 us (12%)
  local copies, waits for them, and re-layouts  2.85 us (6%)
    ppermute x14, starting transfers between devices, swapped(): return lax.ppermute(value, 'slab', [(i, i ^ mask) for i in range(count)])  19.7 us
    ppermute x14, waiting for transfers between devices, swapped(): return lax.ppermute(value, 'slab', [(i, i ^ mask) for i in range(count)])  18.6 us
    pallas_call x10, Pallas kernels, kernel_call(): pl.pallas_call(body, out_shape=[jax.ShapeDtypeStruct(o.shape, o.dtype) fo...  5.57 us
    unnamed x10, local copies, waits for them, and re-layouts  2.85 us
  transfers between devices with their start and end apart: 14, of which 7 were waited for; matrix products, arithmetic and copies ran while one was open for 0% of the time, Pallas kernels for 10%

profile of v5, /device:TPU:0, one launch (start us, length us, event | category | flops | bytes accessed | tf_op | source)
XLA Modules:
  0.0 46.7 jit_solution(675351217221816169)
XLA Ops:
  0.0 0.5 collective-permute-start.3
  0.5 2.5 %collective-permute-start.4 = (bf16[512,1024]{1,0:T(8,128)(2,1)}, bf16[512,1024]{1,0:T(8,128)(2,1)S(1)}, u32[]{:S(2)}, u32[]{:S(2)}) collective-permute-start(bf16[512,1024]{1,0:T(8,128)(2,1)} %refs_0_.1), channel_id=1, source_target_pairs={{0,2},{1,3},{2,0},{3,1},{4,6},{5,7},{6,4},{7,5},{8,10},{9,11},{10,... | collective-permute-start | bytes 3145736 | tf_op jit(solution)/shard_map/ppermute | solution.py:85
  3.0 0.0 copy-start.2
  3.0 0.0 copy-start.3
  3.0 0.0 copy-start.4
  3.0 0.7 %copy-done.2 = s32[512]{0:T(512)S(1)} copy-done((s32[512]{0:T(512)S(1)}, s32[512]{0:T(512)}, u32[]{:S(2)}) %copy-start.2) | copy-done | bytes 2072
  3.7 0.0 copy-done.3
  3.7 0.0 copy-done.4
  3.7 0.1 shard_map.55
  3.8 0.0 copy-start.1
  3.8 0.9 %copy-done.1 = bf16[128,1024]{1,0:T(8,128)(2,1)S(1)} copy-done((bf16[128,1024]{1,0:T(8,128)(2,1)S(1)}, bf16[128,1024]{1,0:T(8,128)(2,1)}, u32[]{:S(2)}) %copy-start.1) | copy-done | bytes 262168
  4.7 0.5 %shard_map.56 = (bf16[784,128]{1,0:T(8,128)(2,1)S(1)}, bf16[784,128]{1,0:T(8,128)(2,1)S(1)}, bf16[784,128]{1,0:T(8,128)(2,1)S(1)}, bf16[784,128]{1,0:T(8,128)(2,1)S(1)}) custom-call(s32[1]{0:T(128)} %bitcast.me_ref, s32[1,128]{1,0:T(1,128)S(1)} %get-tuple-element.26.slot_ref, bf16[16,128]{1,0:T(8,128)(2,1)S(1)} %get-tuple-element.27.charge_ref, ...), custom_call_target="tpu_custom_call" | custom-call | bytes 1 | tf_op jit(solution)/shard_map/pallas_call | solution.py:198
  5.3 2.7 %collective-permute-start = (bf16[784,128]{1,0:T(8,128)(2,1)S(1)}, bf16[784,128]{1,0:T(8,128)(2,1)S(1)}, u32[]{:S(2)}, u32[]{:S(2)}) collective-permute-start(bf16[784,128]{1,0:T(8,128)(2,1)S(1)} %get-tuple-element.28), channel_id=1, source_target_pairs={{0,8},{1,9},{2,10},{3,11},{4,12},{5,13},{6,14},{7,15},{8,0},{9,1},... | collective-permute-start | bytes 602120 | tf_op jit(solution)/shard_map/ppermute | solution.py:85
  7.9 1.6 %collective-permute-start.1 = (bf16[784,128]{1,0:T(8,128)(2,1)S(1)}, bf16[784,128]{1,0:T(8,128)(2,1)S(1)}, u32[]{:S(2)}, u32[]{:S(2)}) collective-permute-start(bf16[784,128]{1,0:T(8,128)(2,1)S(1)} %get-tuple-element.29), channel_id=1, source_target_pairs={{0,4},{1,5},{2,6},{3,7},{4,0},{5,1},{6,2},{7,3},{8,12},{9,13},{10,... | collective-permute-start | bytes 602120 | tf_op jit(solution)/shard_map/ppermute | solution.py:85
  9.5 0.0 collective-permute-start.2
  9.5 1.2 %collective-permute-done.2.other_ref = bf16[16,512]{1,0:T(8,128)(2,1)S(1)} collective-permute-done((bf16[16,512]{1,0:T(8,128)(2,1)S(1)}, bf16[16,512]{1,0:T(8,128)(2,1)S(1)}, u32[]{:S(2)}, u32[]{:S(2)}) %collective-permute-start.2) | collective-permute-done | bytes 16416 | tf_op jit(solution)/shard_map/ppermute | solution.py:85
  10.7 0.2 collective-permute-start.5
  10.9 0.0 collective-permute-done.3.refs_1_
  10.9 0.0 copy-start
  10.9 1.2 %copy-done = bf16[512,1024]{1,0:T(8,128)(2,1)S(1)} copy-done((bf16[512,1024]{1,0:T(8,128)(2,1)S(1)}, bf16[512,1024]{1,0:T(8,128)(2,1)}, u32[]{:S(2)}) %copy-start) | copy-done | bytes 1048600
  12.1 0.6 %shard_map.58 = (bf16[512,1024]{1,0:T(8,128)(2,1)S(1)}, bf16[512,1024]{1,0:T(8,128)(2,1)S(1)}) custom-call(bf16[512,1024]{1,0:T(8,128)(2,1)S(1)} %copy-done, bf16[512,1024]{1,0:T(8,128)(2,1)S(1)} %collective-permute-done.3.refs_1_), custom_call_target="tpu_custom_call" | custom-call | bytes 1 | tf_op jit(solution)/shard_map/pallas_call | solution.py:198
  12.8 6.0 %collective-permute-done.refs_0_ = bf16[784,128]{1,0:T(8,128)(2,1)S(1)} collective-permute-done((bf16[784,128]{1,0:T(8,128)(2,1)S(1)}, bf16[784,128]{1,0:T(8,128)(2,1)S(1)}, u32[]{:S(2)}, u32[]{:S(2)}) %collective-permute-start) | collective-permute-done | bytes 200736 | tf_op jit(solution)/shard_map/ppermute | solution.py:85
  18.8 0.0 collective-permute-done.1.refs_1_
  18.8 0.9 %shard_map.59 = (bf16[96,512]{1,0:T(8,128)(2,1)S(1)}, bf16[96,512]{1,0:T(8,128)(2,1)S(1)}, bf16[96,512]{1,0:T(8,128)(2,1)S(1)}) custom-call(s32[1]{0:T(128)} %bitcast.me_ref, bf16[784,128]{1,0:T(8,128)(2,1)S(1)} %collective-permute-done.refs_0_, bf16[784,128]{1,0:T(8,128)(2,1)S(1)} %collective-permute-done.1.refs_1_, ...), custom_call_target="tpu_custom_call" | custom-call | bytes 1 | tf_op jit(solution)/shard_map/pallas_call | solution.py:198
  19.7 1.2 %collective-permute-start.6 = (bf16[96,512]{1,0:T(8,128)(2,1)S(1)}, bf16[96,512]{1,0:T(8,128)(2,1)S(1)}, u32[]{:S(2)}, u32[]{:S(2)}) collective-permute-start(bf16[96,512]{1,0:T(8,128)(2,1)S(1)} %get-tuple-element.36), channel_id=1, source_target_pairs={{0,8},{1,9},{2,10},{3,11},{4,12},{5,13},{6,14},{7,15},{8,0},{9,1},... | collective-permute-start | bytes 294920 | tf_op jit(solution)/shard_map/ppermute | solution.py:85
  20.9 2.5 %collective-permute-start.7 = (bf16[96,512]{1,0:T(8,128)(2,1)S(1)}, bf16[96,512]{1,0:T(8,128)(2,1)S(1)}, u32[]{:S(2)}, u32[]{:S(2)}) collective-permute-start(bf16[96,512]{1,0:T(8,128)(2,1)S(1)} %get-tuple-element.37), channel_id=1, source_target_pairs={{0,4},{1,5},{2,6},{3,7},{4,0},{5,1},{6,2},{7,3},{8,12},{9,13},{10,... | collective-permute-start | bytes 294920 | tf_op jit(solution)/shard_map/ppermute | solution.py:85
  23.4 0.5 %collective-permute-start.8 = (bf16[16,512]{1,0:T(8,128)(2,1)S(1)}, bf16[16,512]{1,0:T(8,128)(2,1)S(1)}, u32[]{:S(2)}, u32[]{:S(2)}) collective-permute-start(bf16[16,512]{1,0:T(8,128)(2,1)S(1)} %shard_map.57.refs_3_.refs_1_), channel_id=1, source_target_pairs={{0,2},{1,3},{2,0},{3,1},{4,6},{5,7},{6,4},{7,5},{8,10},{9,11},{10,... | collective-permute-start | bytes 49160 | tf_op jit(solution)/shard_map/ppermute | solution.py:85
  23.9 3.4 %collective-permute-done.8.refs_4_ = bf16[16,512]{1,0:T(8,128)(2,1)S(1)} collective-permute-done((bf16[16,512]{1,0:T(8,128)(2,1)S(1)}, bf16[16,512]{1,0:T(8,128)(2,1)S(1)}, u32[]{:S(2)}, u32[]{:S(2)}) %collective-permute-start.8) | collective-permute-done | bytes 16416 | tf_op jit(solution)/shard_map/ppermute | solution.py:85
  27.4 0.0 collective-permute-done.5.refs_0_.refs_2_
  27.4 0.0 collective-permute-done.4.refs_0_
  27.4 3.1 %collective-permute-done.6.refs_2_ = bf16[96,512]{1,0:T(8,128)(2,1)S(1)} collective-permute-done((bf16[96,512]{1,0:T(8,128)(2,1)S(1)}, bf16[96,512]{1,0:T(8,128)(2,1)S(1)}, u32[]{:S(2)}, u32[]{:S(2)}) %collective-permute-start.6) | collective-permute-done | bytes 98336 | tf_op jit(solution)/shard_map/ppermute | solution.py:85
  30.5 0.0 collective-permute-done.7.refs_1_
  30.5 0.0 collective-permute-start.10
  30.5 0.3 shard_map.61.refs_5_
  30.8 0.8 %shard_map.60 = bf16[96,512]{1,0:T(8,128)(2,1)S(1)} custom-call(s32[1]{0:T(128)} %bitcast.me_ref, bf16[784,128]{1,0:T(8,128)(2,1)S(1)} %collective-permute-done.5.refs_0_.refs_2_, bf16[16,512]{1,0:T(8,128)(2,1)S(1)} %shard_map.57.refs_3_.refs_1_, bf16[512,1024]{1,0:T(8,128)(2,1)S(1)} %get-tuple-element.32.refs_4_.refs_2_, ...), custom_call_target="tpu_custom_call" | custom-call | bytes 1 | tf_op jit(solution)/shard_map/pallas_call | solution.py:198
  31.6 3.5 %collective-permute-start.9 = (bf16[96,512]{1,0:T(8,128)(2,1)S(1)}, bf16[96,512]{1,0:T(8,128)(2,1)S(1)}, u32[]{:S(2)}, u32[]{:S(2)}) collective-permute-start(bf16[96,512]{1,0:T(8,128)(2,1)S(1)} %shard_map.60), channel_id=1, source_target_pairs={{0,12},{1,13},{2,14},{3,15},{4,8},{5,9},{6,10},{7,11},{8,4},{9,5},... | collective-permute-start | bytes 294920 | tf_op jit(solution)/shard_map/ppermute | solution.py:85
  35.2 0.0 collective-permute-done.10.refs_0_
  35.2 0.3 shard_map.62.refs_6_
  35.5 0.9 %shard_map.63 = (bf16[96,512]{1,0:T(8,128)(2,1)S(1)}, bf16[96,512]{1,0:T(8,128)(2,1)S(1)}, bf16[96,512]{1,0:T(8,128)(2,1)S(1)}, bf16[96,512]{1,0:T(8,128)(2,1)S(1)}) custom-call(s32[1]{0:T(128)} %bitcast.me_ref, bf16[784,128]{1,0:T(8,128)(2,1)S(1)} %collective-permute-done.refs_0_, bf16[784,128]{1,0:T(8,128)(2,1)S(1)} %collective-permute-done.1.refs_1_, ...), custom_call_target="tpu_custom_call" | custom-call | bytes 1 | tf_op jit(solution)/shard_map/pallas_call | solution.py:198
  36.4 0.1 collective-permute-start.11
  36.5 2.0 %collective-permute-start.12 = (bf16[96,512]{1,0:T(8,128)(2,1)S(1)}, bf16[96,512]{1,0:T(8,128)(2,1)S(1)}, u32[]{:S(2)}, u32[]{:S(2)}) collective-permute-start(bf16[96,512]{1,0:T(8,128)(2,1)S(1)} %get-tuple-element.44), channel_id=1, source_target_pairs={{0,4},{1,5},{2,6},{3,7},{4,0},{5,1},{6,2},{7,3},{8,12},{9,13},{10,... | collective-permute-start | bytes 294920 | tf_op jit(solution)/shard_map/ppermute | solution.py:85
  38.5 2.4 %collective-permute-start.13 = (bf16[96,512]{1,0:T(8,128)(2,1)S(1)}, bf16[96,512]{1,0:T(8,128)(2,1)S(1)}, u32[]{:S(2)}, u32[]{:S(2)}) collective-permute-start(bf16[96,512]{1,0:T(8,128)(2,1)S(1)} %get-tuple-element.45), channel_id=1, source_target_pairs={{0,12},{1,13},{2,14},{3,15},{4,8},{5,9},{6,10},{7,11},{8,4},{9,5},... | collective-permute-start | bytes 294920 | tf_op jit(solution)/shard_map/ppermute | solution.py:85
  40.9 0.0 collective-permute-done.9.refs_3_
  40.9 3.4 %collective-permute-done.11.refs_4_ = bf16[96,512]{1,0:T(8,128)(2,1)S(1)} collective-permute-done((bf16[96,512]{1,0:T(8,128)(2,1)S(1)}, bf16[96,512]{1,0:T(8,128)(2,1)S(1)}, u32[]{:S(2)}, u32[]{:S(2)}) %collective-permute-start.11) | collective-permute-done | bytes 98336 | tf_op jit(solution)/shard_map/ppermute | solution.py:85
  44.3 0.3 collective-permute-done.12.refs_5_
  44.5 1.1 %collective-permute-done.13.refs_6_ = bf16[96,512]{1,0:T(8,128)(2,1)S(1)} collective-permute-done((bf16[96,512]{1,0:T(8,128)(2,1)S(1)}, bf16[96,512]{1,0:T(8,128)(2,1)S(1)}, u32[]{:S(2)}, u32[]{:S(2)}) %collective-permute-start.13) | collective-permute-done | bytes 98336 | tf_op jit(solution)/shard_map/ppermute | solution.py:85
  45.7 1.1 %shard_map.64 = bf16[128,1536]{1,0:T(8,128)(2,1)} custom-call(s32[1]{0:T(128)} %bitcast.me_ref, s32[1,128]{1,0:T(1,128)S(1)} %get-tuple-element.26.slot_ref, bf16[96,512]{1,0:T(8,128)(2,1)S(1)} %get-tuple-element.34.refs_0_, bf16[96,512]{1,0:T(8,128)(2,1)S(1)} %collective-permute-done.7.refs_1_, bf16[96,512]{1,0:T(8,128)(2,1)S(1)} %collective-permute-done.6.refs_2_, ...), custom_call_target="tpu_custom_call" | custom-call | bytes 1 | tf_op jit(solution)/shard_map/pallas_call | solution.py:198
  (1 shorter events, 0.0 us)
Async XLA Ops:
  0.0 10.9 %collective-permute-start.3 = (bf16[512,1024]{1,0:T(8,128)(2,1)}, bf16[512,1024]{1,0:T(8,128)(2,1)S(1)}, u32[]{:S(2)}, u32[]{:S(2)}) collective-permute-start(bf16[512,1024]{1,0:T(8,128)(2,1)} %refs_0_.1), channel_id=1, source_target_pairs={{0,1},{1,0},{2,3},{3,2},{4,5},{5,4},{6,7},{7,6},{8,9},{9,8},{10,11... | collective-permute-start | bytes 3145736 | tf_op jit(solution)/shard_map/ppermute | solution.py:85
  0.5 26.9 %collective-permute-start.4 = (bf16[512,1024]{1,0:T(8,128)(2,1)}, bf16[512,1024]{1,0:T(8,128)(2,1)S(1)}, u32[]{:S(2)}, u32[]{:S(2)}) collective-permute-start(bf16[512,1024]{1,0:T(8,128)(2,1)} %refs_0_.1), channel_id=1, source_target_pairs={{0,2},{1,3},{2,0},{3,1},{4,6},{5,7},{6,4},{7,5},{8,10},{9,11},{10,... | collective-permute-start | bytes 3145736 | tf_op jit(solution)/shard_map/ppermute | solution.py:85
  3.0 0.7 %copy-start.2 = (s32[512]{0:T(512)S(1)}, s32[512]{0:T(512)}, u32[]{:S(2)}) copy-start(s32[512]{0:T(512)} %param.9) | copy-start | bytes 6148
  3.0 0.7 %copy-start.3 = (s32[128,1]{0,1:T(1,128)S(1)}, s32[128,1]{0,1:T(1,128)}, u32[]{:S(2)}) copy-start(s32[128,1]{0,1:T(1,128)} %param.7) | copy-start | bytes 1540
  3.0 0.7 %copy-start.4 = (s32[128]{0:T(128)S(1)}, s32[128]{0:T(128)}, u32[]{:S(2)}) copy-start(s32[128]{0:T(128)} %param.8) | copy-start | bytes 1540
  3.8 1.0 %copy-start.1 = (bf16[128,1024]{1,0:T(8,128)(2,1)S(1)}, bf16[128,1024]{1,0:T(8,128)(2,1)}, u32[]{:S(2)}) copy-start(bf16[128,1024]{1,0:T(8,128)(2,1)} %q_ref.1) | copy-start | bytes 786436
  5.3 13.5 %collective-permute-start = (bf16[784,128]{1,0:T(8,128)(2,1)S(1)}, bf16[784,128]{1,0:T(8,128)(2,1)S(1)}, u32[]{:S(2)}, u32[]{:S(2)}) collective-permute-start(bf16[784,128]{1,0:T(8,128)(2,1)S(1)} %get-tuple-element.28), channel_id=1, source_target_pairs={{0,8},{1,9},{2,10},{3,11},{4,12},{5,13},{6,14},{7,15},{8,0},{9,1},... | collective-permute-start | bytes 602120 | tf_op jit(solution)/shard_map/ppermute | solution.py:85
  7.9 10.9 %collective-permute-start.1 = (bf16[784,128]{1,0:T(8,128)(2,1)S(1)}, bf16[784,128]{1,0:T(8,128)(2,1)S(1)}, u32[]{:S(2)}, u32[]{:S(2)}) collective-permute-start(bf16[784,128]{1,0:T(8,128)(2,1)S(1)} %get-tuple-element.29), channel_id=1, source_target_pairs={{0,4},{1,5},{2,6},{3,7},{4,0},{5,1},{6,2},{7,3},{8,12},{9,13},{10,... | collective-permute-start | bytes 602120 | tf_op jit(solution)/shard_map/ppermute | solution.py:85
  9.5 1.2 %collective-permute-start.2 = (bf16[16,512]{1,0:T(8,128)(2,1)S(1)}, bf16[16,512]{1,0:T(8,128)(2,1)S(1)}, u32[]{:S(2)}, u32[]{:S(2)}) collective-permute-start(bf16[16,512]{1,0:T(8,128)(2,1)S(1)} %get-tuple-element.31.one_ref), channel_id=1, source_target_pairs={{0,1},{1,0},{2,3},{3,2},{4,5},{5,4},{6,7},{7,6},{8,9},{9,8},{10,11... | collective-permute-start | bytes 49160 | tf_op jit(solution)/shard_map/ppermute | solution.py:85
  10.7 16.7 %collective-permute-start.5 = (bf16[784,128]{1,0:T(8,128)(2,1)S(1)}, bf16[784,128]{1,0:T(8,128)(2,1)S(1)}, u32[]{:S(2)}, u32[]{:S(2)}) collective-permute-start(bf16[784,128]{1,0:T(8,128)(2,1)S(1)} %get-tuple-element.35), channel_id=1, source_target_pairs={{0,12},{1,13},{2,14},{3,15},{4,8},{5,9},{6,10},{7,11},{8,4},{9,5},... | collective-permute-start | bytes 602120 | tf_op jit(solution)/shard_map/ppermute | solution.py:85
  10.9 1.2 %copy-start = (bf16[512,1024]{1,0:T(8,128)(2,1)S(1)}, bf16[512,1024]{1,0:T(8,128)(2,1)}, u32[]{:S(2)}) copy-start(bf16[512,1024]{1,0:T(8,128)(2,1)} %refs_0_.1) | copy-start | bytes 3145732
  19.7 10.8 %collective-permute-start.6 = (bf16[96,512]{1,0:T(8,128)(2,1)S(1)}, bf16[96,512]{1,0:T(8,128)(2,1)S(1)}, u32[]{:S(2)}, u32[]{:S(2)}) collective-permute-start(bf16[96,512]{1,0:T(8,128)(2,1)S(1)} %get-tuple-element.36), channel_id=1, source_target_pairs={{0,8},{1,9},{2,10},{3,11},{4,12},{5,13},{6,14},{7,15},{8,0},{9,1},... | collective-permute-start | bytes 294920 | tf_op jit(solution)/shard_map/ppermute | solution.py:85
  20.9 9.6 %collective-permute-start.7 = (bf16[96,512]{1,0:T(8,128)(2,1)S(1)}, bf16[96,512]{1,0:T(8,128)(2,1)S(1)}, u32[]{:S(2)}, u32[]{:S(2)}) collective-permute-start(bf16[96,512]{1,0:T(8,128)(2,1)S(1)} %get-tuple-element.37), channel_id=1, source_target_pairs={{0,4},{1,5},{2,6},{3,7},{4,0},{5,1},{6,2},{7,3},{8,12},{9,13},{10,... | collective-permute-start | bytes 294920 | tf_op jit(solution)/shard_map/ppermute | solution.py:85
  23.4 3.9 %collective-permute-start.8 = (bf16[16,512]{1,0:T(8,128)(2,1)S(1)}, bf16[16,512]{1,0:T(8,128)(2,1)S(1)}, u32[]{:S(2)}, u32[]{:S(2)}) collective-permute-start(bf16[16,512]{1,0:T(8,128)(2,1)S(1)} %shard_map.57.refs_3_.refs_1_), channel_id=1, source_target_pairs={{0,2},{1,3},{2,0},{3,1},{4,6},{5,7},{6,4},{7,5},{8,10},{9,11},{10,... | collective-permute-start | bytes 49160 | tf_op jit(solution)/shard_map/ppermute | solution.py:85
  30.5 4.6 %collective-permute-start.10 = (bf16[512,1024]{1,0:T(8,128)(2,1)S(1)}, bf16[512,1024]{1,0:T(8,128)(2,1)S(1)}, u32[]{:S(2)}, u32[]{:S(2)}) collective-permute-start(bf16[512,1024]{1,0:T(8,128)(2,1)S(1)} %collective-permute-done.4.refs_0_), channel_id=1, source_target_pairs={{0,1},{1,0},{2,3},{3,2},{4,5},{5,4},{6,7},{7,6},{8,9},{9,8},{10,11... | collective-permute-start | bytes 3145736 | tf_op jit(solution)/shard_map/ppermute | solution.py:85
  31.6 9.2 %collective-permute-start.9 = (bf16[96,512]{1,0:T(8,128)(2,1)S(1)}, bf16[96,512]{1,0:T(8,128)(2,1)S(1)}, u32[]{:S(2)}, u32[]{:S(2)}) collective-permute-start(bf16[96,512]{1,0:T(8,128)(2,1)S(1)} %shard_map.60), channel_id=1, source_target_pairs={{0,12},{1,13},{2,14},{3,15},{4,8},{5,9},{6,10},{7,11},{8,4},{9,5},... | collective-permute-start | bytes 294920 | tf_op jit(solution)/shard_map/ppermute | solution.py:85
  36.4 7.9 %collective-permute-start.11 = (bf16[96,512]{1,0:T(8,128)(2,1)S(1)}, bf16[96,512]{1,0:T(8,128)(2,1)S(1)}, u32[]{:S(2)}, u32[]{:S(2)}) collective-permute-start(bf16[96,512]{1,0:T(8,128)(2,1)S(1)} %get-tuple-element.43), channel_id=1, source_target_pairs={{0,8},{1,9},{2,10},{3,11},{4,12},{5,13},{6,14},{7,15},{8,0},{9,1},... | collective-permute-start | bytes 294920 | tf_op jit(solution)/shard_map/ppermute | solution.py:85
  36.5 8.1 %collective-permute-start.12 = (bf16[96,512]{1,0:T(8,128)(2,1)S(1)}, bf16[96,512]{1,0:T(8,128)(2,1)S(1)}, u32[]{:S(2)}, u32[]{:S(2)}) collective-permute-start(bf16[96,512]{1,0:T(8,128)(2,1)S(1)} %get-tuple-element.44), channel_id=1, source_target_pairs={{0,4},{1,5},{2,6},{3,7},{4,0},{5,1},{6,2},{7,3},{8,12},{9,13},{10,... | collective-permute-start | bytes 294920 | tf_op jit(solution)/shard_map/ppermute | solution.py:85
  38.5 7.2 %collective-permute-start.13 = (bf16[96,512]{1,0:T(8,128)(2,1)S(1)}, bf16[96,512]{1,0:T(8,128)(2,1)S(1)}, u32[]{:S(2)}, u32[]{:S(2)}) collective-permute-start(bf16[96,512]{1,0:T(8,128)(2,1)S(1)} %get-tuple-element.45), channel_id=1, source_target_pairs={{0,12},{1,13},{2,14},{3,15},{4,8},{5,9},{6,10},{7,11},{8,4},{9,5},... | collective-permute-start | bytes 294920 | tf_op jit(solution)/shard_map/ppermute | solution.py:85

commit v6 on v5

--- a/solution.py
+++ b/solution.py
@@ -110,16 +110,18 @@
     unit = unit_rows(q_ref[...])
     for k in range(4):
         plane = (me_ref[0] // PLANE) ^ k
-        rel = (slot_ref[...] + (total - (plane * PLANE - 1) * CAP)) % total
+        count = n_slots if k < 3 else n_slots - 2 * CAP
+        skip = plane % 2 * (2 * CAP) if k == 3 else 0
+        rel = (slot_ref[...] + (total - (plane * PLANE - 1) * CAP)) % total - skip
         place = lax.broadcasted_iota(jnp.int32, (q_rows, q_rows), 0) == rel
         select = jnp.where(place, 1.0, 0.0).astype(BF16)
-        rows = jnp.dot(select[:n_slots, :], unit, preferred_element_type=F32).astype(BF16)
+        rows = jnp.dot(select[:count, :], unit, preferred_element_type=F32).astype(BF16)
         for n in range(width // 128):
-            out_refs[k][n * n_slots : (n + 1) * n_slots, :] = rows[:, n * 128 : (n + 1) * 128]
+            out_refs[k][n * count : (n + 1) * count, :] = rows[:, n * 128 : (n + 1) * 128]
         placed = lax.dot_general(
             charge_ref[...], select, (((1,), (1,)), ((), ())), preferred_element_type=F32
         )
-        out_refs[k][width // 128 * n_slots :, :] = placed.astype(BF16)
+        out_refs[k][width // 128 * count :, :] = placed.astype(BF16)
 
 
 def unit_kernel(*refs):
@@ -163,12 +165,60 @@
             ).astype(BF16)
 
 
+def first_kernel(me_ref, *refs):
+    score_kernel(3, 0, me_ref, *refs[:9], *refs[10:])
+    q_ref, out_ref = refs[0], refs[9]
+    n_slots, shared = (PLANE + 2) * CAP, 2 * CAP
+    count = (q_ref.shape[0] - META) // n_slots
+    at = (1 - me_ref[0] // PLANE % 2) * (n_slots - shared)
+    wide = out_ref.shape[1] // 128
+    for n in range(count):
+        row, column = n // wide * shared, n % wide * 128
+        out_ref[row : row + shared, column : column + 128] = q_ref[
+            pl.ds(pl.multiple_of(at + n * n_slots, CAP), shared), :
+        ]
+    row = count // wide * shared
+    out_ref[row:, :] = jnp.zeros((META, out_ref.shape[1]), BF16)
+    out_ref[row:, :128] = q_ref[count * n_slots :, :]
+
+
+def second_kernel(me_ref, q_ref, passed_ref, *refs):
+    charge_refs, lib_refs, out_ref, block_ref = refs[0], refs[1:3], refs[3], refs[4]
+    rows_ref, charge_ref, column_ref = refs[5:]
+    n_slots, shared = (PLANE + 2) * CAP, 2 * CAP
+    part = n_slots - shared
+    count = (q_ref.shape[0] - META) // part
+    wide = passed_ref.shape[1] // 128
+    odd = me_ref[0] // PLANE % 2
+    own_at, passed_at = odd * shared, (1 - odd) * part
+    for n in range(count):
+        row, column = n // wide * shared, n % wide * 128
+        block_ref[pl.ds(pl.multiple_of(n * n_slots + own_at, CAP), part), :] = q_ref[
+            n * part : (n + 1) * part, :
+        ]
+        block_ref[pl.ds(pl.multiple_of(n * n_slots + passed_at, CAP), shared), :] = passed_ref[
+            row : row + shared, column : column + 128
+        ]
+    row = count // wide * shared
+    own_line = q_ref[count * part :, :].astype(F32)[0:1, :]
+    passed_line = passed_ref[row:, :128].astype(F32)[0:1, :]
+    column_ref[0] = jnp.broadcast_to(passed_line, (128, 128)).T
+    column_ref[1] = jnp.broadcast_to(own_line, (128, 128)).T
+    column_ref[2] = jnp.zeros((128, 128), F32)
+    column_ref[2, pl.ds(pl.multiple_of(own_at, CAP), part), :] = column_ref[1, :part, :]
+    column_ref[2, pl.ds(pl.multiple_of(passed_at, CAP), shared), :] = column_ref[
+        0, pl.ds(pl.multiple_of(odd * part, CAP), shared), :
+    ]
+    block_ref[count * n_slots :, :] = column_ref[2].T[:META, :].astype(BF16)
+    score_kernel(1, 0, me_ref, block_ref, charge_refs, *lib_refs, out_ref, rows_ref, charge_ref)
+
+
 def home_kernel(me_ref, slot_ref, *refs):
-    near = [refs[at] for at in (0, 1, 2, 3)]
-    far = [refs[4 + at] for at in (3, 1, 0, 2)]
-    out_ref, flat_ref = refs[8], refs[9]
+    near8, near12, near4, near0, far8, far4, far12, far0, out_ref, flat_ref = refs
+    near = [near0, near4, near8, near12]
+    far = [far0, far4, far8, far12]
     q_rows = slot_ref.shape[1]
-    l_rows = near[0].shape[1]
+    l_rows = near0.shape[1]
     n_slab = 4 * PLANE
     total = n_slab * CAP
     slot = slot_ref[...]
@@ -224,9 +274,10 @@
         [VMEM] * 3,
         cost=1,
     )
+    slots_shape = shape(width // 128 * n_slots + META, 128)
     q0, q4, q8, q12 = kernel_call(
         query_kernel,
-        [shape(width // 128 * n_slots + META, 128)] * 4,
+        [slots_shape] * 3 + [shape(width // 128 * (n_slots - 2 * CAP) + META, 128)],
         [me, slot, qcharge, queries],
         [SMEM] + [VMEM] * 3,
     )
@@ -237,33 +288,47 @@
     (near_charge,) = kernel_call(pair_kernel, [charge], [charge, charge_c], [VMEM] * 2)
     far_charge = swapped(near_charge, 2)
 
-    def scores(turn, q_blocks, *parts):
-        count = len(q_blocks)
-        return kernel_call(
-            functools.partial(score_kernel, count, turn),
-            [shape(2 * seen, l_rows)] * count,
-            [me, *q_blocks, *parts],
-            [SMEM] + [VMEM] * (count + len(parts)),
-            [pltpu.VMEM((count * seen, width), BF16), pltpu.VMEM((count, 128, 128), F32)],
-        )
-
-    near8, near4, near0 = scores(0, [q8, q4, q0], near_charge, unit, unit_c)
-    near8, near4 = swapped(near8, 8), swapped(near4, 4)
-    raw_y, q12, near8, near4, far_charge = lax.optimization_barrier(
-        (raw_y, q12, near8, near4, far_charge)
+    block = shape(2 * seen, l_rows)
+    shared_rows = width // l_rows * 2 * CAP + META
+    first = [q8, q4, q0, near_charge, unit, unit_c]
+    near8, near4, near0, passed = kernel_call(
+        first_kernel,
+        [block] * 3 + [shape(shared_rows, l_rows)],
+        [me, *first],
+        [SMEM] + [VMEM] * len(first),
+        [pltpu.VMEM((3 * seen, width), BF16), pltpu.VMEM((3, 128, 128), F32)],
+    )
+    near8, passed = swapped(near8, 8), swapped(passed, 4)
+    raw_y, q12, near8, near4, passed, far_charge = lax.optimization_barrier(
+        (raw_y, q12, near8, near4, passed, far_charge)
     )
     raw_d = swapped(raw_y, 1)
-    (near12,) = scores(0, [q12], near_charge, unit, unit_c)
-    near12 = swapped(near12, 12)
+    near12, q12 = kernel_call(
+        second_kernel,
+        [block, slots_shape],
+        [me, q12, passed, near_charge, unit, unit_c],
+        [SMEM] + [VMEM] * 5,
+        [
+            pltpu.VMEM((seen, width), BF16),
+            pltpu.VMEM((1, 128, 128), F32),
+            pltpu.VMEM((3, 128, 128), F32),
+        ],
+    )
+    near12, near4 = swapped(near12, 12), swapped(near4, 4)
     (unit_y,) = kernel_call(unit_kernel, [lib], [raw_y], [VMEM])
     (unit_d,) = kernel_call(unit_kernel, [lib], [raw_d], [VMEM])
-    far8, far4, far12, far0 = scores(2, [q8, q4, q12, q0], far_charge, unit_y, unit_d)
+    far8, far4, far12, far0 = kernel_call(
+        functools.partial(score_kernel, 4, 2),
+        [block] * 4,
+        [me, q8, q4, q12, q0, far_charge, unit_y, unit_d],
+        [SMEM] + [VMEM] * 7,
+        [pltpu.VMEM((4 * seen, width), BF16), pltpu.VMEM((4, 128, 128), F32)],
+    )
     far8, far4, far12 = swapped(far8, 8), swapped(far4, 4), swapped(far12, 12)
-    near, far = [near0, near4, near8, near12], [far8, far4, far12, far0]
     (out,) = kernel_call(
         home_kernel,
         [shape(q_rows, 3 * l_rows)],
-        [me, slot, *near, *far],
+        [me, slot, near8, near12, near4, near0, far8, far4, far12, far0],
         [SMEM] + [VMEM] * 9,
         [pltpu.VMEM((4 * PLANE * CAP, l_rows), BF16)],
     )
@@ -274,7 +339,7 @@
     n_slab = lax.axis_size("slab")
     q_rows, width = queries.shape
     fits = n_slab == 4 * PLANE and 2 * q_rows == n_slab * CAP and q_rows == 128
-    plan = line_plan if fits and width % 256 == 0 and library.shape[0] <= width else general_plan
+    plan = line_plan if fits and width % 256 == 0 and width % (2 * library.shape[0]) == 0 else general_plan
     return plan(queries, library, bucket, query_charge, library_charge)
 
 

time: 47.1 us -> 46.5 us (0.987)
  waiting for transfers between devices: 18.6 us -> 17.8 us
    ppermute x14 -> x15, waiting for transfers between devices: 18.6 us -> 17.8 us  [swapped(): return lax.ppermute(value, 'slab', [(i, i ^ mask) for i in range(count)])]
    ppermute x14 -> x15, starting transfers between devices: 19.7 us -> 19.8 us  [swapped(): return lax.ppermute(value, 'slab', [(i, i ^ mask) for i in range(count)])]
  transfers between devices with their start and end apart: 14 -> 15, of which waited for: 7 -> 7; matrix products, arithmetic and copies ran while one was open for 0% -> 0% of each run, Pallas kernels for 10% -> 10%
where the time goes in v6:
time: 46.5 us; the launch traced here: 46.3 us
  starting transfers between devices  19.8 us (43%)
  waiting for transfers between devices  17.8 us (38%)
  Pallas kernels  5.71 us (12%)
  local copies, waits for them, and re-layouts  2.85 us (6%)
    ppermute x15, starting transfers between devices, swapped(): return lax.ppermute(value, 'slab', [(i, i ^ mask) for i in range(count)])  19.8 us
    ppermute x15, waiting for transfers between devices, swapped(): return lax.ppermute(value, 'slab', [(i, i ^ mask) for i in range(count)])  17.8 us
    pallas_call x10, Pallas kernels, kernel_call(): pl.pallas_call(body, out_shape=[jax.ShapeDtypeStruct(o.shape, o.dtype) fo...  5.71 us
    unnamed x10, local copies, waits for them, and re-layouts  2.85 us
  transfers between devices with their start and end apart: 15, of which 7 were waited for; matrix products, arithmetic and copies ran while one was open for 0% of the time, Pallas kernels for 10%

profile of v6, /device:TPU:0, one launch (start us, length us, event | category | flops | bytes accessed | tf_op | source)
XLA Modules:
  0.0 46.3 jit_solution(11562727207561669360)
XLA Ops:
  0.0 0.5 collective-permute-start.5
  0.5 2.5 %collective-permute-start = (bf16[512,1024]{1,0:T(8,128)(2,1)}, bf16[512,1024]{1,0:T(8,128)(2,1)S(1)}, u32[]{:S(2)}, u32[]{:S(2)}) collective-permute-start(bf16[512,1024]{1,0:T(8,128)(2,1)} %refs_0_.1), channel_id=1, source_target_pairs={{0,2},{1,3},{2,0},{3,1},{4,6},{5,7},{6,4},{7,5},{8,10},{9,11},{10,... | collective-permute-start | bytes 3145736 | tf_op jit(solution)/shard_map/ppermute | solution.py:85
  3.0 0.0 copy-start.2
  3.0 0.0 copy-start.3
  3.0 0.7 %copy-done.2 = s32[512]{0:T(512)S(1)} copy-done((s32[512]{0:T(512)S(1)}, s32[512]{0:T(512)}, u32[]{:S(2)}) %copy-start.2) | copy-done | bytes 2072
  3.7 0.0 copy-done.3
  3.7 0.0 copy-done.4
  3.7 0.1 shard_map.55
  3.8 0.0 copy-start.1
  3.8 0.9 %copy-done.1 = bf16[128,1024]{1,0:T(8,128)(2,1)S(1)} copy-done((bf16[128,1024]{1,0:T(8,128)(2,1)S(1)}, bf16[128,1024]{1,0:T(8,128)(2,1)}, u32[]{:S(2)}) %copy-start.1) | copy-done | bytes 262168
  4.7 0.5 %shard_map.56 = (bf16[784,128]{1,0:T(8,128)(2,1)S(1)}, bf16[784,128]{1,0:T(8,128)(2,1)S(1)}, bf16[784,128]{1,0:T(8,128)(2,1)S(1)}, bf16[528,128]{1,0:T(8,128)(2,1)S(1)}) custom-call(s32[1]{0:T(128)} %bitcast.me_ref, s32[1,128]{1,0:T(1,128)S(1)} %get-tuple-element.30.slot_ref, bf16[16,128]{1,0:T(8,128)(2,1)S(1)} %get-tuple-element.31.charge_ref, ...), custom_call_target="tpu_custom_call" | custom-call | bytes 1 | tf_op jit(solution)/shard_map/pallas_call | solution.py:248
  5.2 2.7 %collective-permute-start.2 = (bf16[784,128]{1,0:T(8,128)(2,1)S(1)}, bf16[784,128]{1,0:T(8,128)(2,1)S(1)}, u32[]{:S(2)}, u32[]{:S(2)}) collective-permute-start(bf16[784,128]{1,0:T(8,128)(2,1)S(1)} %get-tuple-element.33), channel_id=1, source_target_pairs={{0,8},{1,9},{2,10},{3,11},{4,12},{5,13},{6,14},{7,15},{8,0},{9,1},... | collective-permute-start | bytes 602120 | tf_op jit(solution)/shard_map/ppermute | solution.py:85
  7.9 1.6 %collective-permute-start.3 = (bf16[784,128]{1,0:T(8,128)(2,1)S(1)}, bf16[784,128]{1,0:T(8,128)(2,1)S(1)}, u32[]{:S(2)}, u32[]{:S(2)}) collective-permute-start(bf16[784,128]{1,0:T(8,128)(2,1)S(1)} %get-tuple-element.34), channel_id=1, source_target_pairs={{0,4},{1,5},{2,6},{3,7},{4,0},{5,1},{6,2},{7,3},{8,12},{9,13},{10,... | collective-permute-start | bytes 602120 | tf_op jit(solution)/shard_map/ppermute | solution.py:85
  9.5 0.0 collective-permute-start.4
  9.5 1.2 %collective-permute-done.4.other_ref = bf16[16,512]{1,0:T(8,128)(2,1)S(1)} collective-permute-done((bf16[16,512]{1,0:T(8,128)(2,1)S(1)}, bf16[16,512]{1,0:T(8,128)(2,1)S(1)}, u32[]{:S(2)}, u32[]{:S(2)}) %collective-permute-start.4) | collective-permute-done | bytes 16416 | tf_op jit(solution)/shard_map/ppermute | solution.py:85
  10.7 0.2 collective-permute-start.1
  10.9 0.0 collective-permute-done.5.refs_1_
  10.9 0.0 copy-start
  10.9 1.2 %copy-done = bf16[512,1024]{1,0:T(8,128)(2,1)S(1)} copy-done((bf16[512,1024]{1,0:T(8,128)(2,1)S(1)}, bf16[512,1024]{1,0:T(8,128)(2,1)}, u32[]{:S(2)}) %copy-start) | copy-done | bytes 1048600
  12.1 0.6 %shard_map.58 = (bf16[512,1024]{1,0:T(8,128)(2,1)S(1)}, bf16[512,1024]{1,0:T(8,128)(2,1)S(1)}) custom-call(bf16[512,1024]{1,0:T(8,128)(2,1)S(1)} %copy-done, bf16[512,1024]{1,0:T(8,128)(2,1)S(1)} %collective-permute-done.5.refs_1_), custom_call_target="tpu_custom_call" | custom-call | bytes 1 | tf_op jit(solution)/shard_map/pallas_call | solution.py:248
  12.8 6.0 %collective-permute-done.2.refs_0_ = bf16[784,128]{1,0:T(8,128)(2,1)S(1)} collective-permute-done((bf16[784,128]{1,0:T(8,128)(2,1)S(1)}, bf16[784,128]{1,0:T(8,128)(2,1)S(1)}, u32[]{:S(2)}, u32[]{:S(2)}) %collective-permute-start.2) | collective-permute-done | bytes 200736 | tf_op jit(solution)/shard_map/ppermute | solution.py:85
  18.8 0.0 collective-permute-done.3.refs_1_
  18.8 0.9 %shard_map.59 = (bf16[96,512]{1,0:T(8,128)(2,1)S(1)}, bf16[96,512]{1,0:T(8,128)(2,1)S(1)}, bf16[96,512]{1,0:T(8,128)(2,1)S(1)}, bf16[80,512]{1,0:T(8,128)(2,1)S(1)}) custom-call(s32[1]{0:T(128)} %bitcast.me_ref, bf16[784,128]{1,0:T(8,128)(2,1)S(1)} %collective-permute-done.2.refs_0_, bf16[784,128]{1,0:T(8,128)(2,1)S(1)} %collective-permute-done.3.refs_1_, ...), custom_call_target="tpu_custom_call" | custom-call | bytes 1 | tf_op jit(solution)/shard_map/pallas_call | solution.py:248
  19.7 1.2 %collective-permute-start.6 = (bf16[96,512]{1,0:T(8,128)(2,1)S(1)}, bf16[96,512]{1,0:T(8,128)(2,1)S(1)}, u32[]{:S(2)}, u32[]{:S(2)}) collective-permute-start(bf16[96,512]{1,0:T(8,128)(2,1)S(1)} %get-tuple-element.39), channel_id=1, source_target_pairs={{0,8},{1,9},{2,10},{3,11},{4,12},{5,13},{6,14},{7,15},{8,0},{9,1},... | collective-permute-start | bytes 294920 | tf_op jit(solution)/shard_map/ppermute | solution.py:85
  20.9 2.5 %collective-permute-start.7 = (bf16[80,512]{1,0:T(8,128)(2,1)S(1)}, bf16[80,512]{1,0:T(8,128)(2,1)S(1)}, u32[]{:S(2)}, u32[]{:S(2)}) collective-permute-start(bf16[80,512]{1,0:T(8,128)(2,1)S(1)} %get-tuple-element.41), channel_id=1, source_target_pairs={{0,4},{1,5},{2,6},{3,7},{4,0},{5,1},{6,2},{7,3},{8,12},{9,13},{10,... | collective-permute-start | bytes 245768 | tf_op jit(solution)/shard_map/ppermute | solution.py:85
  23.4 0.5 %collective-permute-start.8 = (bf16[16,512]{1,0:T(8,128)(2,1)S(1)}, bf16[16,512]{1,0:T(8,128)(2,1)S(1)}, u32[]{:S(2)}, u32[]{:S(2)}) collective-permute-start(bf16[16,512]{1,0:T(8,128)(2,1)S(1)} %shard_map.57.refs_3_.refs_0_), channel_id=1, source_target_pairs={{0,2},{1,3},{2,0},{3,1},{4,6},{5,7},{6,4},{7,5},{8,10},{9,11},{10,... | collective-permute-start | bytes 49160 | tf_op jit(solution)/shard_map/ppermute | solution.py:85
  23.9 3.4 %collective-permute-done.8.refs_4_ = bf16[16,512]{1,0:T(8,128)(2,1)S(1)} collective-permute-done((bf16[16,512]{1,0:T(8,128)(2,1)S(1)}, bf16[16,512]{1,0:T(8,128)(2,1)S(1)}, u32[]{:S(2)}, u32[]{:S(2)}) %collective-permute-start.8) | collective-permute-done | bytes 16416 | tf_op jit(solution)/shard_map/ppermute | solution.py:85
  27.4 0.0 collective-permute-done.1.q_ref
  27.4 0.0 collective-permute-done.refs_0_
  27.4 0.0 collective-permute-done.7.passed_ref
  27.4 0.3 collective-permute-done.6.refs_0_
  27.7 0.0 collective-permute-start.11
  27.7 0.3 shard_map.61.refs_5_
  28.0 0.9 %shard_map.60 = (bf16[96,512]{1,0:T(8,128)(2,1)S(1)}, bf16[784,128]{1,0:T(8,128)(2,1)S(1)}) custom-call(s32[1]{0:T(128)} %bitcast.me_ref, bf16[528,128]{1,0:T(8,128)(2,1)S(1)} %collective-permute-done.1.q_ref, bf16[80,512]{1,0:T(8,128)(2,1)S(1)} %collective-permute-done.7.passed_ref, bf16[16,512]{1,0:T(8,128)(2,1)S(1)} %shard_map.57.refs_3_.refs_0_, ...), custom_call_target="tpu_custom_call" | custom-call | bytes 1 | tf_op jit(solution)/shard_map/pallas_call | solution.py:248
  28.9 3.7 %collective-permute-start.9 = (bf16[96,512]{1,0:T(8,128)(2,1)S(1)}, bf16[96,512]{1,0:T(8,128)(2,1)S(1)}, u32[]{:S(2)}, u32[]{:S(2)}) collective-permute-start(bf16[96,512]{1,0:T(8,128)(2,1)S(1)} %get-tuple-element.45), channel_id=1, source_target_pairs={{0,12},{1,13},{2,14},{3,15},{4,8},{5,9},{6,10},{7,11},{8,4},{9,5},... | collective-permute-start | bytes 294920 | tf_op jit(solution)/shard_map/ppermute | solution.py:85
  32.6 0.0 collective-permute-start.10
  32.6 0.0 collective-permute-done.11.refs_0_
  32.6 0.3 shard_map.62.refs_6_
  32.9 0.9 %shard_map.63 = (bf16[96,512]{1,0:T(8,128)(2,1)S(1)}, bf16[96,512]{1,0:T(8,128)(2,1)S(1)}, bf16[96,512]{1,0:T(8,128)(2,1)S(1)}, bf16[96,512]{1,0:T(8,128)(2,1)S(1)}) custom-call(s32[1]{0:T(128)} %bitcast.me_ref, bf16[784,128]{1,0:T(8,128)(2,1)S(1)} %collective-permute-done.2.refs_0_, bf16[784,128]{1,0:T(8,128)(2,1)S(1)} %collective-permute-done.3.refs_1_, ...), custom_call_target="tpu_custom_call" | custom-call | bytes 1 | tf_op jit(solution)/shard_map/pallas_call | solution.py:248
  33.8 0.8 %collective-permute-start.12 = (bf16[96,512]{1,0:T(8,128)(2,1)S(1)}, bf16[96,512]{1,0:T(8,128)(2,1)S(1)}, u32[]{:S(2)}, u32[]{:S(2)}) collective-permute-start(bf16[96,512]{1,0:T(8,128)(2,1)S(1)} %get-tuple-element.51), channel_id=1, source_target_pairs={{0,8},{1,9},{2,10},{3,11},{4,12},{5,13},{6,14},{7,15},{8,0},{9,1},... | collective-permute-start | bytes 294920 | tf_op jit(solution)/shard_map/ppermute | solution.py:85
  34.7 1.3 %collective-permute-start.13 = (bf16[96,512]{1,0:T(8,128)(2,1)S(1)}, bf16[96,512]{1,0:T(8,128)(2,1)S(1)}, u32[]{:S(2)}, u32[]{:S(2)}) collective-permute-start(bf16[96,512]{1,0:T(8,128)(2,1)S(1)} %get-tuple-element.52), channel_id=1, source_target_pairs={{0,4},{1,5},{2,6},{3,7},{4,0},{5,1},{6,2},{7,3},{8,12},{9,13},{10,... | collective-permute-start | bytes 294920 | tf_op jit(solution)/shard_map/ppermute | solution.py:85
  36.0 2.3 %collective-permute-start.14 = (bf16[96,512]{1,0:T(8,128)(2,1)S(1)}, bf16[96,512]{1,0:T(8,128)(2,1)S(1)}, u32[]{:S(2)}, u32[]{:S(2)}) collective-permute-start(bf16[96,512]{1,0:T(8,128)(2,1)S(1)} %get-tuple-element.53), channel_id=1, source_target_pairs={{0,12},{1,13},{2,14},{3,15},{4,8},{5,9},{6,10},{7,11},{8,4},{9,5},... | collective-permute-start | bytes 294920 | tf_op jit(solution)/shard_map/ppermute | solution.py:85
  38.3 0.0 collective-permute-done.9.refs_1_
  38.3 1.3 %collective-permute-done.10.refs_2_ = bf16[96,512]{1,0:T(8,128)(2,1)S(1)} collective-permute-done((bf16[96,512]{1,0:T(8,128)(2,1)S(1)}, bf16[96,512]{1,0:T(8,128)(2,1)S(1)}, u32[]{:S(2)}, u32[]{:S(2)}) %collective-permute-start.10) | collective-permute-done | bytes 98336 | tf_op jit(solution)/shard_map/ppermute | solution.py:85
  39.6 3.5 %collective-permute-done.12.refs_4_ = bf16[96,512]{1,0:T(8,128)(2,1)S(1)} collective-permute-done((bf16[96,512]{1,0:T(8,128)(2,1)S(1)}, bf16[96,512]{1,0:T(8,128)(2,1)S(1)}, u32[]{:S(2)}, u32[]{:S(2)}) %collective-permute-start.12) | collective-permute-done | bytes 98336 | tf_op jit(solution)/shard_map/ppermute | solution.py:85
  43.2 0.0 collective-permute-done.13.refs_5_
  43.2 2.0 %collective-permute-done.14.refs_6_ = bf16[96,512]{1,0:T(8,128)(2,1)S(1)} collective-permute-done((bf16[96,512]{1,0:T(8,128)(2,1)S(1)}, bf16[96,512]{1,0:T(8,128)(2,1)S(1)}, u32[]{:S(2)}, u32[]{:S(2)}) %collective-permute-start.14) | collective-permute-done | bytes 98336 | tf_op jit(solution)/shard_map/ppermute | solution.py:85
  45.2 1.1 %shard_map.64 = bf16[128,1536]{1,0:T(8,128)(2,1)} custom-call(s32[1]{0:T(128)} %bitcast.me_ref, s32[1,128]{1,0:T(1,128)S(1)} %get-tuple-element.30.slot_ref, bf16[96,512]{1,0:T(8,128)(2,1)S(1)} %collective-permute-done.6.refs_0_, bf16[96,512]{1,0:T(8,128)(2,1)S(1)} %collective-permute-done.9.refs_1_, bf16[96,512]{1,0:T(8,128)(2,1)S(1)} %collective-permute-done.10.refs_2_, ...), custom_call_target="tpu_custom_call" | custom-call | bytes 1 | tf_op jit(solution)/shard_map/pallas_call | solution.py:248
  (2 shorter events, 0.0 us)
Async XLA Ops:
  0.0 10.9 %collective-permute-start.5 = (bf16[512,1024]{1,0:T(8,128)(2,1)}, bf16[512,1024]{1,0:T(8,128)(2,1)S(1)}, u32[]{:S(2)}, u32[]{:S(2)}) collective-permute-start(bf16[512,1024]{1,0:T(8,128)(2,1)} %refs_0_.1), channel_id=1, source_target_pairs={{0,1},{1,0},{2,3},{3,2},{4,5},{5,4},{6,7},{7,6},{8,9},{9,8},{10,11... | collective-permute-start | bytes 3145736 | tf_op jit(solution)/shard_map/ppermute | solution.py:85
  0.5 26.9 %collective-permute-start = (bf16[512,1024]{1,0:T(8,128)(2,1)}, bf16[512,1024]{1,0:T(8,128)(2,1)S(1)}, u32[]{:S(2)}, u32[]{:S(2)}) collective-permute-start(bf16[512,1024]{1,0:T(8,128)(2,1)} %refs_0_.1), channel_id=1, source_target_pairs={{0,2},{1,3},{2,0},{3,1},{4,6},{5,7},{6,4},{7,5},{8,10},{9,11},{10,... | collective-permute-start | bytes 3145736 | tf_op jit(solution)/shard_map/ppermute | solution.py:85
  3.0 0.7 %copy-start.2 = (s32[512]{0:T(512)S(1)}, s32[512]{0:T(512)}, u32[]{:S(2)}) copy-start(s32[512]{0:T(512)} %param.9) | copy-start | bytes 6148
  3.0 0.7 %copy-start.3 = (s32[128,1]{0,1:T(1,128)S(1)}, s32[128,1]{0,1:T(1,128)}, u32[]{:S(2)}) copy-start(s32[128,1]{0,1:T(1,128)} %param.7) | copy-start | bytes 1540
  3.0 0.7 %copy-start.4 = (s32[128]{0:T(128)S(1)}, s32[128]{0:T(128)}, u32[]{:S(2)}) copy-start(s32[128]{0:T(128)} %param.8) | copy-start | bytes 1540
  3.8 1.0 %copy-start.1 = (bf16[128,1024]{1,0:T(8,128)(2,1)S(1)}, bf16[128,1024]{1,0:T(8,128)(2,1)}, u32[]{:S(2)}) copy-start(bf16[128,1024]{1,0:T(8,128)(2,1)} %q_ref.1) | copy-start | bytes 786436
  5.2 13.5 %collective-permute-start.2 = (bf16[784,128]{1,0:T(8,128)(2,1)S(1)}, bf16[784,128]{1,0:T(8,128)(2,1)S(1)}, u32[]{:S(2)}, u32[]{:S(2)}) collective-permute-start(bf16[784,128]{1,0:T(8,128)(2,1)S(1)} %get-tuple-element.33), channel_id=1, source_target_pairs={{0,8},{1,9},{2,10},{3,11},{4,12},{5,13},{6,14},{7,15},{8,0},{9,1},... | collective-permute-start | bytes 602120 | tf_op jit(solution)/shard_map/ppermute | solution.py:85
  7.9 10.9 %collective-permute-start.3 = (bf16[784,128]{1,0:T(8,128)(2,1)S(1)}, bf16[784,128]{1,0:T(8,128)(2,1)S(1)}, u32[]{:S(2)}, u32[]{:S(2)}) collective-permute-start(bf16[784,128]{1,0:T(8,128)(2,1)S(1)} %get-tuple-element.34), channel_id=1, source_target_pairs={{0,4},{1,5},{2,6},{3,7},{4,0},{5,1},{6,2},{7,3},{8,12},{9,13},{10,... | collective-permute-start | bytes 602120 | tf_op jit(solution)/shard_map/ppermute | solution.py:85
  9.5 1.2 %collective-permute-start.4 = (bf16[16,512]{1,0:T(8,128)(2,1)S(1)}, bf16[16,512]{1,0:T(8,128)(2,1)S(1)}, u32[]{:S(2)}, u32[]{:S(2)}) collective-permute-start(bf16[16,512]{1,0:T(8,128)(2,1)S(1)} %get-tuple-element.36.one_ref), channel_id=1, source_target_pairs={{0,1},{1,0},{2,3},{3,2},{4,5},{5,4},{6,7},{7,6},{8,9},{9,8},{10,11... | collective-permute-start | bytes 49160 | tf_op jit(solution)/shard_map/ppermute | solution.py:85
  10.7 16.7 %collective-permute-start.1 = (bf16[528,128]{1,0:T(8,128)(2,1)S(1)}, bf16[528,128]{1,0:T(8,128)(2,1)S(1)}, u32[]{:S(2)}, u32[]{:S(2)}) collective-permute-start(bf16[528,128]{1,0:T(8,128)(2,1)S(1)} %get-tuple-element.32), channel_id=1, source_target_pairs={{0,12},{1,13},{2,14},{3,15},{4,8},{5,9},{6,10},{7,11},{8,4},{9,5},... | collective-permute-start | bytes 405512 | tf_op jit(solution)/shard_map/ppermute | solution.py:85
  10.9 1.2 %copy-start = (bf16[512,1024]{1,0:T(8,128)(2,1)S(1)}, bf16[512,1024]{1,0:T(8,128)(2,1)}, u32[]{:S(2)}) copy-start(bf16[512,1024]{1,0:T(8,128)(2,1)} %refs_0_.1) | copy-start | bytes 3145732
  19.7 8.0 %collective-permute-start.6 = (bf16[96,512]{1,0:T(8,128)(2,1)S(1)}, bf16[96,512]{1,0:T(8,128)(2,1)S(1)}, u32[]{:S(2)}, u32[]{:S(2)}) collective-permute-start(bf16[96,512]{1,0:T(8,128)(2,1)S(1)} %get-tuple-element.39), channel_id=1, source_target_pairs={{0,8},{1,9},{2,10},{3,11},{4,12},{5,13},{6,14},{7,15},{8,0},{9,1},... | collective-permute-start | bytes 294920 | tf_op jit(solution)/shard_map/ppermute | solution.py:85
  20.9 6.5 %collective-permute-start.7 = (bf16[80,512]{1,0:T(8,128)(2,1)S(1)}, bf16[80,512]{1,0:T(8,128)(2,1)S(1)}, u32[]{:S(2)}, u32[]{:S(2)}) collective-permute-start(bf16[80,512]{1,0:T(8,128)(2,1)S(1)} %get-tuple-element.41), channel_id=1, source_target_pairs={{0,4},{1,5},{2,6},{3,7},{4,0},{5,1},{6,2},{7,3},{8,12},{9,13},{10,... | collective-permute-start | bytes 245768 | tf_op jit(solution)/shard_map/ppermute | solution.py:85
  23.4 3.9 %collective-permute-start.8 = (bf16[16,512]{1,0:T(8,128)(2,1)S(1)}, bf16[16,512]{1,0:T(8,128)(2,1)S(1)}, u32[]{:S(2)}, u32[]{:S(2)}) collective-permute-start(bf16[16,512]{1,0:T(8,128)(2,1)S(1)} %shard_map.57.refs_3_.refs_0_), channel_id=1, source_target_pairs={{0,2},{1,3},{2,0},{3,1},{4,6},{5,7},{6,4},{7,5},{8,10},{9,11},{10,... | collective-permute-start | bytes 49160 | tf_op jit(solution)/shard_map/ppermute | solution.py:85
  27.7 4.9 %collective-permute-start.11 = (bf16[512,1024]{1,0:T(8,128)(2,1)S(1)}, bf16[512,1024]{1,0:T(8,128)(2,1)S(1)}, u32[]{:S(2)}, u32[]{:S(2)}) collective-permute-start(bf16[512,1024]{1,0:T(8,128)(2,1)S(1)} %collective-permute-done.refs_0_), channel_id=1, source_target_pairs={{0,1},{1,0},{2,3},{3,2},{4,5},{5,4},{6,7},{7,6},{8,9},{9,8},{10,11... | collective-permute-start | bytes 3145736 | tf_op jit(solution)/shard_map/ppermute | solution.py:85
  28.9 9.4 %collective-permute-start.9 = (bf16[96,512]{1,0:T(8,128)(2,1)S(1)}, bf16[96,512]{1,0:T(8,128)(2,1)S(1)}, u32[]{:S(2)}, u32[]{:S(2)}) collective-permute-start(bf16[96,512]{1,0:T(8,128)(2,1)S(1)} %get-tuple-element.45), channel_id=1, source_target_pairs={{0,12},{1,13},{2,14},{3,15},{4,8},{5,9},{6,10},{7,11},{8,4},{9,5},... | collective-permute-start | bytes 294920 | tf_op jit(solution)/shard_map/ppermute | solution.py:85
  32.6 7.0 %collective-permute-start.10 = (bf16[96,512]{1,0:T(8,128)(2,1)S(1)}, bf16[96,512]{1,0:T(8,128)(2,1)S(1)}, u32[]{:S(2)}, u32[]{:S(2)}) collective-permute-start(bf16[96,512]{1,0:T(8,128)(2,1)S(1)} %get-tuple-element.46), channel_id=1, source_target_pairs={{0,4},{1,5},{2,6},{3,7},{4,0},{5,1},{6,2},{7,3},{8,12},{9,13},{10,... | collective-permute-start | bytes 294920 | tf_op jit(solution)/shard_map/ppermute | solution.py:85
  33.8 9.3 %collective-permute-start.12 = (bf16[96,512]{1,0:T(8,128)(2,1)S(1)}, bf16[96,512]{1,0:T(8,128)(2,1)S(1)}, u32[]{:S(2)}, u32[]{:S(2)}) collective-permute-start(bf16[96,512]{1,0:T(8,128)(2,1)S(1)} %get-tuple-element.51), channel_id=1, source_target_pairs={{0,8},{1,9},{2,10},{3,11},{4,12},{5,13},{6,14},{7,15},{8,0},{9,1},... | collective-permute-start | bytes 294920 | tf_op jit(solution)/shard_map/ppermute | solution.py:85
  34.7 8.5 %collective-permute-start.13 = (bf16[96,512]{1,0:T(8,128)(2,1)S(1)}, bf16[96,512]{1,0:T(8,128)(2,1)S(1)}, u32[]{:S(2)}, u32[]{:S(2)}) collective-permute-start(bf16[96,512]{1,0:T(8,128)(2,1)S(1)} %get-tuple-element.52), channel_id=1, source_target_pairs={{0,4},{1,5},{2,6},{3,7},{4,0},{5,1},{6,2},{7,3},{8,12},{9,13},{10,... | collective-permute-start | bytes 294920 | tf_op jit(solution)/shard_map/ppermute | solution.py:85
  36.0 9.2 %collective-permute-start.14 = (bf16[96,512]{1,0:T(8,128)(2,1)S(1)}, bf16[96,512]{1,0:T(8,128)(2,1)S(1)}, u32[]{:S(2)}, u32[]{:S(2)}) collective-permute-start(bf16[96,512]{1,0:T(8,128)(2,1)S(1)} %get-tuple-element.53), channel_id=1, source_target_pairs={{0,12},{1,13},{2,14},{3,15},{4,8},{5,9},{6,10},{7,11},{8,4},{9,5},... | collective-permute-start | bytes 294920 | tf_op jit(solution)/shard_map/ppermute | solution.py:85

commit v7 on v6

--- a/solution.py
+++ b/solution.py
@@ -299,10 +299,6 @@
         [pltpu.VMEM((3 * seen, width), BF16), pltpu.VMEM((3, 128, 128), F32)],
     )
     near8, passed = swapped(near8, 8), swapped(passed, 4)
-    raw_y, q12, near8, near4, passed, far_charge = lax.optimization_barrier(
-        (raw_y, q12, near8, near4, passed, far_charge)
-    )
-    raw_d = swapped(raw_y, 1)
     near12, q12 = kernel_call(
         second_kernel,
         [block, slots_shape],
@@ -314,6 +310,10 @@
             pltpu.VMEM((3, 128, 128), F32),
         ],
     )
+    raw_y, near8, near4, near12, far_charge = lax.optimization_barrier(
+        (raw_y, near8, near4, near12, far_charge)
+    )
+    raw_d = swapped(raw_y, 1)
     near12, near4 = swapped(near12, 12), swapped(near4, 4)
     (unit_y,) = kernel_call(unit_kernel, [lib], [raw_y], [VMEM])
     (unit_d,) = kernel_call(unit_kernel, [lib], [raw_d], [VMEM])

time: 46.5 us -> 45.1 us (0.970)
  waiting for transfers between devices: 17.8 us -> 16.1 us
    ppermute x15, waiting for transfers between devices: 17.8 us -> 16.1 us  [swapped(): return lax.ppermute(value, 'slab', [(i, i ^ mask) for i in range(count)])]
  transfers between devices with their start and end apart: 15 -> 15, of which waited for: 7 -> 8; matrix products, arithmetic and copies ran while one was open for 0% -> 0% of each run, Pallas kernels for 10% -> 10%
where the time goes in v7:
time: 45.1 us; the launch traced here: 44.9 us
  starting transfers between devices  20.2 us (45%)
  waiting for transfers between devices  16.1 us (36%)
  Pallas kernels  5.7 us (13%)
  local copies, waits for them, and re-layouts  2.85 us (6%)
    ppermute x15, starting transfers between devices, swapped(): return lax.ppermute(value, 'slab', [(i, i ^ mask) for i in range(count)])  20.2 us
    ppermute x15, waiting for transfers between devices, swapped(): return lax.ppermute(value, 'slab', [(i, i ^ mask) for i in range(count)])  16.1 us
    pallas_call x10, Pallas kernels, kernel_call(): pl.pallas_call(body, out_shape=[jax.ShapeDtypeStruct(o.shape, o.dtype) fo...  5.7 us
    unnamed x10, local copies, waits for them, and re-layouts  2.85 us
  transfers between devices with their start and end apart: 15, of which 8 were waited for; matrix products, arithmetic and copies ran while one was open for 0% of the time, Pallas kernels for 10%

profile of v7, /device:TPU:0, one launch (start us, length us, event | category | flops | bytes accessed | tf_op | source)
XLA Modules:
  0.0 44.9 jit_solution(7588325038824888775)
XLA Ops:
  0.0 0.5 %collective-permute-start.4 = (bf16[512,1024]{1,0:T(8,128)(2,1)}, bf16[512,1024]{1,0:T(8,128)(2,1)S(1)}, u32[]{:S(2)}, u32[]{:S(2)}) collective-permute-start(bf16[512,1024]{1,0:T(8,128)(2,1)} %refs_0_.1), channel_id=1, source_target_pairs={{0,1},{1,0},{2,3},{3,2},{4,5},{5,4},{6,7},{7,6},{8,9},{9,8},{10,11... | collective-permute-start | bytes 3145736 | tf_op jit(solution)/shard_map/ppermute | solution.py:85
  0.5 2.5 %collective-permute-start = (bf16[512,1024]{1,0:T(8,128)(2,1)}, bf16[512,1024]{1,0:T(8,128)(2,1)S(1)}, u32[]{:S(2)}, u32[]{:S(2)}) collective-permute-start(bf16[512,1024]{1,0:T(8,128)(2,1)} %refs_0_.1), channel_id=1, source_target_pairs={{0,2},{1,3},{2,0},{3,1},{4,6},{5,7},{6,4},{7,5},{8,10},{9,11},{10,... | collective-permute-start | bytes 3145736 | tf_op jit(solution)/shard_map/ppermute | solution.py:85
  3.0 0.0 copy-start.2
  3.0 0.0 copy-start.3
  3.0 0.7 %copy-done.2 = s32[512]{0:T(512)S(1)} copy-done((s32[512]{0:T(512)S(1)}, s32[512]{0:T(512)}, u32[]{:S(2)}) %copy-start.2) | copy-done | bytes 2072
  3.7 0.0 copy-done.3
  3.7 0.0 copy-done.4
  3.7 0.1 shard_map.55
  3.8 0.0 copy-start.1
  3.8 0.9 %copy-done.1 = bf16[128,1024]{1,0:T(8,128)(2,1)S(1)} copy-done((bf16[128,1024]{1,0:T(8,128)(2,1)S(1)}, bf16[128,1024]{1,0:T(8,128)(2,1)}, u32[]{:S(2)}) %copy-start.1) | copy-done | bytes 262168
  4.7 0.5 %shard_map.56 = (bf16[784,128]{1,0:T(8,128)(2,1)S(1)}, bf16[784,128]{1,0:T(8,128)(2,1)S(1)}, bf16[784,128]{1,0:T(8,128)(2,1)S(1)}, bf16[528,128]{1,0:T(8,128)(2,1)S(1)}) custom-call(s32[1]{0:T(128)} %bitcast.me_ref, s32[1,128]{1,0:T(1,128)S(1)} %get-tuple-element.29.slot_ref, bf16[16,128]{1,0:T(8,128)(2,1)S(1)} %get-tuple-element.30.charge_ref, ...), custom_call_target="tpu_custom_call" | custom-call | bytes 1 | tf_op jit(solution)/shard_map/pallas_call | solution.py:248
  5.2 2.7 %collective-permute-start.1 = (bf16[784,128]{1,0:T(8,128)(2,1)S(1)}, bf16[784,128]{1,0:T(8,128)(2,1)S(1)}, u32[]{:S(2)}, u32[]{:S(2)}) collective-permute-start(bf16[784,128]{1,0:T(8,128)(2,1)S(1)} %get-tuple-element.31), channel_id=1, source_target_pairs={{0,8},{1,9},{2,10},{3,11},{4,12},{5,13},{6,14},{7,15},{8,0},{9,1},... | collective-permute-start | bytes 602120 | tf_op jit(solution)/shard_map/ppermute | solution.py:85
  7.9 1.6 %collective-permute-start.2 = (bf16[784,128]{1,0:T(8,128)(2,1)S(1)}, bf16[784,128]{1,0:T(8,128)(2,1)S(1)}, u32[]{:S(2)}, u32[]{:S(2)}) collective-permute-start(bf16[784,128]{1,0:T(8,128)(2,1)S(1)} %get-tuple-element.32), channel_id=1, source_target_pairs={{0,4},{1,5},{2,6},{3,7},{4,0},{5,1},{6,2},{7,3},{8,12},{9,13},{10,... | collective-permute-start | bytes 602120 | tf_op jit(solution)/shard_map/ppermute | solution.py:85
  9.5 0.0 collective-permute-start.3
  9.5 1.2 %collective-permute-done.3.other_ref = bf16[16,512]{1,0:T(8,128)(2,1)S(1)} collective-permute-done((bf16[16,512]{1,0:T(8,128)(2,1)S(1)}, bf16[16,512]{1,0:T(8,128)(2,1)S(1)}, u32[]{:S(2)}, u32[]{:S(2)}) %collective-permute-start.3) | collective-permute-done | bytes 16416 | tf_op jit(solution)/shard_map/ppermute | solution.py:85
  10.7 0.2 collective-permute-start.6
  10.9 0.0 collective-permute-done.4.refs_1_
  10.9 0.0 copy-start
  10.9 1.2 %copy-done = bf16[512,1024]{1,0:T(8,128)(2,1)S(1)} copy-done((bf16[512,1024]{1,0:T(8,128)(2,1)S(1)}, bf16[512,1024]{1,0:T(8,128)(2,1)}, u32[]{:S(2)}) %copy-start) | copy-done | bytes 1048600
  12.1 0.6 %shard_map.58 = (bf16[512,1024]{1,0:T(8,128)(2,1)S(1)}, bf16[512,1024]{1,0:T(8,128)(2,1)S(1)}) custom-call(bf16[512,1024]{1,0:T(8,128)(2,1)S(1)} %copy-done, bf16[512,1024]{1,0:T(8,128)(2,1)S(1)} %collective-permute-done.4.refs_1_), custom_call_target="tpu_custom_call" | custom-call | bytes 1 | tf_op jit(solution)/shard_map/pallas_call | solution.py:248
  12.8 6.0 %collective-permute-done.1.refs_0_ = bf16[784,128]{1,0:T(8,128)(2,1)S(1)} collective-permute-done((bf16[784,128]{1,0:T(8,128)(2,1)S(1)}, bf16[784,128]{1,0:T(8,128)(2,1)S(1)}, u32[]{:S(2)}, u32[]{:S(2)}) %collective-permute-start.1) | collective-permute-done | bytes 200736 | tf_op jit(solution)/shard_map/ppermute | solution.py:85
  18.8 0.0 collective-permute-done.2.refs_1_
  18.8 0.9 %shard_map.59 = (bf16[96,512]{1,0:T(8,128)(2,1)S(1)}, bf16[96,512]{1,0:T(8,128)(2,1)S(1)}, bf16[96,512]{1,0:T(8,128)(2,1)S(1)}, bf16[80,512]{1,0:T(8,128)(2,1)S(1)}) custom-call(s32[1]{0:T(128)} %bitcast.me_ref, bf16[784,128]{1,0:T(8,128)(2,1)S(1)} %collective-permute-done.1.refs_0_, bf16[784,128]{1,0:T(8,128)(2,1)S(1)} %collective-permute-done.2.refs_1_, ...), custom_call_target="tpu_custom_call" | custom-call | bytes 1 | tf_op jit(solution)/shard_map/pallas_call | solution.py:248
  19.7 1.2 %collective-permute-start.5 = (bf16[96,512]{1,0:T(8,128)(2,1)S(1)}, bf16[96,512]{1,0:T(8,128)(2,1)S(1)}, u32[]{:S(2)}, u32[]{:S(2)}) collective-permute-start(bf16[96,512]{1,0:T(8,128)(2,1)S(1)} %get-tuple-element.37), channel_id=1, source_target_pairs={{0,8},{1,9},{2,10},{3,11},{4,12},{5,13},{6,14},{7,15},{8,0},{9,1},... | collective-permute-start | bytes 294920 | tf_op jit(solution)/shard_map/ppermute | solution.py:85
  20.9 2.5 %collective-permute-start.7 = (bf16[80,512]{1,0:T(8,128)(2,1)S(1)}, bf16[80,512]{1,0:T(8,128)(2,1)S(1)}, u32[]{:S(2)}, u32[]{:S(2)}) collective-permute-start(bf16[80,512]{1,0:T(8,128)(2,1)S(1)} %get-tuple-element.40), channel_id=1, source_target_pairs={{0,4},{1,5},{2,6},{3,7},{4,0},{5,1},{6,2},{7,3},{8,12},{9,13},{10,... | collective-permute-start | bytes 245768 | tf_op jit(solution)/shard_map/ppermute | solution.py:85
  23.4 0.5 %collective-permute-start.8 = (bf16[16,512]{1,0:T(8,128)(2,1)S(1)}, bf16[16,512]{1,0:T(8,128)(2,1)S(1)}, u32[]{:S(2)}, u32[]{:S(2)}) collective-permute-start(bf16[16,512]{1,0:T(8,128)(2,1)S(1)} %shard_map.57.refs_3_.refs_0_), channel_id=1, source_target_pairs={{0,2},{1,3},{2,0},{3,1},{4,6},{5,7},{6,4},{7,5},{8,10},{9,11},{10,... | collective-permute-start | bytes 49160 | tf_op jit(solution)/shard_map/ppermute | solution.py:85
  23.9 0.0 collective-permute-done.6.q_ref
  23.9 2.4 %collective-permute-done.7.passed_ref = bf16[80,512]{1,0:T(8,128)(2,1)S(1)} collective-permute-done((bf16[80,512]{1,0:T(8,128)(2,1)S(1)}, bf16[80,512]{1,0:T(8,128)(2,1)S(1)}, u32[]{:S(2)}, u32[]{:S(2)}) %collective-permute-start.7) | collective-permute-done | bytes 81952 | tf_op jit(solution)/shard_map/ppermute | solution.py:85
  26.3 0.9 %shard_map.60 = (bf16[96,512]{1,0:T(8,128)(2,1)S(1)}, bf16[784,128]{1,0:T(8,128)(2,1)S(1)}) custom-call(s32[1]{0:T(128)} %bitcast.me_ref, bf16[528,128]{1,0:T(8,128)(2,1)S(1)} %collective-permute-done.6.q_ref, bf16[80,512]{1,0:T(8,128)(2,1)S(1)} %collective-permute-done.7.passed_ref, bf16[16,512]{1,0:T(8,128)(2,1)S(1)} %shard_map.57.refs_3_.refs_0_, ...), custom_call_target="tpu_custom_call" | custom-call | bytes 1 | tf_op jit(solution)/shard_map/pallas_call | solution.py:248
  27.2 0.2 collective-permute-done.8.refs_4_
  27.4 0.0 collective-permute-done.refs_0_
  27.4 0.3 collective-permute-done.5.refs_0_
  27.7 0.0 collective-permute-start.11
  27.7 0.3 shard_map.61.refs_5_
  28.0 1.6 %collective-permute-start.10 = (bf16[96,512]{1,0:T(8,128)(2,1)S(1)}, bf16[96,512]{1,0:T(8,128)(2,1)S(1)}, u32[]{:S(2)}, u32[]{:S(2)}) collective-permute-start(bf16[96,512]{1,0:T(8,128)(2,1)S(1)} %get-tuple-element.44), channel_id=1, source_target_pairs={{0,4},{1,5},{2,6},{3,7},{4,0},{5,1},{6,2},{7,3},{8,12},{9,13},{10,... | collective-permute-start | bytes 294920 | tf_op jit(solution)/shard_map/ppermute | solution.py:85
  29.6 2.5 %collective-permute-start.9 = (bf16[96,512]{1,0:T(8,128)(2,1)S(1)}, bf16[96,512]{1,0:T(8,128)(2,1)S(1)}, u32[]{:S(2)}, u32[]{:S(2)}) collective-permute-start(bf16[96,512]{1,0:T(8,128)(2,1)S(1)} %get-tuple-element.43), channel_id=1, source_target_pairs={{0,12},{1,13},{2,14},{3,15},{4,8},{5,9},{6,10},{7,11},{8,4},{9,5},... | collective-permute-start | bytes 294920 | tf_op jit(solution)/shard_map/ppermute | solution.py:85
  32.0 0.0 collective-permute-done.11.refs_0_
  32.1 0.3 shard_map.62.refs_6_
  32.4 0.9 %shard_map.63 = (bf16[96,512]{1,0:T(8,128)(2,1)S(1)}, bf16[96,512]{1,0:T(8,128)(2,1)S(1)}, bf16[96,512]{1,0:T(8,128)(2,1)S(1)}, bf16[96,512]{1,0:T(8,128)(2,1)S(1)}) custom-call(s32[1]{0:T(128)} %bitcast.me_ref, bf16[784,128]{1,0:T(8,128)(2,1)S(1)} %collective-permute-done.1.refs_0_, bf16[784,128]{1,0:T(8,128)(2,1)S(1)} %collective-permute-done.2.refs_1_, ...), custom_call_target="tpu_custom_call" | custom-call | bytes 1 | tf_op jit(solution)/shard_map/pallas_call | solution.py:248
  33.3 0.9 %collective-permute-start.12 = (bf16[96,512]{1,0:T(8,128)(2,1)S(1)}, bf16[96,512]{1,0:T(8,128)(2,1)S(1)}, u32[]{:S(2)}, u32[]{:S(2)}) collective-permute-start(bf16[96,512]{1,0:T(8,128)(2,1)S(1)} %get-tuple-element.49), channel_id=1, source_target_pairs={{0,8},{1,9},{2,10},{3,11},{4,12},{5,13},{6,14},{7,15},{8,0},{9,1},... | collective-permute-start | bytes 294920 | tf_op jit(solution)/shard_map/ppermute | solution.py:85
  34.1 1.6 %collective-permute-start.13 = (bf16[96,512]{1,0:T(8,128)(2,1)S(1)}, bf16[96,512]{1,0:T(8,128)(2,1)S(1)}, u32[]{:S(2)}, u32[]{:S(2)}) collective-permute-start(bf16[96,512]{1,0:T(8,128)(2,1)S(1)} %get-tuple-element.50), channel_id=1, source_target_pairs={{0,4},{1,5},{2,6},{3,7},{4,0},{5,1},{6,2},{7,3},{8,12},{9,13},{10,... | collective-permute-start | bytes 294920 | tf_op jit(solution)/shard_map/ppermute | solution.py:85
  35.7 2.0 %collective-permute-start.14 = (bf16[96,512]{1,0:T(8,128)(2,1)S(1)}, bf16[96,512]{1,0:T(8,128)(2,1)S(1)}, u32[]{:S(2)}, u32[]{:S(2)}) collective-permute-start(bf16[96,512]{1,0:T(8,128)(2,1)S(1)} %get-tuple-element.51), channel_id=1, source_target_pairs={{0,12},{1,13},{2,14},{3,15},{4,8},{5,9},{6,10},{7,11},{8,4},{9,5},... | collective-permute-start | bytes 294920 | tf_op jit(solution)/shard_map/ppermute | solution.py:85
  37.7 0.0 collective-permute-done.10.refs_2_
  37.7 0.1 collective-permute-done.9.refs_1_
  37.8 4.4 %collective-permute-done.12.refs_4_ = bf16[96,512]{1,0:T(8,128)(2,1)S(1)} collective-permute-done((bf16[96,512]{1,0:T(8,128)(2,1)S(1)}, bf16[96,512]{1,0:T(8,128)(2,1)S(1)}, u32[]{:S(2)}, u32[]{:S(2)}) %collective-permute-start.12) | collective-permute-done | bytes 98336 | tf_op jit(solution)/shard_map/ppermute | solution.py:85
  42.2 0.0 collective-permute-done.13.refs_5_
  42.2 1.5 %collective-permute-done.14.refs_6_ = bf16[96,512]{1,0:T(8,128)(2,1)S(1)} collective-permute-done((bf16[96,512]{1,0:T(8,128)(2,1)S(1)}, bf16[96,512]{1,0:T(8,128)(2,1)S(1)}, u32[]{:S(2)}, u32[]{:S(2)}) %collective-permute-start.14) | collective-permute-done | bytes 98336 | tf_op jit(solution)/shard_map/ppermute | solution.py:85
  43.8 1.1 %shard_map.64 = bf16[128,1536]{1,0:T(8,128)(2,1)} custom-call(s32[1]{0:T(128)} %bitcast.me_ref, s32[1,128]{1,0:T(1,128)S(1)} %get-tuple-element.29.slot_ref, bf16[96,512]{1,0:T(8,128)(2,1)S(1)} %collective-permute-done.5.refs_0_, bf16[96,512]{1,0:T(8,128)(2,1)S(1)} %collective-permute-done.9.refs_1_, bf16[96,512]{1,0:T(8,128)(2,1)S(1)} %collective-permute-done.10.refs_2_, ...), custom_call_target="tpu_custom_call" | custom-call | bytes 1 | tf_op jit(solution)/shard_map/pallas_call | solution.py:248
  (2 shorter events, 0.0 us)
Async XLA Ops:
  0.0 10.9 %collective-permute-start.4 = (bf16[512,1024]{1,0:T(8,128)(2,1)}, bf16[512,1024]{1,0:T(8,128)(2,1)S(1)}, u32[]{:S(2)}, u32[]{:S(2)}) collective-permute-start(bf16[512,1024]{1,0:T(8,128)(2,1)} %refs_0_.1), channel_id=1, source_target_pairs={{0,1},{1,0},{2,3},{3,2},{4,5},{5,4},{6,7},{7,6},{8,9},{9,8},{10,11... | collective-permute-start | bytes 3145736 | tf_op jit(solution)/shard_map/ppermute | solution.py:85
  0.5 26.9 %collective-permute-start = (bf16[512,1024]{1,0:T(8,128)(2,1)}, bf16[512,1024]{1,0:T(8,128)(2,1)S(1)}, u32[]{:S(2)}, u32[]{:S(2)}) collective-permute-start(bf16[512,1024]{1,0:T(8,128)(2,1)} %refs_0_.1), channel_id=1, source_target_pairs={{0,2},{1,3},{2,0},{3,1},{4,6},{5,7},{6,4},{7,5},{8,10},{9,11},{10,... | collective-permute-start | bytes 3145736 | tf_op jit(solution)/shard_map/ppermute | solution.py:85
  3.0 0.7 %copy-start.2 = (s32[512]{0:T(512)S(1)}, s32[512]{0:T(512)}, u32[]{:S(2)}) copy-start(s32[512]{0:T(512)} %param.9) | copy-start | bytes 6148
  3.0 0.7 %copy-start.3 = (s32[128,1]{0,1:T(1,128)S(1)}, s32[128,1]{0,1:T(1,128)}, u32[]{:S(2)}) copy-start(s32[128,1]{0,1:T(1,128)} %param.7) | copy-start | bytes 1540
  3.0 0.7 %copy-start.4 = (s32[128]{0:T(128)S(1)}, s32[128]{0:T(128)}, u32[]{:S(2)}) copy-start(s32[128]{0:T(128)} %param.8) | copy-start | bytes 1540
  3.8 1.0 %copy-start.1 = (bf16[128,1024]{1,0:T(8,128)(2,1)S(1)}, bf16[128,1024]{1,0:T(8,128)(2,1)}, u32[]{:S(2)}) copy-start(bf16[128,1024]{1,0:T(8,128)(2,1)} %q_ref.1) | copy-start | bytes 786436
  5.2 13.5 %collective-permute-start.1 = (bf16[784,128]{1,0:T(8,128)(2,1)S(1)}, bf16[784,128]{1,0:T(8,128)(2,1)S(1)}, u32[]{:S(2)}, u32[]{:S(2)}) collective-permute-start(bf16[784,128]{1,0:T(8,128)(2,1)S(1)} %get-tuple-element.31), channel_id=1, source_target_pairs={{0,8},{1,9},{2,10},{3,11},{4,12},{5,13},{6,14},{7,15},{8,0},{9,1},... | collective-permute-start | bytes 602120 | tf_op jit(solution)/shard_map/ppermute | solution.py:85
  7.9 10.9 %collective-permute-start.2 = (bf16[784,128]{1,0:T(8,128)(2,1)S(1)}, bf16[784,128]{1,0:T(8,128)(2,1)S(1)}, u32[]{:S(2)}, u32[]{:S(2)}) collective-permute-start(bf16[784,128]{1,0:T(8,128)(2,1)S(1)} %get-tuple-element.32), channel_id=1, source_target_pairs={{0,4},{1,5},{2,6},{3,7},{4,0},{5,1},{6,2},{7,3},{8,12},{9,13},{10,... | collective-permute-start | bytes 602120 | tf_op jit(solution)/shard_map/ppermute | solution.py:85
  9.5 1.2 %collective-permute-start.3 = (bf16[16,512]{1,0:T(8,128)(2,1)S(1)}, bf16[16,512]{1,0:T(8,128)(2,1)S(1)}, u32[]{:S(2)}, u32[]{:S(2)}) collective-permute-start(bf16[16,512]{1,0:T(8,128)(2,1)S(1)} %get-tuple-element.34.one_ref), channel_id=1, source_target_pairs={{0,1},{1,0},{2,3},{3,2},{4,5},{5,4},{6,7},{7,6},{8,9},{9,8},{10,11... | collective-permute-start | bytes 49160 | tf_op jit(solution)/shard_map/ppermute | solution.py:85
  10.7 13.3 %collective-permute-start.6 = (bf16[528,128]{1,0:T(8,128)(2,1)S(1)}, bf16[528,128]{1,0:T(8,128)(2,1)S(1)}, u32[]{:S(2)}, u32[]{:S(2)}) collective-permute-start(bf16[528,128]{1,0:T(8,128)(2,1)S(1)} %get-tuple-element.39), channel_id=1, source_target_pairs={{0,12},{1,13},{2,14},{3,15},{4,8},{5,9},{6,10},{7,11},{8,4},{9,5},... | collective-permute-start | bytes 405512 | tf_op jit(solution)/shard_map/ppermute | solution.py:85
  10.9 1.2 %copy-start = (bf16[512,1024]{1,0:T(8,128)(2,1)S(1)}, bf16[512,1024]{1,0:T(8,128)(2,1)}, u32[]{:S(2)}) copy-start(bf16[512,1024]{1,0:T(8,128)(2,1)} %refs_0_.1) | copy-start | bytes 3145732
  19.7 8.0 %collective-permute-start.5 = (bf16[96,512]{1,0:T(8,128)(2,1)S(1)}, bf16[96,512]{1,0:T(8,128)(2,1)S(1)}, u32[]{:S(2)}, u32[]{:S(2)}) collective-permute-start(bf16[96,512]{1,0:T(8,128)(2,1)S(1)} %get-tuple-element.37), channel_id=1, source_target_pairs={{0,8},{1,9},{2,10},{3,11},{4,12},{5,13},{6,14},{7,15},{8,0},{9,1},... | collective-permute-start | bytes 294920 | tf_op jit(solution)/shard_map/ppermute | solution.py:85
  20.9 5.4 %collective-permute-start.7 = (bf16[80,512]{1,0:T(8,128)(2,1)S(1)}, bf16[80,512]{1,0:T(8,128)(2,1)S(1)}, u32[]{:S(2)}, u32[]{:S(2)}) collective-permute-start(bf16[80,512]{1,0:T(8,128)(2,1)S(1)} %get-tuple-element.40), channel_id=1, source_target_pairs={{0,4},{1,5},{2,6},{3,7},{4,0},{5,1},{6,2},{7,3},{8,12},{9,13},{10,... | collective-permute-start | bytes 245768 | tf_op jit(solution)/shard_map/ppermute | solution.py:85
  23.4 3.9 %collective-permute-start.8 = (bf16[16,512]{1,0:T(8,128)(2,1)S(1)}, bf16[16,512]{1,0:T(8,128)(2,1)S(1)}, u32[]{:S(2)}, u32[]{:S(2)}) collective-permute-start(bf16[16,512]{1,0:T(8,128)(2,1)S(1)} %shard_map.57.refs_3_.refs_0_), channel_id=1, source_target_pairs={{0,2},{1,3},{2,0},{3,1},{4,6},{5,7},{6,4},{7,5},{8,10},{9,11},{10,... | collective-permute-start | bytes 49160 | tf_op jit(solution)/shard_map/ppermute | solution.py:85
  27.7 4.4 %collective-permute-start.11 = (bf16[512,1024]{1,0:T(8,128)(2,1)S(1)}, bf16[512,1024]{1,0:T(8,128)(2,1)S(1)}, u32[]{:S(2)}, u32[]{:S(2)}) collective-permute-start(bf16[512,1024]{1,0:T(8,128)(2,1)S(1)} %collective-permute-done.refs_0_), channel_id=1, source_target_pairs={{0,1},{1,0},{2,3},{3,2},{4,5},{5,4},{6,7},{7,6},{8,9},{9,8},{10,11... | collective-permute-start | bytes 3145736 | tf_op jit(solution)/shard_map/ppermute | solution.py:85
  28.0 9.7 %collective-permute-start.10 = (bf16[96,512]{1,0:T(8,128)(2,1)S(1)}, bf16[96,512]{1,0:T(8,128)(2,1)S(1)}, u32[]{:S(2)}, u32[]{:S(2)}) collective-permute-start(bf16[96,512]{1,0:T(8,128)(2,1)S(1)} %get-tuple-element.44), channel_id=1, source_target_pairs={{0,4},{1,5},{2,6},{3,7},{4,0},{5,1},{6,2},{7,3},{8,12},{9,13},{10,... | collective-permute-start | bytes 294920 | tf_op jit(solution)/shard_map/ppermute | solution.py:85
  29.6 8.2 %collective-permute-start.9 = (bf16[96,512]{1,0:T(8,128)(2,1)S(1)}, bf16[96,512]{1,0:T(8,128)(2,1)S(1)}, u32[]{:S(2)}, u32[]{:S(2)}) collective-permute-start(bf16[96,512]{1,0:T(8,128)(2,1)S(1)} %get-tuple-element.43), channel_id=1, source_target_pairs={{0,12},{1,13},{2,14},{3,15},{4,8},{5,9},{6,10},{7,11},{8,4},{9,5},... | collective-permute-start | bytes 294920 | tf_op jit(solution)/shard_map/ppermute | solution.py:85
  33.3 9.0 %collective-permute-start.12 = (bf16[96,512]{1,0:T(8,128)(2,1)S(1)}, bf16[96,512]{1,0:T(8,128)(2,1)S(1)}, u32[]{:S(2)}, u32[]{:S(2)}) collective-permute-start(bf16[96,512]{1,0:T(8,128)(2,1)S(1)} %get-tuple-element.49), channel_id=1, source_target_pairs={{0,8},{1,9},{2,10},{3,11},{4,12},{5,13},{6,14},{7,15},{8,0},{9,1},... | collective-permute-start | bytes 294920 | tf_op jit(solution)/shard_map/ppermute | solution.py:85
  34.1 8.1 %collective-permute-start.13 = (bf16[96,512]{1,0:T(8,128)(2,1)S(1)}, bf16[96,512]{1,0:T(8,128)(2,1)S(1)}, u32[]{:S(2)}, u32[]{:S(2)}) collective-permute-start(bf16[96,512]{1,0:T(8,128)(2,1)S(1)} %get-tuple-element.50), channel_id=1, source_target_pairs={{0,4},{1,5},{2,6},{3,7},{4,0},{5,1},{6,2},{7,3},{8,12},{9,13},{10,... | collective-permute-start | bytes 294920 | tf_op jit(solution)/shard_map/ppermute | solution.py:85
  35.7 8.1 %collective-permute-start.14 = (bf16[96,512]{1,0:T(8,128)(2,1)S(1)}, bf16[96,512]{1,0:T(8,128)(2,1)S(1)}, u32[]{:S(2)}, u32[]{:S(2)}) collective-permute-start(bf16[96,512]{1,0:T(8,128)(2,1)S(1)} %get-tuple-element.51), channel_id=1, source_target_pairs={{0,12},{1,13},{2,14},{3,15},{4,8},{5,9},{6,10},{7,11},{8,4},{9,5},... | collective-permute-start | bytes 294920 | tf_op jit(solution)/shard_map/ppermute | solution.py:85

commit v8 on v7

--- a/solution.py
+++ b/solution.py
@@ -213,6 +213,35 @@
     score_kernel(1, 0, me_ref, block_ref, charge_refs, *lib_refs, out_ref, rows_ref, charge_ref)
 
 
+def far_kernel(part, me_ref, *refs):
+    q_refs, lcharge_ref, raw_ref, refs = refs[:4], refs[4], refs[5], refs[6:]
+    upper_refs, refs = (refs[:4], refs[4:]) if part else ((), refs)
+    out_refs, (rows_ref, charge_ref, unit_ref) = refs[:4], refs[4:]
+    n_slots, seen = (PLANE + 2) * CAP, 3 * CAP
+    for start in range(0, raw_ref.shape[0], 64):
+        unit_ref[start : start + 64, :] = unit_rows(raw_ref[start : start + 64, :])
+    at = pl.multiple_of(((me_ref[0] % PLANE) ^ (2 + part)) * CAP, CAP)
+    chunks = raw_ref.shape[1] // 128
+    for k in range(4):
+        for c in range(chunks):
+            rows_ref[k * seen : (k + 1) * seen, c * 128 : (c + 1) * 128] = q_refs[k][
+                pl.ds(pl.multiple_of(at + c * n_slots, CAP), seen), :
+            ]
+        line = q_refs[k][chunks * n_slots :, :].astype(F32)[0:1, :]
+        charge_ref[k] = jnp.broadcast_to(line, (128, 128)).T
+    lib_charge = lcharge_ref[...].astype(F32)[part : part + 1, :]
+    products = lax.dot_general(
+        rows_ref[...], unit_ref[...], (((1,), (1,)), ((), ())), preferred_element_type=F32
+    )
+    for k in range(4):
+        row_charge = charge_ref[k, pl.ds(at, seen), :][:, 0:1]
+        kept = jnp.abs(row_charge - lib_charge) <= 2.0
+        scores = jnp.where(kept, products[k * seen : (k + 1) * seen, :], 0.0).astype(BF16)
+        if part:
+            out_refs[k][:seen, :] = upper_refs[k][...]
+        out_refs[k][part * seen : (part + 1) * seen, :] = scores
+
+
 def home_kernel(me_ref, slot_ref, *refs):
     near8, near12, near4, near0, far8, far4, far12, far0, out_ref, flat_ref = refs
     near = [near0, near4, near8, near12]
@@ -315,15 +344,20 @@
     )
     raw_d = swapped(raw_y, 1)
     near12, near4 = swapped(near12, 12), swapped(near4, 4)
-    (unit_y,) = kernel_call(unit_kernel, [lib], [raw_y], [VMEM])
-    (unit_d,) = kernel_call(unit_kernel, [lib], [raw_d], [VMEM])
-    far8, far4, far12, far0 = kernel_call(
-        functools.partial(score_kernel, 4, 2),
-        [block] * 4,
-        [me, q8, q4, q12, q0, far_charge, unit_y, unit_d],
-        [SMEM] + [VMEM] * 7,
-        [pltpu.VMEM((4 * seen, width), BF16), pltpu.VMEM((4, 128, 128), F32)],
-    )
+    upper = ()
+    for part, raw in enumerate((raw_y, raw_d)):
+        upper = kernel_call(
+            functools.partial(far_kernel, part),
+            [shape((part + 1) * seen, l_rows)] * 4,
+            [me, q8, q4, q12, q0, far_charge, raw, *upper],
+            [SMEM] + [VMEM] * (6 + len(upper)),
+            [
+                pltpu.VMEM((4 * seen, width), BF16),
+                pltpu.VMEM((4, 128, 128), F32),
+                pltpu.VMEM((l_rows, width), BF16),
+            ],
+        )
+    far8, far4, far12, far0 = upper
     far8, far4, far12 = swapped(far8, 8), swapped(far4, 4), swapped(far12, 12)
     (out,) = kernel_call(
         home_kernel,

time: 45.1 us -> 44.6 us (0.989)
    pallas_call x10 -> x9, Pallas kernels: 5.7 us -> 5.64 us  [kernel_call(): pl.pallas_call(body, out_shape=[jax.ShapeDtypeStruct(o.shape, o.dtype) fo...]
  transfers between devices with their start and end apart: 15 -> 15, of which waited for: 8 -> 6; matrix products, arithmetic and copies ran while one was open for 0% -> 0% of each run, Pallas kernels for 10% -> 10%
where the time goes in v8:
time: 44.6 us; the launch traced here: 44.4 us
  starting transfers between devices  20.2 us (45%)
  waiting for transfers between devices  15.7 us (35%)
  Pallas kernels  5.64 us (13%)
  local copies, waits for them, and re-layouts  2.85 us (6%)
    ppermute x15, starting transfers between devices, swapped(): return lax.ppermute(value, 'slab', [(i, i ^ mask) for i in range(count)])  20.2 us
    ppermute x15, waiting for transfers between devices, swapped(): return lax.ppermute(value, 'slab', [(i, i ^ mask) for i in range(count)])  15.7 us
    pallas_call x9, Pallas kernels, kernel_call(): pl.pallas_call(body, out_shape=[jax.ShapeDtypeStruct(o.shape, o.dtype) fo...  5.64 us
    unnamed x10, local copies, waits for them, and re-layouts  2.85 us
  transfers between devices with their start and end apart: 15, of which 6 were waited for; matrix products, arithmetic and copies ran while one was open for 0% of the time, Pallas kernels for 10%

profile of v8, /device:TPU:0, one launch (start us, length us, event | category | flops | bytes accessed | tf_op | source)
XLA Modules:
  0.0 44.4 jit_solution(3439514563305584629)
XLA Ops:
  0.0 0.5 %collective-permute-start.4 = (bf16[512,1024]{1,0:T(8,128)(2,1)}, bf16[512,1024]{1,0:T(8,128)(2,1)S(1)}, u32[]{:S(2)}, u32[]{:S(2)}) collective-permute-start(bf16[512,1024]{1,0:T(8,128)(2,1)} %refs_0_.1), channel_id=1, source_target_pairs={{0,1},{1,0},{2,3},{3,2},{4,5},{5,4},{6,7},{7,6},{8,9},{9,8},{10,11... | collective-permute-start | bytes 3145736 | tf_op jit(solution)/shard_map/ppermute | solution.py:85
  0.5 2.5 %collective-permute-start = (bf16[512,1024]{1,0:T(8,128)(2,1)}, bf16[512,1024]{1,0:T(8,128)(2,1)S(1)}, u32[]{:S(2)}, u32[]{:S(2)}) collective-permute-start(bf16[512,1024]{1,0:T(8,128)(2,1)} %refs_0_.1), channel_id=1, source_target_pairs={{0,2},{1,3},{2,0},{3,1},{4,6},{5,7},{6,4},{7,5},{8,10},{9,11},{10,... | collective-permute-start | bytes 3145736 | tf_op jit(solution)/shard_map/ppermute | solution.py:85
  3.0 0.0 copy-start.2
  3.0 0.0 copy-start.3
  3.0 0.0 copy-start.4
  3.0 0.7 %copy-done.2 = s32[512]{0:T(512)S(1)} copy-done((s32[512]{0:T(512)S(1)}, s32[512]{0:T(512)}, u32[]{:S(2)}) %copy-start.2) | copy-done | bytes 2072
  3.7 0.0 copy-done.3
  3.7 0.0 copy-done.4
  3.7 0.1 shard_map.55
  3.8 0.0 copy-start.1
  3.8 0.9 %copy-done.1 = bf16[128,1024]{1,0:T(8,128)(2,1)S(1)} copy-done((bf16[128,1024]{1,0:T(8,128)(2,1)S(1)}, bf16[128,1024]{1,0:T(8,128)(2,1)}, u32[]{:S(2)}) %copy-start.1) | copy-done | bytes 262168
  4.7 0.5 %shard_map.56 = (bf16[784,128]{1,0:T(8,128)(2,1)S(1)}, bf16[784,128]{1,0:T(8,128)(2,1)S(1)}, bf16[784,128]{1,0:T(8,128)(2,1)S(1)}, bf16[528,128]{1,0:T(8,128)(2,1)S(1)}) custom-call(s32[1]{0:T(128)} %bitcast.me_ref, s32[1,128]{1,0:T(1,128)S(1)} %get-tuple-element.33.slot_ref, bf16[16,128]{1,0:T(8,128)(2,1)S(1)} %get-tuple-element.34.charge_ref, ...), custom_call_target="tpu_custom_call" | custom-call | bytes 1 | tf_op jit(solution)/shard_map/pallas_call | solution.py:277
  5.2 2.7 %collective-permute-start.1 = (bf16[784,128]{1,0:T(8,128)(2,1)S(1)}, bf16[784,128]{1,0:T(8,128)(2,1)S(1)}, u32[]{:S(2)}, u32[]{:S(2)}) collective-permute-start(bf16[784,128]{1,0:T(8,128)(2,1)S(1)} %get-tuple-element.35), channel_id=1, source_target_pairs={{0,8},{1,9},{2,10},{3,11},{4,12},{5,13},{6,14},{7,15},{8,0},{9,1},... | collective-permute-start | bytes 602120 | tf_op jit(solution)/shard_map/ppermute | solution.py:85
  7.9 1.6 %collective-permute-start.2 = (bf16[784,128]{1,0:T(8,128)(2,1)S(1)}, bf16[784,128]{1,0:T(8,128)(2,1)S(1)}, u32[]{:S(2)}, u32[]{:S(2)}) collective-permute-start(bf16[784,128]{1,0:T(8,128)(2,1)S(1)} %get-tuple-element.36), channel_id=1, source_target_pairs={{0,4},{1,5},{2,6},{3,7},{4,0},{5,1},{6,2},{7,3},{8,12},{9,13},{10,... | collective-permute-start | bytes 602120 | tf_op jit(solution)/shard_map/ppermute | solution.py:85
  9.5 0.0 collective-permute-start.3
  9.5 1.2 %collective-permute-done.3.other_ref = bf16[16,512]{1,0:T(8,128)(2,1)S(1)} collective-permute-done((bf16[16,512]{1,0:T(8,128)(2,1)S(1)}, bf16[16,512]{1,0:T(8,128)(2,1)S(1)}, u32[]{:S(2)}, u32[]{:S(2)}) %collective-permute-start.3) | collective-permute-done | bytes 16416 | tf_op jit(solution)/shard_map/ppermute | solution.py:85
  10.7 0.2 collective-permute-start.6
  10.9 0.0 collective-permute-done.4.refs_1_
  10.9 0.0 copy-start
  10.9 1.2 %copy-done = bf16[512,1024]{1,0:T(8,128)(2,1)S(1)} copy-done((bf16[512,1024]{1,0:T(8,128)(2,1)S(1)}, bf16[512,1024]{1,0:T(8,128)(2,1)}, u32[]{:S(2)}) %copy-start) | copy-done | bytes 1048600
  12.1 0.6 %shard_map.58 = (bf16[512,1024]{1,0:T(8,128)(2,1)S(1)}, bf16[512,1024]{1,0:T(8,128)(2,1)S(1)}) custom-call(bf16[512,1024]{1,0:T(8,128)(2,1)S(1)} %copy-done, bf16[512,1024]{1,0:T(8,128)(2,1)S(1)} %collective-permute-done.4.refs_1_), custom_call_target="tpu_custom_call" | custom-call | bytes 1 | tf_op jit(solution)/shard_map/pallas_call | solution.py:277
  12.8 6.0 %collective-permute-done.1.refs_0_ = bf16[784,128]{1,0:T(8,128)(2,1)S(1)} collective-permute-done((bf16[784,128]{1,0:T(8,128)(2,1)S(1)}, bf16[784,128]{1,0:T(8,128)(2,1)S(1)}, u32[]{:S(2)}, u32[]{:S(2)}) %collective-permute-start.1) | collective-permute-done | bytes 200736 | tf_op jit(solution)/shard_map/ppermute | solution.py:85
  18.8 0.0 collective-permute-done.2.refs_1_
  18.8 0.9 %shard_map.59 = (bf16[96,512]{1,0:T(8,128)(2,1)S(1)}, bf16[96,512]{1,0:T(8,128)(2,1)S(1)}, bf16[96,512]{1,0:T(8,128)(2,1)S(1)}, bf16[80,512]{1,0:T(8,128)(2,1)S(1)}) custom-call(s32[1]{0:T(128)} %bitcast.me_ref, bf16[784,128]{1,0:T(8,128)(2,1)S(1)} %collective-permute-done.1.refs_0_, bf16[784,128]{1,0:T(8,128)(2,1)S(1)} %collective-permute-done.2.refs_1_, ...), custom_call_target="tpu_custom_call" | custom-call | bytes 1 | tf_op jit(solution)/shard_map/pallas_call | solution.py:277
  19.7 1.2 %collective-permute-start.5 = (bf16[96,512]{1,0:T(8,128)(2,1)S(1)}, bf16[96,512]{1,0:T(8,128)(2,1)S(1)}, u32[]{:S(2)}, u32[]{:S(2)}) collective-permute-start(bf16[96,512]{1,0:T(8,128)(2,1)S(1)} %get-tuple-element.41), channel_id=1, source_target_pairs={{0,8},{1,9},{2,10},{3,11},{4,12},{5,13},{6,14},{7,15},{8,0},{9,1},... | collective-permute-start | bytes 294920 | tf_op jit(solution)/shard_map/ppermute | solution.py:85
  20.9 2.5 %collective-permute-start.7 = (bf16[80,512]{1,0:T(8,128)(2,1)S(1)}, bf16[80,512]{1,0:T(8,128)(2,1)S(1)}, u32[]{:S(2)}, u32[]{:S(2)}) collective-permute-start(bf16[80,512]{1,0:T(8,128)(2,1)S(1)} %get-tuple-element.44), channel_id=1, source_target_pairs={{0,4},{1,5},{2,6},{3,7},{4,0},{5,1},{6,2},{7,3},{8,12},{9,13},{10,... | collective-permute-start | bytes 245768 | tf_op jit(solution)/shard_map/ppermute | solution.py:85
  23.4 0.5 %collective-permute-start.8 = (bf16[16,512]{1,0:T(8,128)(2,1)S(1)}, bf16[16,512]{1,0:T(8,128)(2,1)S(1)}, u32[]{:S(2)}, u32[]{:S(2)}) collective-permute-start(bf16[16,512]{1,0:T(8,128)(2,1)S(1)} %shard_map.57.refs_3_.refs_0_), channel_id=1, source_target_pairs={{0,2},{1,3},{2,0},{3,1},{4,6},{5,7},{6,4},{7,5},{8,10},{9,11},{10,... | collective-permute-start | bytes 49160 | tf_op jit(solution)/shard_map/ppermute | solution.py:85
  23.9 0.0 collective-permute-done.6.q_ref
  23.9 2.4 %collective-permute-done.7.passed_ref = bf16[80,512]{1,0:T(8,128)(2,1)S(1)} collective-permute-done((bf16[80,512]{1,0:T(8,128)(2,1)S(1)}, bf16[80,512]{1,0:T(8,128)(2,1)S(1)}, u32[]{:S(2)}, u32[]{:S(2)}) %collective-permute-start.7) | collective-permute-done | bytes 81952 | tf_op jit(solution)/shard_map/ppermute | solution.py:85
  26.3 0.9 %shard_map.60 = (bf16[96,512]{1,0:T(8,128)(2,1)S(1)}, bf16[784,128]{1,0:T(8,128)(2,1)S(1)}) custom-call(s32[1]{0:T(128)} %bitcast.me_ref, bf16[528,128]{1,0:T(8,128)(2,1)S(1)} %collective-permute-done.6.q_ref, bf16[80,512]{1,0:T(8,128)(2,1)S(1)} %collective-permute-done.7.passed_ref, bf16[16,512]{1,0:T(8,128)(2,1)S(1)} %shard_map.57.refs_3_.refs_0_, ...), custom_call_target="tpu_custom_call" | custom-call | bytes 1 | tf_op jit(solution)/shard_map/pallas_call | solution.py:277
  27.2 0.2 collective-permute-done.8.refs_4_
  27.4 0.0 collective-permute-done.refs_5_
  27.4 0.3 collective-permute-done.5.refs_0_
  27.7 0.0 collective-permute-start.11
  27.7 1.6 %collective-permute-start.10 = (bf16[96,512]{1,0:T(8,128)(2,1)S(1)}, bf16[96,512]{1,0:T(8,128)(2,1)S(1)}, u32[]{:S(2)}, u32[]{:S(2)}) collective-permute-start(bf16[96,512]{1,0:T(8,128)(2,1)S(1)} %get-tuple-element.48), channel_id=1, source_target_pairs={{0,4},{1,5},{2,6},{3,7},{4,0},{5,1},{6,2},{7,3},{8,12},{9,13},{10,... | collective-permute-start | bytes 294920 | tf_op jit(solution)/shard_map/ppermute | solution.py:85
  29.2 2.5 %collective-permute-start.9 = (bf16[96,512]{1,0:T(8,128)(2,1)S(1)}, bf16[96,512]{1,0:T(8,128)(2,1)S(1)}, u32[]{:S(2)}, u32[]{:S(2)}) collective-permute-start(bf16[96,512]{1,0:T(8,128)(2,1)S(1)} %get-tuple-element.47), channel_id=1, source_target_pairs={{0,12},{1,13},{2,14},{3,15},{4,8},{5,9},{6,10},{7,11},{8,4},{9,5},... | collective-permute-start | bytes 294920 | tf_op jit(solution)/shard_map/ppermute | solution.py:85
  31.7 0.7 %shard_map.61 = (bf16[48,512]{1,0:T(8,128)(2,1)S(1)}, bf16[48,512]{1,0:T(8,128)(2,1)S(1)}, bf16[48,512]{1,0:T(8,128)(2,1)S(1)}, bf16[48,512]{1,0:T(8,128)(2,1)S(1)}) custom-call(s32[1]{0:T(128)} %bitcast.me_ref, bf16[784,128]{1,0:T(8,128)(2,1)S(1)} %collective-permute-done.1.refs_0_, bf16[784,128]{1,0:T(8,128)(2,1)S(1)} %collective-permute-done.2.refs_1_, ...), custom_call_target="tpu_custom_call" | custom-call | bytes 1 | tf_op jit(solution)/shard_map/pallas_call | solution.py:277
  32.5 0.0 collective-permute-done.11.refs_5_
  32.5 0.8 %shard_map.62 = (bf16[96,512]{1,0:T(8,128)(2,1)S(1)}, bf16[96,512]{1,0:T(8,128)(2,1)S(1)}, bf16[96,512]{1,0:T(8,128)(2,1)S(1)}, bf16[96,512]{1,0:T(8,128)(2,1)S(1)}) custom-call(s32[1]{0:T(128)} %bitcast.me_ref, bf16[784,128]{1,0:T(8,128)(2,1)S(1)} %collective-permute-done.1.refs_0_, bf16[784,128]{1,0:T(8,128)(2,1)S(1)} %collective-permute-done.2.refs_1_, ...), custom_call_target="tpu_custom_call" | custom-call | bytes 1 | tf_op jit(solution)/shard_map/pallas_call | solution.py:277
  33.2 0.4 collective-permute-start.12
  33.7 1.6 %collective-permute-start.13 = (bf16[96,512]{1,0:T(8,128)(2,1)S(1)}, bf16[96,512]{1,0:T(8,128)(2,1)S(1)}, u32[]{:S(2)}, u32[]{:S(2)}) collective-permute-start(bf16[96,512]{1,0:T(8,128)(2,1)S(1)} %get-tuple-element.58), channel_id=1, source_target_pairs={{0,4},{1,5},{2,6},{3,7},{4,0},{5,1},{6,2},{7,3},{8,12},{9,13},{10,... | collective-permute-start | bytes 294920 | tf_op jit(solution)/shard_map/ppermute | solution.py:85
  35.2 2.4 %collective-permute-start.14 = (bf16[96,512]{1,0:T(8,128)(2,1)S(1)}, bf16[96,512]{1,0:T(8,128)(2,1)S(1)}, u32[]{:S(2)}, u32[]{:S(2)}) collective-permute-start(bf16[96,512]{1,0:T(8,128)(2,1)S(1)} %get-tuple-element.59), channel_id=1, source_target_pairs={{0,12},{1,13},{2,14},{3,15},{4,8},{5,9},{6,10},{7,11},{8,4},{9,5},... | collective-permute-start | bytes 294920 | tf_op jit(solution)/shard_map/ppermute | solution.py:85
  37.7 0.0 collective-permute-done.10.refs_2_
  37.7 0.0 collective-permute-done.9.refs_1_
  37.7 5.6 %collective-permute-done.12.refs_4_ = bf16[96,512]{1,0:T(8,128)(2,1)S(1)} collective-permute-done((bf16[96,512]{1,0:T(8,128)(2,1)S(1)}, bf16[96,512]{1,0:T(8,128)(2,1)S(1)}, u32[]{:S(2)}, u32[]{:S(2)}) %collective-permute-start.12) | collective-permute-done | bytes 98336 | tf_op jit(solution)/shard_map/ppermute | solution.py:85
  43.3 0.0 collective-permute-done.13.refs_5_
  43.3 0.0 collective-permute-done.14.refs_6_
  43.3 1.1 %shard_map.63 = bf16[128,1536]{1,0:T(8,128)(2,1)} custom-call(s32[1]{0:T(128)} %bitcast.me_ref, s32[1,128]{1,0:T(1,128)S(1)} %get-tuple-element.33.slot_ref, bf16[96,512]{1,0:T(8,128)(2,1)S(1)} %collective-permute-done.5.refs_0_, bf16[96,512]{1,0:T(8,128)(2,1)S(1)} %collective-permute-done.9.refs_1_, bf16[96,512]{1,0:T(8,128)(2,1)S(1)} %collective-permute-done.10.refs_2_, ...), custom_call_target="tpu_custom_call" | custom-call | bytes 1 | tf_op jit(solution)/shard_map/pallas_call | solution.py:277
  (1 shorter events, 0.0 us)
Async XLA Ops:
  0.0 10.9 %collective-permute-start.4 = (bf16[512,1024]{1,0:T(8,128)(2,1)}, bf16[512,1024]{1,0:T(8,128)(2,1)S(1)}, u32[]{:S(2)}, u32[]{:S(2)}) collective-permute-start(bf16[512,1024]{1,0:T(8,128)(2,1)} %refs_0_.1), channel_id=1, source_target_pairs={{0,1},{1,0},{2,3},{3,2},{4,5},{5,4},{6,7},{7,6},{8,9},{9,8},{10,11... | collective-permute-start | bytes 3145736 | tf_op jit(solution)/shard_map/ppermute | solution.py:85
  0.5 26.9 %collective-permute-start = (bf16[512,1024]{1,0:T(8,128)(2,1)}, bf16[512,1024]{1,0:T(8,128)(2,1)S(1)}, u32[]{:S(2)}, u32[]{:S(2)}) collective-permute-start(bf16[512,1024]{1,0:T(8,128)(2,1)} %refs_0_.1), channel_id=1, source_target_pairs={{0,2},{1,3},{2,0},{3,1},{4,6},{5,7},{6,4},{7,5},{8,10},{9,11},{10,... | collective-permute-start | bytes 3145736 | tf_op jit(solution)/shard_map/ppermute | solution.py:85
  3.0 0.7 %copy-start.2 = (s32[512]{0:T(512)S(1)}, s32[512]{0:T(512)}, u32[]{:S(2)}) copy-start(s32[512]{0:T(512)} %param.9) | copy-start | bytes 6148
  3.0 0.7 %copy-start.3 = (s32[128,1]{0,1:T(1,128)S(1)}, s32[128,1]{0,1:T(1,128)}, u32[]{:S(2)}) copy-start(s32[128,1]{0,1:T(1,128)} %param.7) | copy-start | bytes 1540
  3.0 0.7 %copy-start.4 = (s32[128]{0:T(128)S(1)}, s32[128]{0:T(128)}, u32[]{:S(2)}) copy-start(s32[128]{0:T(128)} %param.8) | copy-start | bytes 1540
  3.8 1.0 %copy-start.1 = (bf16[128,1024]{1,0:T(8,128)(2,1)S(1)}, bf16[128,1024]{1,0:T(8,128)(2,1)}, u32[]{:S(2)}) copy-start(bf16[128,1024]{1,0:T(8,128)(2,1)} %q_ref.1) | copy-start | bytes 786436
  5.2 13.5 %collective-permute-start.1 = (bf16[784,128]{1,0:T(8,128)(2,1)S(1)}, bf16[784,128]{1,0:T(8,128)(2,1)S(1)}, u32[]{:S(2)}, u32[]{:S(2)}) collective-permute-start(bf16[784,128]{1,0:T(8,128)(2,1)S(1)} %get-tuple-element.35), channel_id=1, source_target_pairs={{0,8},{1,9},{2,10},{3,11},{4,12},{5,13},{6,14},{7,15},{8,0},{9,1},... | collective-permute-start | bytes 602120 | tf_op jit(solution)/shard_map/ppermute | solution.py:85
  7.9 10.9 %collective-permute-start.2 = (bf16[784,128]{1,0:T(8,128)(2,1)S(1)}, bf16[784,128]{1,0:T(8,128)(2,1)S(1)}, u32[]{:S(2)}, u32[]{:S(2)}) collective-permute-start(bf16[784,128]{1,0:T(8,128)(2,1)S(1)} %get-tuple-element.36), channel_id=1, source_target_pairs={{0,4},{1,5},{2,6},{3,7},{4,0},{5,1},{6,2},{7,3},{8,12},{9,13},{10,... | collective-permute-start | bytes 602120 | tf_op jit(solution)/shard_map/ppermute | solution.py:85
  9.5 1.2 %collective-permute-start.3 = (bf16[16,512]{1,0:T(8,128)(2,1)S(1)}, bf16[16,512]{1,0:T(8,128)(2,1)S(1)}, u32[]{:S(2)}, u32[]{:S(2)}) collective-permute-start(bf16[16,512]{1,0:T(8,128)(2,1)S(1)} %get-tuple-element.38.one_ref), channel_id=1, source_target_pairs={{0,1},{1,0},{2,3},{3,2},{4,5},{5,4},{6,7},{7,6},{8,9},{9,8},{10,11... | collective-permute-start | bytes 49160 | tf_op jit(solution)/shard_map/ppermute | solution.py:85
  10.7 13.3 %collective-permute-start.6 = (bf16[528,128]{1,0:T(8,128)(2,1)S(1)}, bf16[528,128]{1,0:T(8,128)(2,1)S(1)}, u32[]{:S(2)}, u32[]{:S(2)}) collective-permute-start(bf16[528,128]{1,0:T(8,128)(2,1)S(1)} %get-tuple-element.43), channel_id=1, source_target_pairs={{0,12},{1,13},{2,14},{3,15},{4,8},{5,9},{6,10},{7,11},{8,4},{9,5},... | collective-permute-start | bytes 405512 | tf_op jit(solution)/shard_map/ppermute | solution.py:85
  10.9 1.2 %copy-start = (bf16[512,1024]{1,0:T(8,128)(2,1)S(1)}, bf16[512,1024]{1,0:T(8,128)(2,1)}, u32[]{:S(2)}) copy-start(bf16[512,1024]{1,0:T(8,128)(2,1)} %refs_0_.1) | copy-start | bytes 3145732
  19.7 8.0 %collective-permute-start.5 = (bf16[96,512]{1,0:T(8,128)(2,1)S(1)}, bf16[96,512]{1,0:T(8,128)(2,1)S(1)}, u32[]{:S(2)}, u32[]{:S(2)}) collective-permute-start(bf16[96,512]{1,0:T(8,128)(2,1)S(1)} %get-tuple-element.41), channel_id=1, source_target_pairs={{0,8},{1,9},{2,10},{3,11},{4,12},{5,13},{6,14},{7,15},{8,0},{9,1},... | collective-permute-start | bytes 294920 | tf_op jit(solution)/shard_map/ppermute | solution.py:85
  20.9 5.4 %collective-permute-start.7 = (bf16[80,512]{1,0:T(8,128)(2,1)S(1)}, bf16[80,512]{1,0:T(8,128)(2,1)S(1)}, u32[]{:S(2)}, u32[]{:S(2)}) collective-permute-start(bf16[80,512]{1,0:T(8,128)(2,1)S(1)} %get-tuple-element.44), channel_id=1, source_target_pairs={{0,4},{1,5},{2,6},{3,7},{4,0},{5,1},{6,2},{7,3},{8,12},{9,13},{10,... | collective-permute-start | bytes 245768 | tf_op jit(solution)/shard_map/ppermute | solution.py:85
  23.4 3.9 %collective-permute-start.8 = (bf16[16,512]{1,0:T(8,128)(2,1)S(1)}, bf16[16,512]{1,0:T(8,128)(2,1)S(1)}, u32[]{:S(2)}, u32[]{:S(2)}) collective-permute-start(bf16[16,512]{1,0:T(8,128)(2,1)S(1)} %shard_map.57.refs_3_.refs_0_), channel_id=1, source_target_pairs={{0,2},{1,3},{2,0},{3,1},{4,6},{5,7},{6,4},{7,5},{8,10},{9,11},{10,... | collective-permute-start | bytes 49160 | tf_op jit(solution)/shard_map/ppermute | solution.py:85
  27.7 4.8 %collective-permute-start.11 = (bf16[512,1024]{1,0:T(8,128)(2,1)S(1)}, bf16[512,1024]{1,0:T(8,128)(2,1)S(1)}, u32[]{:S(2)}, u32[]{:S(2)}) collective-permute-start(bf16[512,1024]{1,0:T(8,128)(2,1)S(1)} %collective-permute-done.refs_5_), channel_id=1, source_target_pairs={{0,1},{1,0},{2,3},{3,2},{4,5},{5,4},{6,7},{7,6},{8,9},{9,8},{10,11... | collective-permute-start | bytes 3145736 | tf_op jit(solution)/shard_map/ppermute | solution.py:85
  27.7 10.0 %collective-permute-start.10 = (bf16[96,512]{1,0:T(8,128)(2,1)S(1)}, bf16[96,512]{1,0:T(8,128)(2,1)S(1)}, u32[]{:S(2)}, u32[]{:S(2)}) collective-permute-start(bf16[96,512]{1,0:T(8,128)(2,1)S(1)} %get-tuple-element.48), channel_id=1, source_target_pairs={{0,4},{1,5},{2,6},{3,7},{4,0},{5,1},{6,2},{7,3},{8,12},{9,13},{10,... | collective-permute-start | bytes 294920 | tf_op jit(solution)/shard_map/ppermute | solution.py:85
  29.2 8.4 %collective-permute-start.9 = (bf16[96,512]{1,0:T(8,128)(2,1)S(1)}, bf16[96,512]{1,0:T(8,128)(2,1)S(1)}, u32[]{:S(2)}, u32[]{:S(2)}) collective-permute-start(bf16[96,512]{1,0:T(8,128)(2,1)S(1)} %get-tuple-element.47), channel_id=1, source_target_pairs={{0,12},{1,13},{2,14},{3,15},{4,8},{5,9},{6,10},{7,11},{8,4},{9,5},... | collective-permute-start | bytes 294920 | tf_op jit(solution)/shard_map/ppermute | solution.py:85
  33.2 10.1 %collective-permute-start.12 = (bf16[96,512]{1,0:T(8,128)(2,1)S(1)}, bf16[96,512]{1,0:T(8,128)(2,1)S(1)}, u32[]{:S(2)}, u32[]{:S(2)}) collective-permute-start(bf16[96,512]{1,0:T(8,128)(2,1)S(1)} %get-tuple-element.57), channel_id=1, source_target_pairs={{0,8},{1,9},{2,10},{3,11},{4,12},{5,13},{6,14},{7,15},{8,0},{9,1},... | collective-permute-start | bytes 294920 | tf_op jit(solution)/shard_map/ppermute | solution.py:85
  33.7 9.7 %collective-permute-start.13 = (bf16[96,512]{1,0:T(8,128)(2,1)S(1)}, bf16[96,512]{1,0:T(8,128)(2,1)S(1)}, u32[]{:S(2)}, u32[]{:S(2)}) collective-permute-start(bf16[96,512]{1,0:T(8,128)(2,1)S(1)} %get-tuple-element.58), channel_id=1, source_target_pairs={{0,4},{1,5},{2,6},{3,7},{4,0},{5,1},{6,2},{7,3},{8,12},{9,13},{10,... | collective-permute-start | bytes 294920 | tf_op jit(solution)/shard_map/ppermute | solution.py:85
  35.2 8.1 %collective-permute-start.14 = (bf16[96,512]{1,0:T(8,128)(2,1)S(1)}, bf16[96,512]{1,0:T(8,128)(2,1)S(1)}, u32[]{:S(2)}, u32[]{:S(2)}) collective-permute-start(bf16[96,512]{1,0:T(8,128)(2,1)S(1)} %get-tuple-element.59), channel_id=1, source_target_pairs={{0,12},{1,13},{2,14},{3,15},{4,8},{5,9},{6,10},{7,11},{8,4},{9,5},... | collective-permute-start | bytes 294920 | tf_op jit(solution)/shard_map/ppermute | solution.py:85

commit v9 on v8

--- a/solution.py
+++ b/solution.py
@@ -178,8 +178,8 @@
             pl.ds(pl.multiple_of(at + n * n_slots, CAP), shared), :
         ]
     row = count // wide * shared
-    out_ref[row:, :] = jnp.zeros((META, out_ref.shape[1]), BF16)
-    out_ref[row:, :128] = q_ref[count * n_slots :, :]
+    out_ref[row:, :] = jnp.zeros((out_ref.shape[0] - row, out_ref.shape[1]), BF16)
+    out_ref[row : row + META, :128] = q_ref[count * n_slots :, :]
 
 
 def second_kernel(me_ref, q_ref, passed_ref, *refs):
@@ -318,7 +318,7 @@
     far_charge = swapped(near_charge, 2)
 
     block = shape(2 * seen, l_rows)
-    shared_rows = width // l_rows * 2 * CAP + META
+    shared_rows = width // l_rows * 2 * CAP + META + 32
     first = [q8, q4, q0, near_charge, unit, unit_c]
     near8, near4, near0, passed = kernel_call(
         first_kernel,
@@ -339,11 +339,12 @@
             pltpu.VMEM((3, 128, 128), F32),
         ],
     )
+    near4 = swapped(near4, 4)
     raw_y, near8, near4, near12, far_charge = lax.optimization_barrier(
         (raw_y, near8, near4, near12, far_charge)
     )
     raw_d = swapped(raw_y, 1)
-    near12, near4 = swapped(near12, 12), swapped(near4, 4)
+    near12 = swapped(near12, 12)
     upper = ()
     for part, raw in enumerate((raw_y, raw_d)):
         upper = kernel_call(

time: 44.6 us -> 44.4 us (level)
  starting transfers between devices: 20.2 us -> 19.5 us
  waiting for transfers between devices: 15.7 us -> 16.2 us
    ppermute x15, starting transfers between devices: 20.2 us -> 19.5 us  [swapped(): return lax.ppermute(value, 'slab', [(i, i ^ mask) for i in range(count)])]
    ppermute x15, waiting for transfers between devices: 15.7 us -> 16.2 us  [swapped(): return lax.ppermute(value, 'slab', [(i, i ^ mask) for i in range(count)])]
  transfers between devices with their start and end apart: 15 -> 15, of which waited for: 6 -> 7; matrix products, arithmetic and copies ran while one was open for 0% -> 0% of each run, Pallas kernels for 10% -> 10%
where the time goes in v9:
time: 44.4 us; the launch traced here: 44.2 us
  starting transfers between devices  19.5 us (44%)
  waiting for transfers between devices  16.2 us (36%)
  Pallas kernels  5.65 us (13%)
  local copies, waits for them, and re-layouts  2.85 us (6%)
    ppermute x15, starting transfers between devices, swapped(): return lax.ppermute(value, 'slab', [(i, i ^ mask) for i in range(count)])  19.5 us
    ppermute x15, waiting for transfers between devices, swapped(): return lax.ppermute(value, 'slab', [(i, i ^ mask) for i in range(count)])  16.2 us
    pallas_call x9, Pallas kernels, kernel_call(): pl.pallas_call(body, out_shape=[jax.ShapeDtypeStruct(o.shape, o.dtype) fo...  5.65 us
    unnamed x10, local copies, waits for them, and re-layouts  2.85 us
  transfers between devices with their start and end apart: 15, of which 7 were waited for; matrix products, arithmetic and copies ran while one was open for 0% of the time, Pallas kernels for 10%

profile of v9, /device:TPU:0, one launch (start us, length us, event | category | flops | bytes accessed | tf_op | source)
XLA Modules:
  0.0 44.2 jit_solution(13388107710610311522)
XLA Ops:
  0.0 0.5 %collective-permute-start.4 = (bf16[512,1024]{1,0:T(8,128)(2,1)}, bf16[512,1024]{1,0:T(8,128)(2,1)S(1)}, u32[]{:S(2)}, u32[]{:S(2)}) collective-permute-start(bf16[512,1024]{1,0:T(8,128)(2,1)} %refs_0_.1), channel_id=1, source_target_pairs={{0,1},{1,0},{2,3},{3,2},{4,5},{5,4},{6,7},{7,6},{8,9},{9,8},{10,11... | collective-permute-start | bytes 3145736 | tf_op jit(solution)/shard_map/ppermute | solution.py:85
  0.5 2.5 %collective-permute-start = (bf16[512,1024]{1,0:T(8,128)(2,1)}, bf16[512,1024]{1,0:T(8,128)(2,1)S(1)}, u32[]{:S(2)}, u32[]{:S(2)}) collective-permute-start(bf16[512,1024]{1,0:T(8,128)(2,1)} %refs_0_.1), channel_id=1, source_target_pairs={{0,2},{1,3},{2,0},{3,1},{4,6},{5,7},{6,4},{7,5},{8,10},{9,11},{10,... | collective-permute-start | bytes 3145736 | tf_op jit(solution)/shard_map/ppermute | solution.py:85
  3.0 0.0 copy-start.2
  3.0 0.0 copy-start.3
  3.0 0.0 copy-start.4
  3.0 0.7 %copy-done.2 = s32[512]{0:T(512)S(1)} copy-done((s32[512]{0:T(512)S(1)}, s32[512]{0:T(512)}, u32[]{:S(2)}) %copy-start.2) | copy-done | bytes 2072
  3.7 0.0 copy-done.3
  3.7 0.0 copy-done.4
  3.7 0.1 shard_map.55
  3.8 0.0 copy-start.1
  3.8 0.9 %copy-done.1 = bf16[128,1024]{1,0:T(8,128)(2,1)S(1)} copy-done((bf16[128,1024]{1,0:T(8,128)(2,1)S(1)}, bf16[128,1024]{1,0:T(8,128)(2,1)}, u32[]{:S(2)}) %copy-start.1) | copy-done | bytes 262168
  4.7 0.5 %shard_map.56 = (bf16[784,128]{1,0:T(8,128)(2,1)S(1)}, bf16[784,128]{1,0:T(8,128)(2,1)S(1)}, bf16[784,128]{1,0:T(8,128)(2,1)S(1)}, bf16[528,128]{1,0:T(8,128)(2,1)S(1)}) custom-call(s32[1]{0:T(128)} %bitcast.me_ref, s32[1,128]{1,0:T(1,128)S(1)} %get-tuple-element.33.slot_ref, bf16[16,128]{1,0:T(8,128)(2,1)S(1)} %get-tuple-element.34.charge_ref, ...), custom_call_target="tpu_custom_call" | custom-call | bytes 1 | tf_op jit(solution)/shard_map/pallas_call | solution.py:277
  5.2 2.7 %collective-permute-start.1 = (bf16[784,128]{1,0:T(8,128)(2,1)S(1)}, bf16[784,128]{1,0:T(8,128)(2,1)S(1)}, u32[]{:S(2)}, u32[]{:S(2)}) collective-permute-start(bf16[784,128]{1,0:T(8,128)(2,1)S(1)} %get-tuple-element.35), channel_id=1, source_target_pairs={{0,8},{1,9},{2,10},{3,11},{4,12},{5,13},{6,14},{7,15},{8,0},{9,1},... | collective-permute-start | bytes 602120 | tf_op jit(solution)/shard_map/ppermute | solution.py:85
  7.9 1.6 %collective-permute-start.2 = (bf16[784,128]{1,0:T(8,128)(2,1)S(1)}, bf16[784,128]{1,0:T(8,128)(2,1)S(1)}, u32[]{:S(2)}, u32[]{:S(2)}) collective-permute-start(bf16[784,128]{1,0:T(8,128)(2,1)S(1)} %get-tuple-element.36), channel_id=1, source_target_pairs={{0,4},{1,5},{2,6},{3,7},{4,0},{5,1},{6,2},{7,3},{8,12},{9,13},{10,... | collective-permute-start | bytes 602120 | tf_op jit(solution)/shard_map/ppermute | solution.py:85
  9.5 0.0 collective-permute-start.3
  9.5 1.2 %collective-permute-done.3.other_ref = bf16[16,512]{1,0:T(8,128)(2,1)S(1)} collective-permute-done((bf16[16,512]{1,0:T(8,128)(2,1)S(1)}, bf16[16,512]{1,0:T(8,128)(2,1)S(1)}, u32[]{:S(2)}, u32[]{:S(2)}) %collective-permute-start.3) | collective-permute-done | bytes 16416 | tf_op jit(solution)/shard_map/ppermute | solution.py:85
  10.7 0.2 collective-permute-start.7
  10.9 0.0 collective-permute-done.4.refs_1_
  10.9 0.0 copy-start
  10.9 1.2 %copy-done = bf16[512,1024]{1,0:T(8,128)(2,1)S(1)} copy-done((bf16[512,1024]{1,0:T(8,128)(2,1)S(1)}, bf16[512,1024]{1,0:T(8,128)(2,1)}, u32[]{:S(2)}) %copy-start) | copy-done | bytes 1048600
  12.1 0.6 %shard_map.58 = (bf16[512,1024]{1,0:T(8,128)(2,1)S(1)}, bf16[512,1024]{1,0:T(8,128)(2,1)S(1)}) custom-call(bf16[512,1024]{1,0:T(8,128)(2,1)S(1)} %copy-done, bf16[512,1024]{1,0:T(8,128)(2,1)S(1)} %collective-permute-done.4.refs_1_), custom_call_target="tpu_custom_call" | custom-call | bytes 1 | tf_op jit(solution)/shard_map/pallas_call | solution.py:277
  12.8 6.0 %collective-permute-done.1.refs_0_ = bf16[784,128]{1,0:T(8,128)(2,1)S(1)} collective-permute-done((bf16[784,128]{1,0:T(8,128)(2,1)S(1)}, bf16[784,128]{1,0:T(8,128)(2,1)S(1)}, u32[]{:S(2)}, u32[]{:S(2)}) %collective-permute-start.1) | collective-permute-done | bytes 200736 | tf_op jit(solution)/shard_map/ppermute | solution.py:85
  18.8 0.0 collective-permute-done.2.refs_1_
  18.8 0.9 %shard_map.59 = (bf16[96,512]{1,0:T(8,128)(2,1)S(1)}, bf16[96,512]{1,0:T(8,128)(2,1)S(1)}, bf16[96,512]{1,0:T(8,128)(2,1)S(1)}, bf16[112,512]{1,0:T(8,128)(2,1)S(1)}) custom-call(s32[1]{0:T(128)} %bitcast.me_ref, bf16[784,128]{1,0:T(8,128)(2,1)S(1)} %collective-permute-done.1.refs_0_, bf16[784,128]{1,0:T(8,128)(2,1)S(1)} %collective-permute-done.2.refs_1_, ...), custom_call_target="tpu_custom_call" | custom-call | bytes 1 | tf_op jit(solution)/shard_map/pallas_call | solution.py:277
  19.7 1.4 %collective-permute-start.8 = (bf16[112,512]{1,0:T(8,128)(2,1)S(1)}, bf16[112,512]{1,0:T(8,128)(2,1)S(1)}, u32[]{:S(2)}, u32[]{:S(2)}) collective-permute-start(bf16[112,512]{1,0:T(8,128)(2,1)S(1)} %get-tuple-element.44), channel_id=1, source_target_pairs={{0,4},{1,5},{2,6},{3,7},{4,0},{5,1},{6,2},{7,3},{8,12},{9,13},{10,... | collective-permute-start | bytes 344072 | tf_op jit(solution)/shard_map/ppermute | solution.py:85
  21.0 2.4 %collective-permute-start.5 = (bf16[96,512]{1,0:T(8,128)(2,1)S(1)}, bf16[96,512]{1,0:T(8,128)(2,1)S(1)}, u32[]{:S(2)}, u32[]{:S(2)}) collective-permute-start(bf16[96,512]{1,0:T(8,128)(2,1)S(1)} %get-tuple-element.41), channel_id=1, source_target_pairs={{0,8},{1,9},{2,10},{3,11},{4,12},{5,13},{6,14},{7,15},{8,0},{9,1},... | collective-permute-start | bytes 294920 | tf_op jit(solution)/shard_map/ppermute | solution.py:85
  23.4 0.1 collective-permute-start.6
  23.5 0.0 collective-permute-done.7.q_ref
  23.5 0.5 %collective-permute-start.9 = (bf16[16,512]{1,0:T(8,128)(2,1)S(1)}, bf16[16,512]{1,0:T(8,128)(2,1)S(1)}, u32[]{:S(2)}, u32[]{:S(2)}) collective-permute-start(bf16[16,512]{1,0:T(8,128)(2,1)S(1)} %shard_map.57.refs_3_.refs_0_), channel_id=1, source_target_pairs={{0,2},{1,3},{2,0},{3,1},{4,6},{5,7},{6,4},{7,5},{8,10},{9,11},{10,... | collective-permute-start | bytes 49160 | tf_op jit(solution)/shard_map/ppermute | solution.py:85
  24.0 2.0 %collective-permute-done.8.passed_ref = bf16[112,512]{1,0:T(8,128)(2,1)S(1)} collective-permute-done((bf16[112,512]{1,0:T(8,128)(2,1)S(1)}, bf16[112,512]{1,0:T(8,128)(2,1)S(1)}, u32[]{:S(2)}, u32[]{:S(2)}) %collective-permute-start.8) | collective-permute-done | bytes 114720 | tf_op jit(solution)/shard_map/ppermute | solution.py:85
  26.1 0.9 %shard_map.60 = (bf16[96,512]{1,0:T(8,128)(2,1)S(1)}, bf16[784,128]{1,0:T(8,128)(2,1)S(1)}) custom-call(s32[1]{0:T(128)} %bitcast.me_ref, bf16[528,128]{1,0:T(8,128)(2,1)S(1)} %collective-permute-done.7.q_ref, bf16[112,512]{1,0:T(8,128)(2,1)S(1)} %collective-permute-done.8.passed_ref, bf16[16,512]{1,0:T(8,128)(2,1)S(1)} %shard_map.57.refs_3_.refs_0_, ...), custom_call_target="tpu_custom_call" | custom-call | bytes 1 | tf_op jit(solution)/shard_map/pallas_call | solution.py:277
  27.0 0.4 collective-permute-done.9.refs_4_
  27.4 0.0 collective-permute-done.refs_5_
  27.4 0.7 %collective-permute-done.5.refs_0_ = bf16[96,512]{1,0:T(8,128)(2,1)S(1)} collective-permute-done((bf16[96,512]{1,0:T(8,128)(2,1)S(1)}, bf16[96,512]{1,0:T(8,128)(2,1)S(1)}, u32[]{:S(2)}, u32[]{:S(2)}) %collective-permute-start.5) | collective-permute-done | bytes 98336 | tf_op jit(solution)/shard_map/ppermute | solution.py:85
  28.1 0.7 %collective-permute-done.6.refs_2_ = bf16[96,512]{1,0:T(8,128)(2,1)S(1)} collective-permute-done((bf16[96,512]{1,0:T(8,128)(2,1)S(1)}, bf16[96,512]{1,0:T(8,128)(2,1)S(1)}, u32[]{:S(2)}, u32[]{:S(2)}) %collective-permute-start.6) | collective-permute-done | bytes 98336 | tf_op jit(solution)/shard_map/ppermute | solution.py:85
  28.7 0.0 collective-permute-start.11
  28.7 3.2 %collective-permute-start.10 = (bf16[96,512]{1,0:T(8,128)(2,1)S(1)}, bf16[96,512]{1,0:T(8,128)(2,1)S(1)}, u32[]{:S(2)}, u32[]{:S(2)}) collective-permute-start(bf16[96,512]{1,0:T(8,128)(2,1)S(1)} %get-tuple-element.47), channel_id=1, source_target_pairs={{0,12},{1,13},{2,14},{3,15},{4,8},{5,9},{6,10},{7,11},{8,4},{9,5},... | collective-permute-start | bytes 294920 | tf_op jit(solution)/shard_map/ppermute | solution.py:85
  32.0 0.7 %shard_map.61 = (bf16[48,512]{1,0:T(8,128)(2,1)S(1)}, bf16[48,512]{1,0:T(8,128)(2,1)S(1)}, bf16[48,512]{1,0:T(8,128)(2,1)S(1)}, bf16[48,512]{1,0:T(8,128)(2,1)S(1)}) custom-call(s32[1]{0:T(128)} %bitcast.me_ref, bf16[784,128]{1,0:T(8,128)(2,1)S(1)} %collective-permute-done.1.refs_0_, bf16[784,128]{1,0:T(8,128)(2,1)S(1)} %collective-permute-done.2.refs_1_, ...), custom_call_target="tpu_custom_call" | custom-call | bytes 1 | tf_op jit(solution)/shard_map/pallas_call | solution.py:277
  32.7 0.0 collective-permute-done.11.refs_5_
  32.7 0.8 %shard_map.62 = (bf16[96,512]{1,0:T(8,128)(2,1)S(1)}, bf16[96,512]{1,0:T(8,128)(2,1)S(1)}, bf16[96,512]{1,0:T(8,128)(2,1)S(1)}, bf16[96,512]{1,0:T(8,128)(2,1)S(1)}) custom-call(s32[1]{0:T(128)} %bitcast.me_ref, bf16[784,128]{1,0:T(8,128)(2,1)S(1)} %collective-permute-done.1.refs_0_, bf16[784,128]{1,0:T(8,128)(2,1)S(1)} %collective-permute-done.2.refs_1_, ...), custom_call_target="tpu_custom_call" | custom-call | bytes 1 | tf_op jit(solution)/shard_map/pallas_call | solution.py:277
  33.5 0.8 %collective-permute-start.12 = (bf16[96,512]{1,0:T(8,128)(2,1)S(1)}, bf16[96,512]{1,0:T(8,128)(2,1)S(1)}, u32[]{:S(2)}, u32[]{:S(2)}) collective-permute-start(bf16[96,512]{1,0:T(8,128)(2,1)S(1)} %get-tuple-element.57), channel_id=1, source_target_pairs={{0,8},{1,9},{2,10},{3,11},{4,12},{5,13},{6,14},{7,15},{8,0},{9,1},... | collective-permute-start | bytes 294920 | tf_op jit(solution)/shard_map/ppermute | solution.py:85
  34.3 1.7 %collective-permute-start.13 = (bf16[96,512]{1,0:T(8,128)(2,1)S(1)}, bf16[96,512]{1,0:T(8,128)(2,1)S(1)}, u32[]{:S(2)}, u32[]{:S(2)}) collective-permute-start(bf16[96,512]{1,0:T(8,128)(2,1)S(1)} %get-tuple-element.58), channel_id=1, source_target_pairs={{0,4},{1,5},{2,6},{3,7},{4,0},{5,1},{6,2},{7,3},{8,12},{9,13},{10,... | collective-permute-start | bytes 294920 | tf_op jit(solution)/shard_map/ppermute | solution.py:85
  36.0 1.9 %collective-permute-start.14 = (bf16[96,512]{1,0:T(8,128)(2,1)S(1)}, bf16[96,512]{1,0:T(8,128)(2,1)S(1)}, u32[]{:S(2)}, u32[]{:S(2)}) collective-permute-start(bf16[96,512]{1,0:T(8,128)(2,1)S(1)} %get-tuple-element.59), channel_id=1, source_target_pairs={{0,12},{1,13},{2,14},{3,15},{4,8},{5,9},{6,10},{7,11},{8,4},{9,5},... | collective-permute-start | bytes 294920 | tf_op jit(solution)/shard_map/ppermute | solution.py:85
  38.0 0.0 collective-permute-done.10.refs_1_
  38.0 5.2 %collective-permute-done.12.refs_4_ = bf16[96,512]{1,0:T(8,128)(2,1)S(1)} collective-permute-done((bf16[96,512]{1,0:T(8,128)(2,1)S(1)}, bf16[96,512]{1,0:T(8,128)(2,1)S(1)}, u32[]{:S(2)}, u32[]{:S(2)}) %collective-permute-start.12) | collective-permute-done | bytes 98336 | tf_op jit(solution)/shard_map/ppermute | solution.py:85
  43.1 0.0 collective-permute-done.13.refs_5_
  43.1 0.0 collective-permute-done.14.refs_6_
  43.2 1.1 %shard_map.63 = bf16[128,1536]{1,0:T(8,128)(2,1)} custom-call(s32[1]{0:T(128)} %bitcast.me_ref, s32[1,128]{1,0:T(1,128)S(1)} %get-tuple-element.33.slot_ref, bf16[96,512]{1,0:T(8,128)(2,1)S(1)} %collective-permute-done.5.refs_0_, bf16[96,512]{1,0:T(8,128)(2,1)S(1)} %collective-permute-done.10.refs_1_, bf16[96,512]{1,0:T(8,128)(2,1)S(1)} %collective-permute-done.6.refs_2_, ...), custom_call_target="tpu_custom_call" | custom-call | bytes 1 | tf_op jit(solution)/shard_map/pallas_call | solution.py:277
  (1 shorter events, 0.0 us)
Async XLA Ops:
  0.0 10.9 %collective-permute-start.4 = (bf16[512,1024]{1,0:T(8,128)(2,1)}, bf16[512,1024]{1,0:T(8,128)(2,1)S(1)}, u32[]{:S(2)}, u32[]{:S(2)}) collective-permute-start(bf16[512,1024]{1,0:T(8,128)(2,1)} %refs_0_.1), channel_id=1, source_target_pairs={{0,1},{1,0},{2,3},{3,2},{4,5},{5,4},{6,7},{7,6},{8,9},{9,8},{10,11... | collective-permute-start | bytes 3145736 | tf_op jit(solution)/shard_map/ppermute | solution.py:85
  0.5 26.9 %collective-permute-start = (bf16[512,1024]{1,0:T(8,128)(2,1)}, bf16[512,1024]{1,0:T(8,128)(2,1)S(1)}, u32[]{:S(2)}, u32[]{:S(2)}) collective-permute-start(bf16[512,1024]{1,0:T(8,128)(2,1)} %refs_0_.1), channel_id=1, source_target_pairs={{0,2},{1,3},{2,0},{3,1},{4,6},{5,7},{6,4},{7,5},{8,10},{9,11},{10,... | collective-permute-start | bytes 3145736 | tf_op jit(solution)/shard_map/ppermute | solution.py:85
  3.0 0.7 %copy-start.2 = (s32[512]{0:T(512)S(1)}, s32[512]{0:T(512)}, u32[]{:S(2)}) copy-start(s32[512]{0:T(512)} %param.9) | copy-start | bytes 6148
  3.0 0.7 %copy-start.3 = (s32[128,1]{0,1:T(1,128)S(1)}, s32[128,1]{0,1:T(1,128)}, u32[]{:S(2)}) copy-start(s32[128,1]{0,1:T(1,128)} %param.7) | copy-start | bytes 1540
  3.0 0.7 %copy-start.4 = (s32[128]{0:T(128)S(1)}, s32[128]{0:T(128)}, u32[]{:S(2)}) copy-start(s32[128]{0:T(128)} %param.8) | copy-start | bytes 1540
  3.8 1.0 %copy-start.1 = (bf16[128,1024]{1,0:T(8,128)(2,1)S(1)}, bf16[128,1024]{1,0:T(8,128)(2,1)}, u32[]{:S(2)}) copy-start(bf16[128,1024]{1,0:T(8,128)(2,1)} %q_ref.1) | copy-start | bytes 786436
  5.2 13.5 %collective-permute-start.1 = (bf16[784,128]{1,0:T(8,128)(2,1)S(1)}, bf16[784,128]{1,0:T(8,128)(2,1)S(1)}, u32[]{:S(2)}, u32[]{:S(2)}) collective-permute-start(bf16[784,128]{1,0:T(8,128)(2,1)S(1)} %get-tuple-element.35), channel_id=1, source_target_pairs={{0,8},{1,9},{2,10},{3,11},{4,12},{5,13},{6,14},{7,15},{8,0},{9,1},... | collective-permute-start | bytes 602120 | tf_op jit(solution)/shard_map/ppermute | solution.py:85
  7.9 10.9 %collective-permute-start.2 = (bf16[784,128]{1,0:T(8,128)(2,1)S(1)}, bf16[784,128]{1,0:T(8,128)(2,1)S(1)}, u32[]{:S(2)}, u32[]{:S(2)}) collective-permute-start(bf16[784,128]{1,0:T(8,128)(2,1)S(1)} %get-tuple-element.36), channel_id=1, source_target_pairs={{0,4},{1,5},{2,6},{3,7},{4,0},{5,1},{6,2},{7,3},{8,12},{9,13},{10,... | collective-permute-start | bytes 602120 | tf_op jit(solution)/shard_map/ppermute | solution.py:85
  9.5 1.2 %collective-permute-start.3 = (bf16[16,512]{1,0:T(8,128)(2,1)S(1)}, bf16[16,512]{1,0:T(8,128)(2,1)S(1)}, u32[]{:S(2)}, u32[]{:S(2)}) collective-permute-start(bf16[16,512]{1,0:T(8,128)(2,1)S(1)} %get-tuple-element.38.one_ref), channel_id=1, source_target_pairs={{0,1},{1,0},{2,3},{3,2},{4,5},{5,4},{6,7},{7,6},{8,9},{9,8},{10,11... | collective-permute-start | bytes 49160 | tf_op jit(solution)/shard_map/ppermute | solution.py:85
  10.7 12.9 %collective-permute-start.7 = (bf16[528,128]{1,0:T(8,128)(2,1)S(1)}, bf16[528,128]{1,0:T(8,128)(2,1)S(1)}, u32[]{:S(2)}, u32[]{:S(2)}) collective-permute-start(bf16[528,128]{1,0:T(8,128)(2,1)S(1)} %get-tuple-element.43), channel_id=1, source_target_pairs={{0,12},{1,13},{2,14},{3,15},{4,8},{5,9},{6,10},{7,11},{8,4},{9,5},... | collective-permute-start | bytes 405512 | tf_op jit(solution)/shard_map/ppermute | solution.py:85
  10.9 1.2 %copy-start = (bf16[512,1024]{1,0:T(8,128)(2,1)S(1)}, bf16[512,1024]{1,0:T(8,128)(2,1)}, u32[]{:S(2)}) copy-start(bf16[512,1024]{1,0:T(8,128)(2,1)} %refs_0_.1) | copy-start | bytes 3145732
  19.7 6.4 %collective-permute-start.8 = (bf16[112,512]{1,0:T(8,128)(2,1)S(1)}, bf16[112,512]{1,0:T(8,128)(2,1)S(1)}, u32[]{:S(2)}, u32[]{:S(2)}) collective-permute-start(bf16[112,512]{1,0:T(8,128)(2,1)S(1)} %get-tuple-element.44), channel_id=1, source_target_pairs={{0,4},{1,5},{2,6},{3,7},{4,0},{5,1},{6,2},{7,3},{8,12},{9,13},{10,... | collective-permute-start | bytes 344072 | tf_op jit(solution)/shard_map/ppermute | solution.py:85
  21.0 7.0 %collective-permute-start.5 = (bf16[96,512]{1,0:T(8,128)(2,1)S(1)}, bf16[96,512]{1,0:T(8,128)(2,1)S(1)}, u32[]{:S(2)}, u32[]{:S(2)}) collective-permute-start(bf16[96,512]{1,0:T(8,128)(2,1)S(1)} %get-tuple-element.41), channel_id=1, source_target_pairs={{0,8},{1,9},{2,10},{3,11},{4,12},{5,13},{6,14},{7,15},{8,0},{9,1},... | collective-permute-start | bytes 294920 | tf_op jit(solution)/shard_map/ppermute | solution.py:85
  23.4 5.3 %collective-permute-start.6 = (bf16[96,512]{1,0:T(8,128)(2,1)S(1)}, bf16[96,512]{1,0:T(8,128)(2,1)S(1)}, u32[]{:S(2)}, u32[]{:S(2)}) collective-permute-start(bf16[96,512]{1,0:T(8,128)(2,1)S(1)} %get-tuple-element.42), channel_id=1, source_target_pairs={{0,4},{1,5},{2,6},{3,7},{4,0},{5,1},{6,2},{7,3},{8,12},{9,13},{10,... | collective-permute-start | bytes 294920 | tf_op jit(solution)/shard_map/ppermute | solution.py:85
  23.5 3.9 %collective-permute-start.9 = (bf16[16,512]{1,0:T(8,128)(2,1)S(1)}, bf16[16,512]{1,0:T(8,128)(2,1)S(1)}, u32[]{:S(2)}, u32[]{:S(2)}) collective-permute-start(bf16[16,512]{1,0:T(8,128)(2,1)S(1)} %shard_map.57.refs_3_.refs_0_), channel_id=1, source_target_pairs={{0,2},{1,3},{2,0},{3,1},{4,6},{5,7},{6,4},{7,5},{8,10},{9,11},{10,... | collective-permute-start | bytes 49160 | tf_op jit(solution)/shard_map/ppermute | solution.py:85
  28.7 4.0 %collective-permute-start.11 = (bf16[512,1024]{1,0:T(8,128)(2,1)S(1)}, bf16[512,1024]{1,0:T(8,128)(2,1)S(1)}, u32[]{:S(2)}, u32[]{:S(2)}) collective-permute-start(bf16[512,1024]{1,0:T(8,128)(2,1)S(1)} %collective-permute-done.refs_5_), channel_id=1, source_target_pairs={{0,1},{1,0},{2,3},{3,2},{4,5},{5,4},{6,7},{7,6},{8,9},{9,8},{10,11... | collective-permute-start | bytes 3145736 | tf_op jit(solution)/shard_map/ppermute | solution.py:85
  28.7 9.2 %collective-permute-start.10 = (bf16[96,512]{1,0:T(8,128)(2,1)S(1)}, bf16[96,512]{1,0:T(8,128)(2,1)S(1)}, u32[]{:S(2)}, u32[]{:S(2)}) collective-permute-start(bf16[96,512]{1,0:T(8,128)(2,1)S(1)} %get-tuple-element.47), channel_id=1, source_target_pairs={{0,12},{1,13},{2,14},{3,15},{4,8},{5,9},{6,10},{7,11},{8,4},{9,5},... | collective-permute-start | bytes 294920 | tf_op jit(solution)/shard_map/ppermute | solution.py:85
  33.5 9.6 %collective-permute-start.12 = (bf16[96,512]{1,0:T(8,128)(2,1)S(1)}, bf16[96,512]{1,0:T(8,128)(2,1)S(1)}, u32[]{:S(2)}, u32[]{:S(2)}) collective-permute-start(bf16[96,512]{1,0:T(8,128)(2,1)S(1)} %get-tuple-element.57), channel_id=1, source_target_pairs={{0,8},{1,9},{2,10},{3,11},{4,12},{5,13},{6,14},{7,15},{8,0},{9,1},... | collective-permute-start | bytes 294920 | tf_op jit(solution)/shard_map/ppermute | solution.py:85
  34.3 8.9 %collective-permute-start.13 = (bf16[96,512]{1,0:T(8,128)(2,1)S(1)}, bf16[96,512]{1,0:T(8,128)(2,1)S(1)}, u32[]{:S(2)}, u32[]{:S(2)}) collective-permute-start(bf16[96,512]{1,0:T(8,128)(2,1)S(1)} %get-tuple-element.58), channel_id=1, source_target_pairs={{0,4},{1,5},{2,6},{3,7},{4,0},{5,1},{6,2},{7,3},{8,12},{9,13},{10,... | collective-permute-start | bytes 294920 | tf_op jit(solution)/shard_map/ppermute | solution.py:85
  36.0 7.1 %collective-permute-start.14 = (bf16[96,512]{1,0:T(8,128)(2,1)S(1)}, bf16[96,512]{1,0:T(8,128)(2,1)S(1)}, u32[]{:S(2)}, u32[]{:S(2)}) collective-permute-start(bf16[96,512]{1,0:T(8,128)(2,1)S(1)} %get-tuple-element.59), channel_id=1, source_target_pairs={{0,12},{1,13},{2,14},{3,15},{4,8},{5,9},{6,10},{7,11},{8,4},{9,5},... | collective-permute-start | bytes 294920 | tf_op jit(solution)/shard_map/ppermute | solution.py:85

commit v10 on v9

--- a/solution.py
+++ b/solution.py
@@ -242,28 +242,36 @@
         out_refs[k][part * seen : (part + 1) * seen, :] = scores
 
 
-def home_kernel(me_ref, slot_ref, *refs):
-    near8, near12, near4, near0, far8, far4, far12, far0, out_ref, flat_ref = refs
-    near = [near0, near4, near8, near12]
-    far = [far0, far4, far8, far12]
-    q_rows = slot_ref.shape[1]
-    l_rows = near0.shape[1]
-    n_slab = 4 * PLANE
-    total = n_slab * CAP
+def select_kernel(me_ref, slot_ref, out_ref):
+    q_rows, n_slab, total = slot_ref.shape[1], 4 * PLANE, 4 * PLANE * CAP
     slot = slot_ref[...]
     bucket, rank = slot // CAP, slot % CAP
     places = lax.broadcasted_iota(jnp.int32, (total, q_rows), 0)
     for unit in range(3):
-        for m in range(n_slab):
+        slab = (bucket + (unit - 1 + n_slab)) % n_slab
+        want = (slab ^ me_ref[0]) * CAP + rank
+        out_ref[unit] = jnp.where(places == want, 1.0, 0.0).T.astype(BF16)
+
+
+def home_kernel(select_ref, *refs):
+    near8, near12, near4, near0, far8, far4, far12, far0, out_hbm, flat_ref, out_ref, sem = refs
+    near = [near0, near4, near8, near12]
+    far = [far0, far4, far8, far12]
+    l_rows = near0.shape[1]
+    copies = []
+    for unit in range(3):
+        for m in range(4 * PLANE):
             ref = (far if m & 2 else near)[m // PLANE]
             at = (m & 1) * 3 * CAP + (2 - unit) * CAP
-            flat_ref[m * CAP : (m + 1) * CAP, :] = ref[at : at + CAP, :]
-        slab = (bucket + (unit - 1 + n_slab)) % n_slab
-        want = (slab ^ me_ref[0]) * CAP + rank
-        select = jnp.where(places == want, 1.0, 0.0).T.astype(BF16)
-        out_ref[:, unit * l_rows : (unit + 1) * l_rows] = jnp.dot(
-            select, flat_ref[...], preferred_element_type=F32
+            flat_ref[unit, m * CAP : (m + 1) * CAP, :] = ref[at : at + CAP, :]
+        out_ref[unit] = jnp.dot(
+            select_ref[unit], flat_ref[unit], preferred_element_type=F32
         ).astype(BF16)
+        columns = pl.ds(unit * l_rows, l_rows)
+        copies.append(pltpu.make_async_copy(out_ref.at[unit], out_hbm.at[:, columns], sem.at[unit]))
+        copies[unit].start()
+    for copy in copies:
+        copy.wait()
 
 
 VMEM = pl.BlockSpec(memory_space=pltpu.VMEM)
@@ -273,15 +281,15 @@
 MIB = 1024 * 1024
 
 
-def kernel_call(body, outs, args, specs, scratch=(), cost=1):
+def kernel_call(body, outs, args, specs, scratch=(), out_spec=VMEM):
     return pl.pallas_call(
         body,
         out_shape=[jax.ShapeDtypeStruct(o.shape, o.dtype) for o in outs],
         in_specs=specs,
-        out_specs=[VMEM] * len(outs),
+        out_specs=[out_spec] * len(outs),
         scratch_shapes=scratch,
         compiler_params=pltpu.CompilerParams(vmem_limit_bytes=12 * MIB),
-        cost_estimate=pl.CostEstimate(flops=0, bytes_accessed=cost, transcendentals=0),
+        cost_estimate=pl.CostEstimate(flops=0, bytes_accessed=1, transcendentals=0),
     )(*args)
 
 
@@ -301,7 +309,6 @@
         [shape(1, q_rows, dtype=int32), shape(META, q_rows), shape(META, l_rows)],
         [x.reshape(1, -1) for x in (bucket, query_charge, library_charge)],
         [VMEM] * 3,
-        cost=1,
     )
     slots_shape = shape(width // 128 * n_slots + META, 128)
     q0, q4, q8, q12 = kernel_call(
@@ -340,8 +347,11 @@
         ],
     )
     near4 = swapped(near4, 4)
-    raw_y, near8, near4, near12, far_charge = lax.optimization_barrier(
-        (raw_y, near8, near4, near12, far_charge)
+    (select,) = kernel_call(
+        select_kernel, [shape(3, q_rows, 4 * PLANE * CAP)], [me, slot], [SMEM, VMEM]
+    )
+    raw_y, near8, near4, near12, far_charge, select = lax.optimization_barrier(
+        (raw_y, near8, near4, near12, far_charge, select)
     )
     raw_d = swapped(raw_y, 1)
     near12 = swapped(near12, 12)
@@ -363,9 +373,14 @@
     (out,) = kernel_call(
         home_kernel,
         [shape(q_rows, 3 * l_rows)],
-        [me, slot, near8, near12, near4, near0, far8, far4, far12, far0],
-        [SMEM] + [VMEM] * 9,
-        [pltpu.VMEM((4 * PLANE * CAP, l_rows), BF16)],
+        [select, near8, near12, near4, near0, far8, far4, far12, far0],
+        [VMEM] * 9,
+        [
+            pltpu.VMEM((3, 4 * PLANE * CAP, l_rows), BF16),
+            pltpu.VMEM((3, q_rows, l_rows), BF16),
+            pltpu.SemaphoreType.DMA((3,)),
+        ],
+        out_spec=pl.BlockSpec(memory_space=pl.ANY),
     )
     return out
 

time: 44.4 us -> 44.3 us (level)
    pallas_call x9 -> x10, Pallas kernels: 5.65 us -> 5.68 us  [kernel_call(): pl.pallas_call(body, out_shape=[jax.ShapeDtypeStruct(o.shape, o.dtype) fo...]
  transfers between devices with their start and end apart: 15 -> 15, of which waited for: 7 -> 7; matrix products, arithmetic and copies ran while one was open for 0% -> 0% of each run, Pallas kernels for 10% -> 11%
where the time goes in v10:
time: 44.3 us; the launch traced here: 44.1 us
  starting transfers between devices  19.5 us (44%)
  waiting for transfers between devices  16 us (36%)
  Pallas kernels  5.68 us (13%)
  local copies, waits for them, and re-layouts  2.85 us (6%)
    ppermute x15, starting transfers between devices, swapped(): return lax.ppermute(value, 'slab', [(i, i ^ mask) for i in range(count)])  19.5 us
    ppermute x15, waiting for transfers between devices, swapped(): return lax.ppermute(value, 'slab', [(i, i ^ mask) for i in range(count)])  16 us
    pallas_call x10, Pallas kernels, kernel_call(): pl.pallas_call(body, out_shape=[jax.ShapeDtypeStruct(o.shape, o.dtype) fo...  5.68 us
    unnamed x10, local copies, waits for them, and re-layouts  2.85 us
  transfers between devices with their start and end apart: 15, of which 7 were waited for; matrix products, arithmetic and copies ran while one was open for 0% of the time, Pallas kernels for 11%

profile of v10, /device:TPU:0, one launch (start us, length us, event | category | flops | bytes accessed | tf_op | source)
XLA Modules:
  0.0 44.1 jit_solution(8348560498691924379)
XLA Ops:
  0.0 0.5 %collective-permute-start.4 = (bf16[512,1024]{1,0:T(8,128)(2,1)}, bf16[512,1024]{1,0:T(8,128)(2,1)S(1)}, u32[]{:S(2)}, u32[]{:S(2)}) collective-permute-start(bf16[512,1024]{1,0:T(8,128)(2,1)} %refs_0_.1), channel_id=1, source_target_pairs={{0,1},{1,0},{2,3},{3,2},{4,5},{5,4},{6,7},{7,6},{8,9},{9,8},{10,11... | collective-permute-start | bytes 3145736 | tf_op jit(solution)/shard_map/ppermute | solution.py:85
  0.5 2.5 %collective-permute-start = (bf16[512,1024]{1,0:T(8,128)(2,1)}, bf16[512,1024]{1,0:T(8,128)(2,1)S(1)}, u32[]{:S(2)}, u32[]{:S(2)}) collective-permute-start(bf16[512,1024]{1,0:T(8,128)(2,1)} %refs_0_.1), channel_id=1, source_target_pairs={{0,2},{1,3},{2,0},{3,1},{4,6},{5,7},{6,4},{7,5},{8,10},{9,11},{10,... | collective-permute-start | bytes 3145736 | tf_op jit(solution)/shard_map/ppermute | solution.py:85
  3.0 0.0 copy-start.2
  3.0 0.0 copy-start.3
  3.0 0.7 %copy-done.2 = s32[512]{0:T(512)S(1)} copy-done((s32[512]{0:T(512)S(1)}, s32[512]{0:T(512)}, u32[]{:S(2)}) %copy-start.2) | copy-done | bytes 2072
  3.7 0.0 copy-done.3
  3.7 0.0 copy-done.4
  3.7 0.1 shard_map.55
  3.8 0.0 copy-start.1
  3.8 0.9 %copy-done.1 = bf16[128,1024]{1,0:T(8,128)(2,1)S(1)} copy-done((bf16[128,1024]{1,0:T(8,128)(2,1)S(1)}, bf16[128,1024]{1,0:T(8,128)(2,1)}, u32[]{:S(2)}) %copy-start.1) | copy-done | bytes 262168
  4.7 0.5 %shard_map.56 = (bf16[784,128]{1,0:T(8,128)(2,1)S(1)}, bf16[784,128]{1,0:T(8,128)(2,1)S(1)}, bf16[784,128]{1,0:T(8,128)(2,1)S(1)}, bf16[528,128]{1,0:T(8,128)(2,1)S(1)}) custom-call(s32[1]{0:T(128)} %bitcast.me_ref, s32[1,128]{1,0:T(1,128)S(1)} %get-tuple-element.34.slot_ref, bf16[16,128]{1,0:T(8,128)(2,1)S(1)} %get-tuple-element.35.charge_ref, ...), custom_call_target="tpu_custom_call" | custom-call | bytes 1 | tf_op jit(solution)/shard_map/pallas_call | solution.py:285
  5.2 2.7 %collective-permute-start.1 = (bf16[784,128]{1,0:T(8,128)(2,1)S(1)}, bf16[784,128]{1,0:T(8,128)(2,1)S(1)}, u32[]{:S(2)}, u32[]{:S(2)}) collective-permute-start(bf16[784,128]{1,0:T(8,128)(2,1)S(1)} %get-tuple-element.36), channel_id=1, source_target_pairs={{0,8},{1,9},{2,10},{3,11},{4,12},{5,13},{6,14},{7,15},{8,0},{9,1},... | collective-permute-start | bytes 602120 | tf_op jit(solution)/shard_map/ppermute | solution.py:85
  7.9 1.6 %collective-permute-start.2 = (bf16[784,128]{1,0:T(8,128)(2,1)S(1)}, bf16[784,128]{1,0:T(8,128)(2,1)S(1)}, u32[]{:S(2)}, u32[]{:S(2)}) collective-permute-start(bf16[784,128]{1,0:T(8,128)(2,1)S(1)} %get-tuple-element.37), channel_id=1, source_target_pairs={{0,4},{1,5},{2,6},{3,7},{4,0},{5,1},{6,2},{7,3},{8,12},{9,13},{10,... | collective-permute-start | bytes 602120 | tf_op jit(solution)/shard_map/ppermute | solution.py:85
  9.5 0.0 collective-permute-start.3
  9.5 1.2 %collective-permute-done.3.other_ref = bf16[16,512]{1,0:T(8,128)(2,1)S(1)} collective-permute-done((bf16[16,512]{1,0:T(8,128)(2,1)S(1)}, bf16[16,512]{1,0:T(8,128)(2,1)S(1)}, u32[]{:S(2)}, u32[]{:S(2)}) %collective-permute-start.3) | collective-permute-done | bytes 16416 | tf_op jit(solution)/shard_map/ppermute | solution.py:85
  10.7 0.2 collective-permute-start.7
  10.9 0.0 collective-permute-done.4.refs_1_
  10.9 0.0 copy-start
  10.9 1.2 %copy-done = bf16[512,1024]{1,0:T(8,128)(2,1)S(1)} copy-done((bf16[512,1024]{1,0:T(8,128)(2,1)S(1)}, bf16[512,1024]{1,0:T(8,128)(2,1)}, u32[]{:S(2)}) %copy-start) | copy-done | bytes 1048600
  12.1 0.6 %shard_map.58 = (bf16[512,1024]{1,0:T(8,128)(2,1)S(1)}, bf16[512,1024]{1,0:T(8,128)(2,1)S(1)}) custom-call(bf16[512,1024]{1,0:T(8,128)(2,1)S(1)} %copy-done, bf16[512,1024]{1,0:T(8,128)(2,1)S(1)} %collective-permute-done.4.refs_1_), custom_call_target="tpu_custom_call" | custom-call | bytes 1 | tf_op jit(solution)/shard_map/pallas_call | solution.py:285
  12.8 6.0 %collective-permute-done.1.refs_0_ = bf16[784,128]{1,0:T(8,128)(2,1)S(1)} collective-permute-done((bf16[784,128]{1,0:T(8,128)(2,1)S(1)}, bf16[784,128]{1,0:T(8,128)(2,1)S(1)}, u32[]{:S(2)}, u32[]{:S(2)}) %collective-permute-start.1) | collective-permute-done | bytes 200736 | tf_op jit(solution)/shard_map/ppermute | solution.py:85
  18.8 0.0 collective-permute-done.2.refs_1_
  18.8 0.9 %shard_map.59 = (bf16[96,512]{1,0:T(8,128)(2,1)S(1)}, bf16[96,512]{1,0:T(8,128)(2,1)S(1)}, bf16[96,512]{1,0:T(8,128)(2,1)S(1)}, bf16[112,512]{1,0:T(8,128)(2,1)S(1)}) custom-call(s32[1]{0:T(128)} %bitcast.me_ref, bf16[784,128]{1,0:T(8,128)(2,1)S(1)} %collective-permute-done.1.refs_0_, bf16[784,128]{1,0:T(8,128)(2,1)S(1)} %collective-permute-done.2.refs_1_, ...), custom_call_target="tpu_custom_call" | custom-call | bytes 1 | tf_op jit(solution)/shard_map/pallas_call | solution.py:285
  19.7 1.4 %collective-permute-start.8 = (bf16[112,512]{1,0:T(8,128)(2,1)S(1)}, bf16[112,512]{1,0:T(8,128)(2,1)S(1)}, u32[]{:S(2)}, u32[]{:S(2)}) collective-permute-start(bf16[112,512]{1,0:T(8,128)(2,1)S(1)} %get-tuple-element.45), channel_id=1, source_target_pairs={{0,4},{1,5},{2,6},{3,7},{4,0},{5,1},{6,2},{7,3},{8,12},{9,13},{10,... | collective-permute-start | bytes 344072 | tf_op jit(solution)/shard_map/ppermute | solution.py:85
  21.0 2.4 %collective-permute-start.5 = (bf16[96,512]{1,0:T(8,128)(2,1)S(1)}, bf16[96,512]{1,0:T(8,128)(2,1)S(1)}, u32[]{:S(2)}, u32[]{:S(2)}) collective-permute-start(bf16[96,512]{1,0:T(8,128)(2,1)S(1)} %get-tuple-element.42), channel_id=1, source_target_pairs={{0,8},{1,9},{2,10},{3,11},{4,12},{5,13},{6,14},{7,15},{8,0},{9,1},... | collective-permute-start | bytes 294920 | tf_op jit(solution)/shard_map/ppermute | solution.py:85
  23.4 0.1 collective-permute-start.6
  23.5 0.0 collective-permute-done.7.q_ref
  23.5 0.5 %collective-permute-start.9 = (bf16[16,512]{1,0:T(8,128)(2,1)S(1)}, bf16[16,512]{1,0:T(8,128)(2,1)S(1)}, u32[]{:S(2)}, u32[]{:S(2)}) collective-permute-start(bf16[16,512]{1,0:T(8,128)(2,1)S(1)} %shard_map.57.refs_3_.refs_0_), channel_id=1, source_target_pairs={{0,2},{1,3},{2,0},{3,1},{4,6},{5,7},{6,4},{7,5},{8,10},{9,11},{10,... | collective-permute-start | bytes 49160 | tf_op jit(solution)/shard_map/ppermute | solution.py:85
  24.0 0.2 shard_map.61.select_ref
  24.2 1.9 %collective-permute-done.8.passed_ref = bf16[112,512]{1,0:T(8,128)(2,1)S(1)} collective-permute-done((bf16[112,512]{1,0:T(8,128)(2,1)S(1)}, bf16[112,512]{1,0:T(8,128)(2,1)S(1)}, u32[]{:S(2)}, u32[]{:S(2)}) %collective-permute-start.8) | collective-permute-done | bytes 114720 | tf_op jit(solution)/shard_map/ppermute | solution.py:85
  26.1 0.9 %shard_map.60 = (bf16[96,512]{1,0:T(8,128)(2,1)S(1)}, bf16[784,128]{1,0:T(8,128)(2,1)S(1)}) custom-call(s32[1]{0:T(128)} %bitcast.me_ref, bf16[528,128]{1,0:T(8,128)(2,1)S(1)} %collective-permute-done.7.q_ref, bf16[112,512]{1,0:T(8,128)(2,1)S(1)} %collective-permute-done.8.passed_ref, bf16[16,512]{1,0:T(8,128)(2,1)S(1)} %shard_map.57.refs_3_.refs_0_, ...), custom_call_target="tpu_custom_call" | custom-call | bytes 1 | tf_op jit(solution)/shard_map/pallas_call | solution.py:285
  27.0 0.4 collective-permute-done.9.refs_4_
  27.4 0.0 collective-permute-done.refs_5_
  27.4 0.7 %collective-permute-done.5.refs_0_ = bf16[96,512]{1,0:T(8,128)(2,1)S(1)} collective-permute-done((bf16[96,512]{1,0:T(8,128)(2,1)S(1)}, bf16[96,512]{1,0:T(8,128)(2,1)S(1)}, u32[]{:S(2)}, u32[]{:S(2)}) %collective-permute-start.5) | collective-permute-done | bytes 98336 | tf_op jit(solution)/shard_map/ppermute | solution.py:85
  28.1 0.7 %collective-permute-done.6.refs_2_ = bf16[96,512]{1,0:T(8,128)(2,1)S(1)} collective-permute-done((bf16[96,512]{1,0:T(8,128)(2,1)S(1)}, bf16[96,512]{1,0:T(8,128)(2,1)S(1)}, u32[]{:S(2)}, u32[]{:S(2)}) %collective-permute-start.6) | collective-permute-done | bytes 98336 | tf_op jit(solution)/shard_map/ppermute | solution.py:85
  28.7 0.0 collective-permute-start.11
  28.7 3.2 %collective-permute-start.10 = (bf16[96,512]{1,0:T(8,128)(2,1)S(1)}, bf16[96,512]{1,0:T(8,128)(2,1)S(1)}, u32[]{:S(2)}, u32[]{:S(2)}) collective-permute-start(bf16[96,512]{1,0:T(8,128)(2,1)S(1)} %get-tuple-element.49), channel_id=1, source_target_pairs={{0,12},{1,13},{2,14},{3,15},{4,8},{5,9},{6,10},{7,11},{8,4},{9,5},... | collective-permute-start | bytes 294920 | tf_op jit(solution)/shard_map/ppermute | solution.py:85
  32.0 0.7 %shard_map.62 = (bf16[48,512]{1,0:T(8,128)(2,1)S(1)}, bf16[48,512]{1,0:T(8,128)(2,1)S(1)}, bf16[48,512]{1,0:T(8,128)(2,1)S(1)}, bf16[48,512]{1,0:T(8,128)(2,1)S(1)}) custom-call(s32[1]{0:T(128)} %bitcast.me_ref, bf16[784,128]{1,0:T(8,128)(2,1)S(1)} %collective-permute-done.1.refs_0_, bf16[784,128]{1,0:T(8,128)(2,1)S(1)} %collective-permute-done.2.refs_1_, ...), custom_call_target="tpu_custom_call" | custom-call | bytes 1 | tf_op jit(solution)/shard_map/pallas_call | solution.py:285
  32.7 0.0 collective-permute-done.11.refs_5_
  32.7 0.8 %shard_map.63 = (bf16[96,512]{1,0:T(8,128)(2,1)S(1)}, bf16[96,512]{1,0:T(8,128)(2,1)S(1)}, bf16[96,512]{1,0:T(8,128)(2,1)S(1)}, bf16[96,512]{1,0:T(8,128)(2,1)S(1)}) custom-call(s32[1]{0:T(128)} %bitcast.me_ref, bf16[784,128]{1,0:T(8,128)(2,1)S(1)} %collective-permute-done.1.refs_0_, bf16[784,128]{1,0:T(8,128)(2,1)S(1)} %collective-permute-done.2.refs_1_, ...), custom_call_target="tpu_custom_call" | custom-call | bytes 1 | tf_op jit(solution)/shard_map/pallas_call | solution.py:285
  33.5 0.8 %collective-permute-start.12 = (bf16[96,512]{1,0:T(8,128)(2,1)S(1)}, bf16[96,512]{1,0:T(8,128)(2,1)S(1)}, u32[]{:S(2)}, u32[]{:S(2)}) collective-permute-start(bf16[96,512]{1,0:T(8,128)(2,1)S(1)} %get-tuple-element.59), channel_id=1, source_target_pairs={{0,8},{1,9},{2,10},{3,11},{4,12},{5,13},{6,14},{7,15},{8,0},{9,1},... | collective-permute-start | bytes 294920 | tf_op jit(solution)/shard_map/ppermute | solution.py:85
  34.3 1.7 %collective-permute-start.13 = (bf16[96,512]{1,0:T(8,128)(2,1)S(1)}, bf16[96,512]{1,0:T(8,128)(2,1)S(1)}, u32[]{:S(2)}, u32[]{:S(2)}) collective-permute-start(bf16[96,512]{1,0:T(8,128)(2,1)S(1)} %get-tuple-element.60), channel_id=1, source_target_pairs={{0,4},{1,5},{2,6},{3,7},{4,0},{5,1},{6,2},{7,3},{8,12},{9,13},{10,... | collective-permute-start | bytes 294920 | tf_op jit(solution)/shard_map/ppermute | solution.py:85
  36.0 1.9 %collective-permute-start.14 = (bf16[96,512]{1,0:T(8,128)(2,1)S(1)}, bf16[96,512]{1,0:T(8,128)(2,1)S(1)}, u32[]{:S(2)}, u32[]{:S(2)}) collective-permute-start(bf16[96,512]{1,0:T(8,128)(2,1)S(1)} %get-tuple-element.61), channel_id=1, source_target_pairs={{0,12},{1,13},{2,14},{3,15},{4,8},{5,9},{6,10},{7,11},{8,4},{9,5},... | collective-permute-start | bytes 294920 | tf_op jit(solution)/shard_map/ppermute | solution.py:85
  38.0 0.0 collective-permute-done.10.refs_1_
  38.0 5.2 %collective-permute-done.12.refs_4_ = bf16[96,512]{1,0:T(8,128)(2,1)S(1)} collective-permute-done((bf16[96,512]{1,0:T(8,128)(2,1)S(1)}, bf16[96,512]{1,0:T(8,128)(2,1)S(1)}, u32[]{:S(2)}, u32[]{:S(2)}) %collective-permute-start.12) | collective-permute-done | bytes 98336 | tf_op jit(solution)/shard_map/ppermute | solution.py:85
  43.1 0.0 collective-permute-done.13.refs_5_
  43.1 0.0 collective-permute-done.14.refs_6_
  43.2 1.0 %shard_map.64 = bf16[128,1536]{1,0:T(8,128)(2,1)} custom-call(bf16[3,128,256]{2,1,0:T(8,128)(2,1)S(1)} %shard_map.61.select_ref, bf16[96,512]{1,0:T(8,128)(2,1)S(1)} %collective-permute-done.5.refs_0_, bf16[96,512]{1,0:T(8,128)(2,1)S(1)} %collective-permute-done.10.refs_1_, bf16[96,512]{1,0:T(8,128)(2,1)S(1)} %collective-permute-done.6.refs_2_, ...), custom_call_target="tpu_custom_call" | custom-call | bytes 1 | tf_op jit(solution)/shard_map/pallas_call | solution.py:285
  (2 shorter events, 0.0 us)
Async XLA Ops:
  0.0 10.9 %collective-permute-start.4 = (bf16[512,1024]{1,0:T(8,128)(2,1)}, bf16[512,1024]{1,0:T(8,128)(2,1)S(1)}, u32[]{:S(2)}, u32[]{:S(2)}) collective-permute-start(bf16[512,1024]{1,0:T(8,128)(2,1)} %refs_0_.1), channel_id=1, source_target_pairs={{0,1},{1,0},{2,3},{3,2},{4,5},{5,4},{6,7},{7,6},{8,9},{9,8},{10,11... | collective-permute-start | bytes 3145736 | tf_op jit(solution)/shard_map/ppermute | solution.py:85
  0.5 26.9 %collective-permute-start = (bf16[512,1024]{1,0:T(8,128)(2,1)}, bf16[512,1024]{1,0:T(8,128)(2,1)S(1)}, u32[]{:S(2)}, u32[]{:S(2)}) collective-permute-start(bf16[512,1024]{1,0:T(8,128)(2,1)} %refs_0_.1), channel_id=1, source_target_pairs={{0,2},{1,3},{2,0},{3,1},{4,6},{5,7},{6,4},{7,5},{8,10},{9,11},{10,... | collective-permute-start | bytes 3145736 | tf_op jit(solution)/shard_map/ppermute | solution.py:85
  3.0 0.7 %copy-start.2 = (s32[512]{0:T(512)S(1)}, s32[512]{0:T(512)}, u32[]{:S(2)}) copy-start(s32[512]{0:T(512)} %param.9) | copy-start | bytes 6148
  3.0 0.7 %copy-start.3 = (s32[128,1]{0,1:T(1,128)S(1)}, s32[128,1]{0,1:T(1,128)}, u32[]{:S(2)}) copy-start(s32[128,1]{0,1:T(1,128)} %param.7) | copy-start | bytes 1540
  3.0 0.7 %copy-start.4 = (s32[128]{0:T(128)S(1)}, s32[128]{0:T(128)}, u32[]{:S(2)}) copy-start(s32[128]{0:T(128)} %param.8) | copy-start | bytes 1540
  3.8 1.0 %copy-start.1 = (bf16[128,1024]{1,0:T(8,128)(2,1)S(1)}, bf16[128,1024]{1,0:T(8,128)(2,1)}, u32[]{:S(2)}) copy-start(bf16[128,1024]{1,0:T(8,128)(2,1)} %q_ref.1) | copy-start | bytes 786436
  5.2 13.5 %collective-permute-start.1 = (bf16[784,128]{1,0:T(8,128)(2,1)S(1)}, bf16[784,128]{1,0:T(8,128)(2,1)S(1)}, u32[]{:S(2)}, u32[]{:S(2)}) collective-permute-start(bf16[784,128]{1,0:T(8,128)(2,1)S(1)} %get-tuple-element.36), channel_id=1, source_target_pairs={{0,8},{1,9},{2,10},{3,11},{4,12},{5,13},{6,14},{7,15},{8,0},{9,1},... | collective-permute-start | bytes 602120 | tf_op jit(solution)/shard_map/ppermute | solution.py:85
  7.9 10.9 %collective-permute-start.2 = (bf16[784,128]{1,0:T(8,128)(2,1)S(1)}, bf16[784,128]{1,0:T(8,128)(2,1)S(1)}, u32[]{:S(2)}, u32[]{:S(2)}) collective-permute-start(bf16[784,128]{1,0:T(8,128)(2,1)S(1)} %get-tuple-element.37), channel_id=1, source_target_pairs={{0,4},{1,5},{2,6},{3,7},{4,0},{5,1},{6,2},{7,3},{8,12},{9,13},{10,... | collective-permute-start | bytes 602120 | tf_op jit(solution)/shard_map/ppermute | solution.py:85
  9.5 1.2 %collective-permute-start.3 = (bf16[16,512]{1,0:T(8,128)(2,1)S(1)}, bf16[16,512]{1,0:T(8,128)(2,1)S(1)}, u32[]{:S(2)}, u32[]{:S(2)}) collective-permute-start(bf16[16,512]{1,0:T(8,128)(2,1)S(1)} %get-tuple-element.39.one_ref), channel_id=1, source_target_pairs={{0,1},{1,0},{2,3},{3,2},{4,5},{5,4},{6,7},{7,6},{8,9},{9,8},{10,11... | collective-permute-start | bytes 49160 | tf_op jit(solution)/shard_map/ppermute | solution.py:85
  10.7 12.9 %collective-permute-start.7 = (bf16[528,128]{1,0:T(8,128)(2,1)S(1)}, bf16[528,128]{1,0:T(8,128)(2,1)S(1)}, u32[]{:S(2)}, u32[]{:S(2)}) collective-permute-start(bf16[528,128]{1,0:T(8,128)(2,1)S(1)} %get-tuple-element.44), channel_id=1, source_target_pairs={{0,12},{1,13},{2,14},{3,15},{4,8},{5,9},{6,10},{7,11},{8,4},{9,5},... | collective-permute-start | bytes 405512 | tf_op jit(solution)/shard_map/ppermute | solution.py:85
  10.9 1.2 %copy-start = (bf16[512,1024]{1,0:T(8,128)(2,1)S(1)}, bf16[512,1024]{1,0:T(8,128)(2,1)}, u32[]{:S(2)}) copy-start(bf16[512,1024]{1,0:T(8,128)(2,1)} %refs_0_.1) | copy-start | bytes 3145732
  19.7 6.4 %collective-permute-start.8 = (bf16[112,512]{1,0:T(8,128)(2,1)S(1)}, bf16[112,512]{1,0:T(8,128)(2,1)S(1)}, u32[]{:S(2)}, u32[]{:S(2)}) collective-permute-start(bf16[112,512]{1,0:T(8,128)(2,1)S(1)} %get-tuple-element.45), channel_id=1, source_target_pairs={{0,4},{1,5},{2,6},{3,7},{4,0},{5,1},{6,2},{7,3},{8,12},{9,13},{10,... | collective-permute-start | bytes 344072 | tf_op jit(solution)/shard_map/ppermute | solution.py:85
  21.0 7.0 %collective-permute-start.5 = (bf16[96,512]{1,0:T(8,128)(2,1)S(1)}, bf16[96,512]{1,0:T(8,128)(2,1)S(1)}, u32[]{:S(2)}, u32[]{:S(2)}) collective-permute-start(bf16[96,512]{1,0:T(8,128)(2,1)S(1)} %get-tuple-element.42), channel_id=1, source_target_pairs={{0,8},{1,9},{2,10},{3,11},{4,12},{5,13},{6,14},{7,15},{8,0},{9,1},... | collective-permute-start | bytes 294920 | tf_op jit(solution)/shard_map/ppermute | solution.py:85
  23.4 5.3 %collective-permute-start.6 = (bf16[96,512]{1,0:T(8,128)(2,1)S(1)}, bf16[96,512]{1,0:T(8,128)(2,1)S(1)}, u32[]{:S(2)}, u32[]{:S(2)}) collective-permute-start(bf16[96,512]{1,0:T(8,128)(2,1)S(1)} %get-tuple-element.43), channel_id=1, source_target_pairs={{0,4},{1,5},{2,6},{3,7},{4,0},{5,1},{6,2},{7,3},{8,12},{9,13},{10,... | collective-permute-start | bytes 294920 | tf_op jit(solution)/shard_map/ppermute | solution.py:85
  23.5 3.9 %collective-permute-start.9 = (bf16[16,512]{1,0:T(8,128)(2,1)S(1)}, bf16[16,512]{1,0:T(8,128)(2,1)S(1)}, u32[]{:S(2)}, u32[]{:S(2)}) collective-permute-start(bf16[16,512]{1,0:T(8,128)(2,1)S(1)} %shard_map.57.refs_3_.refs_0_), channel_id=1, source_target_pairs={{0,2},{1,3},{2,0},{3,1},{4,6},{5,7},{6,4},{7,5},{8,10},{9,11},{10,... | collective-permute-start | bytes 49160 | tf_op jit(solution)/shard_map/ppermute | solution.py:85
  28.7 4.0 %collective-permute-start.11 = (bf16[512,1024]{1,0:T(8,128)(2,1)S(1)}, bf16[512,1024]{1,0:T(8,128)(2,1)S(1)}, u32[]{:S(2)}, u32[]{:S(2)}) collective-permute-start(bf16[512,1024]{1,0:T(8,128)(2,1)S(1)} %collective-permute-done.refs_5_), channel_id=1, source_target_pairs={{0,1},{1,0},{2,3},{3,2},{4,5},{5,4},{6,7},{7,6},{8,9},{9,8},{10,11... | collective-permute-start | bytes 3145736 | tf_op jit(solution)/shard_map/ppermute | solution.py:85
  28.7 9.2 %collective-permute-start.10 = (bf16[96,512]{1,0:T(8,128)(2,1)S(1)}, bf16[96,512]{1,0:T(8,128)(2,1)S(1)}, u32[]{:S(2)}, u32[]{:S(2)}) collective-permute-start(bf16[96,512]{1,0:T(8,128)(2,1)S(1)} %get-tuple-element.49), channel_id=1, source_target_pairs={{0,12},{1,13},{2,14},{3,15},{4,8},{5,9},{6,10},{7,11},{8,4},{9,5},... | collective-permute-start | bytes 294920 | tf_op jit(solution)/shard_map/ppermute | solution.py:85
  33.5 9.6 %collective-permute-start.12 = (bf16[96,512]{1,0:T(8,128)(2,1)S(1)}, bf16[96,512]{1,0:T(8,128)(2,1)S(1)}, u32[]{:S(2)}, u32[]{:S(2)}) collective-permute-start(bf16[96,512]{1,0:T(8,128)(2,1)S(1)} %get-tuple-element.59), channel_id=1, source_target_pairs={{0,8},{1,9},{2,10},{3,11},{4,12},{5,13},{6,14},{7,15},{8,0},{9,1},... | collective-permute-start | bytes 294920 | tf_op jit(solution)/shard_map/ppermute | solution.py:85
  34.3 8.9 %collective-permute-start.13 = (bf16[96,512]{1,0:T(8,128)(2,1)S(1)}, bf16[96,512]{1,0:T(8,128)(2,1)S(1)}, u32[]{:S(2)}, u32[]{:S(2)}) collective-permute-start(bf16[96,512]{1,0:T(8,128)(2,1)S(1)} %get-tuple-element.60), channel_id=1, source_target_pairs={{0,4},{1,5},{2,6},{3,7},{4,0},{5,1},{6,2},{7,3},{8,12},{9,13},{10,... | collective-permute-start | bytes 294920 | tf_op jit(solution)/shard_map/ppermute | solution.py:85
  36.0 7.1 %collective-permute-start.14 = (bf16[96,512]{1,0:T(8,128)(2,1)S(1)}, bf16[96,512]{1,0:T(8,128)(2,1)S(1)}, u32[]{:S(2)}, u32[]{:S(2)}) collective-permute-start(bf16[96,512]{1,0:T(8,128)(2,1)S(1)} %get-tuple-element.61), channel_id=1, source_target_pairs={{0,12},{1,13},{2,14},{3,15},{4,8},{5,9},{6,10},{7,11},{8,4},{9,5},... | collective-permute-start | bytes 294920 | tf_op jit(solution)/shard_map/ppermute | solution.py:85

commit v11 on v10

--- a/solution.py
+++ b/solution.py
@@ -166,8 +166,8 @@
 
 
 def first_kernel(me_ref, *refs):
-    score_kernel(3, 0, me_ref, *refs[:9], *refs[10:])
-    q_ref, out_ref = refs[0], refs[9]
+    score_kernel(2, 0, me_ref, *refs[:7], *refs[8:])
+    q_ref, out_ref = refs[0], refs[7]
     n_slots, shared = (PLANE + 2) * CAP, 2 * CAP
     count = (q_ref.shape[0] - META) // n_slots
     at = (1 - me_ref[0] // PLANE % 2) * (n_slots - shared)
@@ -182,9 +182,9 @@
     out_ref[row : row + META, :128] = q_ref[count * n_slots :, :]
 
 
-def second_kernel(me_ref, q_ref, passed_ref, *refs):
-    charge_refs, lib_refs, out_ref, block_ref = refs[0], refs[1:3], refs[3], refs[4]
-    rows_ref, charge_ref, column_ref = refs[5:]
+def second_kernel(me_ref, q_ref, passed_ref, own_ref, *refs):
+    charge_refs, lib_refs, out_refs, block_ref = refs[0], refs[1:3], refs[3:5], refs[5]
+    rows_ref, charge_ref, column_ref = refs[6:]
     n_slots, shared = (PLANE + 2) * CAP, 2 * CAP
     part = n_slots - shared
     count = (q_ref.shape[0] - META) // part
@@ -210,7 +210,8 @@
         0, pl.ds(pl.multiple_of(odd * part, CAP), shared), :
     ]
     block_ref[count * n_slots :, :] = column_ref[2].T[:META, :].astype(BF16)
-    score_kernel(1, 0, me_ref, block_ref, charge_refs, *lib_refs, out_ref, rows_ref, charge_ref)
+    q_refs = (block_ref, own_ref)
+    score_kernel(2, 0, me_ref, *q_refs, charge_refs, *lib_refs, *out_refs, rows_ref, charge_ref)
 
 
 def far_kernel(part, me_ref, *refs):
@@ -326,23 +327,23 @@
 
     block = shape(2 * seen, l_rows)
     shared_rows = width // l_rows * 2 * CAP + META + 32
-    first = [q8, q4, q0, near_charge, unit, unit_c]
-    near8, near4, near0, passed = kernel_call(
+    first = [q8, q4, near_charge, unit, unit_c]
+    near8, near4, passed = kernel_call(
         first_kernel,
-        [block] * 3 + [shape(shared_rows, l_rows)],
+        [block] * 2 + [shape(shared_rows, l_rows)],
         [me, *first],
         [SMEM] + [VMEM] * len(first),
-        [pltpu.VMEM((3 * seen, width), BF16), pltpu.VMEM((3, 128, 128), F32)],
+        [pltpu.VMEM((2 * seen, width), BF16), pltpu.VMEM((2, 128, 128), F32)],
     )
     near8, passed = swapped(near8, 8), swapped(passed, 4)
-    near12, q12 = kernel_call(
+    near12, near0, q12 = kernel_call(
         second_kernel,
-        [block, slots_shape],
-        [me, q12, passed, near_charge, unit, unit_c],
-        [SMEM] + [VMEM] * 5,
+        [block, block, slots_shape],
+        [me, q12, passed, q0, near_charge, unit, unit_c],
+        [SMEM] + [VMEM] * 6,
         [
-            pltpu.VMEM((seen, width), BF16),
-            pltpu.VMEM((1, 128, 128), F32),
+            pltpu.VMEM((2 * seen, width), BF16),
+            pltpu.VMEM((2, 128, 128), F32),
             pltpu.VMEM((3, 128, 128), F32),
         ],
     )

time: 44.3 us -> 44.2 us (level)
  no operation moved by 1% of the time
where the time goes in v11:
time: 44.2 us; the launch traced here: 44 us
  starting transfers between devices  19.5 us (44%)
  waiting for transfers between devices  16 us (36%)
  Pallas kernels  5.63 us (13%)
  local copies, waits for them, and re-layouts  2.85 us (6%)
    ppermute x15, starting transfers between devices, swapped(): return lax.ppermute(value, 'slab', [(i, i ^ mask) for i in range(count)])  19.5 us
    ppermute x15, waiting for transfers between devices, swapped(): return lax.ppermute(value, 'slab', [(i, i ^ mask) for i in range(count)])  16 us
    pallas_call x10, Pallas kernels, kernel_call(): pl.pallas_call(body, out_shape=[jax.ShapeDtypeStruct(o.shape, o.dtype) fo...  5.63 us
    unnamed x10, local copies, waits for them, and re-layouts  2.85 us
  transfers between devices with their start and end apart: 15, of which 7 were waited for; matrix products, arithmetic and copies ran while one was open for 0% of the time, Pallas kernels for 11%

profile of v11, /device:TPU:0, one launch (start us, length us, event | category | flops | bytes accessed | tf_op | source)
XLA Modules:
  0.0 44.0 jit_solution(16507938447092177381)
XLA Ops:
  0.0 0.5 %collective-permute-start.4 = (bf16[512,1024]{1,0:T(8,128)(2,1)}, bf16[512,1024]{1,0:T(8,128)(2,1)S(1)}, u32[]{:S(2)}, u32[]{:S(2)}) collective-permute-start(bf16[512,1024]{1,0:T(8,128)(2,1)} %refs_0_.1), channel_id=1, source_target_pairs={{0,1},{1,0},{2,3},{3,2},{4,5},{5,4},{6,7},{7,6},{8,9},{9,8},{10,11... | collective-permute-start | bytes 3145736 | tf_op jit(solution)/shard_map/ppermute | solution.py:85
  0.5 2.5 %collective-permute-start = (bf16[512,1024]{1,0:T(8,128)(2,1)}, bf16[512,1024]{1,0:T(8,128)(2,1)S(1)}, u32[]{:S(2)}, u32[]{:S(2)}) collective-permute-start(bf16[512,1024]{1,0:T(8,128)(2,1)} %refs_0_.1), channel_id=1, source_target_pairs={{0,2},{1,3},{2,0},{3,1},{4,6},{5,7},{6,4},{7,5},{8,10},{9,11},{10,... | collective-permute-start | bytes 3145736 | tf_op jit(solution)/shard_map/ppermute | solution.py:85
  3.0 0.0 copy-start.2
  3.0 0.0 copy-start.3
  3.0 0.7 %copy-done.2 = s32[512]{0:T(512)S(1)} copy-done((s32[512]{0:T(512)S(1)}, s32[512]{0:T(512)}, u32[]{:S(2)}) %copy-start.2) | copy-done | bytes 2072
  3.7 0.0 copy-done.3
  3.7 0.0 copy-done.4
  3.7 0.1 shard_map.55
  3.8 0.0 copy-start.1
  3.8 0.9 %copy-done.1 = bf16[128,1024]{1,0:T(8,128)(2,1)S(1)} copy-done((bf16[128,1024]{1,0:T(8,128)(2,1)S(1)}, bf16[128,1024]{1,0:T(8,128)(2,1)}, u32[]{:S(2)}) %copy-start.1) | copy-done | bytes 262168
  4.7 0.5 %shard_map.56 = (bf16[784,128]{1,0:T(8,128)(2,1)S(1)}, bf16[784,128]{1,0:T(8,128)(2,1)S(1)}, bf16[784,128]{1,0:T(8,128)(2,1)S(1)}, bf16[528,128]{1,0:T(8,128)(2,1)S(1)}) custom-call(s32[1]{0:T(128)} %bitcast.me_ref, s32[1,128]{1,0:T(1,128)S(1)} %get-tuple-element.34.slot_ref, bf16[16,128]{1,0:T(8,128)(2,1)S(1)} %get-tuple-element.35.charge_ref, ...), custom_call_target="tpu_custom_call" | custom-call | bytes 1 | tf_op jit(solution)/shard_map/pallas_call | solution.py:286
  5.2 2.7 %collective-permute-start.1 = (bf16[784,128]{1,0:T(8,128)(2,1)S(1)}, bf16[784,128]{1,0:T(8,128)(2,1)S(1)}, u32[]{:S(2)}, u32[]{:S(2)}) collective-permute-start(bf16[784,128]{1,0:T(8,128)(2,1)S(1)} %get-tuple-element.36), channel_id=1, source_target_pairs={{0,8},{1,9},{2,10},{3,11},{4,12},{5,13},{6,14},{7,15},{8,0},{9,1},... | collective-permute-start | bytes 602120 | tf_op jit(solution)/shard_map/ppermute | solution.py:85
  7.9 1.6 %collective-permute-start.2 = (bf16[784,128]{1,0:T(8,128)(2,1)S(1)}, bf16[784,128]{1,0:T(8,128)(2,1)S(1)}, u32[]{:S(2)}, u32[]{:S(2)}) collective-permute-start(bf16[784,128]{1,0:T(8,128)(2,1)S(1)} %get-tuple-element.37), channel_id=1, source_target_pairs={{0,4},{1,5},{2,6},{3,7},{4,0},{5,1},{6,2},{7,3},{8,12},{9,13},{10,... | collective-permute-start | bytes 602120 | tf_op jit(solution)/shard_map/ppermute | solution.py:85
  9.5 0.0 collective-permute-start.3
  9.5 1.2 %collective-permute-done.3.other_ref = bf16[16,512]{1,0:T(8,128)(2,1)S(1)} collective-permute-done((bf16[16,512]{1,0:T(8,128)(2,1)S(1)}, bf16[16,512]{1,0:T(8,128)(2,1)S(1)}, u32[]{:S(2)}, u32[]{:S(2)}) %collective-permute-start.3) | collective-permute-done | bytes 16416 | tf_op jit(solution)/shard_map/ppermute | solution.py:85
  10.7 0.2 collective-permute-start.7
  10.9 0.0 collective-permute-done.4.refs_1_
  10.9 0.0 copy-start
  10.9 1.2 %copy-done = bf16[512,1024]{1,0:T(8,128)(2,1)S(1)} copy-done((bf16[512,1024]{1,0:T(8,128)(2,1)S(1)}, bf16[512,1024]{1,0:T(8,128)(2,1)}, u32[]{:S(2)}) %copy-start) | copy-done | bytes 1048600
  12.1 0.6 %shard_map.58 = (bf16[512,1024]{1,0:T(8,128)(2,1)S(1)}, bf16[512,1024]{1,0:T(8,128)(2,1)S(1)}) custom-call(bf16[512,1024]{1,0:T(8,128)(2,1)S(1)} %copy-done, bf16[512,1024]{1,0:T(8,128)(2,1)S(1)} %collective-permute-done.4.refs_1_), custom_call_target="tpu_custom_call" | custom-call | bytes 1 | tf_op jit(solution)/shard_map/pallas_call | solution.py:286
  12.8 6.0 %collective-permute-done.1.refs_0_ = bf16[784,128]{1,0:T(8,128)(2,1)S(1)} collective-permute-done((bf16[784,128]{1,0:T(8,128)(2,1)S(1)}, bf16[784,128]{1,0:T(8,128)(2,1)S(1)}, u32[]{:S(2)}, u32[]{:S(2)}) %collective-permute-start.1) | collective-permute-done | bytes 200736 | tf_op jit(solution)/shard_map/ppermute | solution.py:85
  18.8 0.0 collective-permute-done.2.refs_1_
  18.8 0.8 %shard_map.59 = (bf16[96,512]{1,0:T(8,128)(2,1)S(1)}, bf16[96,512]{1,0:T(8,128)(2,1)S(1)}, bf16[112,512]{1,0:T(8,128)(2,1)S(1)}) custom-call(s32[1]{0:T(128)} %bitcast.me_ref, bf16[784,128]{1,0:T(8,128)(2,1)S(1)} %collective-permute-done.1.refs_0_, bf16[784,128]{1,0:T(8,128)(2,1)S(1)} %collective-permute-done.2.refs_1_, ...), custom_call_target="tpu_custom_call" | custom-call | bytes 1 | tf_op jit(solution)/shard_map/pallas_call | solution.py:286
  19.6 1.4 %collective-permute-start.8 = (bf16[112,512]{1,0:T(8,128)(2,1)S(1)}, bf16[112,512]{1,0:T(8,128)(2,1)S(1)}, u32[]{:S(2)}, u32[]{:S(2)}) collective-permute-start(bf16[112,512]{1,0:T(8,128)(2,1)S(1)} %get-tuple-element.44), channel_id=1, source_target_pairs={{0,4},{1,5},{2,6},{3,7},{4,0},{5,1},{6,2},{7,3},{8,12},{9,13},{10,... | collective-permute-start | bytes 344072 | tf_op jit(solution)/shard_map/ppermute | solution.py:85
  20.9 2.4 %collective-permute-start.5 = (bf16[96,512]{1,0:T(8,128)(2,1)S(1)}, bf16[96,512]{1,0:T(8,128)(2,1)S(1)}, u32[]{:S(2)}, u32[]{:S(2)}) collective-permute-start(bf16[96,512]{1,0:T(8,128)(2,1)S(1)} %get-tuple-element.41), channel_id=1, source_target_pairs={{0,8},{1,9},{2,10},{3,11},{4,12},{5,13},{6,14},{7,15},{8,0},{9,1},... | collective-permute-start | bytes 294920 | tf_op jit(solution)/shard_map/ppermute | solution.py:85
  23.3 0.1 collective-permute-start.6
  23.4 0.0 collective-permute-done.7.q_ref
  23.4 0.5 %collective-permute-start.9 = (bf16[16,512]{1,0:T(8,128)(2,1)S(1)}, bf16[16,512]{1,0:T(8,128)(2,1)S(1)}, u32[]{:S(2)}, u32[]{:S(2)}) collective-permute-start(bf16[16,512]{1,0:T(8,128)(2,1)S(1)} %shard_map.57.refs_2_.refs_0_), channel_id=1, source_target_pairs={{0,2},{1,3},{2,0},{3,1},{4,6},{5,7},{6,4},{7,5},{8,10},{9,11},{10,... | collective-permute-start | bytes 49160 | tf_op jit(solution)/shard_map/ppermute | solution.py:85
  23.9 0.2 shard_map.61.select_ref
  24.1 1.9 %collective-permute-done.8.passed_ref = bf16[112,512]{1,0:T(8,128)(2,1)S(1)} collective-permute-done((bf16[112,512]{1,0:T(8,128)(2,1)S(1)}, bf16[112,512]{1,0:T(8,128)(2,1)S(1)}, u32[]{:S(2)}, u32[]{:S(2)}) %collective-permute-start.8) | collective-permute-done | bytes 114720 | tf_op jit(solution)/shard_map/ppermute | solution.py:85
  26.0 1.0 %shard_map.60 = (bf16[96,512]{1,0:T(8,128)(2,1)S(1)}, bf16[96,512]{1,0:T(8,128)(2,1)S(1)}, bf16[784,128]{1,0:T(8,128)(2,1)S(1)}) custom-call(s32[1]{0:T(128)} %bitcast.me_ref, bf16[528,128]{1,0:T(8,128)(2,1)S(1)} %collective-permute-done.7.q_ref, bf16[112,512]{1,0:T(8,128)(2,1)S(1)} %collective-permute-done.8.passed_ref, ...), custom_call_target="tpu_custom_call" | custom-call | bytes 1 | tf_op jit(solution)/shard_map/pallas_call | solution.py:286
  26.9 0.4 %collective-permute-done.9.refs_4_ = bf16[16,512]{1,0:T(8,128)(2,1)S(1)} collective-permute-done((bf16[16,512]{1,0:T(8,128)(2,1)S(1)}, bf16[16,512]{1,0:T(8,128)(2,1)S(1)}, u32[]{:S(2)}, u32[]{:S(2)}) %collective-permute-start.9) | collective-permute-done | bytes 16416 | tf_op jit(solution)/shard_map/ppermute | solution.py:85
  27.4 0.0 collective-permute-done.refs_5_
  27.4 0.6 %collective-permute-done.5.refs_0_ = bf16[96,512]{1,0:T(8,128)(2,1)S(1)} collective-permute-done((bf16[96,512]{1,0:T(8,128)(2,1)S(1)}, bf16[96,512]{1,0:T(8,128)(2,1)S(1)}, u32[]{:S(2)}, u32[]{:S(2)}) %collective-permute-start.5) | collective-permute-done | bytes 98336 | tf_op jit(solution)/shard_map/ppermute | solution.py:85
  28.0 0.7 %collective-permute-done.6.refs_2_ = bf16[96,512]{1,0:T(8,128)(2,1)S(1)} collective-permute-done((bf16[96,512]{1,0:T(8,128)(2,1)S(1)}, bf16[96,512]{1,0:T(8,128)(2,1)S(1)}, u32[]{:S(2)}, u32[]{:S(2)}) %collective-permute-start.6) | collective-permute-done | bytes 98336 | tf_op jit(solution)/shard_map/ppermute | solution.py:85
  28.6 0.0 collective-permute-start.11
  28.6 3.2 %collective-permute-start.10 = (bf16[96,512]{1,0:T(8,128)(2,1)S(1)}, bf16[96,512]{1,0:T(8,128)(2,1)S(1)}, u32[]{:S(2)}, u32[]{:S(2)}) collective-permute-start(bf16[96,512]{1,0:T(8,128)(2,1)S(1)} %get-tuple-element.49), channel_id=1, source_target_pairs={{0,12},{1,13},{2,14},{3,15},{4,8},{5,9},{6,10},{7,11},{8,4},{9,5},... | collective-permute-start | bytes 294920 | tf_op jit(solution)/shard_map/ppermute | solution.py:85
  31.9 0.7 %shard_map.62 = (bf16[48,512]{1,0:T(8,128)(2,1)S(1)}, bf16[48,512]{1,0:T(8,128)(2,1)S(1)}, bf16[48,512]{1,0:T(8,128)(2,1)S(1)}, bf16[48,512]{1,0:T(8,128)(2,1)S(1)}) custom-call(s32[1]{0:T(128)} %bitcast.me_ref, bf16[784,128]{1,0:T(8,128)(2,1)S(1)} %collective-permute-done.1.refs_0_, bf16[784,128]{1,0:T(8,128)(2,1)S(1)} %collective-permute-done.2.refs_1_, ...), custom_call_target="tpu_custom_call" | custom-call | bytes 1 | tf_op jit(solution)/shard_map/pallas_call | solution.py:286
  32.6 0.0 collective-permute-done.11.refs_5_
  32.6 0.8 %shard_map.63 = (bf16[96,512]{1,0:T(8,128)(2,1)S(1)}, bf16[96,512]{1,0:T(8,128)(2,1)S(1)}, bf16[96,512]{1,0:T(8,128)(2,1)S(1)}, bf16[96,512]{1,0:T(8,128)(2,1)S(1)}) custom-call(s32[1]{0:T(128)} %bitcast.me_ref, bf16[784,128]{1,0:T(8,128)(2,1)S(1)} %collective-permute-done.1.refs_0_, bf16[784,128]{1,0:T(8,128)(2,1)S(1)} %collective-permute-done.2.refs_1_, ...), custom_call_target="tpu_custom_call" | custom-call | bytes 1 | tf_op jit(solution)/shard_map/pallas_call | solution.py:286
  33.4 0.8 %collective-permute-start.12 = (bf16[96,512]{1,0:T(8,128)(2,1)S(1)}, bf16[96,512]{1,0:T(8,128)(2,1)S(1)}, u32[]{:S(2)}, u32[]{:S(2)}) collective-permute-start(bf16[96,512]{1,0:T(8,128)(2,1)S(1)} %get-tuple-element.59), channel_id=1, source_target_pairs={{0,8},{1,9},{2,10},{3,11},{4,12},{5,13},{6,14},{7,15},{8,0},{9,1},... | collective-permute-start | bytes 294920 | tf_op jit(solution)/shard_map/ppermute | solution.py:85
  34.2 1.7 %collective-permute-start.13 = (bf16[96,512]{1,0:T(8,128)(2,1)S(1)}, bf16[96,512]{1,0:T(8,128)(2,1)S(1)}, u32[]{:S(2)}, u32[]{:S(2)}) collective-permute-start(bf16[96,512]{1,0:T(8,128)(2,1)S(1)} %get-tuple-element.60), channel_id=1, source_target_pairs={{0,4},{1,5},{2,6},{3,7},{4,0},{5,1},{6,2},{7,3},{8,12},{9,13},{10,... | collective-permute-start | bytes 294920 | tf_op jit(solution)/shard_map/ppermute | solution.py:85
  35.9 1.9 %collective-permute-start.14 = (bf16[96,512]{1,0:T(8,128)(2,1)S(1)}, bf16[96,512]{1,0:T(8,128)(2,1)S(1)}, u32[]{:S(2)}, u32[]{:S(2)}) collective-permute-start(bf16[96,512]{1,0:T(8,128)(2,1)S(1)} %get-tuple-element.61), channel_id=1, source_target_pairs={{0,12},{1,13},{2,14},{3,15},{4,8},{5,9},{6,10},{7,11},{8,4},{9,5},... | collective-permute-start | bytes 294920 | tf_op jit(solution)/shard_map/ppermute | solution.py:85
  37.9 0.0 collective-permute-done.10.refs_1_
  37.9 5.2 %collective-permute-done.12.refs_4_ = bf16[96,512]{1,0:T(8,128)(2,1)S(1)} collective-permute-done((bf16[96,512]{1,0:T(8,128)(2,1)S(1)}, bf16[96,512]{1,0:T(8,128)(2,1)S(1)}, u32[]{:S(2)}, u32[]{:S(2)}) %collective-permute-start.12) | collective-permute-done | bytes 98336 | tf_op jit(solution)/shard_map/ppermute | solution.py:85
  43.1 0.0 collective-permute-done.13.refs_5_
  43.1 0.0 collective-permute-done.14.refs_6_
  43.1 1.0 %shard_map.64 = bf16[128,1536]{1,0:T(8,128)(2,1)} custom-call(bf16[3,128,256]{2,1,0:T(8,128)(2,1)S(1)} %shard_map.61.select_ref, bf16[96,512]{1,0:T(8,128)(2,1)S(1)} %collective-permute-done.5.refs_0_, bf16[96,512]{1,0:T(8,128)(2,1)S(1)} %collective-permute-done.10.refs_1_, bf16[96,512]{1,0:T(8,128)(2,1)S(1)} %collective-permute-done.6.refs_2_, ...), custom_call_target="tpu_custom_call" | custom-call | bytes 1 | tf_op jit(solution)/shard_map/pallas_call | solution.py:286
  (2 shorter events, 0.0 us)
Async XLA Ops:
  0.0 10.9 %collective-permute-start.4 = (bf16[512,1024]{1,0:T(8,128)(2,1)}, bf16[512,1024]{1,0:T(8,128)(2,1)S(1)}, u32[]{:S(2)}, u32[]{:S(2)}) collective-permute-start(bf16[512,1024]{1,0:T(8,128)(2,1)} %refs_0_.1), channel_id=1, source_target_pairs={{0,1},{1,0},{2,3},{3,2},{4,5},{5,4},{6,7},{7,6},{8,9},{9,8},{10,11... | collective-permute-start | bytes 3145736 | tf_op jit(solution)/shard_map/ppermute | solution.py:85
  0.5 26.9 %collective-permute-start = (bf16[512,1024]{1,0:T(8,128)(2,1)}, bf16[512,1024]{1,0:T(8,128)(2,1)S(1)}, u32[]{:S(2)}, u32[]{:S(2)}) collective-permute-start(bf16[512,1024]{1,0:T(8,128)(2,1)} %refs_0_.1), channel_id=1, source_target_pairs={{0,2},{1,3},{2,0},{3,1},{4,6},{5,7},{6,4},{7,5},{8,10},{9,11},{10,... | collective-permute-start | bytes 3145736 | tf_op jit(solution)/shard_map/ppermute | solution.py:85
  3.0 0.7 %copy-start.2 = (s32[512]{0:T(512)S(1)}, s32[512]{0:T(512)}, u32[]{:S(2)}) copy-start(s32[512]{0:T(512)} %param.9) | copy-start | bytes 6148
  3.0 0.7 %copy-start.3 = (s32[128,1]{0,1:T(1,128)S(1)}, s32[128,1]{0,1:T(1,128)}, u32[]{:S(2)}) copy-start(s32[128,1]{0,1:T(1,128)} %param.7) | copy-start | bytes 1540
  3.0 0.7 %copy-start.4 = (s32[128]{0:T(128)S(1)}, s32[128]{0:T(128)}, u32[]{:S(2)}) copy-start(s32[128]{0:T(128)} %param.8) | copy-start | bytes 1540
  3.8 1.0 %copy-start.1 = (bf16[128,1024]{1,0:T(8,128)(2,1)S(1)}, bf16[128,1024]{1,0:T(8,128)(2,1)}, u32[]{:S(2)}) copy-start(bf16[128,1024]{1,0:T(8,128)(2,1)} %q_ref.1) | copy-start | bytes 786436
  5.2 13.5 %collective-permute-start.1 = (bf16[784,128]{1,0:T(8,128)(2,1)S(1)}, bf16[784,128]{1,0:T(8,128)(2,1)S(1)}, u32[]{:S(2)}, u32[]{:S(2)}) collective-permute-start(bf16[784,128]{1,0:T(8,128)(2,1)S(1)} %get-tuple-element.36), channel_id=1, source_target_pairs={{0,8},{1,9},{2,10},{3,11},{4,12},{5,13},{6,14},{7,15},{8,0},{9,1},... | collective-permute-start | bytes 602120 | tf_op jit(solution)/shard_map/ppermute | solution.py:85
  7.9 10.9 %collective-permute-start.2 = (bf16[784,128]{1,0:T(8,128)(2,1)S(1)}, bf16[784,128]{1,0:T(8,128)(2,1)S(1)}, u32[]{:S(2)}, u32[]{:S(2)}) collective-permute-start(bf16[784,128]{1,0:T(8,128)(2,1)S(1)} %get-tuple-element.37), channel_id=1, source_target_pairs={{0,4},{1,5},{2,6},{3,7},{4,0},{5,1},{6,2},{7,3},{8,12},{9,13},{10,... | collective-permute-start | bytes 602120 | tf_op jit(solution)/shard_map/ppermute | solution.py:85
  9.5 1.2 %collective-permute-start.3 = (bf16[16,512]{1,0:T(8,128)(2,1)S(1)}, bf16[16,512]{1,0:T(8,128)(2,1)S(1)}, u32[]{:S(2)}, u32[]{:S(2)}) collective-permute-start(bf16[16,512]{1,0:T(8,128)(2,1)S(1)} %get-tuple-element.38.one_ref), channel_id=1, source_target_pairs={{0,1},{1,0},{2,3},{3,2},{4,5},{5,4},{6,7},{7,6},{8,9},{9,8},{10,11... | collective-permute-start | bytes 49160 | tf_op jit(solution)/shard_map/ppermute | solution.py:85
  10.7 12.8 %collective-permute-start.7 = (bf16[528,128]{1,0:T(8,128)(2,1)S(1)}, bf16[528,128]{1,0:T(8,128)(2,1)S(1)}, u32[]{:S(2)}, u32[]{:S(2)}) collective-permute-start(bf16[528,128]{1,0:T(8,128)(2,1)S(1)} %get-tuple-element.43), channel_id=1, source_target_pairs={{0,12},{1,13},{2,14},{3,15},{4,8},{5,9},{6,10},{7,11},{8,4},{9,5},... | collective-permute-start | bytes 405512 | tf_op jit(solution)/shard_map/ppermute | solution.py:85
  10.9 1.2 %copy-start = (bf16[512,1024]{1,0:T(8,128)(2,1)S(1)}, bf16[512,1024]{1,0:T(8,128)(2,1)}, u32[]{:S(2)}) copy-start(bf16[512,1024]{1,0:T(8,128)(2,1)} %refs_0_.1) | copy-start | bytes 3145732
  19.6 6.4 %collective-permute-start.8 = (bf16[112,512]{1,0:T(8,128)(2,1)S(1)}, bf16[112,512]{1,0:T(8,128)(2,1)S(1)}, u32[]{:S(2)}, u32[]{:S(2)}) collective-permute-start(bf16[112,512]{1,0:T(8,128)(2,1)S(1)} %get-tuple-element.44), channel_id=1, source_target_pairs={{0,4},{1,5},{2,6},{3,7},{4,0},{5,1},{6,2},{7,3},{8,12},{9,13},{10,... | collective-permute-start | bytes 344072 | tf_op jit(solution)/shard_map/ppermute | solution.py:85
  20.9 7.1 %collective-permute-start.5 = (bf16[96,512]{1,0:T(8,128)(2,1)S(1)}, bf16[96,512]{1,0:T(8,128)(2,1)S(1)}, u32[]{:S(2)}, u32[]{:S(2)}) collective-permute-start(bf16[96,512]{1,0:T(8,128)(2,1)S(1)} %get-tuple-element.41), channel_id=1, source_target_pairs={{0,8},{1,9},{2,10},{3,11},{4,12},{5,13},{6,14},{7,15},{8,0},{9,1},... | collective-permute-start | bytes 294920 | tf_op jit(solution)/shard_map/ppermute | solution.py:85
  23.3 5.3 %collective-permute-start.6 = (bf16[96,512]{1,0:T(8,128)(2,1)S(1)}, bf16[96,512]{1,0:T(8,128)(2,1)S(1)}, u32[]{:S(2)}, u32[]{:S(2)}) collective-permute-start(bf16[96,512]{1,0:T(8,128)(2,1)S(1)} %get-tuple-element.42), channel_id=1, source_target_pairs={{0,4},{1,5},{2,6},{3,7},{4,0},{5,1},{6,2},{7,3},{8,12},{9,13},{10,... | collective-permute-start | bytes 294920 | tf_op jit(solution)/shard_map/ppermute | solution.py:85
  23.4 3.9 %collective-permute-start.9 = (bf16[16,512]{1,0:T(8,128)(2,1)S(1)}, bf16[16,512]{1,0:T(8,128)(2,1)S(1)}, u32[]{:S(2)}, u32[]{:S(2)}) collective-permute-start(bf16[16,512]{1,0:T(8,128)(2,1)S(1)} %shard_map.57.refs_2_.refs_0_), channel_id=1, source_target_pairs={{0,2},{1,3},{2,0},{3,1},{4,6},{5,7},{6,4},{7,5},{8,10},{9,11},{10,... | collective-permute-start | bytes 49160 | tf_op jit(solution)/shard_map/ppermute | solution.py:85
  28.6 4.0 %collective-permute-start.11 = (bf16[512,1024]{1,0:T(8,128)(2,1)S(1)}, bf16[512,1024]{1,0:T(8,128)(2,1)S(1)}, u32[]{:S(2)}, u32[]{:S(2)}) collective-permute-start(bf16[512,1024]{1,0:T(8,128)(2,1)S(1)} %collective-permute-done.refs_5_), channel_id=1, source_target_pairs={{0,1},{1,0},{2,3},{3,2},{4,5},{5,4},{6,7},{7,6},{8,9},{9,8},{10,11... | collective-permute-start | bytes 3145736 | tf_op jit(solution)/shard_map/ppermute | solution.py:85
  28.6 9.2 %collective-permute-start.10 = (bf16[96,512]{1,0:T(8,128)(2,1)S(1)}, bf16[96,512]{1,0:T(8,128)(2,1)S(1)}, u32[]{:S(2)}, u32[]{:S(2)}) collective-permute-start(bf16[96,512]{1,0:T(8,128)(2,1)S(1)} %get-tuple-element.49), channel_id=1, source_target_pairs={{0,12},{1,13},{2,14},{3,15},{4,8},{5,9},{6,10},{7,11},{8,4},{9,5},... | collective-permute-start | bytes 294920 | tf_op jit(solution)/shard_map/ppermute | solution.py:85
  33.4 9.6 %collective-permute-start.12 = (bf16[96,512]{1,0:T(8,128)(2,1)S(1)}, bf16[96,512]{1,0:T(8,128)(2,1)S(1)}, u32[]{:S(2)}, u32[]{:S(2)}) collective-permute-start(bf16[96,512]{1,0:T(8,128)(2,1)S(1)} %get-tuple-element.59), channel_id=1, source_target_pairs={{0,8},{1,9},{2,10},{3,11},{4,12},{5,13},{6,14},{7,15},{8,0},{9,1},... | collective-permute-start | bytes 294920 | tf_op jit(solution)/shard_map/ppermute | solution.py:85
  34.2 8.9 %collective-permute-start.13 = (bf16[96,512]{1,0:T(8,128)(2,1)S(1)}, bf16[96,512]{1,0:T(8,128)(2,1)S(1)}, u32[]{:S(2)}, u32[]{:S(2)}) collective-permute-start(bf16[96,512]{1,0:T(8,128)(2,1)S(1)} %get-tuple-element.60), channel_id=1, source_target_pairs={{0,4},{1,5},{2,6},{3,7},{4,0},{5,1},{6,2},{7,3},{8,12},{9,13},{10,... | collective-permute-start | bytes 294920 | tf_op jit(solution)/shard_map/ppermute | solution.py:85
  35.9 7.1 %collective-permute-start.14 = (bf16[96,512]{1,0:T(8,128)(2,1)S(1)}, bf16[96,512]{1,0:T(8,128)(2,1)S(1)}, u32[]{:S(2)}, u32[]{:S(2)}) collective-permute-start(bf16[96,512]{1,0:T(8,128)(2,1)S(1)} %get-tuple-element.61), channel_id=1, source_target_pairs={{0,12},{1,13},{2,14},{3,15},{4,8},{5,9},{6,10},{7,11},{8,4},{9,5},... | collective-permute-start | bytes 294920 | tf_op jit(solution)/shard_map/ppermute | solution.py:85
